TPU v7x, 32 devices: a whole 2x2x4 slice. The times are simulated.
32 devices in a mesh: row: 4 (over x, core), col: 8 (over z, y).
Axes of the slice: x: 2, y: 2, z: 4, core: 2. Of those that a mesh axis runs over, the one named last changes fastest.
Arguments:
- pair: bfloat16 [64, 64, 128], P('row', 'col'), may hold values from -6 to 6
- pair_mask: int32 [64, 64], P('row', 'col'), may hold values 0 or 1
- contact_mask: int32 [64, 64], P('row', 'col'), may hold values 0 or 1
- dilations: int32 [2], replicated, may hold values from 1 to 8, as said below
- w_proj: bfloat16 [128, 512], replicated, may hold values from -0.5 to 0.5
- w_gate: bfloat16 [128, 128], replicated, may hold values from -0.5 to 0.5
- w_out: bfloat16 [128, 128], replicated, may hold values from -0.5 to 0.5
- conv_one: bfloat16 [9, 128, 128], replicated, may hold values from -0.1875 to 0.1875
- conv_two: bfloat16 [9, 128, 128], replicated, may hold values from -0.1875 to 0.1875
- cotangent: bfloat16 [64, 64, 128], P('row', 'col'), may hold values from -6 to 6
Outputs:
- output: bfloat16 [64, 64, 128], P('row', 'col')
- grad_pair: bfloat16 [64, 64, 128], P('row', 'col')
- grad_one: float32 [9, 128, 128], replicated
- grad_two: float32 [9, 128, 128], replicated
Inputs may be any that keep to these rules, and one draw needn't show every extreme that they name: `dilations`: one of the two rates equals 8, the other is smaller.
All inputs are finite; a program needn't handle non-finite values. No bound on the sum of `pair_mask` or of `contact_mask` on one device may be relied on, other than what follows from the above.
Results may differ from a plain program's by a relative error of at most 0.015.
Values may be sent and summed in bfloat16 or wider, within the bound.
No kernel may reach another device: no remote copies, remote signals or barrier semaphores. Data moves between devices by JAX's collectives and lax.ppermute only.
A program may use at most 64 MiB of HBM per device.

v0:
```python
import jax
import jax.numpy as jnp
from jax import lax
from jax.sharding import PartitionSpec as P

DMAX = 8


EPSILON = 1e-05


def with_halo(block, sides, width):
    for axis, dim in sides:
        count = lax.axis_size(axis)
        forward = [(i, i + 1) for i in range(count - 1)]
        backward = [(target, source) for source, target in forward]
        low = lax.ppermute(
            lax.slice_in_dim(block, block.shape[dim] - width, None, axis=dim), axis, forward
        )
        high = lax.ppermute(lax.slice_in_dim(block, 0, width, axis=dim), axis, backward)
        block = jnp.concatenate([low, block, high], axis=dim)
    return block


def broadcast(x, axis, root):
    mine = lax.axis_index(axis) == root
    return lax.psum(jnp.where(mine, x, jnp.zeros_like(x)), axis)


def layer_norm(values):
    centre = values - jnp.mean(values, axis=-1, keepdims=True)
    spread = jnp.mean(centre * centre, axis=-1, keepdims=True)
    return centre * lax.rsqrt(spread + EPSILON)


def with_rim(field):
    return with_halo(field, (("row", 0), ("col", 1)), DMAX)


def gather_taps(padded, dilation, mirrored, height, breadth):
    windows = []
    for tap_index in range(9):
        row_tap = tap_index // 3
        col_tap = tap_index % 3
        if mirrored:
            row_tap = 2 - row_tap
            col_tap = 2 - col_tap
        row_start = DMAX + (row_tap - 1) * dilation
        col_start = DMAX + (col_tap - 1) * dilation
        windows.append(
            lax.dynamic_slice(
                padded, (row_start, col_start, jnp.int32(0)), (height, breadth, padded.shape[2])
            )
        )
    return jnp.concatenate(windows, axis=2).reshape(height * breadth, -1)


def local(
    pair, pair_mask, contact_mask, dilations, w_proj, w_gate, w_out, conv_one, conv_two, cotangent
):
    height, breadth, channels = pair.shape
    hidden = w_out.shape[0]
    row_count = lax.axis_size("row")
    col_count = lax.axis_size("col")
    ratio = col_count // row_count
    row_place = lax.axis_index("row")
    col_place = lax.axis_index("col")
    tokens = breadth * col_count
    pixels = height * breadth
    pair_flat = pair.astype(jnp.float32).reshape(pixels, channels)
    normed = layer_norm(pair_flat).astype(jnp.bfloat16)
    projected = jnp.dot(normed, w_proj, preferred_element_type=jnp.float32)
    mask_col = pair_mask.reshape(pixels, 1).astype(jnp.float32)
    left_side = (
        (mask_col * jax.nn.sigmoid(projected[:, hidden : 2 * hidden]) * projected[:, :hidden])
        .astype(jnp.bfloat16)
        .reshape(height, breadth, hidden)
    )
    right_side = (
        (
            mask_col
            * jax.nn.sigmoid(projected[:, 3 * hidden :])
            * projected[:, 2 * hidden : 3 * hidden]
        )
        .astype(jnp.bfloat16)
        .reshape(height, breadth, hidden)
    )
    right_all = lax.all_gather(right_side, "col", axis=1, tiled=True)
    offset = jnp.clip(col_place * breadth - row_place * height, 0, height - breadth)
    right_local = lax.dynamic_slice_in_dim(right_all, offset, breadth, 0)
    right_rows = broadcast(right_local, "row", col_place // ratio)
    products = jnp.einsum(
        "ikh,jkh->ijh",
        lax.all_gather(left_side, "col", axis=1, tiled=True),
        right_rows,
        preferred_element_type=jnp.float32,
    )
    product_norm = layer_norm(products.reshape(pixels, hidden)).astype(jnp.bfloat16)
    gating = jax.nn.sigmoid(jnp.dot(normed, w_gate, preferred_element_type=jnp.float32))
    updated = (
        pair_flat + gating * jnp.dot(product_norm, w_out, preferred_element_type=jnp.float32)
    ).astype(jnp.bfloat16)
    updated_f = updated.astype(jnp.float32)
    centre = updated_f - jnp.mean(updated_f, axis=-1, keepdims=True)
    inv_spread = lax.rsqrt(jnp.mean(centre * centre, axis=-1, keepdims=True) + EPSILON)
    scaled = centre * inv_spread
    contact = contact_mask.reshape(pixels, 1).astype(jnp.float32)
    first_in = (scaled * contact).astype(jnp.bfloat16).reshape(height, breadth, channels)
    rate_one = dilations[0]
    rate_two = dilations[1]
    first_taps = gather_taps(with_rim(first_in), rate_one, False, height, breadth)
    first_pre = jnp.dot(
        first_taps, conv_one.reshape(9 * channels, channels), preferred_element_type=jnp.float32
    )
    sigma = jax.nn.sigmoid(first_pre)
    second_in = (first_pre * sigma).astype(jnp.bfloat16).reshape(height, breadth, channels)
    second_taps = gather_taps(with_rim(second_in), rate_two, False, height, breadth)
    second_pre = jnp.dot(
        second_taps, conv_two.reshape(9 * channels, channels), preferred_element_type=jnp.float32
    )
    output = (updated_f + second_pre).astype(jnp.bfloat16).reshape(height, breadth, channels)
    cot_flat = cotangent.reshape(pixels, channels)
    grad_two = (
        lax.dot_general(
            second_taps, cot_flat, (((0,), (0,)), ((), ())), preferred_element_type=jnp.float32
        ).reshape(9, channels, channels)
        / tokens
    )
    cot_taps = gather_taps(with_rim(cotangent), rate_two, True, height, breadth)
    grad_hidden = jnp.dot(
        cot_taps,
        conv_two.transpose(0, 2, 1).reshape(9 * channels, channels),
        preferred_element_type=jnp.float32,
    )
    grad_pre = (grad_hidden * sigma * (1.0 + first_pre * (1.0 - sigma))).astype(jnp.bfloat16)
    grad_one = (
        lax.dot_general(
            first_taps, grad_pre, (((0,), (0,)), ((), ())), preferred_element_type=jnp.float32
        ).reshape(9, channels, channels)
        / tokens
    )
    grad_taps = gather_taps(
        with_rim(grad_pre.reshape(height, breadth, channels)), rate_one, True, height, breadth
    )
    grad_input = (
        jnp.dot(
            grad_taps,
            conv_one.transpose(0, 2, 1).reshape(9 * channels, channels),
            preferred_element_type=jnp.float32,
        )
        * contact
    )
    grad_norm = inv_spread * (
        grad_input
        - jnp.mean(grad_input, axis=-1, keepdims=True)
        - scaled * jnp.mean(grad_input * scaled, axis=-1, keepdims=True)
    )
    grad_pair = (
        (cot_flat.astype(jnp.float32) + grad_norm)
        .astype(jnp.bfloat16)
        .reshape(height, breadth, channels)
    )
    grad_one, grad_two = lax.psum((grad_one, grad_two), ("row", "col"))
    return (output, grad_pair, grad_one, grad_two)


def solution(mesh):
    in_specs = (
        P("row", "col", None),
        P("row", "col"),
        P("row", "col"),
        P(),
        P(),
        P(),
        P(),
        P(),
        P(),
        P("row", "col", None),
    )
    out_specs = (P("row", "col", None), P("row", "col", None), P(), P())
    return jax.shard_map(local, mesh=mesh, in_specs=in_specs, out_specs=out_specs, check_vma=False)
```

profile of v0, /device:TPU:0, one launch (start us, length us, event | category | flops | bytes accessed | tf_op | source)
XLA Modules:
  0.0 300.1 jit_solution(10007885213145601419)
XLA Ops:
  7.3 0.9 convert_reduce_fusion
  8.1 0.9 fusion.15
  9.1 0.1 div.55
  9.2 0.1 rsqrt.31
  9.3 0.7 convert_element_type.63
  10.0 0.1 copy.46
  10.0 0.1 convert_element_type.64
  10.1 1.0 fusion.36
  11.1 0.1 fusion.35
  11.2 32.5 %all_gather.6 = bf16[16,64,128]{2,0,1:T(8,128)(2,1)S(1)} all-gather(bf16[16,8,128]{2,0,1:T(8,128)(2,1)S(1)} %copy.47), channel_id=1, replica_groups=mesh['row'=4,'col'=8] {'col'}, dimensions={1}, use_global_device_ids=true | all-gather | bytes 294912 | tf_op jit(solution)/shard_map/all_gather | solution.py:88
  43.8 0.2 copy.59
  44.1 0.7 broadcast_select_fusion
  44.9 1.3 collective-permute-start.8
  46.2 1.3 collective-permute-start.9
  47.5 0.2 fusion.3
  47.8 0.2 copy.49
  48.0 45.0 %all_gather.7 = bf16[16,64,128]{0,1,2:T(8,128)(2,1)S(1)} all-gather(bf16[16,8,128]{0,1,2:T(8,128)(2,1)S(1)} %copy.49), channel_id=1, replica_groups=mesh['row'=4,'col'=8] {'col'}, dimensions={1}, use_global_device_ids=true | all-gather | bytes 294912 | tf_op jit(solution)/shard_map/all_gather | solution.py:94
  93.0 0.6 fusion.41
  98.8 0.1 copy.54
  98.8 0.1 convert_element_type.71
  99.0 0.9 copy.55
  99.9 0.2 copy.56
  100.2 1.3 collective-permute-start.11
  101.5 5.2 %collective-permute-start.10 = (bf16[32,8,128]{2,1,0:T(8,128)(2,1)S(1)}, bf16[32,8,128]{2,1,0:T(8,128)(2,1)}, u32[]{:S(2)}, u32[]{:S(2)}) collective-permute-start(bf16[32,8,128]{2,1,0:T(8,128)(2,1)S(1)} %constant_dynamic-update-slice_fusion.18), channel_id=1, source_target_pairs={{0,1},{1,2},{2,3},{3,4},{4,5},{5,6},{6,7},{8,9},{9,10},{10,11},{11... | collective-permute-start | bytes 196616 | tf_op jit(solution)/shard_map/ppermute | solution.py:17
  106.6 1.6 fusion.42
  108.2 0.1 copy.51
  108.4 0.1 div.64
  108.5 0.2 copy.50
  108.7 0.1 multiply_reduce_fusion
  108.9 0.1 copy.53
  108.9 0.1 rsqrt.33
  109.0 1.1 fusion.43
  110.1 0.2 multiply_reduce_fusion.2
  110.3 0.1 multiply_convert_fusion.1
  110.4 1.3 collective-permute-start.1
  111.7 3.0 %collective-permute-start = (bf16[8,8,128]{2,1,0:T(8,128)(2,1)S(1)}, bf16[8,8,128]{2,1,0:T(8,128)(2,1)S(1)}, u32[]{:S(2)}, u32[]{:S(2)}) collective-permute-start(bf16[8,8,128]{2,1,0:T(8,128)(2,1)S(1)} %get-tuple-element.16), channel_id=1, source_target_pairs={{0,8},{8,16},{16,24},{1,9},{9,17},{17,25},{2,10},{10,18},{18,26},{... | collective-permute-start | bytes 49160 | tf_op jit(solution)/shard_map/ppermute | solution.py:17
  114.8 0.1 fusion.58
  114.9 0.7 collective-permute-done
  115.6 1.3 collective-permute-start.3
  116.9 4.5 %collective-permute-start.2 = (bf16[32,8,128]{2,1,0:T(8,128)(2,1)S(1)}, bf16[32,8,128]{2,1,0:T(8,128)(2,1)S(1)}, u32[]{:S(2)}, u32[]{:S(2)}) collective-permute-start(bf16[32,8,128]{2,1,0:T(8,128)(2,1)S(1)} %pad_maximum_fusion.4), channel_id=1, source_target_pairs={{0,1},{1,2},{2,3},{3,4},{4,5},{5,6},{6,7},{8,9},{9,10},{10,11},{11... | collective-permute-start | bytes 196616 | tf_op jit(solution)/shard_map/ppermute | solution.py:17
  121.5 0.9 pad_maximum_fusion.2
  122.7 0.6 collective-permute-done.2
  123.5 0.1 constant_dynamic-update-slice_fusion.4
  123.8 0.2 multiply_convert_fusion
  124.1 1.3 collective-permute-start.5
  125.4 5.0 %collective-permute-start.4 = (bf16[8,8,128]{2,1,0:T(8,128)(2,1)S(1)}, bf16[8,8,128]{2,1,0:T(8,128)(2,1)S(1)}, u32[]{:S(2)}, u32[]{:S(2)}) collective-permute-start(bf16[8,8,128]{2,1,0:T(8,128)(2,1)S(1)} %get-tuple-element.14), channel_id=1, source_target_pairs={{0,8},{8,16},{16,24},{1,9},{9,17},{17,25},{2,10},{10,18},{18,26},{... | collective-permute-start | bytes 49160 | tf_op jit(solution)/shard_map/ppermute | solution.py:17
  130.4 0.2 fusion.6
  130.7 1.3 collective-permute-start.13
  132.0 6.0 %collective-permute-start.12 = (bf16[8,8,128]{2,1,0:T(8,128)(2,1)S(1)}, bf16[8,8,128]{2,1,0:T(8,128)(2,1)S(1)}, u32[]{:S(2)}, u32[]{:S(2)}) collective-permute-start(bf16[8,8,128]{2,1,0:T(8,128)(2,1)S(1)} %get-tuple-element.10), channel_id=1, source_target_pairs={{0,8},{8,16},{16,24},{1,9},{9,17},{17,25},{2,10},{10,18},{18,26},{... | collective-permute-start | bytes 49160 | tf_op jit(solution)/shard_map/ppermute | solution.py:17
  138.0 0.2 copy.57
  138.2 1.0 convolution_multiply_fusion.1
  139.2 1.3 collective-permute-start.7
  140.5 4.9 %collective-permute-start.6 = (bf16[32,8,128]{2,1,0:T(8,128)(2,1)S(1)}, bf16[32,8,128]{2,1,0:T(8,128)(2,1)S(1)}, u32[]{:S(2)}, u32[]{:S(2)}) collective-permute-start(bf16[32,8,128]{2,1,0:T(8,128)(2,1)S(1)} %pad_maximum_fusion.5), channel_id=1, source_target_pairs={{0,1},{1,2},{2,3},{3,4},{4,5},{5,6},{6,7},{8,9},{9,10},{10,11},{11... | collective-permute-start | bytes 196616 | tf_op jit(solution)/shard_map/ppermute | solution.py:17
  145.5 1.3 collective-permute-start.15
  146.8 5.8 %collective-permute-start.14 = (bf16[32,8,128]{2,1,0:T(8,128)(2,1)S(1)}, bf16[32,8,128]{2,1,0:T(8,128)(2,1)S(1)}, u32[]{:S(2)}, u32[]{:S(2)}) collective-permute-start(bf16[32,8,128]{2,1,0:T(8,128)(2,1)S(1)} %pad_maximum_fusion.6), channel_id=1, source_target_pairs={{0,1},{1,2},{2,3},{3,4},{4,5},{5,6},{6,7},{8,9},{9,10},{10,11},{11... | collective-permute-start | bytes 196616 | tf_op jit(solution)/shard_map/ppermute | solution.py:17
  152.9 2.3 collective-permute-done.14
  155.6 0.2 copy.58
  155.9 1.0 convolution_multiply_fusion
  156.9 0.3 fusion.39
  157.3 0.8 fusion.9
  158.1 0.8 fusion.28
  158.9 130.5 %all-reduce.6.cloned.1.call-done = (f32[9,128,128]{2,1,0:T(8,128)}, f32[9,128,128]{2,1,0:T(8,128)}) async-done(((f32[9,128,128]{2,1,0:T(8,128)}, f32[9,128,128]{2,1,0:T(8,128)}), (f32[9,128,128]{2,1,0:T(8,128)}, f32[9,128,128]{2,1,0:T(8,128)})) %all-reduce.6.cloned.1.call-update) | async-done | bytes 1179664 | tf_op jit(solution)/shard_map/psum | solution.py:163
  289.4 1.9 copy.97
  291.3 1.9 copy.98
  (97 shorter events, 1.6 us)
Async XLA Ops:
  7.2 3.0 copy-start
  7.2 40.3 %copy-start.3 = (bf16[16,8,128]{2,1,0:T(8,128)(2,1)S(1)}, bf16[16,8,128]{2,1,0:T(8,128)(2,1)}, u32[]{:S(2)}) copy-start(bf16[16,8,128]{2,1,0:T(8,128)(2,1)} %param.10) | copy-start | bytes 98308
  7.2 37.7 %copy-start.2 = (bf16[16,8,128]{2,1,0:T(8,128)(2,1)S(1)}, bf16[16,8,128]{2,1,0:T(8,128)(2,1)}, u32[]{:S(2)}) copy-start(bf16[16,8,128]{2,1,0:T(8,128)(2,1)} %param.19) | copy-start | bytes 98308
  7.2 40.3 %copy-start.9 = (bf16[128,128]{1,0:T(8,128)(2,1)S(1)}, bf16[128,128]{1,0:T(8,128)(2,1)}, u32[]{:S(2)}) copy-start(bf16[128,128]{1,0:T(8,128)(2,1)} %param.15) | copy-start | bytes 98308
  7.2 99.4 %all-reduce.4.cloned.1.call-start = ((), (), s32[]{:S(2)}) async-start(), calls=%async_computation | async-start | bytes 524288 | tf_op jit(solution)/shard_map/psum | solution.py:27
  43.8 49.2 %copy-start.8 = (s32[2]{0:T(128)S(1)}, s32[2]{0:T(128)}, u32[]{:S(2)}) copy-start(s32[2]{0:T(128)} %param.13) | copy-start | bytes 28
  43.8 54.9 %copy-start.7 = (s32[16,8]{0,1:T(8,128)S(1)}, s32[16,8]{0,1:T(8,128)}, u32[]{:S(2)}) copy-start(s32[16,8]{0,1:T(8,128)} %param.12) | copy-start | bytes 1540
  44.1 54.9 %copy-start.1 = (bf16[9,128,128]{2,1,0:T(8,128)(2,1)S(1)}, bf16[9,128,128]{2,1,0:T(8,128)(2,1)}, u32[]{:S(2)}) copy-start(bf16[9,128,128]{2,1,0:T(8,128)(2,1)} %param.18) | copy-start | bytes 884740
  44.8 55.1 %copy-start.4 = (bf16[9,128,128]{2,1,0:T(8,128)(2,1)S(1)}, bf16[9,128,128]{2,1,0:T(8,128)(2,1)}, u32[]{:S(2)}) copy-start(bf16[9,128,128]{2,1,0:T(8,128)(2,1)} %param.17) | copy-start | bytes 884740
  44.8 244.6 %all-reduce.6.cloned.1.call-start = ((), (), s32[]{:S(2)}) async-start(), calls=%async_computation.1 | async-start | bytes 2359296 | tf_op jit(solution)/shard_map/psum | solution.py:163
  44.9 55.2 %collective-permute-start.8 = (bf16[8,8,128]{2,1,0:T(8,128)(2,1)S(1)}, bf16[8,8,128]{2,1,0:T(8,128)(2,1)S(1)}, u32[]{:S(2)}, u32[]{:S(2)}) collective-permute-start(bf16[8,8,128]{2,1,0:T(8,128)(2,1)S(1)} %get-tuple-element.13), channel_id=1, source_target_pairs={{0,8},{8,16},{16,24},{1,9},{9,17},{17,25},{2,10},{10,18},{18,26},{... | collective-permute-start | bytes 49160 | tf_op jit(solution)/shard_map/ppermute | solution.py:17
  46.2 53.9 %collective-permute-start.9 = (bf16[8,8,128]{2,1,0:T(8,128)(2,1)S(1)}, bf16[8,8,128]{2,1,0:T(8,128)(2,1)S(1)}, u32[]{:S(2)}, u32[]{:S(2)}) collective-permute-start(bf16[8,8,128]{2,1,0:T(8,128)(2,1)S(1)} %get-tuple-element.12), channel_id=1, source_target_pairs={{8,0},{16,8},{24,16},{9,1},{17,9},{25,17},{10,2},{18,10},{26,18},{... | collective-permute-start | bytes 49160 | tf_op jit(solution)/shard_map/ppermute | solution.py:20
  100.2 21.3 %collective-permute-start.11 = (bf16[32,8,128]{2,1,0:T(8,128)(2,1)S(1)}, bf16[32,8,128]{2,1,0:T(8,128)(2,1)}, u32[]{:S(2)}, u32[]{:S(2)}) collective-permute-start(bf16[32,8,128]{2,1,0:T(8,128)(2,1)S(1)} %constant_dynamic-update-slice_fusion.18), channel_id=1, source_target_pairs={{1,0},{2,1},{3,2},{4,3},{5,4},{6,5},{7,6},{9,8},{10,9},{11,10},{12... | collective-permute-start | bytes 196616 | tf_op jit(solution)/shard_map/ppermute | solution.py:20
  101.5 20.0 %collective-permute-start.10 = (bf16[32,8,128]{2,1,0:T(8,128)(2,1)S(1)}, bf16[32,8,128]{2,1,0:T(8,128)(2,1)}, u32[]{:S(2)}, u32[]{:S(2)}) collective-permute-start(bf16[32,8,128]{2,1,0:T(8,128)(2,1)S(1)} %constant_dynamic-update-slice_fusion.18), channel_id=1, source_target_pairs={{0,1},{1,2},{2,3},{3,4},{4,5},{5,6},{6,7},{8,9},{9,10},{10,11},{11... | collective-permute-start | bytes 196616 | tf_op jit(solution)/shard_map/ppermute | solution.py:17
  108.2 15.6 %copy-start.5 = (bf16[9,128,128]{2,1,0:T(8,128)(2,1)S(1)}, bf16[9,128,128]{2,1,0:T(8,128)(2,1)}, u32[]{:S(2)}) copy-start(bf16[9,128,128]{2,1,0:T(8,128)(2,1)} %param.17) | copy-start | bytes 884740
  108.7 21.7 %copy-start.6 = (bf16[9,128,128]{1,2,0:T(8,128)(2,1)S(1)}, bf16[9,128,128]{1,2,0:T(8,128)(2,1)}, u32[]{:S(2)}) copy-start(bf16[9,128,128]{1,2,0:T(8,128)(2,1)} %copy.55) | copy-start | bytes 884740
  110.4 4.5 %collective-permute-start.1 = (bf16[8,8,128]{2,1,0:T(8,128)(2,1)S(1)}, bf16[8,8,128]{2,1,0:T(8,128)(2,1)S(1)}, u32[]{:S(2)}, u32[]{:S(2)}) collective-permute-start(bf16[8,8,128]{2,1,0:T(8,128)(2,1)S(1)} %get-tuple-element.17), channel_id=1, source_target_pairs={{8,0},{16,8},{24,16},{9,1},{17,9},{25,17},{10,2},{18,10},{26,18},{... | collective-permute-start | bytes 49160 | tf_op jit(solution)/shard_map/ppermute | solution.py:20
  111.7 3.9 %collective-permute-start = (bf16[8,8,128]{2,1,0:T(8,128)(2,1)S(1)}, bf16[8,8,128]{2,1,0:T(8,128)(2,1)S(1)}, u32[]{:S(2)}, u32[]{:S(2)}) collective-permute-start(bf16[8,8,128]{2,1,0:T(8,128)(2,1)S(1)} %get-tuple-element.16), channel_id=1, source_target_pairs={{0,8},{8,16},{16,24},{1,9},{9,17},{17,25},{2,10},{10,18},{18,26},{... | collective-permute-start | bytes 49160 | tf_op jit(solution)/shard_map/ppermute | solution.py:17
  115.6 7.1 %collective-permute-start.3 = (bf16[32,8,128]{2,1,0:T(8,128)(2,1)S(1)}, bf16[32,8,128]{2,1,0:T(8,128)(2,1)S(1)}, u32[]{:S(2)}, u32[]{:S(2)}) collective-permute-start(bf16[32,8,128]{2,1,0:T(8,128)(2,1)S(1)} %pad_maximum_fusion.4), channel_id=1, source_target_pairs={{1,0},{2,1},{3,2},{4,3},{5,4},{6,5},{7,6},{9,8},{10,9},{11,10},{12... | collective-permute-start | bytes 196616 | tf_op jit(solution)/shard_map/ppermute | solution.py:20
  116.9 6.4 %collective-permute-start.2 = (bf16[32,8,128]{2,1,0:T(8,128)(2,1)S(1)}, bf16[32,8,128]{2,1,0:T(8,128)(2,1)S(1)}, u32[]{:S(2)}, u32[]{:S(2)}) collective-permute-start(bf16[32,8,128]{2,1,0:T(8,128)(2,1)S(1)} %pad_maximum_fusion.4), channel_id=1, source_target_pairs={{0,1},{1,2},{2,3},{3,4},{4,5},{5,6},{6,7},{8,9},{9,10},{10,11},{11... | collective-permute-start | bytes 196616 | tf_op jit(solution)/shard_map/ppermute | solution.py:17
  124.1 15.1 %collective-permute-start.5 = (bf16[8,8,128]{2,1,0:T(8,128)(2,1)S(1)}, bf16[8,8,128]{2,1,0:T(8,128)(2,1)S(1)}, u32[]{:S(2)}, u32[]{:S(2)}) collective-permute-start(bf16[8,8,128]{2,1,0:T(8,128)(2,1)S(1)} %get-tuple-element.15), channel_id=1, source_target_pairs={{8,0},{16,8},{24,16},{9,1},{17,9},{25,17},{10,2},{18,10},{26,18},{... | collective-permute-start | bytes 49160 | tf_op jit(solution)/shard_map/ppermute | solution.py:20
  125.4 13.8 %collective-permute-start.4 = (bf16[8,8,128]{2,1,0:T(8,128)(2,1)S(1)}, bf16[8,8,128]{2,1,0:T(8,128)(2,1)S(1)}, u32[]{:S(2)}, u32[]{:S(2)}) collective-permute-start(bf16[8,8,128]{2,1,0:T(8,128)(2,1)S(1)} %get-tuple-element.14), channel_id=1, source_target_pairs={{0,8},{8,16},{16,24},{1,9},{9,17},{17,25},{2,10},{10,18},{18,26},{... | collective-permute-start | bytes 49160 | tf_op jit(solution)/shard_map/ppermute | solution.py:17
  130.7 14.8 %collective-permute-start.13 = (bf16[8,8,128]{2,1,0:T(8,128)(2,1)S(1)}, bf16[8,8,128]{2,1,0:T(8,128)(2,1)S(1)}, u32[]{:S(2)}, u32[]{:S(2)}) collective-permute-start(bf16[8,8,128]{2,1,0:T(8,128)(2,1)S(1)} %get-tuple-element.11), channel_id=1, source_target_pairs={{8,0},{16,8},{24,16},{9,1},{17,9},{25,17},{10,2},{18,10},{26,18},{... | collective-permute-start | bytes 49160 | tf_op jit(solution)/shard_map/ppermute | solution.py:20
  132.0 13.5 %collective-permute-start.12 = (bf16[8,8,128]{2,1,0:T(8,128)(2,1)S(1)}, bf16[8,8,128]{2,1,0:T(8,128)(2,1)S(1)}, u32[]{:S(2)}, u32[]{:S(2)}) collective-permute-start(bf16[8,8,128]{2,1,0:T(8,128)(2,1)S(1)} %get-tuple-element.10), channel_id=1, source_target_pairs={{0,8},{8,16},{16,24},{1,9},{9,17},{17,25},{2,10},{10,18},{18,26},{... | collective-permute-start | bytes 49160 | tf_op jit(solution)/shard_map/ppermute | solution.py:17
  139.2 13.3 %collective-permute-start.7 = (bf16[32,8,128]{2,1,0:T(8,128)(2,1)S(1)}, bf16[32,8,128]{2,1,0:T(8,128)(2,1)S(1)}, u32[]{:S(2)}, u32[]{:S(2)}) collective-permute-start(bf16[32,8,128]{2,1,0:T(8,128)(2,1)S(1)} %pad_maximum_fusion.5), channel_id=1, source_target_pairs={{1,0},{2,1},{3,2},{4,3},{5,4},{6,5},{7,6},{9,8},{10,9},{11,10},{12... | collective-permute-start | bytes 196616 | tf_op jit(solution)/shard_map/ppermute | solution.py:20
  140.5 12.0 %collective-permute-start.6 = (bf16[32,8,128]{2,1,0:T(8,128)(2,1)S(1)}, bf16[32,8,128]{2,1,0:T(8,128)(2,1)S(1)}, u32[]{:S(2)}, u32[]{:S(2)}) collective-permute-start(bf16[32,8,128]{2,1,0:T(8,128)(2,1)S(1)} %pad_maximum_fusion.5), channel_id=1, source_target_pairs={{0,1},{1,2},{2,3},{3,4},{4,5},{5,6},{6,7},{8,9},{9,10},{10,11},{11... | collective-permute-start | bytes 196616 | tf_op jit(solution)/shard_map/ppermute | solution.py:17
  145.5 7.5 %collective-permute-start.15 = (bf16[32,8,128]{2,1,0:T(8,128)(2,1)S(1)}, bf16[32,8,128]{2,1,0:T(8,128)(2,1)S(1)}, u32[]{:S(2)}, u32[]{:S(2)}) collective-permute-start(bf16[32,8,128]{2,1,0:T(8,128)(2,1)S(1)} %pad_maximum_fusion.6), channel_id=1, source_target_pairs={{1,0},{2,1},{3,2},{4,3},{5,4},{6,5},{7,6},{9,8},{10,9},{11,10},{12... | collective-permute-start | bytes 196616 | tf_op jit(solution)/shard_map/ppermute | solution.py:20
  146.8 8.5 %collective-permute-start.14 = (bf16[32,8,128]{2,1,0:T(8,128)(2,1)S(1)}, bf16[32,8,128]{2,1,0:T(8,128)(2,1)S(1)}, u32[]{:S(2)}, u32[]{:S(2)}) collective-permute-start(bf16[32,8,128]{2,1,0:T(8,128)(2,1)S(1)} %pad_maximum_fusion.6), channel_id=1, source_target_pairs={{0,1},{1,2},{2,3},{3,4},{4,5},{5,6},{6,7},{8,9},{9,10},{10,11},{11... | collective-permute-start | bytes 196616 | tf_op jit(solution)/shard_map/ppermute | solution.py:17
Sparse Core Ops, SparseCore 0:
  45.0 32.9 all-reduce.3
  157.4 131.9 all-reduce.5
where the time goes:
time: 301 us; the launch traced here: 300 us
  waiting for transfers between devices  134 us (45%)
  blocking collectives  77.6 us (26%)
  starting transfers between devices  46.1 us (15%)
  between operations  20.1 us (7%)
  local copies, waits for them, and re-layouts  8.65 us (3%)
  matrix products  7.62 us (3%)
  other arithmetic  5.82 us (2%)
    psum x1, waiting for transfers between devices, local(): grad_one, grad_two = lax.psum((grad_one, grad_two), ('row', 'col'))  131 us
    all_gather x1, blocking collectives, local(): lax.all_gather(left_side, 'col', axis=1, tiled=True)  45 us
    ppermute x8, starting transfers between devices, with_halo(): lax.ppermute(lax.slice_in_dim(block, block.shape[dim] - width, None, axis...  35.7 us
    all_gather x1, blocking collectives, local(): right_all = lax.all_gather(right_side, 'col', axis=1, tiled=True)  32.5 us
    ppermute x8, starting transfers between devices, with_halo(): lax.ppermute(lax.slice_in_dim(block, 0, width, axis=dim), axis, backward)  10.3 us
    unnamed x58, local copies, waits for them, and re-layouts  6.12 us
  transfers between devices with their start and end apart: 18, of which 4 were waited for; matrix products, arithmetic and copies ran while one was open for 4% of the time, Pallas kernels for 0%

commit v1 on v0

--- a/solution.py
+++ b/solution.py
@@ -1,9 +1,15 @@
+import functools
+
 import jax
 import jax.numpy as jnp
 from jax import lax
+from jax.experimental import pallas as pl
+from jax.experimental.pallas import tpu as pltpu
 from jax.sharding import PartitionSpec as P
 
 DMAX = 8
+MASK_ROWS = 16
+VMEM_LIMIT = 56 * 1024 * 1024
 
 
 EPSILON = 1e-05
@@ -55,7 +61,7 @@
     return jnp.concatenate(windows, axis=2).reshape(height * breadth, -1)
 
 
-def local(
+def sharded(
     pair, pair_mask, contact_mask, dilations, w_proj, w_gate, w_out, conv_one, conv_two, cotangent
 ):
     height, breadth, channels = pair.shape
@@ -164,6 +170,398 @@
     return (output, grad_pair, grad_one, grad_two)
 
 
+def exchange_plan(row_count, col_count):
+    rounds = []
+    distance = col_count // 2
+    while distance:
+        rounds.append(("col", distance))
+        distance //= 2
+    distance = row_count // 2
+    while distance:
+        rounds.append(("row", distance))
+        distance //= 2
+    return rounds
+
+
+def gather_blocks(block, rounds):
+    held = block[None]
+    for step, (axis, distance) in enumerate(rounds):
+        pairs = [(i, i ^ distance) for i in range(lax.axis_size(axis))]
+        other = lax.ppermute(held, axis, pairs)
+        if step < len(rounds) - 1:
+            held = jnp.concatenate([held, other], axis=0)
+    return held, other
+
+
+def place_of(position, rounds, row_place, col_place):
+    row, col = row_place, col_place
+    for step, (axis, distance) in enumerate(rounds):
+        bit = ((position >> step) & 1) * distance
+        if axis == "row":
+            row = row ^ bit
+        else:
+            col = col ^ bit
+    return row, col
+
+
+def sigmoid(values):
+    return 1.0 / (1.0 + jnp.exp(-values))
+
+
+def matmul(left, right):
+    return jnp.dot(left, right, preferred_element_type=jnp.float32)
+
+
+def block_kernel(
+    rounds,
+    height,
+    breadth,
+    tokens,
+    scalars,
+    near,
+    far,
+    cot_all,
+    w_all,
+    w_out,
+    one,
+    one_t,
+    two,
+    two_t,
+    output,
+    grad_pair,
+    grad_one,
+    grad_two,
+    left,
+    right,
+    gating,
+    start,
+    contact,
+    updated,
+    field,
+    wide,
+    wide_cot,
+    second,
+    factor,
+    grad_pre,
+    flipped,
+    flipped_two,
+    sum_one,
+    sum_two,
+):
+    channels = w_out.shape[1]
+    hidden = w_out.shape[0]
+    pixels = height * breadth
+    row_place, col_place = scalars[0], scalars[1]
+    rate_one, rate_two = scalars[2], scalars[3]
+    half = near.shape[0]
+    line = tokens + 2 * DMAX
+
+    rim = jnp.zeros((tokens, DMAX, channels), jnp.float32)
+    field[:, 0:DMAX, :] = rim
+    field[:, DMAX + tokens :, :] = rim
+    edge = jnp.zeros((DMAX, tokens, 3 * channels), jnp.bfloat16)
+    for target in (wide, wide_cot):
+        target[0:DMAX] = edge
+        target[DMAX + tokens :] = edge
+    border = jnp.zeros((DMAX, line, channels), jnp.float32)
+    side = jnp.zeros((tokens, DMAX, channels), jnp.float32)
+    for target in (second, grad_pre):
+        target[0:DMAX] = border
+        target[DMAX + tokens :] = border
+        target[DMAX : DMAX + tokens, 0:DMAX, :] = side
+        target[DMAX : DMAX + tokens, DMAX + tokens :, :] = side
+
+    pick_rows = lax.broadcasted_iota(jnp.int32, (MASK_ROWS, 2 * channels), 0)
+    pick_lanes = lax.broadcasted_iota(jnp.int32, (MASK_ROWS, 2 * channels), 1)
+    pick = jnp.where(pick_rows == pick_lanes // channels, 1.0, 0.0).astype(jnp.bfloat16)
+
+    def project(source, base):
+        def body(slot, carry):
+            row, col = place_of(base + slot, rounds, row_place, col_place)
+            rows = pl.ds(row * height, height)
+            cols = pl.ds(pl.multiple_of(col * breadth, breadth), breadth)
+            values = source[slot, 0:pixels, :].astype(jnp.float32)
+            masks = lax.dot_general(
+                source[slot, pixels:, :],
+                pick,
+                (((0,), (0,)), ((), ())),
+                preferred_element_type=jnp.float32,
+            )
+            normed = layer_norm(values).astype(jnp.bfloat16)
+            projected = matmul(normed, w_all[...])
+            shape = (height, breadth, hidden)
+            mask = masks[:, :hidden]
+            left[rows, cols, :] = (
+                mask * sigmoid(projected[:, hidden : 2 * hidden]) * projected[:, :hidden]
+            ).reshape(shape)
+            right_side = (
+                mask
+                * sigmoid(projected[:, 3 * hidden : 4 * hidden])
+                * projected[:, 2 * hidden : 3 * hidden]
+            ).reshape(shape)
+            right[cols, pl.ds(pl.multiple_of(row * height, height), height), :] = jnp.swapaxes(
+                right_side, 0, 1
+            )
+            gating[rows, cols, :] = sigmoid(projected[:, 4 * hidden :]).reshape(shape)
+            start[rows, cols, :] = values.reshape(shape)
+            contact[rows, cols, :] = masks[:, channels:].reshape(shape)
+            return carry
+
+        lax.fori_loop(0, half, body, 0)
+
+    project(near, 0)
+    project(far, half)
+
+    def spread(rows, rate, target):
+        for tap in range(3):
+            moved = field[rows, pl.ds(DMAX + (tap - 1) * rate, tokens), :]
+            target[
+                pl.ds(DMAX + rows.start, rows.size), :, tap * channels : (tap + 1) * channels
+            ] = moved.astype(jnp.bfloat16)
+
+    def taps(source, first, count, rate):
+        views = [
+            source[pl.ds(DMAX + first + (tap - 1) * rate, count)].reshape(count * tokens, -1)
+            for tap in range(3)
+        ]
+        return jnp.concatenate(views, axis=1)
+
+    def place_cot(slot, carry):
+        row, col = cot_place(slot)
+        cols = pl.ds(pl.multiple_of(DMAX + col * breadth, breadth), breadth)
+        field[pl.ds(row * height, height), cols, :] = (
+            cot_all[slot].astype(jnp.float32).reshape(height, breadth, channels)
+        )
+        return carry
+
+    def cot_place(slot):
+        col_count = tokens // breadth
+        return slot // col_count, slot % col_count
+
+    lax.fori_loop(0, 2 * half, place_cot, 0)
+    lax.fori_loop(
+        0, tokens // 4, lambda i, c: (spread(pl.ds(i * 4, 4), -rate_two, wide_cot), c)[1], 0
+    )
+
+    group = 4
+
+    def triangle(step, carry):
+        rows = pl.ds(step * group, group)
+
+        def inner(part, sums):
+            base = part * 8
+            for k in range(8):
+                others = right[base + k]
+                sums = tuple(
+                    total + left[step * group + i, pl.ds(base + k, 1), :] * others
+                    for i, total in enumerate(sums)
+                )
+            return sums
+
+        sums = lax.fori_loop(
+            0,
+            tokens // 8,
+            inner,
+            tuple(jnp.zeros((tokens, hidden), jnp.float32) for _ in range(group)),
+        )
+        product_norm = layer_norm(jnp.concatenate(sums, axis=0)).astype(jnp.bfloat16)
+        change = matmul(product_norm, w_out[...]).reshape(group, tokens, channels)
+        fresh = (start[rows] + gating[rows] * change).astype(jnp.bfloat16).astype(jnp.float32)
+        updated[rows] = fresh
+        first_in = layer_norm(fresh) * contact[rows]
+        field[rows, DMAX : DMAX + tokens, :] = first_in
+        spread(rows, rate_one, wide)
+        flat = first_in.reshape(group * tokens, channels)
+        flipped[:, pl.ds(pl.multiple_of(step * group * tokens, group * tokens), group * tokens)] = (
+            flat.T.astype(jnp.bfloat16)
+        )
+        return carry
+
+    lax.fori_loop(0, tokens // group, triangle, 0)
+
+    chunk = 8
+    size = chunk * tokens
+
+    def first_conv(step, carry):
+        first = step * chunk
+        pre = matmul(taps(wide, first, chunk, rate_one), one[...])
+        sigma = sigmoid(pre)
+        second_in = pre * sigma
+        factor[pl.ds(first, chunk)] = (sigma * (1.0 + pre * (1.0 - sigma))).reshape(
+            chunk, tokens, channels
+        )
+        second[pl.ds(DMAX + first, chunk), DMAX : DMAX + tokens, :] = second_in.reshape(
+            chunk, tokens, channels
+        )
+        flipped_two[:, pl.ds(pl.multiple_of(step * size, size), size)] = second_in.T.astype(
+            jnp.bfloat16
+        )
+        return carry
+
+    lax.fori_loop(0, tokens // chunk, first_conv, 0)
+
+    sum_two[...] = jnp.zeros_like(sum_two)
+
+    def back_two(step, carry):
+        first = step * chunk
+        shifted = taps(wide_cot, first, chunk, -rate_two)
+        sum_two[...] += matmul(
+            flipped_two[:, pl.ds(pl.multiple_of(step * size, size), size)], shifted
+        )
+        rows = pl.ds(first, chunk)
+        pre = matmul(shifted, two_t[...]).reshape(chunk, tokens, channels) * factor[rows]
+        pre = pre.astype(jnp.bfloat16).astype(jnp.float32)
+        grad_pre[pl.ds(DMAX + first, chunk), DMAX : DMAX + tokens, :] = pre
+        return carry
+
+    lax.fori_loop(0, tokens // chunk, back_two, 0)
+
+    def spread_pre(step, carry):
+        rows = pl.ds(DMAX + step * 4, 4)
+        for tap in range(3):
+            moved = grad_pre[rows, pl.ds(DMAX - (tap - 1) * rate_one, tokens), :]
+            wide[rows, :, tap * channels : (tap + 1) * channels] = moved.astype(jnp.bfloat16)
+        return carry
+
+    lax.fori_loop(0, tokens // 4, spread_pre, 0)
+
+    sum_one[...] = jnp.zeros_like(sum_one)
+
+    def back_one(step, carry):
+        shifted = taps(wide, step * chunk, chunk, -rate_one)
+        sum_one[...] += matmul(
+            flipped[:, pl.ds(pl.multiple_of(step * size, size), size)], shifted
+        )
+        return carry
+
+    lax.fori_loop(0, tokens // chunk, back_one, 0)
+    for tap in range(9):
+        lanes = slice(tap * channels, (tap + 1) * channels)
+        grad_one[tap] = sum_one[:, lanes] * (1.0 / tokens)
+        grad_two[tap] = sum_two[:, lanes] * (1.0 / tokens)
+
+    row_start, col_start = row_place * height, col_place * breadth
+
+    def windows(source, rate):
+        views = [
+            source[
+                pl.ds(row_start + DMAX + (tap // 3 - 1) * rate, height),
+                pl.ds(col_start + DMAX + (tap % 3 - 1) * rate, breadth),
+                :,
+            ].reshape(pixels, channels)
+            for tap in range(9)
+        ]
+        return jnp.concatenate(views, axis=1).astype(jnp.bfloat16)
+
+    rows = pl.ds(row_start, height)
+    cols = pl.ds(pl.multiple_of(col_start, breadth), breadth)
+    mine = updated[rows, cols, :].reshape(pixels, channels)
+    second_pre = matmul(windows(second, rate_two), two[...])
+    output[...] = (mine + second_pre).astype(jnp.bfloat16)
+    grad_input = matmul(windows(grad_pre, -rate_one), one_t[...]) * contact[rows, cols, :].reshape(
+        pixels, channels
+    )
+    centre = mine - jnp.mean(mine, axis=-1, keepdims=True)
+    inv_spread = lax.rsqrt(jnp.mean(centre * centre, axis=-1, keepdims=True) + EPSILON)
+    scaled = centre * inv_spread
+    grad_norm = inv_spread * (
+        grad_input
+        - jnp.mean(grad_input, axis=-1, keepdims=True)
+        - scaled * jnp.mean(grad_input * scaled, axis=-1, keepdims=True)
+    )
+    own = row_place * (tokens // breadth) + col_place
+    grad_pair[...] = (cot_all[own].astype(jnp.float32) + grad_norm).astype(jnp.bfloat16)
+
+
+def replicated(
+    pair, pair_mask, contact_mask, dilations, w_proj, w_gate, w_out, conv_one, conv_two, cotangent
+):
+    height, breadth, channels = pair.shape
+    hidden = w_out.shape[0]
+    row_count, col_count = lax.axis_size("row"), lax.axis_size("col")
+    tokens = height * row_count
+    pixels = height * breadth
+    rounds = exchange_plan(row_count, col_count)
+    masks = [
+        mask.reshape(1, pixels).astype(jnp.bfloat16) for mask in (pair_mask, contact_mask)
+    ]
+    filler = jnp.zeros((MASK_ROWS - 2, channels), jnp.bfloat16)
+    packed = jnp.concatenate([pair.reshape(pixels, channels), *masks, filler], axis=0)
+    near, far = gather_blocks(packed, rounds)
+    cot_all = lax.all_gather(cotangent.reshape(pixels, channels), ("row", "col"), axis=0)
+    scalars = jnp.concatenate(
+        [
+            jnp.stack([lax.axis_index("row"), lax.axis_index("col")]).astype(jnp.int32),
+            dilations,
+        ]
+    )
+    f32, bf16 = jnp.float32, jnp.bfloat16
+    line = tokens + 2 * DMAX
+    in_vmem = pl.BlockSpec(memory_space=pltpu.VMEM)
+    output, grad_pair, grad_one, grad_two = pl.pallas_call(
+        functools.partial(block_kernel, rounds, height, breadth, tokens),
+        in_specs=[pl.BlockSpec(memory_space=pltpu.SMEM)] + [in_vmem] * 9,
+        out_specs=[in_vmem] * 4,
+        out_shape=[
+            jax.ShapeDtypeStruct((pixels, channels), bf16),
+            jax.ShapeDtypeStruct((pixels, channels), bf16),
+            jax.ShapeDtypeStruct((9, channels, channels), f32),
+            jax.ShapeDtypeStruct((9, channels, channels), f32),
+        ],
+        scratch_shapes=[
+            pltpu.VMEM((tokens, tokens, hidden), f32),
+            pltpu.VMEM((tokens, tokens, hidden), f32),
+            pltpu.VMEM((tokens, tokens, channels), f32),
+            pltpu.VMEM((tokens, tokens, channels), f32),
+            pltpu.VMEM((tokens, tokens, channels), f32),
+            pltpu.VMEM((tokens, tokens, channels), f32),
+            pltpu.VMEM((tokens, line, channels), f32),
+            pltpu.VMEM((line, tokens, 3 * channels), bf16),
+            pltpu.VMEM((line, tokens, 3 * channels), bf16),
+            pltpu.VMEM((line, line, channels), f32),
+            pltpu.VMEM((tokens, tokens, channels), f32),
+            pltpu.VMEM((line, line, channels), f32),
+            pltpu.VMEM((channels, tokens * tokens), bf16),
+            pltpu.VMEM((channels, tokens * tokens), bf16),
+            pltpu.VMEM((channels, 9 * channels), f32),
+            pltpu.VMEM((channels, 9 * channels), f32),
+        ],
+        compiler_params=pltpu.CompilerParams(vmem_limit_bytes=VMEM_LIMIT),
+    )(
+        scalars,
+        near,
+        far,
+        cot_all,
+        jnp.concatenate([w_proj, w_gate], axis=1),
+        w_out,
+        conv_one.reshape(9 * channels, channels),
+        conv_one.transpose(0, 2, 1).reshape(9 * channels, channels),
+        conv_two.reshape(9 * channels, channels),
+        conv_two.transpose(0, 2, 1).reshape(9 * channels, channels),
+    )
+    block = (height, breadth, channels)
+    return output.reshape(block), grad_pair.reshape(block), grad_one, grad_two
+
+
+def fits(pair, w_out, row_count, col_count):
+    height, breadth, channels = pair.shape
+    tokens = height * row_count
+    powers = all(count & (count - 1) == 0 for count in (row_count, col_count))
+    whole = (tokens + 2 * DMAX) ** 2 * channels
+    return (
+        powers
+        and height * breadth == channels == w_out.shape[0]
+        and whole * 60 <= VMEM_LIMIT
+    )
+
+
+def local(*arguments):
+    pair, w_out = arguments[0], arguments[6]
+    if fits(pair, w_out, lax.axis_size("row"), lax.axis_size("col")):
+        return replicated(*arguments)
+    return sharded(*arguments)
+
+
 def solution(mesh):
     in_specs = (
         P("row", "col", None),

time: 301 us -> 125 us (0.42)
  waiting for transfers between devices: 134 us -> 45.8 us
  blocking collectives: 77.6 us -> 0 us
  Pallas kernels: 0 us -> 50.1 us
  starting transfers between devices: 46.1 us -> 9.39 us
  matrix products: 7.62 us -> 0 us
  between operations: 20.1 us -> 14.2 us
  local copies, waits for them, and re-layouts: 8.65 us -> 3.68 us
  other arithmetic: 5.82 us -> 1.52 us
    psum x2 -> x0, waiting for transfers between devices: 131 us -> none  [the longest x1 131 us: local(): grad_one, grad_two = lax.psum((grad_one, grad_two), ('row', 'col'))]
    all_gather x2 -> x0, blocking collectives: 77.6 us -> none  [the longest x1 45 us: local(): lax.all_gather(left_side, 'col', axis=1, tiled=True)]
    pallas_call x0 -> x1, Pallas kernels: none -> 50.1 us  [replicated(): pl.pallas_call(functools.partial(block_kernel, rounds, height, breadth, t...]
    ppermute x16 -> x5, starting transfers between devices: 46 us -> 9.35 us  [gather_blocks(): other = lax.ppermute(held, axis, pairs)]
    all_gather x0 -> x1, waiting for transfers between devices: none -> 31.6 us  [replicated(): lax.all_gather(cotangent.reshape(pixels, channels), ('row', 'col'), axis=0)]
    ppermute x16 -> x5, waiting for transfers between devices: 3.7 us -> 13.4 us  [gather_blocks(): other = lax.ppermute(held, axis, pairs)]
    dot_general x10 -> x0, matrix products: 7.62 us -> none  [the longest x1 1.6 us: local(): jnp.einsum('ikh,jkh->ijh', lax.all_gather(left_side, 'col', axis=1, tiled...]
    unnamed x58 -> x23, local copies, waits for them, and re-layouts: 6.12 us -> 1.4 us
  transfers between devices with their start and end apart: 18 -> 6, of which waited for: 4 -> 5; matrix products, arithmetic and copies ran while one was open for 4% -> 3% of each run, Pallas kernels for 0% -> 0%
where the time goes in v1:
time: 125 us
  Pallas kernels  50.1 us (40%)
  waiting for transfers between devices  45.8 us (37%)
  between operations  14.2 us (11%)
  starting transfers between devices  9.39 us (8%)
  local copies, waits for them, and re-layouts  3.68 us (3%)
  other arithmetic  1.52 us (1%)
    pallas_call x1, Pallas kernels, replicated(): pl.pallas_call(functools.partial(block_kernel, rounds, height, breadth, t...  50.1 us
    all_gather x1, waiting for transfers between devices, replicated(): lax.all_gather(cotangent.reshape(pixels, channels), ('row', 'col'), axis=0)  31.6 us
    ppermute x5, waiting for transfers between devices, gather_blocks(): other = lax.ppermute(held, axis, pairs)  13.4 us
    ppermute x5, starting transfers between devices, gather_blocks(): other = lax.ppermute(held, axis, pairs)  9.35 us
  transfers between devices with their start and end apart: 6, of which 5 were waited for; matrix products, arithmetic and copies ran while one was open for 3% of the time, Pallas kernels for 0%

profile of v1, /device:TPU:0, one launch (start us, length us, event | category | flops | bytes accessed | tf_op | source)
XLA Modules:
  0.0 124.6 jit_solution(3656318215728521494)
XLA Ops:
  7.2 0.0 all-gather.2.cloned.1.call-start
  7.2 0.0 copy-start.7
  7.2 0.0 copy-start.5
  7.2 0.7 all-gather.2.cloned.1.call-update
  7.9 0.0 copy-done.7
  7.9 0.0 copy-start.8
  7.9 0.1 copy.22
  8.0 0.1 convert_element_type.29
  8.1 0.5 copy-done.8
  8.6 0.1 copy.23
  8.7 0.1 convert_element_type.31
  8.8 0.1 pad.14.clone
  8.9 0.0 copy-done.5
  8.9 0.1 maximum_bitcast_fusion
  9.0 4.1 %collective-permute-start = (bf16[1,144,128]{2,1,0:T(8,128)(2,1)S(1)}, bf16[1,144,128]{2,1,0:T(8,128)(2,1)S(1)}, u32[]{:S(2)}, u32[]{:S(2)}) collective-permute-start(bf16[1,144,128]{2,1,0:T(8,128)(2,1)S(1)} %maximum_bitcast_fusion), channel_id=1, source_target_pairs={{0,4},{1,5},{2,6},{3,7},{4,0},{5,1},{6,2},{7,3},{8,12},{9,13},{10,... | collective-permute-start | bytes 110600 | tf_op jit(solution)/shard_map/ppermute | solution.py:190
  13.1 2.3 %collective-permute-done = bf16[1,144,128]{2,1,0:T(8,128)(2,1)S(1)} collective-permute-done((bf16[1,144,128]{2,1,0:T(8,128)(2,1)S(1)}, bf16[1,144,128]{2,1,0:T(8,128)(2,1)S(1)}, u32[]{:S(2)}, u32[]{:S(2)}) %collective-permute-start) | collective-permute-done | bytes 36896 | tf_op jit(solution)/shard_map/ppermute | solution.py:190
  15.4 1.6 %collective-permute-start.1 = (bf16[2,144,128]{2,1,0:T(8,128)(2,1)S(1)}, bf16[2,144,128]{2,1,0:T(8,128)(2,1)S(1)}, u32[]{:S(2)}, u32[]{:S(2)}) collective-permute-start(bf16[2,144,128]{2,1,0:T(8,128)(2,1)S(1)} %pad_maximum_fusion.3), channel_id=1, source_target_pairs={{0,2},{1,3},{2,0},{3,1},{4,6},{5,7},{6,4},{7,5},{8,10},{9,11},{10,... | collective-permute-start | bytes 221192 | tf_op jit(solution)/shard_map/ppermute | solution.py:190
  17.0 2.8 %collective-permute-done.1 = bf16[2,144,128]{2,1,0:T(8,128)(2,1)S(1)} collective-permute-done((bf16[2,144,128]{2,1,0:T(8,128)(2,1)S(1)}, bf16[2,144,128]{2,1,0:T(8,128)(2,1)S(1)}, u32[]{:S(2)}, u32[]{:S(2)}) %collective-permute-start.1) | collective-permute-done | bytes 73760 | tf_op jit(solution)/shard_map/ppermute | solution.py:190
  19.9 1.8 %collective-permute-start.2 = (bf16[4,144,128]{2,1,0:T(8,128)(2,1)S(1)}, bf16[4,144,128]{2,1,0:T(8,128)(2,1)S(1)}, u32[]{:S(2)}, u32[]{:S(2)}) collective-permute-start(bf16[4,144,128]{2,1,0:T(8,128)(2,1)S(1)} %pad_maximum_fusion.2), channel_id=1, source_target_pairs={{0,1},{1,0},{2,3},{3,2},{4,5},{5,4},{6,7},{7,6},{8,9},{9,8},{10,11... | collective-permute-start | bytes 442376 | tf_op jit(solution)/shard_map/ppermute | solution.py:190
  21.7 0.1 constant_dynamic-update-slice_fusion.4
  21.7 3.4 %collective-permute-done.2 = bf16[4,144,128]{2,1,0:T(8,128)(2,1)S(1)} collective-permute-done((bf16[4,144,128]{2,1,0:T(8,128)(2,1)S(1)}, bf16[4,144,128]{2,1,0:T(8,128)(2,1)S(1)}, u32[]{:S(2)}, u32[]{:S(2)}) %collective-permute-start.2) | collective-permute-done | bytes 147488 | tf_op jit(solution)/shard_map/ppermute | solution.py:190
  25.1 1.8 %collective-permute-start.3 = (bf16[8,144,128]{2,1,0:T(8,128)(2,1)S(1)}, bf16[8,144,128]{2,1,0:T(8,128)(2,1)S(1)}, u32[]{:S(2)}, u32[]{:S(2)}) collective-permute-start(bf16[8,144,128]{2,1,0:T(8,128)(2,1)S(1)} %pad_maximum_fusion), channel_id=1, source_target_pairs={{0,16},{8,24},{16,0},{24,8},{1,17},{9,25},{17,1},{25,9},{2,18},{10... | collective-permute-start | bytes 884744 | tf_op jit(solution)/shard_map/ppermute | solution.py:190
  27.0 0.0 copy-start.1
  27.0 4.9 %collective-permute-done.3 = bf16[8,144,128]{2,1,0:T(8,128)(2,1)S(1)} collective-permute-done((bf16[8,144,128]{2,1,0:T(8,128)(2,1)S(1)}, bf16[8,144,128]{2,1,0:T(8,128)(2,1)S(1)}, u32[]{:S(2)}, u32[]{:S(2)}) %collective-permute-start.3) | collective-permute-done | bytes 294944 | tf_op jit(solution)/shard_map/ppermute | solution.py:190
  32.0 0.0 copy-start.2
  32.0 0.1 collective-permute-start.4
  32.1 0.0 copy-done.1
  32.1 0.0 copy-start
  32.1 0.9 copy.25
  33.0 0.2 copy-done
  33.2 0.0 copy-start.4
  33.2 0.0 copy-start.6
  33.2 0.9 copy.24
  34.1 0.0 copy-done.2
  34.1 0.0 copy-start.9
  34.1 0.7 copy-done.9
  34.7 0.6 pad_add_fusion.scalars
  35.3 0.0 copy-done.4
  35.3 0.0 copy-done.6
  35.3 0.7 pad_maximum_fusion.1.w_all
  36.0 0.0 collective-permute-done.4.far
  36.0 0.0 copy-start.3
  36.0 31.6 %all-gather.2.cloned.1.call-done.cot_all = bf16[32,128,128]{2,1,0:T(8,128)(2,1)} async-done(((bf16[1,128,128]{2,1,0:T(8,128)(2,1)}), bf16[32,128,128]{2,1,0:T(8,128)(2,1)}) %all-gather.2.cloned.1.call-update) | async-done | bytes 1048592 | tf_op jit(solution)/shard_map/all_gather | solution.py:491
  67.7 0.0 copy-done.3
  67.7 50.1 %shard_map.129 = (bf16[128,128]{1,0:T(8,128)(2,1)}, bf16[128,128]{1,0:T(8,128)(2,1)}, f32[9,128,128]{2,1,0:T(8,128)}, f32[9,128,128]{2,1,0:T(8,128)}) custom-call(s32[4]{0:T(128)} %pad_add_fusion.scalars, bf16[16,144,128]{2,1,0:T(8,128)(2,1)} %copy-done.2, bf16[16,144,128]{2,1,0:T(8,128)(2,1)} %copy-done.3, ...), custom_call_target="tpu_custom_call" | custom-call | tf_op jit(solution)/shard_map/pallas_call | solution.py:501
  (10 shorter events, 0.2 us)
Async XLA Ops:
  7.2 60.5 %all-gather.2.cloned.1.call-start = ((), (), s32[]{:S(2)}) async-start(), calls=%async_computation | async-start | bytes 1081344 | tf_op jit(solution)/shard_map/all_gather | solution.py:491
  7.2 0.7 copy-start.7
  7.2 1.7 %copy-start.5 = (bf16[16,8,128]{2,1,0:T(8,128)(2,1)S(1)}, bf16[16,8,128]{2,1,0:T(8,128)(2,1)}, u32[]{:S(2)}) copy-start(bf16[16,8,128]{2,1,0:T(8,128)(2,1)} %param.10) | copy-start | bytes 98308
  7.9 0.7 copy-start.8
  9.0 6.4 %collective-permute-start = (bf16[1,144,128]{2,1,0:T(8,128)(2,1)S(1)}, bf16[1,144,128]{2,1,0:T(8,128)(2,1)S(1)}, u32[]{:S(2)}, u32[]{:S(2)}) collective-permute-start(bf16[1,144,128]{2,1,0:T(8,128)(2,1)S(1)} %maximum_bitcast_fusion), channel_id=1, source_target_pairs={{0,4},{1,5},{2,6},{3,7},{4,0},{5,1},{6,2},{7,3},{8,12},{9,13},{10,... | collective-permute-start | bytes 110600 | tf_op jit(solution)/shard_map/ppermute | solution.py:190
  15.4 4.4 %collective-permute-start.1 = (bf16[2,144,128]{2,1,0:T(8,128)(2,1)S(1)}, bf16[2,144,128]{2,1,0:T(8,128)(2,1)S(1)}, u32[]{:S(2)}, u32[]{:S(2)}) collective-permute-start(bf16[2,144,128]{2,1,0:T(8,128)(2,1)S(1)} %pad_maximum_fusion.3), channel_id=1, source_target_pairs={{0,2},{1,3},{2,0},{3,1},{4,6},{5,7},{6,4},{7,5},{8,10},{9,11},{10,... | collective-permute-start | bytes 221192 | tf_op jit(solution)/shard_map/ppermute | solution.py:190
  19.9 5.2 %collective-permute-start.2 = (bf16[4,144,128]{2,1,0:T(8,128)(2,1)S(1)}, bf16[4,144,128]{2,1,0:T(8,128)(2,1)S(1)}, u32[]{:S(2)}, u32[]{:S(2)}) collective-permute-start(bf16[4,144,128]{2,1,0:T(8,128)(2,1)S(1)} %pad_maximum_fusion.2), channel_id=1, source_target_pairs={{0,1},{1,0},{2,3},{3,2},{4,5},{5,4},{6,7},{7,6},{8,9},{9,8},{10,11... | collective-permute-start | bytes 442376 | tf_op jit(solution)/shard_map/ppermute | solution.py:190
  25.1 6.8 %collective-permute-start.3 = (bf16[8,144,128]{2,1,0:T(8,128)(2,1)S(1)}, bf16[8,144,128]{2,1,0:T(8,128)(2,1)S(1)}, u32[]{:S(2)}, u32[]{:S(2)}) collective-permute-start(bf16[8,144,128]{2,1,0:T(8,128)(2,1)S(1)} %pad_maximum_fusion), channel_id=1, source_target_pairs={{0,16},{8,24},{16,0},{24,8},{1,17},{9,25},{17,1},{25,9},{2,18},{10... | collective-permute-start | bytes 884744 | tf_op jit(solution)/shard_map/ppermute | solution.py:190
  27.0 5.1 %copy-start.1 = (bf16[9,128,128]{2,1,0:T(8,128)(2,1)S(1)}, bf16[9,128,128]{2,1,0:T(8,128)(2,1)}, u32[]{:S(2)}) copy-start(bf16[9,128,128]{2,1,0:T(8,128)(2,1)} %param.18) | copy-start | bytes 884740
  32.0 2.1 %copy-start.2 = (bf16[16,144,128]{2,1,0:T(8,128)(2,1)}, bf16[16,144,128]{2,1,0:T(8,128)(2,1)S(1)}, u32[]{:S(2)}) copy-start(bf16[16,144,128]{2,1,0:T(8,128)(2,1)S(1)} %constant_dynamic-update-slice_fusion.near) | copy-start | bytes 1769476
  32.0 4.0 %collective-permute-start.4 = (bf16[16,144,128]{2,1,0:T(8,128)(2,1)S(1)}, bf16[16,144,128]{2,1,0:T(8,128)(2,1)S(1)}, u32[]{:S(2)}, u32[]{:S(2)}) collective-permute-start(bf16[16,144,128]{2,1,0:T(8,128)(2,1)S(1)} %constant_dynamic-update-slice_fusion.near), channel_id=1, source_target_pairs={{0,8},{8,0},{16,24},{24,16},{1,9},{9,1},{17,25},{25,17},{2,10},{10... | collective-permute-start | bytes 1769480 | tf_op jit(solution)/shard_map/ppermute | solution.py:190
  32.1 1.1 copy-start
  33.2 2.2 %copy-start.4 = (bf16[128,512]{1,0:T(8,128)(2,1)S(1)}, bf16[128,512]{1,0:T(8,128)(2,1)}, u32[]{:S(2)}) copy-start(bf16[128,512]{1,0:T(8,128)(2,1)} %param.14) | copy-start | bytes 393220
  33.2 2.2 %copy-start.6 = (bf16[128,128]{1,0:T(8,128)(2,1)S(1)}, bf16[128,128]{1,0:T(8,128)(2,1)}, u32[]{:S(2)}) copy-start(bf16[128,128]{1,0:T(8,128)(2,1)} %param.15) | copy-start | bytes 98308
  34.1 0.7 copy-start.9
  36.0 31.7 %copy-start.3 = (bf16[16,144,128]{2,1,0:T(8,128)(2,1)}, bf16[16,144,128]{2,1,0:T(8,128)(2,1)S(1)}, u32[]{:S(2)}) copy-start(bf16[16,144,128]{2,1,0:T(8,128)(2,1)S(1)} %collective-permute-done.4.far) | copy-start | bytes 1769476
Sparse Core Ops, SparseCore 0:
  11.1 56.5 all-gather.1

commit v2 on v1

--- a/solution.py
+++ b/solution.py
@@ -8,7 +8,6 @@
 from jax.sharding import PartitionSpec as P
 
 DMAX = 8
-MASK_ROWS = 16
 VMEM_LIMIT = 56 * 1024 * 1024
 
 
@@ -170,17 +169,13 @@
     return (output, grad_pair, grad_one, grad_two)
 
 
+def halvings(axis, count):
+    return [(axis, count >> step) for step in range(1, count.bit_length())]
+
+
 def exchange_plan(row_count, col_count):
-    rounds = []
-    distance = col_count // 2
-    while distance:
-        rounds.append(("col", distance))
-        distance //= 2
-    distance = row_count // 2
-    while distance:
-        rounds.append(("row", distance))
-        distance //= 2
-    return rounds
+    rows, cols = halvings("row", row_count), halvings("col", col_count)
+    return cols + rows, rows[:-1] + cols + rows[-1:]
 
 
 def gather_blocks(block, rounds):
@@ -205,7 +200,7 @@
 
 
 def sigmoid(values):
-    return 1.0 / (1.0 + jnp.exp(-values))
+    return 0.5 + 0.5 * jnp.tanh(0.5 * values)
 
 
 def matmul(left, right):
@@ -214,13 +209,15 @@
 
 def block_kernel(
     rounds,
+    cot_rounds,
     height,
     breadth,
     tokens,
     scalars,
     near,
     far,
-    cot_all,
+    cot_near,
+    cot_far,
     w_all,
     w_out,
     one,
@@ -271,43 +268,57 @@
         target[DMAX : DMAX + tokens, 0:DMAX, :] = side
         target[DMAX : DMAX + tokens, DMAX + tokens :, :] = side
 
-    pick_rows = lax.broadcasted_iota(jnp.int32, (MASK_ROWS, 2 * channels), 0)
-    pick_lanes = lax.broadcasted_iota(jnp.int32, (MASK_ROWS, 2 * channels), 1)
-    pick = jnp.where(pick_rows == pick_lanes // channels, 1.0, 0.0).astype(jnp.bfloat16)
+    lane = lax.broadcasted_iota(jnp.int32, (breadth, channels), 1)
+    place = lax.broadcasted_iota(jnp.int32, (breadth, channels), 0)
+    own_lane = jnp.where((lane % breadth == place) & (lane < 2 * breadth), 1.0, 0.0)
+    pick_lane = lax.broadcasted_iota(jnp.int32, (channels, 2 * channels), 0)
+    pick_half = lax.broadcasted_iota(jnp.int32, (channels, 2 * channels), 1) // channels
+    pick = jnp.where(pick_lane // breadth == pick_half, 1.0, 0.0).astype(jnp.bfloat16)
+    several = 4
 
     def project(source, base):
-        def body(slot, carry):
-            row, col = place_of(base + slot, rounds, row_place, col_place)
-            rows = pl.ds(row * height, height)
-            cols = pl.ds(pl.multiple_of(col * breadth, breadth), breadth)
-            values = source[slot, 0:pixels, :].astype(jnp.float32)
-            masks = lax.dot_general(
-                source[slot, pixels:, :],
-                pick,
-                (((0,), (0,)), ((), ())),
-                preferred_element_type=jnp.float32,
-            )
+        def body(step, carry):
+            first = step * several
+            masks = jnp.concatenate(
+                [
+                    (
+                        source[first + i, pixels:, :].astype(jnp.float32)[:, None, :]
+                        * own_lane[None]
+                    ).reshape(pixels, channels)
+                    for i in range(several)
+                ],
+                axis=0,
+            ).astype(jnp.bfloat16)
+            masks = matmul(masks, pick)
+            values = jnp.concatenate(
+                [source[first + i, 0:pixels, :] for i in range(several)], axis=0
+            ).astype(jnp.float32)
             normed = layer_norm(values).astype(jnp.bfloat16)
             projected = matmul(normed, w_all[...])
-            shape = (height, breadth, hidden)
             mask = masks[:, :hidden]
-            left[rows, cols, :] = (
+            left_side = (
                 mask * sigmoid(projected[:, hidden : 2 * hidden]) * projected[:, :hidden]
-            ).reshape(shape)
+            )
             right_side = (
                 mask
                 * sigmoid(projected[:, 3 * hidden : 4 * hidden])
                 * projected[:, 2 * hidden : 3 * hidden]
-            ).reshape(shape)
-            right[cols, pl.ds(pl.multiple_of(row * height, height), height), :] = jnp.swapaxes(
-                right_side, 0, 1
             )
-            gating[rows, cols, :] = sigmoid(projected[:, 4 * hidden :]).reshape(shape)
-            start[rows, cols, :] = values.reshape(shape)
-            contact[rows, cols, :] = masks[:, channels:].reshape(shape)
+            gates = sigmoid(projected[:, 4 * hidden :])
+            shape = (height, breadth, channels)
+            for i in range(several):
+                row, col = place_of(base + first + i, rounds, row_place, col_place)
+                rows = pl.ds(pl.multiple_of(row * height, height), height)
+                cols = pl.ds(pl.multiple_of(col * breadth, breadth), breadth)
+                part = slice(i * pixels, (i + 1) * pixels)
+                left[rows, cols, :] = left_side[part].reshape(shape)
+                right[cols, rows, :] = jnp.swapaxes(right_side[part].reshape(shape), 0, 1)
+                gating[rows, cols, :] = gates[part].reshape(shape)
+                start[rows, cols, :] = values[part].reshape(shape)
+                contact[rows, cols, :] = masks[part, channels:].reshape(shape)
             return carry
 
-        lax.fori_loop(0, half, body, 0)
+        lax.fori_loop(0, half // several, body, 0)
 
     project(near, 0)
     project(far, half)
@@ -326,30 +337,33 @@
         ]
         return jnp.concatenate(views, axis=1)
 
-    def place_cot(slot, carry):
-        row, col = cot_place(slot)
-        cols = pl.ds(pl.multiple_of(DMAX + col * breadth, breadth), breadth)
-        field[pl.ds(row * height, height), cols, :] = (
-            cot_all[slot].astype(jnp.float32).reshape(height, breadth, channels)
-        )
-        return carry
-
-    def cot_place(slot):
-        col_count = tokens // breadth
-        return slot // col_count, slot % col_count
-
-    lax.fori_loop(0, 2 * half, place_cot, 0)
+    def place_cot(source, base):
+        def body(step, carry):
+            for i in range(several):
+                slot = step * several + i
+                row, col = place_of(base + slot, cot_rounds, row_place, col_place)
+                cols = pl.ds(pl.multiple_of(DMAX + col * breadth, breadth), breadth)
+                field[pl.ds(row * height, height), cols, :] = (
+                    source[slot].astype(jnp.float32).reshape(height, breadth, channels)
+                )
+            return carry
+
+        lax.fori_loop(0, half // several, body, 0)
+
+    chunk = 8
+    size = chunk * tokens
+    steps = tokens // chunk
+    place_cot(cot_near, 0)
+    place_cot(cot_far, half)
     lax.fori_loop(
-        0, tokens // 4, lambda i, c: (spread(pl.ds(i * 4, 4), -rate_two, wide_cot), c)[1], 0
+        0, steps, lambda i, c: (spread(pl.ds(i * chunk, chunk), -rate_two, wide_cot), c)[1], 0
     )
 
     group = 4
 
     def triangle(step, carry):
-        rows = pl.ds(step * group, group)
-
         def inner(part, sums):
-            base = part * 8
+            base = pl.multiple_of(part * 8, 8)
             for k in range(8):
                 others = right[base + k]
                 sums = tuple(
@@ -364,23 +378,28 @@
             inner,
             tuple(jnp.zeros((tokens, hidden), jnp.float32) for _ in range(group)),
         )
-        product_norm = layer_norm(jnp.concatenate(sums, axis=0)).astype(jnp.bfloat16)
-        change = matmul(product_norm, w_out[...]).reshape(group, tokens, channels)
+        for i, total in enumerate(sums):
+            left[step * group + i] = total
+        return carry
+
+    lax.fori_loop(0, tokens // group, triangle, 0)
+
+    def update(step, carry):
+        rows = pl.ds(step * chunk, chunk)
+        products = left[rows].reshape(size, hidden)
+        product_norm = layer_norm(products).astype(jnp.bfloat16)
+        change = matmul(product_norm, w_out[...]).reshape(chunk, tokens, channels)
         fresh = (start[rows] + gating[rows] * change).astype(jnp.bfloat16).astype(jnp.float32)
         updated[rows] = fresh
         first_in = layer_norm(fresh) * contact[rows]
         field[rows, DMAX : DMAX + tokens, :] = first_in
         spread(rows, rate_one, wide)
-        flat = first_in.reshape(group * tokens, channels)
-        flipped[:, pl.ds(pl.multiple_of(step * group * tokens, group * tokens), group * tokens)] = (
-            flat.T.astype(jnp.bfloat16)
+        flipped[:, pl.ds(pl.multiple_of(step * size, size), size)] = (
+            first_in.reshape(size, channels).astype(jnp.bfloat16).T
         )
         return carry
 
-    lax.fori_loop(0, tokens // group, triangle, 0)
-
-    chunk = 8
-    size = chunk * tokens
+    lax.fori_loop(0, steps, update, 0)
 
     def first_conv(step, carry):
         first = step * chunk
@@ -393,12 +412,12 @@
         second[pl.ds(DMAX + first, chunk), DMAX : DMAX + tokens, :] = second_in.reshape(
             chunk, tokens, channels
         )
-        flipped_two[:, pl.ds(pl.multiple_of(step * size, size), size)] = second_in.T.astype(
+        flipped_two[:, pl.ds(pl.multiple_of(step * size, size), size)] = second_in.astype(
             jnp.bfloat16
-        )
+        ).T
         return carry
 
-    lax.fori_loop(0, tokens // chunk, first_conv, 0)
+    lax.fori_loop(0, steps, first_conv, 0)
 
     sum_two[...] = jnp.zeros_like(sum_two)
 
@@ -414,16 +433,16 @@
         grad_pre[pl.ds(DMAX + first, chunk), DMAX : DMAX + tokens, :] = pre
         return carry
 
-    lax.fori_loop(0, tokens // chunk, back_two, 0)
+    lax.fori_loop(0, steps, back_two, 0)
 
     def spread_pre(step, carry):
-        rows = pl.ds(DMAX + step * 4, 4)
+        rows = pl.ds(DMAX + step * chunk, chunk)
         for tap in range(3):
             moved = grad_pre[rows, pl.ds(DMAX - (tap - 1) * rate_one, tokens), :]
             wide[rows, :, tap * channels : (tap + 1) * channels] = moved.astype(jnp.bfloat16)
         return carry
 
-    lax.fori_loop(0, tokens // 4, spread_pre, 0)
+    lax.fori_loop(0, steps, spread_pre, 0)
 
     sum_one[...] = jnp.zeros_like(sum_one)
 
@@ -434,7 +453,7 @@
         )
         return carry
 
-    lax.fori_loop(0, tokens // chunk, back_one, 0)
+    lax.fori_loop(0, steps, back_one, 0)
     for tap in range(9):
         lanes = slice(tap * channels, (tap + 1) * channels)
         grad_one[tap] = sum_one[:, lanes] * (1.0 / tokens)
@@ -469,8 +488,7 @@
         - jnp.mean(grad_input, axis=-1, keepdims=True)
         - scaled * jnp.mean(grad_input * scaled, axis=-1, keepdims=True)
     )
-    own = row_place * (tokens // breadth) + col_place
-    grad_pair[...] = (cot_all[own].astype(jnp.float32) + grad_norm).astype(jnp.bfloat16)
+    grad_pair[...] = (cot_near[0].astype(jnp.float32) + grad_norm).astype(jnp.bfloat16)
 
 
 def replicated(
@@ -481,14 +499,18 @@
     row_count, col_count = lax.axis_size("row"), lax.axis_size("col")
     tokens = height * row_count
     pixels = height * breadth
-    rounds = exchange_plan(row_count, col_count)
-    masks = [
-        mask.reshape(1, pixels).astype(jnp.bfloat16) for mask in (pair_mask, contact_mask)
-    ]
-    filler = jnp.zeros((MASK_ROWS - 2, channels), jnp.bfloat16)
-    packed = jnp.concatenate([pair.reshape(pixels, channels), *masks, filler], axis=0)
+    rounds, cot_rounds = exchange_plan(row_count, col_count)
+    masks = jnp.concatenate(
+        [
+            pair_mask.astype(jnp.bfloat16),
+            contact_mask.astype(jnp.bfloat16),
+            jnp.zeros((height, channels - 2 * breadth), jnp.bfloat16),
+        ],
+        axis=1,
+    )
+    packed = jnp.concatenate([pair.reshape(pixels, channels), masks], axis=0)
     near, far = gather_blocks(packed, rounds)
-    cot_all = lax.all_gather(cotangent.reshape(pixels, channels), ("row", "col"), axis=0)
+    cot_near, cot_far = gather_blocks(cotangent.reshape(pixels, channels), cot_rounds)
     scalars = jnp.concatenate(
         [
             jnp.stack([lax.axis_index("row"), lax.axis_index("col")]).astype(jnp.int32),
@@ -499,8 +521,8 @@
     line = tokens + 2 * DMAX
     in_vmem = pl.BlockSpec(memory_space=pltpu.VMEM)
     output, grad_pair, grad_one, grad_two = pl.pallas_call(
-        functools.partial(block_kernel, rounds, height, breadth, tokens),
-        in_specs=[pl.BlockSpec(memory_space=pltpu.SMEM)] + [in_vmem] * 9,
+        functools.partial(block_kernel, rounds, cot_rounds, height, breadth, tokens),
+        in_specs=[pl.BlockSpec(memory_space=pltpu.SMEM)] + [in_vmem] * 10,
         out_specs=[in_vmem] * 4,
         out_shape=[
             jax.ShapeDtypeStruct((pixels, channels), bf16),
@@ -531,7 +553,8 @@
         scalars,
         near,
         far,
-        cot_all,
+        cot_near,
+        cot_far,
         jnp.concatenate([w_proj, w_gate], axis=1),
         w_out,
         conv_one.reshape(9 * channels, channels),
@@ -550,6 +573,7 @@
     whole = (tokens + 2 * DMAX) ** 2 * channels
     return (
         powers
+        and row_count * col_count >= 8
         and height * breadth == channels == w_out.shape[0]
         and whole * 60 <= VMEM_LIMIT
     )

time: 125 us -> 73.3 us (0.59)
  the two profiles are of different devices: /device:TPU:0 before, /device:TPU:28 now
where the time goes in v2:
time: 73.3 us; the launch traced here: 73 us
  Pallas kernels  38.3 us (52%)
  waiting for transfers between devices  19.5 us (27%)
  starting transfers between devices  6.83 us (9%)
  local copies, waits for them, and re-layouts  4.7 us (6%)
  other arithmetic  2.88 us (4%)
  between operations  0.79 us (1%)
    pallas_call x1, Pallas kernels, replicated(): pl.pallas_call(functools.partial(block_kernel, rounds, cot_rounds, height...  38.3 us
    ppermute x10, waiting for transfers between devices, gather_blocks(): other = lax.ppermute(held, axis, pairs)  19.5 us
    ppermute x10, starting transfers between devices, gather_blocks(): other = lax.ppermute(held, axis, pairs)  6.83 us
    unnamed x29, local copies, waits for them, and re-layouts  2.63 us
  transfers between devices with their start and end apart: 10, of which 6 were waited for; matrix products, arithmetic and copies ran while one was open for 7% of the time, Pallas kernels for 0%

profile of v2, /device:TPU:28, one launch (start us, length us, event | category | flops | bytes accessed | tf_op | source)
XLA Modules:
  0.0 73.0 jit_solution(4731896053904146409)
XLA Ops:
  0.6 0.0 copy-start.9
  0.6 1.6 %collective-permute-start.5 = (bf16[1,128,128]{2,1,0:T(8,128)(2,1)}, bf16[1,128,128]{2,1,0:T(8,128)(2,1)S(1)}, u32[]{:S(2)}, u32[]{:S(2)}) collective-permute-start(bf16[1,128,128]{2,1,0:T(8,128)(2,1)} %bitcast.22), channel_id=1, source_target_pairs={{0,16},{8,24},{16,0},{24,8},{1,17},{9,25},{17,1},{25,9},{2,18},{10... | collective-permute-start | bytes 98312 | tf_op jit(solution)/shard_map/ppermute | solution.py:185
  2.2 0.7 convert_element_type.6
  2.9 0.1 copy.18
  3.0 0.7 convert_element_type.7
  3.7 0.1 copy.19
  3.8 0.0 copy-done.9
  3.8 0.0 copy-start.5
  3.8 0.1 constant_dynamic-update-slice_fusion.4
  3.8 0.3 collective-permute-start
  4.2 0.3 copy-done.5
  4.5 0.3 collective-permute-done.5
  4.8 2.0 %collective-permute-start.6 = (bf16[2,128,128]{2,1,0:T(8,128)(2,1)S(1)}, bf16[2,128,128]{2,1,0:T(8,128)(2,1)S(1)}, u32[]{:S(2)}, u32[]{:S(2)}) collective-permute-start(bf16[2,128,128]{2,1,0:T(8,128)(2,1)S(1)} %pad_maximum_fusion.6), channel_id=1, source_target_pairs={{0,4},{1,5},{2,6},{3,7},{4,0},{5,1},{6,2},{7,3},{8,12},{9,13},{10,... | collective-permute-start | bytes 196616 | tf_op jit(solution)/shard_map/ppermute | solution.py:185
  6.9 3.1 %collective-permute-done = bf16[1,144,128]{2,1,0:T(8,128)(2,1)S(1)} collective-permute-done((bf16[1,144,128]{2,1,0:T(8,128)(2,1)S(1)}, bf16[1,144,128]{2,1,0:T(8,128)(2,1)S(1)}, u32[]{:S(2)}, u32[]{:S(2)}) %collective-permute-start) | collective-permute-done | bytes 36896 | tf_op jit(solution)/shard_map/ppermute | solution.py:185
  10.0 0.1 collective-permute-start.1
  10.1 1.1 %collective-permute-done.6 = bf16[2,128,128]{2,1,0:T(8,128)(2,1)S(1)} collective-permute-done((bf16[2,128,128]{2,1,0:T(8,128)(2,1)S(1)}, bf16[2,128,128]{2,1,0:T(8,128)(2,1)S(1)}, u32[]{:S(2)}, u32[]{:S(2)}) %collective-permute-start.6) | collective-permute-done | bytes 65568 | tf_op jit(solution)/shard_map/ppermute | solution.py:185
  11.2 1.0 %collective-permute-start.7 = (bf16[4,128,128]{2,1,0:T(8,128)(2,1)S(1)}, bf16[4,128,128]{2,1,0:T(8,128)(2,1)S(1)}, u32[]{:S(2)}, u32[]{:S(2)}) collective-permute-start(bf16[4,128,128]{2,1,0:T(8,128)(2,1)S(1)} %pad_maximum_fusion.4), channel_id=1, source_target_pairs={{0,2},{1,3},{2,0},{3,1},{4,6},{5,7},{6,4},{7,5},{8,10},{9,11},{10,... | collective-permute-start | bytes 393224 | tf_op jit(solution)/shard_map/ppermute | solution.py:185
  12.2 3.0 %collective-permute-done.1 = bf16[2,144,128]{2,1,0:T(8,128)(2,1)S(1)} collective-permute-done((bf16[2,144,128]{2,1,0:T(8,128)(2,1)S(1)}, bf16[2,144,128]{2,1,0:T(8,128)(2,1)S(1)}, u32[]{:S(2)}, u32[]{:S(2)}) %collective-permute-start.1) | collective-permute-done | bytes 73760 | tf_op jit(solution)/shard_map/ppermute | solution.py:185
  15.2 0.6 collective-permute-start.2
  15.8 6.0 %collective-permute-done.2 = bf16[4,144,128]{2,1,0:T(8,128)(2,1)S(1)} collective-permute-done((bf16[4,144,128]{2,1,0:T(8,128)(2,1)S(1)}, bf16[4,144,128]{2,1,0:T(8,128)(2,1)S(1)}, u32[]{:S(2)}, u32[]{:S(2)}) %collective-permute-start.2) | collective-permute-done | bytes 147488 | tf_op jit(solution)/shard_map/ppermute | solution.py:185
  21.8 0.1 collective-permute-start.3
  21.9 0.0 collective-permute-done.7
  21.9 0.6 collective-permute-start.8
  22.6 6.0 %collective-permute-done.3 = bf16[8,144,128]{2,1,0:T(8,128)(2,1)S(1)} collective-permute-done((bf16[8,144,128]{2,1,0:T(8,128)(2,1)S(1)}, bf16[8,144,128]{2,1,0:T(8,128)(2,1)S(1)}, u32[]{:S(2)}, u32[]{:S(2)}) %collective-permute-start.3) | collective-permute-done | bytes 294944 | tf_op jit(solution)/shard_map/ppermute | solution.py:185
  28.6 0.0 copy-start.2
  28.7 0.0 copy-start.1
  28.7 0.1 collective-permute-start.4
  28.8 0.0 collective-permute-done.8
  28.8 0.0 copy-start.3
  28.8 0.6 collective-permute-start.9
  29.4 0.5 copy-done.1
  29.8 0.0 copy-start
  29.8 0.9 %copy.21 = bf16[9,128,128]{2,1,0:T(8,128)(2,1)} copy(bf16[9,128,128]{1,2,0:T(8,128)(2,1)S(1)} %bitcast.19) | data formatting | bytes 589824 | tf_op jit(solution)/shard_map/transpose | solution.py:563
  30.8 0.0 copy-done
  30.8 0.0 copy-start.7
  30.8 0.0 copy-start.8
  30.8 0.9 %copy.20 = bf16[9,128,128]{2,1,0:T(8,128)(2,1)} copy(bf16[9,128,128]{1,2,0:T(8,128)(2,1)S(1)} %bitcast.17) | data formatting | bytes 589824 | tf_op jit(solution)/shard_map/transpose | solution.py:561
  31.7 0.0 copy-done.2
  31.7 0.0 copy-done.3
  31.7 0.0 copy-start.10
  31.7 0.7 copy-done.10
  32.4 0.6 pad_add_fusion.scalars
  33.0 0.0 copy-done.7
  33.0 0.0 copy-done.8
  33.0 0.7 pad_maximum_fusion.2.w_all
  33.7 0.0 collective-permute-done.9.cot_far
  33.7 0.0 copy-start.6
  33.7 0.0 collective-permute-done.4.far
  33.7 0.0 copy-start.4
  33.7 0.8 %copy-done.6 = bf16[16,128,128]{2,1,0:T(8,128)(2,1)} copy-done((bf16[16,128,128]{2,1,0:T(8,128)(2,1)}, bf16[16,128,128]{2,1,0:T(8,128)(2,1)S(1)}, u32[]{:S(2)}) %copy-start.6) | copy-done | bytes 524312
  34.5 0.2 copy-done.4
  34.7 38.3 %shard_map.129 = (bf16[128,128]{1,0:T(8,128)(2,1)}, bf16[128,128]{1,0:T(8,128)(2,1)}, f32[9,128,128]{2,1,0:T(8,128)}, f32[9,128,128]{2,1,0:T(8,128)}) custom-call(s32[4]{0:T(128)} %pad_add_fusion.scalars, bf16[16,144,128]{2,1,0:T(8,128)(2,1)} %copy-done.2, bf16[16,144,128]{2,1,0:T(8,128)(2,1)} %copy-done.4, bf16[16,128,128]{2,1,0:T(8,128)(2,1)} %copy-done.3, ...), custom_call_target="tpu_custom_call" | custom-call | tf_op jit(solution)/shard_map/pallas_call | solution.py:523
  (16 shorter events, 0.3 us)
Async XLA Ops:
  0.6 3.1 %copy-start.9 = (bf16[16,8,128]{2,1,0:T(8,128)(2,1)S(1)}, bf16[16,8,128]{2,1,0:T(8,128)(2,1)}, u32[]{:S(2)}) copy-start(bf16[16,8,128]{2,1,0:T(8,128)(2,1)} %param.10) | copy-start | bytes 98308
  0.6 4.2 %collective-permute-start.5 = (bf16[1,128,128]{2,1,0:T(8,128)(2,1)}, bf16[1,128,128]{2,1,0:T(8,128)(2,1)S(1)}, u32[]{:S(2)}, u32[]{:S(2)}) collective-permute-start(bf16[1,128,128]{2,1,0:T(8,128)(2,1)} %bitcast.22), channel_id=1, source_target_pairs={{0,16},{8,24},{16,0},{24,8},{1,17},{9,25},{17,1},{25,9},{2,18},{10... | collective-permute-start | bytes 98312 | tf_op jit(solution)/shard_map/ppermute | solution.py:185
  3.8 0.8 %copy-start.5 = (bf16[16,8,128]{2,1,0:T(8,128)(2,1)S(1)}, bf16[16,8,128]{2,1,0:T(8,128)(2,1)}, u32[]{:S(2)}) copy-start(bf16[16,8,128]{2,1,0:T(8,128)(2,1)} %param.19) | copy-start | bytes 98308
  3.8 6.1 %collective-permute-start = (bf16[1,144,128]{2,1,0:T(8,128)(2,1)S(1)}, bf16[1,144,128]{2,1,0:T(8,128)(2,1)S(1)}, u32[]{:S(2)}, u32[]{:S(2)}) collective-permute-start(bf16[1,144,128]{2,1,0:T(8,128)(2,1)S(1)} %get-tuple-element.13), channel_id=1, source_target_pairs={{0,4},{1,5},{2,6},{3,7},{4,0},{5,1},{6,2},{7,3},{8,12},{9,13},{10,... | collective-permute-start | bytes 110600 | tf_op jit(solution)/shard_map/ppermute | solution.py:185
  4.8 6.3 %collective-permute-start.6 = (bf16[2,128,128]{2,1,0:T(8,128)(2,1)S(1)}, bf16[2,128,128]{2,1,0:T(8,128)(2,1)S(1)}, u32[]{:S(2)}, u32[]{:S(2)}) collective-permute-start(bf16[2,128,128]{2,1,0:T(8,128)(2,1)S(1)} %pad_maximum_fusion.6), channel_id=1, source_target_pairs={{0,4},{1,5},{2,6},{3,7},{4,0},{5,1},{6,2},{7,3},{8,12},{9,13},{10,... | collective-permute-start | bytes 196616 | tf_op jit(solution)/shard_map/ppermute | solution.py:185
  10.0 5.2 %collective-permute-start.1 = (bf16[2,144,128]{2,1,0:T(8,128)(2,1)S(1)}, bf16[2,144,128]{2,1,0:T(8,128)(2,1)S(1)}, u32[]{:S(2)}, u32[]{:S(2)}) collective-permute-start(bf16[2,144,128]{2,1,0:T(8,128)(2,1)S(1)} %pad_maximum_fusion.5), channel_id=1, source_target_pairs={{0,2},{1,3},{2,0},{3,1},{4,6},{5,7},{6,4},{7,5},{8,10},{9,11},{10,... | collective-permute-start | bytes 221192 | tf_op jit(solution)/shard_map/ppermute | solution.py:185
  11.2 10.7 %collective-permute-start.7 = (bf16[4,128,128]{2,1,0:T(8,128)(2,1)S(1)}, bf16[4,128,128]{2,1,0:T(8,128)(2,1)S(1)}, u32[]{:S(2)}, u32[]{:S(2)}) collective-permute-start(bf16[4,128,128]{2,1,0:T(8,128)(2,1)S(1)} %pad_maximum_fusion.4), channel_id=1, source_target_pairs={{0,2},{1,3},{2,0},{3,1},{4,6},{5,7},{6,4},{7,5},{8,10},{9,11},{10,... | collective-permute-start | bytes 393224 | tf_op jit(solution)/shard_map/ppermute | solution.py:185
  15.2 6.6 %collective-permute-start.2 = (bf16[4,144,128]{2,1,0:T(8,128)(2,1)S(1)}, bf16[4,144,128]{2,1,0:T(8,128)(2,1)S(1)}, u32[]{:S(2)}, u32[]{:S(2)}) collective-permute-start(bf16[4,144,128]{2,1,0:T(8,128)(2,1)S(1)} %pad_maximum_fusion.3), channel_id=1, source_target_pairs={{0,1},{1,0},{2,3},{3,2},{4,5},{5,4},{6,7},{7,6},{8,9},{9,8},{10,11... | collective-permute-start | bytes 442376 | tf_op jit(solution)/shard_map/ppermute | solution.py:185
  21.8 6.8 %collective-permute-start.3 = (bf16[8,144,128]{2,1,0:T(8,128)(2,1)S(1)}, bf16[8,144,128]{2,1,0:T(8,128)(2,1)S(1)}, u32[]{:S(2)}, u32[]{:S(2)}) collective-permute-start(bf16[8,144,128]{2,1,0:T(8,128)(2,1)S(1)} %pad_maximum_fusion), channel_id=1, source_target_pairs={{0,16},{8,24},{16,0},{24,8},{1,17},{9,25},{17,1},{25,9},{2,18},{10... | collective-permute-start | bytes 884744 | tf_op jit(solution)/shard_map/ppermute | solution.py:185
  21.9 6.8 %collective-permute-start.8 = (bf16[8,128,128]{2,1,0:T(8,128)(2,1)S(1)}, bf16[8,128,128]{2,1,0:T(8,128)(2,1)S(1)}, u32[]{:S(2)}, u32[]{:S(2)}) collective-permute-start(bf16[8,128,128]{2,1,0:T(8,128)(2,1)S(1)} %pad_maximum_fusion.1), channel_id=1, source_target_pairs={{0,1},{1,0},{2,3},{3,2},{4,5},{5,4},{6,7},{7,6},{8,9},{9,8},{10,11... | collective-permute-start | bytes 786440 | tf_op jit(solution)/shard_map/ppermute | solution.py:185
  28.6 3.1 %copy-start.2 = (bf16[16,144,128]{2,1,0:T(8,128)(2,1)}, bf16[16,144,128]{2,1,0:T(8,128)(2,1)S(1)}, u32[]{:S(2)}) copy-start(bf16[16,144,128]{2,1,0:T(8,128)(2,1)S(1)} %constant_dynamic-update-slice_fusion.near) | copy-start | bytes 1769476
  28.7 1.2 %copy-start.1 = (bf16[9,128,128]{2,1,0:T(8,128)(2,1)S(1)}, bf16[9,128,128]{2,1,0:T(8,128)(2,1)}, u32[]{:S(2)}) copy-start(bf16[9,128,128]{2,1,0:T(8,128)(2,1)} %param.18) | copy-start | bytes 884740
  28.7 5.0 %collective-permute-start.4 = (bf16[16,144,128]{2,1,0:T(8,128)(2,1)S(1)}, bf16[16,144,128]{2,1,0:T(8,128)(2,1)S(1)}, u32[]{:S(2)}, u32[]{:S(2)}) collective-permute-start(bf16[16,144,128]{2,1,0:T(8,128)(2,1)S(1)} %constant_dynamic-update-slice_fusion.near), channel_id=1, source_target_pairs={{0,8},{8,0},{16,24},{24,16},{1,9},{9,1},{17,25},{25,17},{2,10},{10... | collective-permute-start | bytes 1769480 | tf_op jit(solution)/shard_map/ppermute | solution.py:185
  28.8 2.9 %copy-start.3 = (bf16[16,128,128]{2,1,0:T(8,128)(2,1)}, bf16[16,128,128]{2,1,0:T(8,128)(2,1)S(1)}, u32[]{:S(2)}) copy-start(bf16[16,128,128]{2,1,0:T(8,128)(2,1)S(1)} %constant_dynamic-update-slice_fusion.5.cot_near) | copy-start | bytes 1572868
  28.8 4.9 %collective-permute-start.9 = (bf16[16,128,128]{2,1,0:T(8,128)(2,1)S(1)}, bf16[16,128,128]{2,1,0:T(8,128)(2,1)S(1)}, u32[]{:S(2)}, u32[]{:S(2)}) collective-permute-start(bf16[16,128,128]{2,1,0:T(8,128)(2,1)S(1)} %constant_dynamic-update-slice_fusion.5.cot_near), channel_id=1, source_target_pairs={{0,8},{8,0},{16,24},{24,16},{1,9},{9,1},{17,25},{25,17},{2,10},{10... | collective-permute-start | bytes 1572872 | tf_op jit(solution)/shard_map/ppermute | solution.py:185
  29.8 1.0 %copy-start = (bf16[9,128,128]{2,1,0:T(8,128)(2,1)S(1)}, bf16[9,128,128]{2,1,0:T(8,128)(2,1)}, u32[]{:S(2)}) copy-start(bf16[9,128,128]{2,1,0:T(8,128)(2,1)} %param.17) | copy-start | bytes 884740
  30.8 2.2 %copy-start.7 = (bf16[128,512]{1,0:T(8,128)(2,1)S(1)}, bf16[128,512]{1,0:T(8,128)(2,1)}, u32[]{:S(2)}) copy-start(bf16[128,512]{1,0:T(8,128)(2,1)} %param.14) | copy-start | bytes 393220
  30.8 2.2 %copy-start.8 = (bf16[128,128]{1,0:T(8,128)(2,1)S(1)}, bf16[128,128]{1,0:T(8,128)(2,1)}, u32[]{:S(2)}) copy-start(bf16[128,128]{1,0:T(8,128)(2,1)} %param.15) | copy-start | bytes 98308
  31.7 0.7 copy-start.10
  33.7 0.8 %copy-start.6 = (bf16[16,128,128]{2,1,0:T(8,128)(2,1)}, bf16[16,128,128]{2,1,0:T(8,128)(2,1)S(1)}, u32[]{:S(2)}) copy-start(bf16[16,128,128]{2,1,0:T(8,128)(2,1)S(1)} %collective-permute-done.9.cot_far) | copy-start | bytes 1572868
  33.7 1.0 %copy-start.4 = (bf16[16,144,128]{2,1,0:T(8,128)(2,1)}, bf16[16,144,128]{2,1,0:T(8,128)(2,1)S(1)}, u32[]{:S(2)}) copy-start(bf16[16,144,128]{2,1,0:T(8,128)(2,1)S(1)} %collective-permute-done.4.far) | copy-start | bytes 1769476

commit v3 on v2

--- a/solution.py
+++ b/solution.py
@@ -8,7 +8,7 @@
 from jax.sharding import PartitionSpec as P
 
 DMAX = 8
-VMEM_LIMIT = 56 * 1024 * 1024
+VMEM_LIMIT = 48 * 1024 * 1024
 
 
 EPSILON = 1e-05
@@ -199,6 +199,13 @@
     return row, col
 
 
+def same_place(position, rounds, others):
+    moved = 0
+    for step, hop in enumerate(rounds):
+        moved = moved | (((position >> step) & 1) << others.index(hop))
+    return moved
+
+
 def sigmoid(values):
     return 0.5 + 0.5 * jnp.tanh(0.5 * values)
 
@@ -213,17 +220,16 @@
     height,
     breadth,
     tokens,
-    scalars,
+    dilations,
     near,
     far,
     cot_near,
     cot_far,
-    w_all,
+    w_proj,
+    w_gate,
     w_out,
     one,
-    one_t,
     two,
-    two_t,
     output,
     grad_pair,
     grad_one,
@@ -234,39 +240,46 @@
     start,
     contact,
     updated,
+    products,
     field,
+    cot_field,
     wide,
     wide_cot,
+    wide_pre,
     second,
-    factor,
+    hidden_grad,
     grad_pre,
     flipped,
     flipped_two,
     sum_one,
     sum_two,
+    two_t,
 ):
     channels = w_out.shape[1]
     hidden = w_out.shape[0]
     pixels = height * breadth
-    row_place, col_place = scalars[0], scalars[1]
-    rate_one, rate_two = scalars[2], scalars[3]
+    row_place, col_place = lax.axis_index("row"), lax.axis_index("col")
+    rate_one, rate_two = dilations[0], dilations[1]
     half = near.shape[0]
     line = tokens + 2 * DMAX
+    inside = slice(DMAX, DMAX + tokens)
 
     rim = jnp.zeros((tokens, DMAX, channels), jnp.float32)
-    field[:, 0:DMAX, :] = rim
-    field[:, DMAX + tokens :, :] = rim
     edge = jnp.zeros((DMAX, tokens, 3 * channels), jnp.bfloat16)
-    for target in (wide, wide_cot):
+    border = jnp.zeros((DMAX, line, channels), jnp.float32)
+    for target in (field, cot_field):
+        target[:, 0:DMAX, :] = rim
+        target[:, DMAX + tokens :, :] = rim
+    for target in (wide, wide_cot, wide_pre):
         target[0:DMAX] = edge
         target[DMAX + tokens :] = edge
-    border = jnp.zeros((DMAX, line, channels), jnp.float32)
-    side = jnp.zeros((tokens, DMAX, channels), jnp.float32)
     for target in (second, grad_pre):
         target[0:DMAX] = border
         target[DMAX + tokens :] = border
-        target[DMAX : DMAX + tokens, 0:DMAX, :] = side
-        target[DMAX : DMAX + tokens, DMAX + tokens :, :] = side
+        target[inside, 0:DMAX, :] = rim
+        target[inside, DMAX + tokens :, :] = rim
+    for tap in range(9):
+        two_t[tap * channels : (tap + 1) * channels] = two[tap].T
 
     lane = lax.broadcasted_iota(jnp.int32, (breadth, channels), 1)
     place = lax.broadcasted_iota(jnp.int32, (breadth, channels), 0)
@@ -276,56 +289,67 @@
     pick = jnp.where(pick_lane // breadth == pick_half, 1.0, 0.0).astype(jnp.bfloat16)
     several = 4
 
-    def project(source, base):
+    def project(source, cot_source, base):
         def body(step, carry):
             first = step * several
+            partners = [
+                same_place(first + i, rounds[:-1], cot_rounds[:-1]) for i in range(several)
+            ]
             masks = jnp.concatenate(
                 [
                     (
-                        source[first + i, pixels:, :].astype(jnp.float32)[:, None, :]
+                        cot_source[partner, pixels:, :].astype(jnp.float32)[:, None, :]
                         * own_lane[None]
                     ).reshape(pixels, channels)
-                    for i in range(several)
+                    for partner in partners
                 ],
                 axis=0,
             ).astype(jnp.bfloat16)
             masks = matmul(masks, pick)
-            values = jnp.concatenate(
-                [source[first + i, 0:pixels, :] for i in range(several)], axis=0
-            ).astype(jnp.float32)
+            values = (
+                source[pl.ds(first, several)]
+                .reshape(several * pixels, channels)
+                .astype(jnp.float32)
+            )
             normed = layer_norm(values).astype(jnp.bfloat16)
-            projected = matmul(normed, w_all[...])
+            projected = matmul(normed, w_proj[...])
             mask = masks[:, :hidden]
             left_side = (
                 mask * sigmoid(projected[:, hidden : 2 * hidden]) * projected[:, :hidden]
             )
             right_side = (
                 mask
-                * sigmoid(projected[:, 3 * hidden : 4 * hidden])
+                * sigmoid(projected[:, 3 * hidden :])
                 * projected[:, 2 * hidden : 3 * hidden]
             )
-            gates = sigmoid(projected[:, 4 * hidden :])
+            gates = sigmoid(matmul(normed, w_gate[...]))
             shape = (height, breadth, channels)
             for i in range(several):
                 row, col = place_of(base + first + i, rounds, row_place, col_place)
                 rows = pl.ds(pl.multiple_of(row * height, height), height)
                 cols = pl.ds(pl.multiple_of(col * breadth, breadth), breadth)
+                padded = pl.ds(pl.multiple_of(DMAX + col * breadth, breadth), breadth)
                 part = slice(i * pixels, (i + 1) * pixels)
                 left[rows, cols, :] = left_side[part].reshape(shape)
                 right[cols, rows, :] = jnp.swapaxes(right_side[part].reshape(shape), 0, 1)
                 gating[rows, cols, :] = gates[part].reshape(shape)
                 start[rows, cols, :] = values[part].reshape(shape)
                 contact[rows, cols, :] = masks[part, channels:].reshape(shape)
+                cot_field[rows, padded, :] = (
+                    cot_source[partners[i], 0:pixels, :].astype(jnp.float32).reshape(shape)
+                )
             return carry
 
         lax.fori_loop(0, half // several, body, 0)
 
-    project(near, 0)
-    project(far, half)
-
-    def spread(rows, rate, target):
+    project(near, cot_near, 0)
+    project(far, cot_far, half)
+
+    def spread(source, rows, pad, rate, target):
         for tap in range(3):
-            moved = field[rows, pl.ds(DMAX + (tap - 1) * rate, tokens), :]
+            moved = source[
+                pl.ds(pad + rows.start, rows.size), pl.ds(DMAX + (tap - 1) * rate, tokens), :
+            ]
             target[
                 pl.ds(DMAX + rows.start, rows.size), :, tap * channels : (tap + 1) * channels
             ] = moved.astype(jnp.bfloat16)
@@ -337,127 +361,105 @@
         ]
         return jnp.concatenate(views, axis=1)
 
-    def place_cot(source, base):
-        def body(step, carry):
-            for i in range(several):
-                slot = step * several + i
-                row, col = place_of(base + slot, cot_rounds, row_place, col_place)
-                cols = pl.ds(pl.multiple_of(DMAX + col * breadth, breadth), breadth)
-                field[pl.ds(row * height, height), cols, :] = (
-                    source[slot].astype(jnp.float32).reshape(height, breadth, channels)
-                )
-            return carry
-
-        lax.fori_loop(0, half // several, body, 0)
+    def lanes(step, size):
+        return pl.ds(pl.multiple_of(step * size, size), size)
 
     chunk = 8
     size = chunk * tokens
     steps = tokens // chunk
-    place_cot(cot_near, 0)
-    place_cot(cot_far, half)
-    lax.fori_loop(
-        0, steps, lambda i, c: (spread(pl.ds(i * chunk, chunk), -rate_two, wide_cot), c)[1], 0
-    )
+
+    def spread_cot(step, carry):
+        spread(cot_field, pl.ds(step * chunk, chunk), 0, -rate_two, wide_cot)
+        return carry
+
+    lax.fori_loop(0, steps, spread_cot, 0)
 
     group = 4
 
-    def triangle(step, carry):
-        def inner(part, sums):
-            base = pl.multiple_of(part * 8, 8)
-            for k in range(8):
-                others = right[base + k]
-                sums = tuple(
-                    total + left[step * group + i, pl.ds(base + k, 1), :] * others
-                    for i, total in enumerate(sums)
-                )
-            return sums
-
-        sums = lax.fori_loop(
-            0,
-            tokens // 8,
-            inner,
-            tuple(jnp.zeros((tokens, hidden), jnp.float32) for _ in range(group)),
-        )
+    def triangle(step):
+        sums = [jnp.zeros((tokens, hidden), jnp.float32)] * group
+        for k in range(tokens):
+            others = right[k]
+            sums = [
+                total + left[step * group + i, k : k + 1, :] * others
+                for i, total in enumerate(sums)
+            ]
         for i, total in enumerate(sums):
-            left[step * group + i] = total
-        return carry
-
-    lax.fori_loop(0, tokens // group, triangle, 0)
-
-    def update(step, carry):
-        rows = pl.ds(step * chunk, chunk)
-        products = left[rows].reshape(size, hidden)
-        product_norm = layer_norm(products).astype(jnp.bfloat16)
-        change = matmul(product_norm, w_out[...]).reshape(chunk, tokens, channels)
+            products[step * group + i] = total
+
+    def hidden_conv(step):
+        hidden_grad[pl.ds(step * group, group)] = matmul(
+            taps(wide_cot, step * group, group, -rate_two), two_t[...]
+        ).reshape(group, tokens, channels)
+
+    def update(step):
+        rows = pl.ds(step * group, group)
+        flat = products[rows].reshape(group * tokens, hidden)
+        product_norm = layer_norm(flat).astype(jnp.bfloat16)
+        change = matmul(product_norm, w_out[...]).reshape(group, tokens, channels)
         fresh = (start[rows] + gating[rows] * change).astype(jnp.bfloat16).astype(jnp.float32)
         updated[rows] = fresh
         first_in = layer_norm(fresh) * contact[rows]
-        field[rows, DMAX : DMAX + tokens, :] = first_in
-        spread(rows, rate_one, wide)
-        flipped[:, pl.ds(pl.multiple_of(step * size, size), size)] = (
-            first_in.reshape(size, channels).astype(jnp.bfloat16).T
-        )
+        field[rows, inside, :] = first_in
+        spread(field, rows, 0, rate_one, wide)
+        flipped[:, lanes(step, group * tokens)] = (
+            first_in.reshape(group * tokens, channels).astype(jnp.bfloat16).T
+        )
+
+    def early(step, carry):
+        triangle(step)
+        hidden_conv(step)
+        update(step - 1)
         return carry
 
-    lax.fori_loop(0, steps, update, 0)
-
-    def first_conv(step, carry):
+    triangle(0)
+    hidden_conv(0)
+    lax.fori_loop(1, tokens // group, early, 0)
+    update(tokens // group - 1)
+
+    def first_conv(step):
         first = step * chunk
+        rows = pl.ds(DMAX + first, chunk)
+        shape = (chunk, tokens, channels)
         pre = matmul(taps(wide, first, chunk, rate_one), one[...])
         sigma = sigmoid(pre)
         second_in = pre * sigma
-        factor[pl.ds(first, chunk)] = (sigma * (1.0 + pre * (1.0 - sigma))).reshape(
-            chunk, tokens, channels
-        )
-        second[pl.ds(DMAX + first, chunk), DMAX : DMAX + tokens, :] = second_in.reshape(
-            chunk, tokens, channels
-        )
-        flipped_two[:, pl.ds(pl.multiple_of(step * size, size), size)] = second_in.astype(
-            jnp.bfloat16
-        ).T
+        second[rows, inside, :] = second_in.reshape(shape)
+        flipped_two[:, lanes(step, size)] = second_in.astype(jnp.bfloat16).T
+        factor = (sigma * (1.0 + pre * (1.0 - sigma))).reshape(shape)
+        grad_pre[rows, inside, :] = (
+            (hidden_grad[pl.ds(first, chunk)] * factor).astype(jnp.bfloat16).astype(jnp.float32)
+        )
+
+    def after_conv(step):
+        sum_two[...] += matmul(
+            flipped_two[:, lanes(step, size)], taps(wide_cot, step * chunk, chunk, -rate_two)
+        )
+        spread(grad_pre, pl.ds(step * chunk, chunk), DMAX, -rate_one, wide_pre)
+
+    def middle(step, carry):
+        first_conv(step)
+        after_conv(step - 1)
         return carry
 
-    lax.fori_loop(0, steps, first_conv, 0)
-
     sum_two[...] = jnp.zeros_like(sum_two)
-
-    def back_two(step, carry):
-        first = step * chunk
-        shifted = taps(wide_cot, first, chunk, -rate_two)
-        sum_two[...] += matmul(
-            flipped_two[:, pl.ds(pl.multiple_of(step * size, size), size)], shifted
-        )
-        rows = pl.ds(first, chunk)
-        pre = matmul(shifted, two_t[...]).reshape(chunk, tokens, channels) * factor[rows]
-        pre = pre.astype(jnp.bfloat16).astype(jnp.float32)
-        grad_pre[pl.ds(DMAX + first, chunk), DMAX : DMAX + tokens, :] = pre
-        return carry
-
-    lax.fori_loop(0, steps, back_two, 0)
-
-    def spread_pre(step, carry):
-        rows = pl.ds(DMAX + step * chunk, chunk)
-        for tap in range(3):
-            moved = grad_pre[rows, pl.ds(DMAX - (tap - 1) * rate_one, tokens), :]
-            wide[rows, :, tap * channels : (tap + 1) * channels] = moved.astype(jnp.bfloat16)
-        return carry
-
-    lax.fori_loop(0, steps, spread_pre, 0)
+    first_conv(0)
+    lax.fori_loop(1, steps, middle, 0)
+    after_conv(steps - 1)
 
     sum_one[...] = jnp.zeros_like(sum_one)
 
     def back_one(step, carry):
-        shifted = taps(wide, step * chunk, chunk, -rate_one)
         sum_one[...] += matmul(
-            flipped[:, pl.ds(pl.multiple_of(step * size, size), size)], shifted
+            flipped[:, lanes(step, size)], taps(wide_pre, step * chunk, chunk, -rate_one)
         )
         return carry
 
     lax.fori_loop(0, steps, back_one, 0)
     for tap in range(9):
-        lanes = slice(tap * channels, (tap + 1) * channels)
-        grad_one[tap] = sum_one[:, lanes] * (1.0 / tokens)
-        grad_two[tap] = sum_two[:, lanes] * (1.0 / tokens)
+        columns = slice(tap * channels, (tap + 1) * channels)
+        grad_one[tap] = sum_one[:, columns] * (1.0 / tokens)
+        grad_two[tap] = sum_two[:, columns] * (1.0 / tokens)
 
     row_start, col_start = row_place * height, col_place * breadth
 
@@ -475,11 +477,15 @@
     rows = pl.ds(row_start, height)
     cols = pl.ds(pl.multiple_of(col_start, breadth), breadth)
     mine = updated[rows, cols, :].reshape(pixels, channels)
-    second_pre = matmul(windows(second, rate_two), two[...])
+    second_pre = matmul(windows(second, rate_two), two[...].reshape(9 * channels, channels))
     output[...] = (mine + second_pre).astype(jnp.bfloat16)
-    grad_input = matmul(windows(grad_pre, -rate_one), one_t[...]) * contact[rows, cols, :].reshape(
-        pixels, channels
-    )
+    one_rows = [one[tap * channels : (tap + 1) * channels] for tap in range(9)]
+    grad_input = lax.dot_general(
+        windows(grad_pre, -rate_one),
+        jnp.concatenate(one_rows, axis=1),
+        (((1,), (1,)), ((), ())),
+        preferred_element_type=jnp.float32,
+    ) * contact[rows, cols, :].reshape(pixels, channels)
     centre = mine - jnp.mean(mine, axis=-1, keepdims=True)
     inv_spread = lax.rsqrt(jnp.mean(centre * centre, axis=-1, keepdims=True) + EPSILON)
     scaled = centre * inv_spread
@@ -488,7 +494,9 @@
         - jnp.mean(grad_input, axis=-1, keepdims=True)
         - scaled * jnp.mean(grad_input * scaled, axis=-1, keepdims=True)
     )
-    grad_pair[...] = (cot_near[0].astype(jnp.float32) + grad_norm).astype(jnp.bfloat16)
+    grad_pair[...] = (cot_near[0, 0:pixels, :].astype(jnp.float32) + grad_norm).astype(
+        jnp.bfloat16
+    )
 
 
 def replicated(
@@ -508,21 +516,21 @@
         ],
         axis=1,
     )
-    packed = jnp.concatenate([pair.reshape(pixels, channels), masks], axis=0)
-    near, far = gather_blocks(packed, rounds)
-    cot_near, cot_far = gather_blocks(cotangent.reshape(pixels, channels), cot_rounds)
-    scalars = jnp.concatenate(
-        [
-            jnp.stack([lax.axis_index("row"), lax.axis_index("col")]).astype(jnp.int32),
-            dilations,
-        ]
-    )
+    packed = jnp.concatenate([cotangent.reshape(pixels, channels), masks], axis=0)
+    near, far = gather_blocks(pair.reshape(pixels, channels), rounds)
+    cot_near, cot_far = gather_blocks(packed, cot_rounds)
     f32, bf16 = jnp.float32, jnp.bfloat16
     line = tokens + 2 * DMAX
     in_vmem = pl.BlockSpec(memory_space=pltpu.VMEM)
+    whole = pltpu.VMEM((tokens, tokens, channels), f32)
+    padded = pltpu.VMEM((tokens, line, channels), f32)
+    bordered = pltpu.VMEM((line, line, channels), f32)
+    tripled = pltpu.VMEM((line, tokens, 3 * channels), bf16)
+    turned = pltpu.VMEM((channels, tokens * tokens), bf16)
+    sums = pltpu.VMEM((channels, 9 * channels), f32)
     output, grad_pair, grad_one, grad_two = pl.pallas_call(
         functools.partial(block_kernel, rounds, cot_rounds, height, breadth, tokens),
-        in_specs=[pl.BlockSpec(memory_space=pltpu.SMEM)] + [in_vmem] * 10,
+        in_specs=[pl.BlockSpec(memory_space=pltpu.SMEM)] + [in_vmem] * 9,
         out_specs=[in_vmem] * 4,
         out_shape=[
             jax.ShapeDtypeStruct((pixels, channels), bf16),
@@ -530,37 +538,25 @@
             jax.ShapeDtypeStruct((9, channels, channels), f32),
             jax.ShapeDtypeStruct((9, channels, channels), f32),
         ],
-        scratch_shapes=[
-            pltpu.VMEM((tokens, tokens, hidden), f32),
-            pltpu.VMEM((tokens, tokens, hidden), f32),
-            pltpu.VMEM((tokens, tokens, channels), f32),
-            pltpu.VMEM((tokens, tokens, channels), f32),
-            pltpu.VMEM((tokens, tokens, channels), f32),
-            pltpu.VMEM((tokens, tokens, channels), f32),
-            pltpu.VMEM((tokens, line, channels), f32),
-            pltpu.VMEM((line, tokens, 3 * channels), bf16),
-            pltpu.VMEM((line, tokens, 3 * channels), bf16),
-            pltpu.VMEM((line, line, channels), f32),
-            pltpu.VMEM((tokens, tokens, channels), f32),
-            pltpu.VMEM((line, line, channels), f32),
-            pltpu.VMEM((channels, tokens * tokens), bf16),
-            pltpu.VMEM((channels, tokens * tokens), bf16),
-            pltpu.VMEM((channels, 9 * channels), f32),
-            pltpu.VMEM((channels, 9 * channels), f32),
-        ],
+        scratch_shapes=[whole] * 7
+        + [padded] * 2
+        + [tripled] * 3
+        + [bordered, whole, bordered]
+        + [turned] * 2
+        + [sums] * 2
+        + [pltpu.VMEM((9 * channels, channels), bf16)],
         compiler_params=pltpu.CompilerParams(vmem_limit_bytes=VMEM_LIMIT),
     )(
-        scalars,
+        dilations,
         near,
         far,
         cot_near,
         cot_far,
-        jnp.concatenate([w_proj, w_gate], axis=1),
+        w_proj,
+        w_gate,
         w_out,
         conv_one.reshape(9 * channels, channels),
-        conv_one.transpose(0, 2, 1).reshape(9 * channels, channels),
-        conv_two.reshape(9 * channels, channels),
-        conv_two.transpose(0, 2, 1).reshape(9 * channels, channels),
+        conv_two,
     )
     block = (height, breadth, channels)
     return output.reshape(block), grad_pair.reshape(block), grad_one, grad_two

time: 73.3 us -> 70.5 us (0.962)
  the two profiles are of different devices: /device:TPU:28 before, /device:TPU:0 now
where the time goes in v3:
time: 70.5 us; the launch traced here: 70.3 us
  Pallas kernels  39.2 us (56%)
  starting transfers between devices  15.1 us (21%)
  waiting for transfers between devices  13.2 us (19%)
  other arithmetic  1.57 us (2%)
  between operations  0.8 us (1%)
    pallas_call x1, Pallas kernels, replicated(): pl.pallas_call(functools.partial(block_kernel, rounds, cot_rounds, height...  39.2 us
    ppermute x10, starting transfers between devices, gather_blocks(): other = lax.ppermute(held, axis, pairs)  15.1 us
    ppermute x10, waiting for transfers between devices, gather_blocks(): other = lax.ppermute(held, axis, pairs)  13.2 us
  transfers between devices with their start and end apart: 10, of which 7 were waited for; matrix products, arithmetic and copies ran while one was open for 3% of the time, Pallas kernels for 0%

profile of v3, /device:TPU:0, one launch (start us, length us, event | category | flops | bytes accessed | tf_op | source)
XLA Modules:
  0.0 70.3 jit_solution(4286549007477157062)
XLA Ops:
  0.6 0.0 copy-start.7
  0.6 4.1 %collective-permute-start = (bf16[1,128,128]{2,1,0:T(8,128)(2,1)}, bf16[1,128,128]{2,1,0:T(8,128)(2,1)S(1)}, u32[]{:S(2)}, u32[]{:S(2)}) collective-permute-start(bf16[1,128,128]{2,1,0:T(8,128)(2,1)} %bitcast.10), channel_id=1, source_target_pairs={{0,4},{1,5},{2,6},{3,7},{4,0},{5,1},{6,2},{7,3},{8,12},{9,13},{10,... | collective-permute-start | bytes 98312 | tf_op jit(solution)/shard_map/ppermute | solution.py:185
  4.7 0.7 convert_element_type.6
  5.4 0.1 copy.16
  5.5 0.7 convert_element_type.7
  6.2 0.1 copy.17
  6.3 0.0 copy-done.7
  6.3 0.0 copy-start.6
  6.3 0.1 constant_dynamic-update-slice_fusion.9
  6.4 1.5 %collective-permute-start.5 = (bf16[1,144,128]{2,1,0:T(8,128)(2,1)S(1)}, bf16[1,144,128]{2,1,0:T(8,128)(2,1)S(1)}, u32[]{:S(2)}, u32[]{:S(2)}) collective-permute-start(bf16[1,144,128]{2,1,0:T(8,128)(2,1)S(1)} %get-tuple-element.13), channel_id=1, source_target_pairs={{0,16},{8,24},{16,0},{24,8},{1,17},{9,25},{17,1},{25,9},{2,18},{10... | collective-permute-start | bytes 110600 | tf_op jit(solution)/shard_map/ppermute | solution.py:185
  7.9 0.0 copy-done.6
  7.9 0.0 collective-permute-done
  7.9 1.6 %collective-permute-start.1 = (bf16[2,128,128]{2,1,0:T(8,128)(2,1)S(1)}, bf16[2,128,128]{2,1,0:T(8,128)(2,1)S(1)}, u32[]{:S(2)}, u32[]{:S(2)}) collective-permute-start(bf16[2,128,128]{2,1,0:T(8,128)(2,1)S(1)} %pad_maximum_fusion.5), channel_id=1, source_target_pairs={{0,2},{1,3},{2,0},{3,1},{4,6},{5,7},{6,4},{7,5},{8,10},{9,11},{10,... | collective-permute-start | bytes 196616 | tf_op jit(solution)/shard_map/ppermute | solution.py:185
  9.6 0.8 %collective-permute-done.5 = bf16[1,144,128]{2,1,0:T(8,128)(2,1)S(1)} collective-permute-done((bf16[1,144,128]{2,1,0:T(8,128)(2,1)S(1)}, bf16[1,144,128]{2,1,0:T(8,128)(2,1)S(1)}, u32[]{:S(2)}, u32[]{:S(2)}) %collective-permute-start.5) | collective-permute-done | bytes 36896 | tf_op jit(solution)/shard_map/ppermute | solution.py:185
  10.4 1.4 %collective-permute-start.6 = (bf16[2,144,128]{2,1,0:T(8,128)(2,1)S(1)}, bf16[2,144,128]{2,1,0:T(8,128)(2,1)S(1)}, u32[]{:S(2)}, u32[]{:S(2)}) collective-permute-start(bf16[2,144,128]{2,1,0:T(8,128)(2,1)S(1)} %pad_maximum_fusion.4), channel_id=1, source_target_pairs={{0,4},{1,5},{2,6},{3,7},{4,0},{5,1},{6,2},{7,3},{8,12},{9,13},{10,... | collective-permute-start | bytes 221192 | tf_op jit(solution)/shard_map/ppermute | solution.py:185
  11.8 0.5 collective-permute-done.1
  12.3 1.6 %collective-permute-start.2 = (bf16[4,128,128]{2,1,0:T(8,128)(2,1)S(1)}, bf16[4,128,128]{2,1,0:T(8,128)(2,1)S(1)}, u32[]{:S(2)}, u32[]{:S(2)}) collective-permute-start(bf16[4,128,128]{2,1,0:T(8,128)(2,1)S(1)} %pad_maximum_fusion.3), channel_id=1, source_target_pairs={{0,1},{1,0},{2,3},{3,2},{4,5},{5,4},{6,7},{7,6},{8,9},{9,8},{10,11... | collective-permute-start | bytes 393224 | tf_op jit(solution)/shard_map/ppermute | solution.py:185
  13.8 1.8 %collective-permute-done.6 = bf16[2,144,128]{2,1,0:T(8,128)(2,1)S(1)} collective-permute-done((bf16[2,144,128]{2,1,0:T(8,128)(2,1)S(1)}, bf16[2,144,128]{2,1,0:T(8,128)(2,1)S(1)}, u32[]{:S(2)}, u32[]{:S(2)}) %collective-permute-start.6) | collective-permute-done | bytes 73760 | tf_op jit(solution)/shard_map/ppermute | solution.py:185
  15.7 1.6 %collective-permute-start.7 = (bf16[4,144,128]{2,1,0:T(8,128)(2,1)S(1)}, bf16[4,144,128]{2,1,0:T(8,128)(2,1)S(1)}, u32[]{:S(2)}, u32[]{:S(2)}) collective-permute-start(bf16[4,144,128]{2,1,0:T(8,128)(2,1)S(1)} %pad_maximum_fusion.2), channel_id=1, source_target_pairs={{0,2},{1,3},{2,0},{3,1},{4,6},{5,7},{6,4},{7,5},{8,10},{9,11},{10,... | collective-permute-start | bytes 442376 | tf_op jit(solution)/shard_map/ppermute | solution.py:185
  17.4 3.5 %collective-permute-done.7 = bf16[4,144,128]{2,1,0:T(8,128)(2,1)S(1)} collective-permute-done((bf16[4,144,128]{2,1,0:T(8,128)(2,1)S(1)}, bf16[4,144,128]{2,1,0:T(8,128)(2,1)S(1)}, u32[]{:S(2)}, u32[]{:S(2)}) %collective-permute-start.7) | collective-permute-done | bytes 147488 | tf_op jit(solution)/shard_map/ppermute | solution.py:185
  20.9 1.6 %collective-permute-start.8 = (bf16[8,144,128]{2,1,0:T(8,128)(2,1)S(1)}, bf16[8,144,128]{2,1,0:T(8,128)(2,1)S(1)}, u32[]{:S(2)}, u32[]{:S(2)}) collective-permute-start(bf16[8,144,128]{2,1,0:T(8,128)(2,1)S(1)} %pad_maximum_fusion), channel_id=1, source_target_pairs={{0,1},{1,0},{2,3},{3,2},{4,5},{5,4},{6,7},{7,6},{8,9},{9,8},{10,11... | collective-permute-start | bytes 884744 | tf_op jit(solution)/shard_map/ppermute | solution.py:185
  22.5 0.0 collective-permute-done.2
  22.6 1.6 %collective-permute-start.3 = (bf16[8,128,128]{2,1,0:T(8,128)(2,1)S(1)}, bf16[8,128,128]{2,1,0:T(8,128)(2,1)S(1)}, u32[]{:S(2)}, u32[]{:S(2)}) collective-permute-start(bf16[8,128,128]{2,1,0:T(8,128)(2,1)S(1)} %pad_maximum_fusion.1), channel_id=1, source_target_pairs={{0,16},{8,24},{16,0},{24,8},{1,17},{9,25},{17,1},{25,9},{2,18},{10... | collective-permute-start | bytes 786440 | tf_op jit(solution)/shard_map/ppermute | solution.py:185
  24.2 3.6 %collective-permute-done.8 = bf16[8,144,128]{2,1,0:T(8,128)(2,1)S(1)} collective-permute-done((bf16[8,144,128]{2,1,0:T(8,128)(2,1)S(1)}, bf16[8,144,128]{2,1,0:T(8,128)(2,1)S(1)}, u32[]{:S(2)}, u32[]{:S(2)}) %collective-permute-start.8) | collective-permute-done | bytes 294944 | tf_op jit(solution)/shard_map/ppermute | solution.py:185
  27.7 0.0 copy-start.1
  27.8 0.0 copy-start
  27.8 0.0 copy-start.2
  27.8 0.0 copy-start.3
  27.8 0.0 copy-start.4
  27.8 0.1 collective-permute-start.9
  27.9 1.1 %collective-permute-done.3 = bf16[8,128,128]{2,1,0:T(8,128)(2,1)S(1)} collective-permute-done((bf16[8,128,128]{2,1,0:T(8,128)(2,1)S(1)}, bf16[8,128,128]{2,1,0:T(8,128)(2,1)S(1)}, u32[]{:S(2)}, u32[]{:S(2)}) %collective-permute-start.3) | collective-permute-done | bytes 262176 | tf_op jit(solution)/shard_map/ppermute | solution.py:185
  29.0 0.0 copy-start.5
  29.1 0.1 collective-permute-start.4
  29.1 1.9 %collective-permute-done.4.far = bf16[16,128,128]{2,1,0:T(8,128)(2,1)S(1)} collective-permute-done((bf16[16,128,128]{2,1,0:T(8,128)(2,1)S(1)}, bf16[16,128,128]{2,1,0:T(8,128)(2,1)S(1)}, u32[]{:S(2)}, u32[]{:S(2)}) %collective-permute-start.4) | collective-permute-done | bytes 524320 | tf_op jit(solution)/shard_map/ppermute | solution.py:185
  31.0 0.0 collective-permute-done.9.cot_far
  31.0 0.0 copy-done.1
  31.0 0.0 copy-done
  31.0 0.0 copy-done.2
  31.1 0.0 copy-done.3
  31.1 0.0 copy-done.4
  31.1 0.0 copy-done.5
  31.1 39.2 %shard_map.129 = (bf16[128,128]{1,0:T(8,128)(2,1)}, bf16[128,128]{1,0:T(8,128)(2,1)}, f32[9,128,128]{2,1,0:T(8,128)}, f32[9,128,128]{2,1,0:T(8,128)}) custom-call(s32[2]{0:T(128)S(1)} %copy-done.5, bf16[16,128,128]{2,1,0:T(8,128)(2,1)S(1)} %constant_dynamic-update-slice_fusion.near, bf16[16,128,128]{2,1,0:T(8,128)(2,1)S(1)} %collective-permute-done.4.far, ...), custom_call_target="tpu_custom_call" | custom-call | tf_op jit(solution)/shard_map/pallas_call | solution.py:531
  (16 shorter events, 0.3 us)
Async XLA Ops:
  0.6 5.7 %copy-start.7 = (bf16[16,8,128]{2,1,0:T(8,128)(2,1)S(1)}, bf16[16,8,128]{2,1,0:T(8,128)(2,1)}, u32[]{:S(2)}) copy-start(bf16[16,8,128]{2,1,0:T(8,128)(2,1)} %param.19) | copy-start | bytes 98308
  0.6 7.3 %collective-permute-start = (bf16[1,128,128]{2,1,0:T(8,128)(2,1)}, bf16[1,128,128]{2,1,0:T(8,128)(2,1)S(1)}, u32[]{:S(2)}, u32[]{:S(2)}) collective-permute-start(bf16[1,128,128]{2,1,0:T(8,128)(2,1)} %bitcast.10), channel_id=1, source_target_pairs={{0,4},{1,5},{2,6},{3,7},{4,0},{5,1},{6,2},{7,3},{8,12},{9,13},{10,... | collective-permute-start | bytes 98312 | tf_op jit(solution)/shard_map/ppermute | solution.py:185
  6.3 1.6 %copy-start.6 = (bf16[16,8,128]{2,1,0:T(8,128)(2,1)S(1)}, bf16[16,8,128]{2,1,0:T(8,128)(2,1)}, u32[]{:S(2)}) copy-start(bf16[16,8,128]{2,1,0:T(8,128)(2,1)} %param.10) | copy-start | bytes 98308
  6.4 4.0 %collective-permute-start.5 = (bf16[1,144,128]{2,1,0:T(8,128)(2,1)S(1)}, bf16[1,144,128]{2,1,0:T(8,128)(2,1)S(1)}, u32[]{:S(2)}, u32[]{:S(2)}) collective-permute-start(bf16[1,144,128]{2,1,0:T(8,128)(2,1)S(1)} %get-tuple-element.13), channel_id=1, source_target_pairs={{0,16},{8,24},{16,0},{24,8},{1,17},{9,25},{17,1},{25,9},{2,18},{10... | collective-permute-start | bytes 110600 | tf_op jit(solution)/shard_map/ppermute | solution.py:185
  7.9 4.3 %collective-permute-start.1 = (bf16[2,128,128]{2,1,0:T(8,128)(2,1)S(1)}, bf16[2,128,128]{2,1,0:T(8,128)(2,1)S(1)}, u32[]{:S(2)}, u32[]{:S(2)}) collective-permute-start(bf16[2,128,128]{2,1,0:T(8,128)(2,1)S(1)} %pad_maximum_fusion.5), channel_id=1, source_target_pairs={{0,2},{1,3},{2,0},{3,1},{4,6},{5,7},{6,4},{7,5},{8,10},{9,11},{10,... | collective-permute-start | bytes 196616 | tf_op jit(solution)/shard_map/ppermute | solution.py:185
  10.4 5.3 %collective-permute-start.6 = (bf16[2,144,128]{2,1,0:T(8,128)(2,1)S(1)}, bf16[2,144,128]{2,1,0:T(8,128)(2,1)S(1)}, u32[]{:S(2)}, u32[]{:S(2)}) collective-permute-start(bf16[2,144,128]{2,1,0:T(8,128)(2,1)S(1)} %pad_maximum_fusion.4), channel_id=1, source_target_pairs={{0,4},{1,5},{2,6},{3,7},{4,0},{5,1},{6,2},{7,3},{8,12},{9,13},{10,... | collective-permute-start | bytes 221192 | tf_op jit(solution)/shard_map/ppermute | solution.py:185
  12.3 10.3 %collective-permute-start.2 = (bf16[4,128,128]{2,1,0:T(8,128)(2,1)S(1)}, bf16[4,128,128]{2,1,0:T(8,128)(2,1)S(1)}, u32[]{:S(2)}, u32[]{:S(2)}) collective-permute-start(bf16[4,128,128]{2,1,0:T(8,128)(2,1)S(1)} %pad_maximum_fusion.3), channel_id=1, source_target_pairs={{0,1},{1,0},{2,3},{3,2},{4,5},{5,4},{6,7},{7,6},{8,9},{9,8},{10,11... | collective-permute-start | bytes 393224 | tf_op jit(solution)/shard_map/ppermute | solution.py:185
  15.7 5.2 %collective-permute-start.7 = (bf16[4,144,128]{2,1,0:T(8,128)(2,1)S(1)}, bf16[4,144,128]{2,1,0:T(8,128)(2,1)S(1)}, u32[]{:S(2)}, u32[]{:S(2)}) collective-permute-start(bf16[4,144,128]{2,1,0:T(8,128)(2,1)S(1)} %pad_maximum_fusion.2), channel_id=1, source_target_pairs={{0,2},{1,3},{2,0},{3,1},{4,6},{5,7},{6,4},{7,5},{8,10},{9,11},{10,... | collective-permute-start | bytes 442376 | tf_op jit(solution)/shard_map/ppermute | solution.py:185
  20.9 6.8 %collective-permute-start.8 = (bf16[8,144,128]{2,1,0:T(8,128)(2,1)S(1)}, bf16[8,144,128]{2,1,0:T(8,128)(2,1)S(1)}, u32[]{:S(2)}, u32[]{:S(2)}) collective-permute-start(bf16[8,144,128]{2,1,0:T(8,128)(2,1)S(1)} %pad_maximum_fusion), channel_id=1, source_target_pairs={{0,1},{1,0},{2,3},{3,2},{4,5},{5,4},{6,7},{7,6},{8,9},{9,8},{10,11... | collective-permute-start | bytes 884744 | tf_op jit(solution)/shard_map/ppermute | solution.py:185
  22.6 6.4 %collective-permute-start.3 = (bf16[8,128,128]{2,1,0:T(8,128)(2,1)S(1)}, bf16[8,128,128]{2,1,0:T(8,128)(2,1)S(1)}, u32[]{:S(2)}, u32[]{:S(2)}) collective-permute-start(bf16[8,128,128]{2,1,0:T(8,128)(2,1)S(1)} %pad_maximum_fusion.1), channel_id=1, source_target_pairs={{0,16},{8,24},{16,0},{24,8},{1,17},{9,25},{17,1},{25,9},{2,18},{10... | collective-permute-start | bytes 786440 | tf_op jit(solution)/shard_map/ppermute | solution.py:185
  27.7 3.3 %copy-start.1 = (bf16[9,128,128]{2,1,0:T(8,128)(2,1)S(1)}, bf16[9,128,128]{2,1,0:T(8,128)(2,1)}, u32[]{:S(2)}) copy-start(bf16[9,128,128]{2,1,0:T(8,128)(2,1)} %two.1) | copy-start | bytes 884740
  27.8 3.3 %copy-start = (bf16[9,128,128]{2,1,0:T(8,128)(2,1)S(1)}, bf16[9,128,128]{2,1,0:T(8,128)(2,1)}, u32[]{:S(2)}) copy-start(bf16[9,128,128]{2,1,0:T(8,128)(2,1)} %param.17) | copy-start | bytes 884740
  27.8 3.3 %copy-start.2 = (bf16[128,512]{1,0:T(8,128)(2,1)S(1)}, bf16[128,512]{1,0:T(8,128)(2,1)}, u32[]{:S(2)}) copy-start(bf16[128,512]{1,0:T(8,128)(2,1)} %w_proj.1) | copy-start | bytes 393220
  27.8 3.3 %copy-start.3 = (bf16[128,128]{1,0:T(8,128)(2,1)S(1)}, bf16[128,128]{1,0:T(8,128)(2,1)}, u32[]{:S(2)}) copy-start(bf16[128,128]{1,0:T(8,128)(2,1)} %w_gate.1) | copy-start | bytes 98308
  27.8 3.2 %copy-start.4 = (bf16[128,128]{1,0:T(8,128)(2,1)S(1)}, bf16[128,128]{1,0:T(8,128)(2,1)}, u32[]{:S(2)}) copy-start(bf16[128,128]{1,0:T(8,128)(2,1)} %w_out.1) | copy-start | bytes 98308
  27.8 3.2 %collective-permute-start.9 = (bf16[16,144,128]{2,1,0:T(8,128)(2,1)S(1)}, bf16[16,144,128]{2,1,0:T(8,128)(2,1)S(1)}, u32[]{:S(2)}, u32[]{:S(2)}) collective-permute-start(bf16[16,144,128]{2,1,0:T(8,128)(2,1)S(1)} %constant_dynamic-update-slice_fusion.5.cot_near), channel_id=1, source_target_pairs={{0,8},{8,0},{16,24},{24,16},{1,9},{9,1},{17,25},{25,17},{2,10},{10... | collective-permute-start | bytes 1769480 | tf_op jit(solution)/shard_map/ppermute | solution.py:185
  29.0 2.0 %copy-start.5 = (s32[2]{0:T(128)S(1)}, s32[2]{0:T(128)}, u32[]{:S(2)}) copy-start(s32[2]{0:T(128)} %dilations.1) | copy-start | bytes 28
  29.1 2.0 %collective-permute-start.4 = (bf16[16,128,128]{2,1,0:T(8,128)(2,1)S(1)}, bf16[16,128,128]{2,1,0:T(8,128)(2,1)S(1)}, u32[]{:S(2)}, u32[]{:S(2)}) collective-permute-start(bf16[16,128,128]{2,1,0:T(8,128)(2,1)S(1)} %constant_dynamic-update-slice_fusion.near), channel_id=1, source_target_pairs={{0,8},{8,0},{16,24},{24,16},{1,9},{9,1},{17,25},{25,17},{2,10},{10... | collective-permute-start | bytes 1572872 | tf_op jit(solution)/shard_map/ppermute | solution.py:185

commit v4 on v3

--- a/solution.py
+++ b/solution.py
@@ -32,9 +32,9 @@
     return lax.psum(jnp.where(mine, x, jnp.zeros_like(x)), axis)
 
 
-def layer_norm(values):
-    centre = values - jnp.mean(values, axis=-1, keepdims=True)
-    spread = jnp.mean(centre * centre, axis=-1, keepdims=True)
+def layer_norm(values, axis=-1):
+    centre = values - jnp.mean(values, axis=axis, keepdims=True)
+    spread = jnp.mean(centre * centre, axis=axis, keepdims=True)
     return centre * lax.rsqrt(spread + EPSILON)
 
 
@@ -199,11 +199,12 @@
     return row, col
 
 
-def same_place(position, rounds, others):
-    moved = 0
-    for step, hop in enumerate(rounds):
-        moved = moved | (((position >> step) & 1) << others.index(hop))
-    return moved
+def slot_of(row_change, col_change, rounds):
+    slot = 0
+    for step, (axis, distance) in enumerate(rounds[:-1]):
+        change = row_change if axis == "row" else col_change
+        slot = slot | (((change // distance) & 1) << step)
+    return slot
 
 
 def sigmoid(values):
@@ -214,14 +215,114 @@
     return jnp.dot(left, right, preferred_element_type=jnp.float32)
 
 
-def block_kernel(
-    rounds,
-    cot_rounds,
-    height,
-    breadth,
-    tokens,
+def matmul_nt(left, right):
+    return lax.dot_general(
+        left, right, (((1,), (1,)), ((), ())), preferred_element_type=jnp.float32
+    )
+
+
+def project_half(
+    plan, core, pairs, cots, w_proj, w_gate, left, right, swapped, gating, contact, start, turned
+):
+    rounds, cot_rounds, height, breadth, tokens = plan
+    channels, hidden = w_gate.shape[0], w_gate.shape[1]
+    col_count, chips = tokens // breadth, tokens // height // 2
+    row_place, col_place = lax.axis_index("row"), lax.axis_index("col")
+    lane = lax.broadcasted_iota(jnp.int32, (breadth, channels), 1)
+    place = lax.broadcasted_iota(jnp.int32, (breadth, channels), 0)
+    own_lane = jnp.where((lane % breadth == place) & (lane < 2 * breadth), 1.0, 0.0)
+    pick_lane = lax.broadcasted_iota(jnp.int32, (channels, 2 * channels), 0)
+    pick_half = lax.broadcasted_iota(jnp.int32, (channels, 2 * channels), 1) // channels
+    pick = jnp.where(pick_lane // breadth == pick_half, 1.0, 0.0).astype(jnp.bfloat16)
+    pixels = height * breadth
+    rows = 8
+    for first in range(0, height, rows):
+        values, masks = [], []
+        for chip in range(chips):
+            row_change = (chip * 2 + core) ^ row_place
+            blocks, marks = [], []
+            for col in range(col_count):
+                col_change = col_place ^ col
+                slot = slot_of(row_change, col_change, rounds)
+                cot_slot = slot_of(row_change, col_change, cot_rounds)
+                blocks.append(
+                    pairs[slot, first * breadth : (first + rows) * breadth, :]
+                    .astype(jnp.float32)
+                    .reshape(rows, breadth, channels)
+                )
+                mark = cots[cot_slot, pixels:, :].astype(jnp.float32)[first : first + rows]
+                marks.append(mark[:, None, :] * own_lane[None])
+            values.append(jnp.concatenate(blocks, axis=1).reshape(rows * tokens, channels))
+            masks.append(jnp.concatenate(marks, axis=1).reshape(rows * tokens, channels))
+        values = jnp.concatenate(values, axis=0)
+        masks = matmul(jnp.concatenate(masks, axis=0).astype(jnp.bfloat16), pick)
+        normed = layer_norm(values)
+        gates = sigmoid(matmul(normed.astype(jnp.bfloat16), w_gate[...]))
+        masked = (normed * masks[:, :channels]).astype(jnp.bfloat16)
+        projected = matmul(masked, w_proj[...])
+        sides = [
+            sigmoid(projected[:, (2 * side + 1) * hidden : (2 * side + 2) * hidden])
+            * projected[:, 2 * side * hidden : (2 * side + 1) * hidden]
+            for side in range(2)
+        ]
+        for side, target in zip(sides, turned):
+            side = side.reshape(chips, rows, tokens, hidden)
+            for row in range(rows):
+                strip = jnp.concatenate([side[chip, row] for chip in range(chips)], axis=0)
+                target[pl.ds(first + row, hidden, stride=height), :] = strip.T
+        shape = (chips, rows, tokens, channels)
+        span = slice(first, first + rows)
+        gating[:, span] = gates.reshape(shape)
+        contact[:, span] = masks[:, channels:].astype(jnp.bfloat16).reshape(shape)
+        start[:, span] = values.astype(jnp.bfloat16).reshape(shape)
+    shape = (hidden, height, chips * tokens)
+    left[...] = turned[0][...].reshape(shape).astype(jnp.bfloat16)
+    other = turned[1][...]
+    right[...] = other.reshape(shape).astype(jnp.bfloat16)
+    swapped[...] = pltpu.roll(other, tokens, 1).reshape(shape).astype(jnp.bfloat16)
+
+
+def near_kernel(
+    plan,
+    near,
+    cot_near,
+    w_proj,
+    w_gate,
+    two,
+    left,
+    right,
+    swapped,
+    gating,
+    contact,
+    start,
+    two_t,
+    turned_left,
+    turned_right,
+):
+    core = lax.axis_index("row") % 2
+    channels = two.shape[1]
+    for tap in range(9):
+        two_t[tap * channels : (tap + 1) * channels] = two[tap].T
+    project_half(
+        plan,
+        core,
+        near,
+        cot_near,
+        w_proj,
+        w_gate,
+        left,
+        right,
+        swapped,
+        gating,
+        contact,
+        start,
+        (turned_left, turned_right),
+    )
+
+
+def map_kernel(
+    plan,
     dilations,
-    near,
     far,
     cot_near,
     cot_far,
@@ -230,46 +331,55 @@
     w_out,
     one,
     two,
+    near_left,
+    near_right,
+    near_swapped,
+    near_gating,
+    near_contact,
+    near_start,
+    two_t,
     output,
     grad_pair,
     grad_one,
     grad_two,
     left,
     right,
+    swapped,
     gating,
+    contact,
     start,
-    contact,
+    turned_left,
+    turned_right,
+    products,
     updated,
-    products,
+    hidden_grad,
     field,
-    cot_field,
     wide,
     wide_cot,
     wide_pre,
     second,
-    hidden_grad,
     grad_pre,
     flipped,
     flipped_two,
     sum_one,
     sum_two,
-    two_t,
 ):
-    channels = w_out.shape[1]
-    hidden = w_out.shape[0]
+    rounds, cot_rounds, height, breadth, tokens = plan
+    hidden, channels = w_out.shape
     pixels = height * breadth
+    chips = tokens // height // 2
     row_place, col_place = lax.axis_index("row"), lax.axis_index("col")
+    core = row_place % 2
     rate_one, rate_two = dilations[0], dilations[1]
-    half = near.shape[0]
+    half = far.shape[0]
     line = tokens + 2 * DMAX
     inside = slice(DMAX, DMAX + tokens)
 
     rim = jnp.zeros((tokens, DMAX, channels), jnp.float32)
     edge = jnp.zeros((DMAX, tokens, 3 * channels), jnp.bfloat16)
     border = jnp.zeros((DMAX, line, channels), jnp.float32)
-    for target in (field, cot_field):
-        target[:, 0:DMAX, :] = rim
-        target[:, DMAX + tokens :, :] = rim
+    field[:, 0:DMAX, :] = rim
+    field[:, DMAX + tokens :, :] = rim
     for target in (wide, wide_cot, wide_pre):
         target[0:DMAX] = edge
         target[DMAX + tokens :] = edge
@@ -278,72 +388,49 @@
         target[DMAX + tokens :] = border
         target[inside, 0:DMAX, :] = rim
         target[inside, DMAX + tokens :, :] = rim
-    for tap in range(9):
-        two_t[tap * channels : (tap + 1) * channels] = two[tap].T
-
-    lane = lax.broadcasted_iota(jnp.int32, (breadth, channels), 1)
-    place = lax.broadcasted_iota(jnp.int32, (breadth, channels), 0)
-    own_lane = jnp.where((lane % breadth == place) & (lane < 2 * breadth), 1.0, 0.0)
-    pick_lane = lax.broadcasted_iota(jnp.int32, (channels, 2 * channels), 0)
-    pick_half = lax.broadcasted_iota(jnp.int32, (channels, 2 * channels), 1) // channels
-    pick = jnp.where(pick_lane // breadth == pick_half, 1.0, 0.0).astype(jnp.bfloat16)
+
+    for whole, part in (
+        (left, near_left),
+        (right, near_right),
+        (swapped, near_swapped),
+        (gating, near_gating),
+        (contact, near_contact),
+        (start, near_start),
+    ):
+        whole[core] = part[...]
+    targets = [
+        whole.at[1 - core] for whole in (left, right, swapped, gating, contact, start)
+    ]
+    project_half(
+        plan,
+        1 - core,
+        far,
+        cot_far,
+        w_proj,
+        w_gate,
+        *targets,
+        (turned_left, turned_right),
+    )
+
     several = 4
 
-    def project(source, cot_source, base):
+    def place_cot(source, base):
         def body(step, carry):
-            first = step * several
-            partners = [
-                same_place(first + i, rounds[:-1], cot_rounds[:-1]) for i in range(several)
-            ]
-            masks = jnp.concatenate(
-                [
-                    (
-                        cot_source[partner, pixels:, :].astype(jnp.float32)[:, None, :]
-                        * own_lane[None]
-                    ).reshape(pixels, channels)
-                    for partner in partners
-                ],
-                axis=0,
-            ).astype(jnp.bfloat16)
-            masks = matmul(masks, pick)
-            values = (
-                source[pl.ds(first, several)]
-                .reshape(several * pixels, channels)
-                .astype(jnp.float32)
-            )
-            normed = layer_norm(values).astype(jnp.bfloat16)
-            projected = matmul(normed, w_proj[...])
-            mask = masks[:, :hidden]
-            left_side = (
-                mask * sigmoid(projected[:, hidden : 2 * hidden]) * projected[:, :hidden]
-            )
-            right_side = (
-                mask
-                * sigmoid(projected[:, 3 * hidden :])
-                * projected[:, 2 * hidden : 3 * hidden]
-            )
-            gates = sigmoid(matmul(normed, w_gate[...]))
-            shape = (height, breadth, channels)
             for i in range(several):
-                row, col = place_of(base + first + i, rounds, row_place, col_place)
-                rows = pl.ds(pl.multiple_of(row * height, height), height)
-                cols = pl.ds(pl.multiple_of(col * breadth, breadth), breadth)
-                padded = pl.ds(pl.multiple_of(DMAX + col * breadth, breadth), breadth)
-                part = slice(i * pixels, (i + 1) * pixels)
-                left[rows, cols, :] = left_side[part].reshape(shape)
-                right[cols, rows, :] = jnp.swapaxes(right_side[part].reshape(shape), 0, 1)
-                gating[rows, cols, :] = gates[part].reshape(shape)
-                start[rows, cols, :] = values[part].reshape(shape)
-                contact[rows, cols, :] = masks[part, channels:].reshape(shape)
-                cot_field[rows, padded, :] = (
-                    cot_source[partners[i], 0:pixels, :].astype(jnp.float32).reshape(shape)
+                slot = step * several + i
+                row, col = place_of(base + slot, cot_rounds, row_place, col_place)
+                cols = pl.ds(pl.multiple_of(DMAX + col * breadth, breadth), breadth)
+                field[pl.ds(row * height, height), cols, :] = (
+                    source[slot, 0:pixels, :]
+                    .astype(jnp.float32)
+                    .reshape(height, breadth, channels)
                 )
             return carry
 
         lax.fori_loop(0, half // several, body, 0)
 
-    project(near, cot_near, 0)
-    project(far, cot_far, half)
+    place_cot(cot_near, 0)
+    place_cot(cot_far, half)
 
     def spread(source, rows, pad, rate, target):
         for tap in range(3):
@@ -369,53 +456,66 @@
     steps = tokens // chunk
 
     def spread_cot(step, carry):
-        spread(cot_field, pl.ds(step * chunk, chunk), 0, -rate_two, wide_cot)
+        spread(field, pl.ds(step * chunk, chunk), 0, -rate_two, wide_cot)
         return carry
 
     lax.fori_loop(0, steps, spread_cot, 0)
 
-    group = 4
-
-    def triangle(step):
-        sums = [jnp.zeros((tokens, hidden), jnp.float32)] * group
-        for k in range(tokens):
-            others = right[k]
-            sums = [
-                total + left[step * group + i, k : k + 1, :] * others
-                for i, total in enumerate(sums)
-            ]
-        for i, total in enumerate(sums):
-            products[step * group + i] = total
-
-    def hidden_conv(step):
-        hidden_grad[pl.ds(step * group, group)] = matmul(
-            taps(wide_cot, step * group, group, -rate_two), two_t[...]
-        ).reshape(group, tokens, channels)
-
-    def update(step):
-        rows = pl.ds(step * group, group)
-        flat = products[rows].reshape(group * tokens, hidden)
-        product_norm = layer_norm(flat).astype(jnp.bfloat16)
-        change = matmul(product_norm, w_out[...]).reshape(group, tokens, channels)
-        fresh = (start[rows] + gating[rows] * change).astype(jnp.bfloat16).astype(jnp.float32)
-        updated[rows] = fresh
-        first_in = layer_norm(fresh) * contact[rows]
-        field[rows, inside, :] = first_in
-        spread(field, rows, 0, rate_one, wide)
-        flipped[:, lanes(step, group * tokens)] = (
-            first_in.reshape(group * tokens, channels).astype(jnp.bfloat16).T
+    lane = lax.broadcasted_iota(jnp.int32, (height, chips * tokens), 1)
+    low = jnp.where(lane < tokens, 1.0, 0.0).astype(jnp.bfloat16)
+    high = jnp.where(lane < tokens, 0.0, 1.0).astype(jnp.bfloat16)
+    batch = 8
+
+    def multiply(step, carry):
+        for part in range(batch):
+            h = step * batch + part
+            ahead = [right[0, h], right[1, h]]
+            back = [swapped[0, h], swapped[1, h]]
+            strips = [strip * low for strip in ahead + back]
+            strips += [strip * high for strip in back + ahead]
+            mine = jnp.concatenate([left[0, h], left[1, h]], axis=0)
+            products[pl.ds(pl.multiple_of(h * 2 * height, 2 * height), 2 * height), :] = (
+                matmul_nt(mine, jnp.concatenate(strips, axis=0))
+            )
+        return carry
+
+    lax.fori_loop(0, hidden // batch, multiply, 0)
+
+    def update(step, carry):
+        side, first = step // (height // chunk), (step % (height // chunk)) * chunk
+        turned = []
+        for row in range(chunk):
+            strip = products[pl.ds(side * height + first + row, hidden, stride=2 * height), :]
+            turned.append(layer_norm(strip, axis=0).astype(jnp.bfloat16).T)
+        product_norm = jnp.concatenate(
+            [
+                strip[chip * tokens : (chip + 1) * tokens]
+                for chip in range(chips)
+                for strip in turned
+            ],
+            axis=0,
         )
-
-    def early(step, carry):
-        triangle(step)
-        hidden_conv(step)
-        update(step - 1)
+        shape = (chips, chunk, tokens, channels)
+        change = matmul(product_norm, w_out[...]).reshape(shape)
+        rows = pl.ds(first, chunk)
+        fresh = start[side, :, rows].astype(jnp.float32) + gating[side, :, rows] * change
+        fresh = fresh.astype(jnp.bfloat16).astype(jnp.float32)
+        first_in = layer_norm(fresh) * contact[side, :, rows].astype(jnp.float32)
+        for chip in range(chips):
+            base = (chip * 2 + side) * height + first
+            rows = pl.ds(base, chunk)
+            updated[rows] = fresh[chip]
+            field[rows, inside, :] = first_in[chip]
+            spread(field, rows, 0, rate_one, wide)
+            flipped[:, pl.ds(pl.multiple_of(base * tokens, size), size)] = (
+                first_in[chip].reshape(size, channels).astype(jnp.bfloat16).T
+            )
+            hidden_grad[rows] = matmul(
+                taps(wide_cot, base, chunk, -rate_two), two_t[...]
+            ).reshape(chunk, tokens, channels)
         return carry
 
-    triangle(0)
-    hidden_conv(0)
-    lax.fori_loop(1, tokens // group, early, 0)
-    update(tokens // group - 1)
+    lax.fori_loop(0, 2 * (height // chunk), update, 0)
 
     def first_conv(step):
         first = step * chunk
@@ -479,13 +579,19 @@
     mine = updated[rows, cols, :].reshape(pixels, channels)
     second_pre = matmul(windows(second, rate_two), two[...].reshape(9 * channels, channels))
     output[...] = (mine + second_pre).astype(jnp.bfloat16)
+    own_contact = contact[core, row_place // 2].astype(jnp.float32)
+    own_contact = own_contact.reshape(height, tokens, channels)
+    place_col = lax.broadcasted_iota(jnp.int32, (tokens, channels), 0) // breadth
+    own_contact = jnp.where((place_col == col_place)[None], own_contact, 0.0)
+    own_contact = own_contact.reshape(height, tokens // breadth, breadth, channels)
+    own_contact = jnp.sum(own_contact, axis=1).reshape(pixels, channels)
     one_rows = [one[tap * channels : (tap + 1) * channels] for tap in range(9)]
     grad_input = lax.dot_general(
         windows(grad_pre, -rate_one),
         jnp.concatenate(one_rows, axis=1),
         (((1,), (1,)), ((), ())),
         preferred_element_type=jnp.float32,
-    ) * contact[rows, cols, :].reshape(pixels, channels)
+    ) * own_contact
     centre = mine - jnp.mean(mine, axis=-1, keepdims=True)
     inv_spread = lax.rsqrt(jnp.mean(centre * centre, axis=-1, keepdims=True) + EPSILON)
     scaled = centre * inv_spread
@@ -520,17 +626,39 @@
     near, far = gather_blocks(pair.reshape(pixels, channels), rounds)
     cot_near, cot_far = gather_blocks(packed, cot_rounds)
     f32, bf16 = jnp.float32, jnp.bfloat16
+    plan = (rounds, cot_rounds, height, breadth, tokens)
+    chips = row_count // 2
     line = tokens + 2 * DMAX
     in_vmem = pl.BlockSpec(memory_space=pltpu.VMEM)
+    side = ((hidden, height, chips * tokens), bf16)
+    rows = (chips, height, tokens, channels)
+    halves = [side] * 3 + [(rows, f32), (rows, bf16), (rows, bf16)]
+    turned = pltpu.VMEM((hidden * height, chips * tokens), f32)
+    near_parts = pl.pallas_call(
+        functools.partial(near_kernel, plan),
+        in_specs=[in_vmem] * 5,
+        out_specs=[in_vmem] * 7,
+        out_shape=[
+            jax.ShapeDtypeStruct(shape, dtype)
+            for shape, dtype in halves + [((9 * channels, channels), bf16)]
+        ],
+        scratch_shapes=[turned] * 2,
+        compiler_params=pltpu.CompilerParams(vmem_limit_bytes=VMEM_LIMIT // 3),
+        cost_estimate=pl.CostEstimate(
+            flops=tokens * tokens * channels * 5 * hidden,
+            bytes_accessed=8 * tokens * tokens * channels,
+            transcendentals=3 * tokens * tokens * channels // 2,
+        ),
+    )(near, cot_near, w_proj, w_gate, conv_two)
     whole = pltpu.VMEM((tokens, tokens, channels), f32)
     padded = pltpu.VMEM((tokens, line, channels), f32)
     bordered = pltpu.VMEM((line, line, channels), f32)
     tripled = pltpu.VMEM((line, tokens, 3 * channels), bf16)
-    turned = pltpu.VMEM((channels, tokens * tokens), bf16)
+    flat = pltpu.VMEM((channels, tokens * tokens), bf16)
     sums = pltpu.VMEM((channels, 9 * channels), f32)
     output, grad_pair, grad_one, grad_two = pl.pallas_call(
-        functools.partial(block_kernel, rounds, cot_rounds, height, breadth, tokens),
-        in_specs=[pl.BlockSpec(memory_space=pltpu.SMEM)] + [in_vmem] * 9,
+        functools.partial(map_kernel, plan),
+        in_specs=[pl.BlockSpec(memory_space=pltpu.SMEM)] + [in_vmem] * 15,
         out_specs=[in_vmem] * 4,
         out_shape=[
             jax.ShapeDtypeStruct((pixels, channels), bf16),
@@ -538,17 +666,18 @@
             jax.ShapeDtypeStruct((9, channels, channels), f32),
             jax.ShapeDtypeStruct((9, channels, channels), f32),
         ],
-        scratch_shapes=[whole] * 7
-        + [padded] * 2
+        scratch_shapes=[pltpu.VMEM((2,) + shape, dtype) for shape, dtype in halves]
+        + [turned] * 2
+        + [pltpu.VMEM((hidden * 2 * height, chips * tokens), f32)]
+        + [whole] * 2
+        + [padded]
         + [tripled] * 3
-        + [bordered, whole, bordered]
-        + [turned] * 2
-        + [sums] * 2
-        + [pltpu.VMEM((9 * channels, channels), bf16)],
+        + [bordered] * 2
+        + [flat] * 2
+        + [sums] * 2,
         compiler_params=pltpu.CompilerParams(vmem_limit_bytes=VMEM_LIMIT),
     )(
         dilations,
-        near,
         far,
         cot_near,
         cot_far,
@@ -557,6 +686,7 @@
         w_out,
         conv_one.reshape(9 * channels, channels),
         conv_two,
+        *near_parts,
     )
     block = (height, breadth, channels)
     return output.reshape(block), grad_pair.reshape(block), grad_one, grad_two
@@ -571,6 +701,7 @@
         powers
         and row_count * col_count >= 8
         and height * breadth == channels == w_out.shape[0]
+        and row_count // 2 * tokens == channels
         and whole * 60 <= VMEM_LIMIT
     )
 

time: 70.5 us -> 61.2 us (0.87)
  Pallas kernels: 39.2 us -> 30.1 us
  waiting for transfers between devices: 13.2 us -> 11.3 us
  local copies, waits for them, and re-layouts: 0.38 us -> 1.99 us
    pallas_call x1 -> x2, Pallas kernels: 39.2 us -> 30.1 us  [the longest x1 27.9 us: replicated(): pl.pallas_call(functools.partial(map_kernel, plan), in_specs=[pl.BlockSpe...]
    ppermute x10, waiting for transfers between devices: 13.2 us -> 11.3 us  [gather_blocks(): other = lax.ppermute(held, axis, pairs)]
    unnamed x23 -> x25, local copies, waits for them, and re-layouts: 0.13 us -> 1.74 us
  transfers between devices with their start and end apart: 10 -> 10, of which waited for: 7 -> 6; matrix products, arithmetic and copies ran while one was open for 3% -> 3% of each run, Pallas kernels for 0% -> 4%
where the time goes in v4:
time: 61.2 us; the launch traced here: 60.9 us
  Pallas kernels  30.1 us (49%)
  starting transfers between devices  15.1 us (25%)
  waiting for transfers between devices  11.3 us (18%)
  local copies, waits for them, and re-layouts  1.99 us (3%)
  other arithmetic  1.57 us (3%)
  between operations  0.82 us (1%)
    pallas_call x1, Pallas kernels, replicated(): pl.pallas_call(functools.partial(map_kernel, plan), in_specs=[pl.BlockSpe...  27.9 us
    ppermute x10, starting transfers between devices, gather_blocks(): other = lax.ppermute(held, axis, pairs)  15.1 us
    ppermute x10, waiting for transfers between devices, gather_blocks(): other = lax.ppermute(held, axis, pairs)  11.3 us
    pallas_call x1, Pallas kernels, replicated(): pl.pallas_call(functools.partial(near_kernel, plan), in_specs=[in_vmem] *...  2.2 us
    unnamed x25, local copies, waits for them, and re-layouts  1.74 us
  transfers between devices with their start and end apart: 10, of which 6 were waited for; matrix products, arithmetic and copies ran while one was open for 3% of the time, Pallas kernels for 4%

profile of v4, /device:TPU:0, one launch (start us, length us, event | category | flops | bytes accessed | tf_op | source)
XLA Modules:
  0.0 60.9 jit_solution(16216760133611851463)
XLA Ops:
  0.6 0.0 copy-start.8
  0.6 4.1 %collective-permute-start = (bf16[1,128,128]{2,1,0:T(8,128)(2,1)}, bf16[1,128,128]{2,1,0:T(8,128)(2,1)S(1)}, u32[]{:S(2)}, u32[]{:S(2)}) collective-permute-start(bf16[1,128,128]{2,1,0:T(8,128)(2,1)} %bitcast.10), channel_id=1, source_target_pairs={{0,4},{1,5},{2,6},{3,7},{4,0},{5,1},{6,2},{7,3},{8,12},{9,13},{10,... | collective-permute-start | bytes 98312 | tf_op jit(solution)/shard_map/ppermute | solution.py:185
  4.7 0.7 %convert_element_type.6 = bf16[16,8]{0,1:T(8,128)(2,1)S(1)} convert(s32[16,8]{0,1:T(8,128)} %param.11) | non-fusion elementwise | flops 128 | bytes 768 | tf_op jit(solution)/shard_map/convert_element_type | solution.py:619
  5.4 0.1 copy.16
  5.5 0.7 %convert_element_type.7 = bf16[16,8]{0,1:T(8,128)(2,1)S(1)} convert(s32[16,8]{0,1:T(8,128)} %param.12) | non-fusion elementwise | flops 128 | bytes 768 | tf_op jit(solution)/shard_map/convert_element_type | solution.py:620
  6.2 0.1 copy.17
  6.3 0.0 copy-done.8
  6.3 0.0 copy-start.7
  6.3 0.1 constant_dynamic-update-slice_fusion.9
  6.4 1.5 %collective-permute-start.5 = (bf16[1,144,128]{2,1,0:T(8,128)(2,1)S(1)}, bf16[1,144,128]{2,1,0:T(8,128)(2,1)S(1)}, u32[]{:S(2)}, u32[]{:S(2)}) collective-permute-start(bf16[1,144,128]{2,1,0:T(8,128)(2,1)S(1)} %get-tuple-element.27), channel_id=1, source_target_pairs={{0,16},{8,24},{16,0},{24,8},{1,17},{9,25},{17,1},{25,9},{2,18},{10... | collective-permute-start | bytes 110600 | tf_op jit(solution)/shard_map/ppermute | solution.py:185
  7.9 0.0 copy-done.7
  7.9 0.0 collective-permute-done
  7.9 1.6 %collective-permute-start.1 = (bf16[2,128,128]{2,1,0:T(8,128)(2,1)S(1)}, bf16[2,128,128]{2,1,0:T(8,128)(2,1)S(1)}, u32[]{:S(2)}, u32[]{:S(2)}) collective-permute-start(bf16[2,128,128]{2,1,0:T(8,128)(2,1)S(1)} %pad_maximum_fusion.5), channel_id=1, source_target_pairs={{0,2},{1,3},{2,0},{3,1},{4,6},{5,7},{6,4},{7,5},{8,10},{9,11},{10,... | collective-permute-start | bytes 196616 | tf_op jit(solution)/shard_map/ppermute | solution.py:185
  9.6 0.8 %collective-permute-done.5 = bf16[1,144,128]{2,1,0:T(8,128)(2,1)S(1)} collective-permute-done((bf16[1,144,128]{2,1,0:T(8,128)(2,1)S(1)}, bf16[1,144,128]{2,1,0:T(8,128)(2,1)S(1)}, u32[]{:S(2)}, u32[]{:S(2)}) %collective-permute-start.5) | collective-permute-done | bytes 36896 | tf_op jit(solution)/shard_map/ppermute | solution.py:185
  10.4 1.4 %collective-permute-start.6 = (bf16[2,144,128]{2,1,0:T(8,128)(2,1)S(1)}, bf16[2,144,128]{2,1,0:T(8,128)(2,1)S(1)}, u32[]{:S(2)}, u32[]{:S(2)}) collective-permute-start(bf16[2,144,128]{2,1,0:T(8,128)(2,1)S(1)} %pad_maximum_fusion.4), channel_id=1, source_target_pairs={{0,4},{1,5},{2,6},{3,7},{4,0},{5,1},{6,2},{7,3},{8,12},{9,13},{10,... | collective-permute-start | bytes 221192 | tf_op jit(solution)/shard_map/ppermute | solution.py:185
  11.8 0.5 collective-permute-done.1
  12.3 1.6 %collective-permute-start.2 = (bf16[4,128,128]{2,1,0:T(8,128)(2,1)S(1)}, bf16[4,128,128]{2,1,0:T(8,128)(2,1)S(1)}, u32[]{:S(2)}, u32[]{:S(2)}) collective-permute-start(bf16[4,128,128]{2,1,0:T(8,128)(2,1)S(1)} %pad_maximum_fusion.3), channel_id=1, source_target_pairs={{0,1},{1,0},{2,3},{3,2},{4,5},{5,4},{6,7},{7,6},{8,9},{9,8},{10,11... | collective-permute-start | bytes 393224 | tf_op jit(solution)/shard_map/ppermute | solution.py:185
  13.8 1.8 %collective-permute-done.6 = bf16[2,144,128]{2,1,0:T(8,128)(2,1)S(1)} collective-permute-done((bf16[2,144,128]{2,1,0:T(8,128)(2,1)S(1)}, bf16[2,144,128]{2,1,0:T(8,128)(2,1)S(1)}, u32[]{:S(2)}, u32[]{:S(2)}) %collective-permute-start.6) | collective-permute-done | bytes 73760 | tf_op jit(solution)/shard_map/ppermute | solution.py:185
  15.7 1.6 %collective-permute-start.7 = (bf16[4,144,128]{2,1,0:T(8,128)(2,1)S(1)}, bf16[4,144,128]{2,1,0:T(8,128)(2,1)S(1)}, u32[]{:S(2)}, u32[]{:S(2)}) collective-permute-start(bf16[4,144,128]{2,1,0:T(8,128)(2,1)S(1)} %pad_maximum_fusion.2), channel_id=1, source_target_pairs={{0,2},{1,3},{2,0},{3,1},{4,6},{5,7},{6,4},{7,5},{8,10},{9,11},{10,... | collective-permute-start | bytes 442376 | tf_op jit(solution)/shard_map/ppermute | solution.py:185
  17.4 3.5 %collective-permute-done.7 = bf16[4,144,128]{2,1,0:T(8,128)(2,1)S(1)} collective-permute-done((bf16[4,144,128]{2,1,0:T(8,128)(2,1)S(1)}, bf16[4,144,128]{2,1,0:T(8,128)(2,1)S(1)}, u32[]{:S(2)}, u32[]{:S(2)}) %collective-permute-start.7) | collective-permute-done | bytes 147488 | tf_op jit(solution)/shard_map/ppermute | solution.py:185
  20.9 1.6 %collective-permute-start.8 = (bf16[8,144,128]{2,1,0:T(8,128)(2,1)S(1)}, bf16[8,144,128]{2,1,0:T(8,128)(2,1)S(1)}, u32[]{:S(2)}, u32[]{:S(2)}) collective-permute-start(bf16[8,144,128]{2,1,0:T(8,128)(2,1)S(1)} %pad_maximum_fusion), channel_id=1, source_target_pairs={{0,1},{1,0},{2,3},{3,2},{4,5},{5,4},{6,7},{7,6},{8,9},{9,8},{10,11... | collective-permute-start | bytes 884744 | tf_op jit(solution)/shard_map/ppermute | solution.py:185
  22.5 0.0 collective-permute-done.2
  22.6 1.6 %collective-permute-start.3 = (bf16[8,128,128]{2,1,0:T(8,128)(2,1)S(1)}, bf16[8,128,128]{2,1,0:T(8,128)(2,1)S(1)}, u32[]{:S(2)}, u32[]{:S(2)}) collective-permute-start(bf16[8,128,128]{2,1,0:T(8,128)(2,1)S(1)} %pad_maximum_fusion.1), channel_id=1, source_target_pairs={{0,16},{8,24},{16,0},{24,8},{1,17},{9,25},{17,1},{25,9},{2,18},{10... | collective-permute-start | bytes 786440 | tf_op jit(solution)/shard_map/ppermute | solution.py:185
  24.2 3.6 %collective-permute-done.8 = bf16[8,144,128]{2,1,0:T(8,128)(2,1)S(1)} collective-permute-done((bf16[8,144,128]{2,1,0:T(8,128)(2,1)S(1)}, bf16[8,144,128]{2,1,0:T(8,128)(2,1)S(1)}, u32[]{:S(2)}, u32[]{:S(2)}) %collective-permute-start.8) | collective-permute-done | bytes 294944 | tf_op jit(solution)/shard_map/ppermute | solution.py:185
  27.8 0.0 copy-start
  27.8 0.0 copy-start.2
  27.8 0.0 copy-start.4
  27.8 0.1 collective-permute-start.9
  27.9 1.1 %collective-permute-done.3 = bf16[8,128,128]{2,1,0:T(8,128)(2,1)S(1)} collective-permute-done((bf16[8,128,128]{2,1,0:T(8,128)(2,1)S(1)}, bf16[8,128,128]{2,1,0:T(8,128)(2,1)S(1)}, u32[]{:S(2)}, u32[]{:S(2)}) %collective-permute-start.3) | collective-permute-done | bytes 262176 | tf_op jit(solution)/shard_map/ppermute | solution.py:185
  29.0 0.0 copy-start.3
  29.1 0.1 collective-permute-start.4
  29.1 0.0 copy-done
  29.1 0.0 copy-done.2
  29.2 0.0 copy-done.4
  29.2 0.0 copy-start.5
  29.2 2.2 %shard_map.129 = (bf16[128,16,128]{2,1,0:T(8,128)(2,1)S(1)}, bf16[128,16,128]{2,1,0:T(8,128)(2,1)S(1)}, bf16[128,16,128]{2,1,0:T(8,128)(2,1)S(1)}, f32[2,16,64,1...) custom-call(bf16[16,128,128]{2,1,0:T(8,128)(2,1)S(1)} %constant_dyna, ...), custom_call_target="tpu_custom_call" | custom-call | flops 335544320 | bytes 4194304 | tf_op jit(solution)/shard_map/pallas_call | solution.py:637
  31.4 0.0 copy-start.1
  31.4 1.0 %copy-done.1 = f32[2,16,64,128]{3,2,1,0:T(8,128)} copy-done((f32[2,16,64,128]{3,2,1,0:T(8,128)}, f32[2,16,64,128]{3,2,1,0:T(8,128)S(1)}, u32[]{:S(2)}) %copy-start.1) | copy-done | bytes 1048600
  32.4 0.0 collective-permute-done.4.far
  32.4 0.0 collective-permute-done.9.cot_far
  32.4 0.0 copy-start.6
  32.4 0.0 copy-done.3
  32.4 0.0 copy-done.5
  32.4 0.6 %copy-done.6 = s32[2]{0:T(128)S(1)} copy-done((s32[2]{0:T(128)S(1)}, s32[2]{0:T(128)}, u32[]{:S(2)}) %copy-start.6) | copy-done | bytes 32
  33.0 27.9 %shard_map.130 = (bf16[128,128]{1,0:T(8,128)(2,1)}, bf16[128,128]{1,0:T(8,128)(2,1)}, f32[9,128,128]{2,1,0:T(8,128)}, f32[9,128,128]{2,1,0:T(8,128)}) custom-call(s32[2]{0:T(128)S(1)} %copy-done.6, bf16[16,128,128]{2,1,0:T(8,128)(2,1)S(1)} %collective-permute-done.4.far, bf16[16,144,128]{2,1,0:T(8,128)(2,1)S(1)} %constant_dynamic-update-slice_fusion.5.cot_near, ...), custom_call_target="tpu_custom_call" | custom-call | tf_op jit(solution)/shard_map/pallas_call | solution.py:659
  (16 shorter events, 0.3 us)
Async XLA Ops:
  0.6 5.7 %copy-start.8 = (bf16[16,8,128]{2,1,0:T(8,128)(2,1)S(1)}, bf16[16,8,128]{2,1,0:T(8,128)(2,1)}, u32[]{:S(2)}) copy-start(bf16[16,8,128]{2,1,0:T(8,128)(2,1)} %param.19) | copy-start | bytes 98308
  0.6 7.3 %collective-permute-start = (bf16[1,128,128]{2,1,0:T(8,128)(2,1)}, bf16[1,128,128]{2,1,0:T(8,128)(2,1)S(1)}, u32[]{:S(2)}, u32[]{:S(2)}) collective-permute-start(bf16[1,128,128]{2,1,0:T(8,128)(2,1)} %bitcast.10), channel_id=1, source_target_pairs={{0,4},{1,5},{2,6},{3,7},{4,0},{5,1},{6,2},{7,3},{8,12},{9,13},{10,... | collective-permute-start | bytes 98312 | tf_op jit(solution)/shard_map/ppermute | solution.py:185
  6.3 1.6 %copy-start.7 = (bf16[16,8,128]{2,1,0:T(8,128)(2,1)S(1)}, bf16[16,8,128]{2,1,0:T(8,128)(2,1)}, u32[]{:S(2)}) copy-start(bf16[16,8,128]{2,1,0:T(8,128)(2,1)} %param.10) | copy-start | bytes 98308
  6.4 4.0 %collective-permute-start.5 = (bf16[1,144,128]{2,1,0:T(8,128)(2,1)S(1)}, bf16[1,144,128]{2,1,0:T(8,128)(2,1)S(1)}, u32[]{:S(2)}, u32[]{:S(2)}) collective-permute-start(bf16[1,144,128]{2,1,0:T(8,128)(2,1)S(1)} %get-tuple-element.27), channel_id=1, source_target_pairs={{0,16},{8,24},{16,0},{24,8},{1,17},{9,25},{17,1},{25,9},{2,18},{10... | collective-permute-start | bytes 110600 | tf_op jit(solution)/shard_map/ppermute | solution.py:185
  7.9 4.3 %collective-permute-start.1 = (bf16[2,128,128]{2,1,0:T(8,128)(2,1)S(1)}, bf16[2,128,128]{2,1,0:T(8,128)(2,1)S(1)}, u32[]{:S(2)}, u32[]{:S(2)}) collective-permute-start(bf16[2,128,128]{2,1,0:T(8,128)(2,1)S(1)} %pad_maximum_fusion.5), channel_id=1, source_target_pairs={{0,2},{1,3},{2,0},{3,1},{4,6},{5,7},{6,4},{7,5},{8,10},{9,11},{10,... | collective-permute-start | bytes 196616 | tf_op jit(solution)/shard_map/ppermute | solution.py:185
  10.4 5.3 %collective-permute-start.6 = (bf16[2,144,128]{2,1,0:T(8,128)(2,1)S(1)}, bf16[2,144,128]{2,1,0:T(8,128)(2,1)S(1)}, u32[]{:S(2)}, u32[]{:S(2)}) collective-permute-start(bf16[2,144,128]{2,1,0:T(8,128)(2,1)S(1)} %pad_maximum_fusion.4), channel_id=1, source_target_pairs={{0,4},{1,5},{2,6},{3,7},{4,0},{5,1},{6,2},{7,3},{8,12},{9,13},{10,... | collective-permute-start | bytes 221192 | tf_op jit(solution)/shard_map/ppermute | solution.py:185
  12.3 10.3 %collective-permute-start.2 = (bf16[4,128,128]{2,1,0:T(8,128)(2,1)S(1)}, bf16[4,128,128]{2,1,0:T(8,128)(2,1)S(1)}, u32[]{:S(2)}, u32[]{:S(2)}) collective-permute-start(bf16[4,128,128]{2,1,0:T(8,128)(2,1)S(1)} %pad_maximum_fusion.3), channel_id=1, source_target_pairs={{0,1},{1,0},{2,3},{3,2},{4,5},{5,4},{6,7},{7,6},{8,9},{9,8},{10,11... | collective-permute-start | bytes 393224 | tf_op jit(solution)/shard_map/ppermute | solution.py:185
  15.7 5.2 %collective-permute-start.7 = (bf16[4,144,128]{2,1,0:T(8,128)(2,1)S(1)}, bf16[4,144,128]{2,1,0:T(8,128)(2,1)S(1)}, u32[]{:S(2)}, u32[]{:S(2)}) collective-permute-start(bf16[4,144,128]{2,1,0:T(8,128)(2,1)S(1)} %pad_maximum_fusion.2), channel_id=1, source_target_pairs={{0,2},{1,3},{2,0},{3,1},{4,6},{5,7},{6,4},{7,5},{8,10},{9,11},{10,... | collective-permute-start | bytes 442376 | tf_op jit(solution)/shard_map/ppermute | solution.py:185
  20.9 6.8 %collective-permute-start.8 = (bf16[8,144,128]{2,1,0:T(8,128)(2,1)S(1)}, bf16[8,144,128]{2,1,0:T(8,128)(2,1)S(1)}, u32[]{:S(2)}, u32[]{:S(2)}) collective-permute-start(bf16[8,144,128]{2,1,0:T(8,128)(2,1)S(1)} %pad_maximum_fusion), channel_id=1, source_target_pairs={{0,1},{1,0},{2,3},{3,2},{4,5},{5,4},{6,7},{7,6},{8,9},{9,8},{10,11... | collective-permute-start | bytes 884744 | tf_op jit(solution)/shard_map/ppermute | solution.py:185
  22.6 6.4 %collective-permute-start.3 = (bf16[8,128,128]{2,1,0:T(8,128)(2,1)S(1)}, bf16[8,128,128]{2,1,0:T(8,128)(2,1)S(1)}, u32[]{:S(2)}, u32[]{:S(2)}) collective-permute-start(bf16[8,128,128]{2,1,0:T(8,128)(2,1)S(1)} %pad_maximum_fusion.1), channel_id=1, source_target_pairs={{0,16},{8,24},{16,0},{24,8},{1,17},{9,25},{17,1},{25,9},{2,18},{10... | collective-permute-start | bytes 786440 | tf_op jit(solution)/shard_map/ppermute | solution.py:185
  27.8 1.4 %copy-start = (bf16[9,128,128]{2,1,0:T(8,128)(2,1)S(1)}, bf16[9,128,128]{2,1,0:T(8,128)(2,1)}, u32[]{:S(2)}) copy-start(bf16[9,128,128]{2,1,0:T(8,128)(2,1)} %two.3) | copy-start | bytes 884740
  27.8 1.4 %copy-start.2 = (bf16[128,512]{1,0:T(8,128)(2,1)S(1)}, bf16[128,512]{1,0:T(8,128)(2,1)}, u32[]{:S(2)}) copy-start(bf16[128,512]{1,0:T(8,128)(2,1)} %w_proj.3) | copy-start | bytes 393220
  27.8 1.4 %copy-start.4 = (bf16[128,128]{1,0:T(8,128)(2,1)S(1)}, bf16[128,128]{1,0:T(8,128)(2,1)}, u32[]{:S(2)}) copy-start(bf16[128,128]{1,0:T(8,128)(2,1)} %w_gate.3) | copy-start | bytes 98308
  27.8 4.6 %collective-permute-start.9 = (bf16[16,144,128]{2,1,0:T(8,128)(2,1)S(1)}, bf16[16,144,128]{2,1,0:T(8,128)(2,1)S(1)}, u32[]{:S(2)}, u32[]{:S(2)}) collective-permute-start(bf16[16,144,128]{2,1,0:T(8,128)(2,1)S(1)} %constant_dynamic-update-slice_fusion.5.cot_near), channel_id=1, source_target_pairs={{0,8},{8,0},{16,24},{24,16},{1,9},{9,1},{17,25},{25,17},{2,10},{10... | collective-permute-start | bytes 1769480 | tf_op jit(solution)/shard_map/ppermute | solution.py:185
  29.0 3.3 %copy-start.3 = (bf16[9,128,128]{2,1,0:T(8,128)(2,1)S(1)}, bf16[9,128,128]{2,1,0:T(8,128)(2,1)}, u32[]{:S(2)}) copy-start(bf16[9,128,128]{2,1,0:T(8,128)(2,1)} %param.17) | copy-start | bytes 884740
  29.1 3.3 %collective-permute-start.4 = (bf16[16,128,128]{2,1,0:T(8,128)(2,1)S(1)}, bf16[16,128,128]{2,1,0:T(8,128)(2,1)S(1)}, u32[]{:S(2)}, u32[]{:S(2)}) collective-permute-start(bf16[16,128,128]{2,1,0:T(8,128)(2,1)S(1)} %constant_dynamic-update-slice_fusion.near), channel_id=1, source_target_pairs={{0,8},{8,0},{16,24},{24,16},{1,9},{9,1},{17,25},{25,17},{2,10},{10... | collective-permute-start | bytes 1572872 | tf_op jit(solution)/shard_map/ppermute | solution.py:185
  29.2 3.2 %copy-start.5 = (bf16[128,128]{1,0:T(8,128)(2,1)S(1)}, bf16[128,128]{1,0:T(8,128)(2,1)}, u32[]{:S(2)}) copy-start(bf16[128,128]{1,0:T(8,128)(2,1)} %w_out.1) | copy-start | bytes 98308
  31.4 1.0 %copy-start.1 = (f32[2,16,64,128]{3,2,1,0:T(8,128)}, f32[2,16,64,128]{3,2,1,0:T(8,128)S(1)}, u32[]{:S(2)}) copy-start(f32[2,16,64,128]{3,2,1,0:T(8,128)S(1)} %get-tuple-element.18.near_gating) | copy-start | bytes 3145732
  32.4 0.7 %copy-start.6 = (s32[2]{0:T(128)S(1)}, s32[2]{0:T(128)}, u32[]{:S(2)}) copy-start(s32[2]{0:T(128)} %dilations.1) | copy-start | bytes 28

commit v5 on v4

--- a/solution.py
+++ b/solution.py
@@ -9,6 +9,8 @@
 
 DMAX = 8
 VMEM_LIMIT = 48 * 1024 * 1024
+FORWARD_VMEM = 36 * 1024 * 1024
+BACKWARD_VMEM = 28 * 1024 * 1024
 
 
 EPSILON = 1e-05
@@ -178,14 +180,16 @@
     return cols + rows, rows[:-1] + cols + rows[-1:]
 
 
-def gather_blocks(block, rounds):
+def gather_blocks(block, rounds, early=None):
     held = block[None]
     for step, (axis, distance) in enumerate(rounds):
+        if step == 2 and early is not None:
+            held, early = lax.optimization_barrier((held, early))
         pairs = [(i, i ^ distance) for i in range(lax.axis_size(axis))]
         other = lax.ppermute(held, axis, pairs)
         if step < len(rounds) - 1:
             held = jnp.concatenate([held, other], axis=0)
-    return held, other
+    return held, other, early
 
 
 def place_of(position, rounds, row_place, col_place):
@@ -222,9 +226,9 @@
 
 
 def project_half(
-    plan, core, pairs, cots, w_proj, w_gate, left, right, swapped, gating, contact, start, turned
+    plan, core, pairs, w_proj, w_gate, left, right, swapped, gating, contact, start, turned
 ):
-    rounds, cot_rounds, height, breadth, tokens = plan
+    rounds, _, height, breadth, tokens = plan
     channels, hidden = w_gate.shape[0], w_gate.shape[1]
     col_count, chips = tokens // breadth, tokens // height // 2
     row_place, col_place = lax.axis_index("row"), lax.axis_index("col")
@@ -244,13 +248,12 @@
             for col in range(col_count):
                 col_change = col_place ^ col
                 slot = slot_of(row_change, col_change, rounds)
-                cot_slot = slot_of(row_change, col_change, cot_rounds)
                 blocks.append(
                     pairs[slot, first * breadth : (first + rows) * breadth, :]
                     .astype(jnp.float32)
                     .reshape(rows, breadth, channels)
                 )
-                mark = cots[cot_slot, pixels:, :].astype(jnp.float32)[first : first + rows]
+                mark = pairs[slot, pixels:, :].astype(jnp.float32)[first : first + rows]
                 marks.append(mark[:, None, :] * own_lane[None])
             values.append(jnp.concatenate(blocks, axis=1).reshape(rows * tokens, channels))
             masks.append(jnp.concatenate(marks, axis=1).reshape(rows * tokens, channels))
@@ -272,7 +275,7 @@
                 target[pl.ds(first + row, hidden, stride=height), :] = strip.T
         shape = (chips, rows, tokens, channels)
         span = slice(first, first + rows)
-        gating[:, span] = gates.reshape(shape)
+        gating[:, span] = gates.astype(jnp.bfloat16).reshape(shape)
         contact[:, span] = masks[:, channels:].astype(jnp.bfloat16).reshape(shape)
         start[:, span] = values.astype(jnp.bfloat16).reshape(shape)
     shape = (hidden, height, chips * tokens)
@@ -285,7 +288,6 @@
 def near_kernel(
     plan,
     near,
-    cot_near,
     w_proj,
     w_gate,
     two,
@@ -307,7 +309,6 @@
         plan,
         core,
         near,
-        cot_near,
         w_proj,
         w_gate,
         left,
@@ -320,12 +321,61 @@
     )
 
 
-def map_kernel(
+def spread(source, rows, pad, rate, target):
+    tokens, channels = target.shape[1], source.shape[2]
+    for tap in range(3):
+        moved = source[
+            pl.ds(pad + rows.start, rows.size), pl.ds(DMAX + (tap - 1) * rate, tokens), :
+        ]
+        target[pl.ds(DMAX + rows.start, rows.size), :, tap * channels : (tap + 1) * channels] = (
+            moved.astype(jnp.bfloat16)
+        )
+
+
+def taps(source, first, count, rate):
+    tokens = source.shape[1]
+    views = [
+        source[pl.ds(DMAX + first + (tap - 1) * rate, count)].reshape(count * tokens, -1)
+        for tap in range(3)
+    ]
+    return jnp.concatenate(views, axis=1)
+
+
+def windows(source, rate, row_start, col_start, height, breadth):
+    views = [
+        source[
+            pl.ds(row_start + DMAX + (tap // 3 - 1) * rate, height),
+            pl.ds(col_start + DMAX + (tap % 3 - 1) * rate, breadth),
+            :,
+        ].reshape(height * breadth, -1)
+        for tap in range(9)
+    ]
+    return jnp.concatenate(views, axis=1).astype(jnp.bfloat16)
+
+
+def lanes(step, size):
+    return pl.ds(pl.multiple_of(step * size, size), size)
+
+
+def clear_border(target, tokens):
+    line, channels = target.shape[1], target.shape[2]
+    border = jnp.zeros((DMAX, line, channels), target.dtype)
+    rim = jnp.zeros((tokens, DMAX, channels), target.dtype)
+    if target.shape[0] > tokens:
+        target[0:DMAX] = border
+        target[DMAX + tokens :] = border
+    if line > tokens:
+        rows = slice(target.shape[0] - tokens - DMAX, target.shape[0] - DMAX)
+        if target.shape[0] == tokens:
+            rows = slice(0, tokens)
+        target[rows, 0:DMAX, :] = rim
+        target[rows, DMAX + tokens :, :] = rim
+
+
+def forward_kernel(
     plan,
     dilations,
     far,
-    cot_near,
-    cot_far,
     w_proj,
     w_gate,
     w_out,
@@ -337,129 +387,53 @@
     near_gating,
     near_contact,
     near_start,
-    two_t,
     output,
-    grad_pair,
-    grad_one,
-    grad_two,
-    left,
+    flipped,
+    flipped_two,
+    factor,
+    mine,
+    own_contact,
+    far_left,
     right,
     swapped,
-    gating,
-    contact,
-    start,
+    far_gating,
+    far_contact,
+    far_start,
     turned_left,
     turned_right,
     products,
     updated,
-    hidden_grad,
     field,
     wide,
-    wide_cot,
-    wide_pre,
     second,
-    grad_pre,
-    flipped,
-    flipped_two,
-    sum_one,
-    sum_two,
 ):
-    rounds, cot_rounds, height, breadth, tokens = plan
+    _, _, height, breadth, tokens = plan
     hidden, channels = w_out.shape
     pixels = height * breadth
     chips = tokens // height // 2
     row_place, col_place = lax.axis_index("row"), lax.axis_index("col")
     core = row_place % 2
     rate_one, rate_two = dilations[0], dilations[1]
-    half = far.shape[0]
-    line = tokens + 2 * DMAX
     inside = slice(DMAX, DMAX + tokens)
-
-    rim = jnp.zeros((tokens, DMAX, channels), jnp.float32)
-    edge = jnp.zeros((DMAX, tokens, 3 * channels), jnp.bfloat16)
-    border = jnp.zeros((DMAX, line, channels), jnp.float32)
-    field[:, 0:DMAX, :] = rim
-    field[:, DMAX + tokens :, :] = rim
-    for target in (wide, wide_cot, wide_pre):
-        target[0:DMAX] = edge
-        target[DMAX + tokens :] = edge
-    for target in (second, grad_pre):
-        target[0:DMAX] = border
-        target[DMAX + tokens :] = border
-        target[inside, 0:DMAX, :] = rim
-        target[inside, DMAX + tokens :, :] = rim
-
-    for whole, part in (
-        (left, near_left),
-        (right, near_right),
-        (swapped, near_swapped),
-        (gating, near_gating),
-        (contact, near_contact),
-        (start, near_start),
-    ):
-        whole[core] = part[...]
-    targets = [
-        whole.at[1 - core] for whole in (left, right, swapped, gating, contact, start)
-    ]
+    for target in (field, wide, second):
+        clear_border(target, tokens)
+
+    right[core] = near_right[...]
+    swapped[core] = near_swapped[...]
     project_half(
         plan,
         1 - core,
         far,
-        cot_far,
         w_proj,
         w_gate,
-        *targets,
+        far_left,
+        right.at[1 - core],
+        swapped.at[1 - core],
+        far_gating,
+        far_contact,
+        far_start,
         (turned_left, turned_right),
     )
-
-    several = 4
-
-    def place_cot(source, base):
-        def body(step, carry):
-            for i in range(several):
-                slot = step * several + i
-                row, col = place_of(base + slot, cot_rounds, row_place, col_place)
-                cols = pl.ds(pl.multiple_of(DMAX + col * breadth, breadth), breadth)
-                field[pl.ds(row * height, height), cols, :] = (
-                    source[slot, 0:pixels, :]
-                    .astype(jnp.float32)
-                    .reshape(height, breadth, channels)
-                )
-            return carry
-
-        lax.fori_loop(0, half // several, body, 0)
-
-    place_cot(cot_near, 0)
-    place_cot(cot_far, half)
-
-    def spread(source, rows, pad, rate, target):
-        for tap in range(3):
-            moved = source[
-                pl.ds(pad + rows.start, rows.size), pl.ds(DMAX + (tap - 1) * rate, tokens), :
-            ]
-            target[
-                pl.ds(DMAX + rows.start, rows.size), :, tap * channels : (tap + 1) * channels
-            ] = moved.astype(jnp.bfloat16)
-
-    def taps(source, first, count, rate):
-        views = [
-            source[pl.ds(DMAX + first + (tap - 1) * rate, count)].reshape(count * tokens, -1)
-            for tap in range(3)
-        ]
-        return jnp.concatenate(views, axis=1)
-
-    def lanes(step, size):
-        return pl.ds(pl.multiple_of(step * size, size), size)
-
-    chunk = 8
-    size = chunk * tokens
-    steps = tokens // chunk
-
-    def spread_cot(step, carry):
-        spread(field, pl.ds(step * chunk, chunk), 0, -rate_two, wide_cot)
-        return carry
-
-    lax.fori_loop(0, steps, spread_cot, 0)
 
     lane = lax.broadcasted_iota(jnp.int32, (height, chips * tokens), 1)
     low = jnp.where(lane < tokens, 1.0, 0.0).astype(jnp.bfloat16)
@@ -473,7 +447,7 @@
             back = [swapped[0, h], swapped[1, h]]
             strips = [strip * low for strip in ahead + back]
             strips += [strip * high for strip in back + ahead]
-            mine = jnp.concatenate([left[0, h], left[1, h]], axis=0)
+            mine = jnp.concatenate([near_left[h], far_left[h]], axis=0)
             products[pl.ds(pl.multiple_of(h * 2 * height, 2 * height), 2 * height), :] = (
                 matmul_nt(mine, jnp.concatenate(strips, axis=0))
             )
@@ -481,11 +455,14 @@
 
     lax.fori_loop(0, hidden // batch, multiply, 0)
 
-    def update(step, carry):
-        side, first = step // (height // chunk), (step % (height // chunk)) * chunk
+    chunk = 8
+    size = chunk * tokens
+
+    def update(step, half, side, gating, contact, start):
+        first = step * chunk
         turned = []
         for row in range(chunk):
-            strip = products[pl.ds(side * height + first + row, hidden, stride=2 * height), :]
+            strip = products[pl.ds(half * height + first + row, hidden, stride=2 * height), :]
             turned.append(layer_norm(strip, axis=0).astype(jnp.bfloat16).T)
         product_norm = jnp.concatenate(
             [
@@ -495,12 +472,11 @@
             ],
             axis=0,
         )
-        shape = (chips, chunk, tokens, channels)
-        change = matmul(product_norm, w_out[...]).reshape(shape)
+        change = matmul(product_norm, w_out[...]).reshape(chips, chunk, tokens, channels)
         rows = pl.ds(first, chunk)
-        fresh = start[side, :, rows].astype(jnp.float32) + gating[side, :, rows] * change
+        fresh = start[:, rows].astype(jnp.float32) + gating[:, rows].astype(jnp.float32) * change
         fresh = fresh.astype(jnp.bfloat16).astype(jnp.float32)
-        first_in = layer_norm(fresh) * contact[side, :, rows].astype(jnp.float32)
+        first_in = layer_norm(fresh) * contact[:, rows].astype(jnp.float32)
         for chip in range(chips):
             base = (chip * 2 + side) * height + first
             rows = pl.ds(base, chunk)
@@ -510,42 +486,118 @@
             flipped[:, pl.ds(pl.multiple_of(base * tokens, size), size)] = (
                 first_in[chip].reshape(size, channels).astype(jnp.bfloat16).T
             )
-            hidden_grad[rows] = matmul(
-                taps(wide_cot, base, chunk, -rate_two), two_t[...]
-            ).reshape(chunk, tokens, channels)
-        return carry
-
-    lax.fori_loop(0, 2 * (height // chunk), update, 0)
-
-    def first_conv(step):
+
+    halves = (
+        (core, near_gating, near_contact, near_start),
+        (1 - core, far_gating, far_contact, far_start),
+    )
+    for half, parts in enumerate(halves):
+        lax.fori_loop(0, height // chunk, lambda i, c: (update(i, half, *parts), c)[1], 0)
+
+    def first_conv(step, carry):
         first = step * chunk
-        rows = pl.ds(DMAX + first, chunk)
         shape = (chunk, tokens, channels)
         pre = matmul(taps(wide, first, chunk, rate_one), one[...])
         sigma = sigmoid(pre)
         second_in = pre * sigma
-        second[rows, inside, :] = second_in.reshape(shape)
+        second[pl.ds(DMAX + first, chunk), inside, :] = second_in.reshape(shape)
         flipped_two[:, lanes(step, size)] = second_in.astype(jnp.bfloat16).T
-        factor = (sigma * (1.0 + pre * (1.0 - sigma))).reshape(shape)
-        grad_pre[rows, inside, :] = (
-            (hidden_grad[pl.ds(first, chunk)] * factor).astype(jnp.bfloat16).astype(jnp.float32)
-        )
-
-    def after_conv(step):
-        sum_two[...] += matmul(
-            flipped_two[:, lanes(step, size)], taps(wide_cot, step * chunk, chunk, -rate_two)
-        )
-        spread(grad_pre, pl.ds(step * chunk, chunk), DMAX, -rate_one, wide_pre)
-
-    def middle(step, carry):
-        first_conv(step)
-        after_conv(step - 1)
+        factor[pl.ds(first, chunk)] = (sigma * (1.0 + pre * (1.0 - sigma))).reshape(shape)
         return carry
 
+    lax.fori_loop(0, tokens // chunk, first_conv, 0)
+
+    row_start, col_start = row_place * height, col_place * breadth
+    cols = pl.ds(pl.multiple_of(col_start, breadth), breadth)
+    fresh = updated[pl.ds(row_start, height), cols, :].reshape(pixels, channels)
+    mine[...] = fresh
+    second_pre = matmul(
+        windows(second, rate_two, row_start, col_start, height, breadth),
+        two[...].reshape(9 * channels, channels),
+    )
+    output[...] = (fresh + second_pre).astype(jnp.bfloat16)
+    marks = near_contact[row_place // 2].astype(jnp.float32)
+    place_col = lax.broadcasted_iota(jnp.int32, (tokens, channels), 0) // breadth
+    marks = jnp.where((place_col == col_place)[None], marks, 0.0)
+    marks = marks.reshape(height, tokens // breadth, breadth, channels)
+    own_contact[...] = jnp.sum(marks, axis=1).reshape(pixels, channels)
+
+
+def backward_kernel(
+    plan,
+    dilations,
+    cot_near,
+    cot_far,
+    one,
+    two_t,
+    flipped,
+    flipped_two,
+    factor,
+    mine,
+    own_contact,
+    grad_pair,
+    grad_one,
+    grad_two,
+    field,
+    wide_cot,
+    wide_pre,
+    grad_pre,
+    sum_one,
+    sum_two,
+):
+    _, cot_rounds, height, breadth, tokens = plan
+    channels = one.shape[1]
+    pixels = height * breadth
+    row_place, col_place = lax.axis_index("row"), lax.axis_index("col")
+    rate_one, rate_two = dilations[0], dilations[1]
+    half = cot_far.shape[0]
+    inside = slice(DMAX, DMAX + tokens)
+    for target in (field, wide_cot, wide_pre, grad_pre):
+        clear_border(target, tokens)
+
+    several = 4
+
+    def place_cot(source, base):
+        def body(step, carry):
+            for i in range(several):
+                slot = step * several + i
+                row, col = place_of(base + slot, cot_rounds, row_place, col_place)
+                cols = pl.ds(pl.multiple_of(DMAX + col * breadth, breadth), breadth)
+                field[pl.ds(row * height, height), cols, :] = (
+                    source[slot]
+                    .astype(jnp.float32)
+                    .reshape(height, breadth, channels)
+                )
+            return carry
+
+        lax.fori_loop(0, half // several, body, 0)
+
+    place_cot(cot_near, 0)
+    place_cot(cot_far, half)
+
+    chunk = 8
+    size = chunk * tokens
+    steps = tokens // chunk
+
+    def spread_cot(step, carry):
+        spread(field, pl.ds(step * chunk, chunk), 0, -rate_two, wide_cot)
+        return carry
+
+    lax.fori_loop(0, steps, spread_cot, 0)
+
     sum_two[...] = jnp.zeros_like(sum_two)
-    first_conv(0)
-    lax.fori_loop(1, steps, middle, 0)
-    after_conv(steps - 1)
+
+    def back_two(step, carry):
+        first = step * chunk
+        shifted = taps(wide_cot, first, chunk, -rate_two)
+        before = matmul(shifted, two_t[...]).reshape(chunk, tokens, channels)
+        before = (before * factor[pl.ds(first, chunk)]).astype(jnp.bfloat16).astype(jnp.float32)
+        grad_pre[pl.ds(DMAX + first, chunk), inside, :] = before
+        sum_two[...] += matmul(flipped_two[:, lanes(step, size)], shifted)
+        spread(grad_pre, pl.ds(first, chunk), DMAX, -rate_one, wide_pre)
+        return carry
+
+    lax.fori_loop(0, steps, back_two, 0)
 
     sum_one[...] = jnp.zeros_like(sum_one)
 
@@ -561,38 +613,14 @@
         grad_one[tap] = sum_one[:, columns] * (1.0 / tokens)
         grad_two[tap] = sum_two[:, columns] * (1.0 / tokens)
 
-    row_start, col_start = row_place * height, col_place * breadth
-
-    def windows(source, rate):
-        views = [
-            source[
-                pl.ds(row_start + DMAX + (tap // 3 - 1) * rate, height),
-                pl.ds(col_start + DMAX + (tap % 3 - 1) * rate, breadth),
-                :,
-            ].reshape(pixels, channels)
-            for tap in range(9)
-        ]
-        return jnp.concatenate(views, axis=1).astype(jnp.bfloat16)
-
-    rows = pl.ds(row_start, height)
-    cols = pl.ds(pl.multiple_of(col_start, breadth), breadth)
-    mine = updated[rows, cols, :].reshape(pixels, channels)
-    second_pre = matmul(windows(second, rate_two), two[...].reshape(9 * channels, channels))
-    output[...] = (mine + second_pre).astype(jnp.bfloat16)
-    own_contact = contact[core, row_place // 2].astype(jnp.float32)
-    own_contact = own_contact.reshape(height, tokens, channels)
-    place_col = lax.broadcasted_iota(jnp.int32, (tokens, channels), 0) // breadth
-    own_contact = jnp.where((place_col == col_place)[None], own_contact, 0.0)
-    own_contact = own_contact.reshape(height, tokens // breadth, breadth, channels)
-    own_contact = jnp.sum(own_contact, axis=1).reshape(pixels, channels)
     one_rows = [one[tap * channels : (tap + 1) * channels] for tap in range(9)]
-    grad_input = lax.dot_general(
-        windows(grad_pre, -rate_one),
+    grad_input = own_contact[...] * matmul_nt(
+        windows(
+            grad_pre, -rate_one, row_place * height, col_place * breadth, height, breadth
+        ),
         jnp.concatenate(one_rows, axis=1),
-        (((1,), (1,)), ((), ())),
-        preferred_element_type=jnp.float32,
-    ) * own_contact
-    centre = mine - jnp.mean(mine, axis=-1, keepdims=True)
+    )
+    centre = mine[...] - jnp.mean(mine[...], axis=-1, keepdims=True)
     inv_spread = lax.rsqrt(jnp.mean(centre * centre, axis=-1, keepdims=True) + EPSILON)
     scaled = centre * inv_spread
     grad_norm = inv_spread * (
@@ -600,9 +628,7 @@
         - jnp.mean(grad_input, axis=-1, keepdims=True)
         - scaled * jnp.mean(grad_input * scaled, axis=-1, keepdims=True)
     )
-    grad_pair[...] = (cot_near[0, 0:pixels, :].astype(jnp.float32) + grad_norm).astype(
-        jnp.bfloat16
-    )
+    grad_pair[...] = (cot_near[0].astype(jnp.float32) + grad_norm).astype(jnp.bfloat16)
 
 
 def replicated(
@@ -614,17 +640,16 @@
     tokens = height * row_count
     pixels = height * breadth
     rounds, cot_rounds = exchange_plan(row_count, col_count)
-    masks = jnp.concatenate(
-        [
-            pair_mask.astype(jnp.bfloat16),
-            contact_mask.astype(jnp.bfloat16),
-            jnp.zeros((height, channels - 2 * breadth), jnp.bfloat16),
-        ],
-        axis=1,
-    )
-    packed = jnp.concatenate([cotangent.reshape(pixels, channels), masks], axis=0)
-    near, far = gather_blocks(pair.reshape(pixels, channels), rounds)
-    cot_near, cot_far = gather_blocks(packed, cot_rounds)
+    free = channels - 2 * breadth
+    masks = jnp.pad(pair_mask, ((0, 0), (0, breadth + free))) + jnp.pad(
+        contact_mask, ((0, 0), (breadth, free))
+    )
+    packed = jnp.concatenate(
+        [pair.reshape(pixels, channels), masks.astype(jnp.bfloat16)], axis=0
+    )
+    rates = jnp.clip(dilations, 1, DMAX)
+    near, far, rates = gather_blocks(packed, rounds, rates)
+    cot_near, cot_far, _ = gather_blocks(cotangent.reshape(pixels, channels), cot_rounds)
     f32, bf16 = jnp.float32, jnp.bfloat16
     plan = (rounds, cot_rounds, height, breadth, tokens)
     chips = row_count // 2
@@ -632,16 +657,18 @@
     in_vmem = pl.BlockSpec(memory_space=pltpu.VMEM)
     side = ((hidden, height, chips * tokens), bf16)
     rows = (chips, height, tokens, channels)
-    halves = [side] * 3 + [(rows, f32), (rows, bf16), (rows, bf16)]
+    halves = [side] * 3 + [(rows, bf16)] * 3
     turned = pltpu.VMEM((hidden * height, chips * tokens), f32)
-    near_parts = pl.pallas_call(
+    stat = ((pixels, channels), f32)
+
+    def shapes(*entries):
+        return [jax.ShapeDtypeStruct(shape, dtype) for shape, dtype in entries]
+
+    *near_parts, two_t = pl.pallas_call(
         functools.partial(near_kernel, plan),
-        in_specs=[in_vmem] * 5,
+        in_specs=[in_vmem] * 4,
         out_specs=[in_vmem] * 7,
-        out_shape=[
-            jax.ShapeDtypeStruct(shape, dtype)
-            for shape, dtype in halves + [((9 * channels, channels), bf16)]
-        ],
+        out_shape=shapes(*halves, ((9 * channels, channels), bf16)),
         scratch_shapes=[turned] * 2,
         compiler_params=pltpu.CompilerParams(vmem_limit_bytes=VMEM_LIMIT // 3),
         cost_estimate=pl.CostEstimate(
@@ -649,44 +676,66 @@
             bytes_accessed=8 * tokens * tokens * channels,
             transcendentals=3 * tokens * tokens * channels // 2,
         ),
-    )(near, cot_near, w_proj, w_gate, conv_two)
+    )(near, w_proj, w_gate, conv_two)
     whole = pltpu.VMEM((tokens, tokens, channels), f32)
     padded = pltpu.VMEM((tokens, line, channels), f32)
     bordered = pltpu.VMEM((line, line, channels), f32)
     tripled = pltpu.VMEM((line, tokens, 3 * channels), bf16)
-    flat = pltpu.VMEM((channels, tokens * tokens), bf16)
+    both = pltpu.VMEM((2,) + side[0], bf16)
+    alone = pltpu.VMEM(rows, bf16)
+    flat = ((channels, tokens * tokens), bf16)
     sums = pltpu.VMEM((channels, 9 * channels), f32)
-    output, grad_pair, grad_one, grad_two = pl.pallas_call(
-        functools.partial(map_kernel, plan),
-        in_specs=[pl.BlockSpec(memory_space=pltpu.SMEM)] + [in_vmem] * 15,
-        out_specs=[in_vmem] * 4,
-        out_shape=[
-            jax.ShapeDtypeStruct((pixels, channels), bf16),
-            jax.ShapeDtypeStruct((pixels, channels), bf16),
-            jax.ShapeDtypeStruct((9, channels, channels), f32),
-            jax.ShapeDtypeStruct((9, channels, channels), f32),
-        ],
-        scratch_shapes=[pltpu.VMEM((2,) + shape, dtype) for shape, dtype in halves]
+    in_smem = pl.BlockSpec(memory_space=pltpu.SMEM)
+    output, *held = pl.pallas_call(
+        functools.partial(forward_kernel, plan),
+        in_specs=[in_smem] + [in_vmem] * 12,
+        out_specs=[in_vmem] * 6,
+        out_shape=shapes(
+            ((pixels, channels), bf16),
+            flat,
+            flat,
+            ((tokens, tokens, channels), f32),
+            stat,
+            stat,
+        ),
+        scratch_shapes=[pltpu.VMEM(*side), both, both, alone, alone, alone]
         + [turned] * 2
         + [pltpu.VMEM((hidden * 2 * height, chips * tokens), f32)]
-        + [whole] * 2
-        + [padded]
-        + [tripled] * 3
-        + [bordered] * 2
-        + [flat] * 2
-        + [sums] * 2,
-        compiler_params=pltpu.CompilerParams(vmem_limit_bytes=VMEM_LIMIT),
+        + [whole, padded, tripled, bordered],
+        compiler_params=pltpu.CompilerParams(vmem_limit_bytes=FORWARD_VMEM),
+        cost_estimate=pl.CostEstimate(
+            flops=tokens * tokens * channels * 40 * hidden,
+            bytes_accessed=40 * tokens * tokens * channels,
+            transcendentals=4 * tokens * tokens * channels,
+        ),
     )(
-        dilations,
+        rates,
         far,
-        cot_near,
-        cot_far,
         w_proj,
         w_gate,
         w_out,
         conv_one.reshape(9 * channels, channels),
         conv_two,
         *near_parts,
+    )
+    grad_pair, grad_one, grad_two = pl.pallas_call(
+        functools.partial(backward_kernel, plan),
+        in_specs=[in_smem] + [in_vmem] * 9,
+        out_specs=[in_vmem] * 3,
+        out_shape=shapes(
+            ((pixels, channels), bf16),
+            ((9, channels, channels), f32),
+            ((9, channels, channels), f32),
+        ),
+        scratch_shapes=[padded, tripled, tripled, bordered, sums, sums],
+        compiler_params=pltpu.CompilerParams(vmem_limit_bytes=BACKWARD_VMEM),
+    )(
+        rates,
+        cot_near,
+        cot_far,
+        conv_one.reshape(9 * channels, channels),
+        two_t,
+        *held,
     )
     block = (height, breadth, channels)
     return output.reshape(block), grad_pair.reshape(block), grad_one, grad_two

time: 61.2 us -> 62.3 us (1.018)
  other arithmetic: 1.57 us -> 3.87 us
  waiting for transfers between devices: 11.3 us -> 9.57 us
    concatenate x6, other arithmetic: 0.11 us -> 2.38 us  [gather_blocks(): held = jnp.concatenate([held, other], axis=0)]
    ppermute x10, waiting for transfers between devices: 11.3 us -> 9.57 us  [gather_blocks(): other = lax.ppermute(held, axis, pairs)]
    convert_element_type x2 -> x1, other arithmetic: 1.38 us -> 0.08 us  [replicated(): masks.astype(jnp.bfloat16)]
    broadcast_in_dim x0 -> x1, other arithmetic: none -> 0.76 us  [gather_blocks(): held = block[None]]
    unnamed x25 -> x18, local copies, waits for them, and re-layouts: 1.74 us -> 2.41 us
    min x0 -> x1, other arithmetic: none -> 0.66 us  [replicated(): rates = jnp.clip(dilations, 1, DMAX)]
    pallas_call x1 -> x2, Pallas kernels: 27.9 us -> 28 us  [the longest x1 16.7 us: replicated(): pl.pallas_call(functools.partial(forward_kernel, plan), in_specs=[in_smem...]
  transfers between devices with their start and end apart: 10 -> 10, of which waited for: 6 -> 5; matrix products, arithmetic and copies ran while one was open for 3% -> 6% of each run, Pallas kernels for 4% -> 31%
where the time goes in v5:
time: 62.3 us; the launch traced here: 61.8 us
  Pallas kernels  30.2 us (48%)
  starting transfers between devices  14.9 us (24%)
  waiting for transfers between devices  9.57 us (15%)
  other arithmetic  3.87 us (6%)
  local copies, waits for them, and re-layouts  2.48 us (4%)
  between operations  0.78 us (1%)
    pallas_call x1, Pallas kernels, replicated(): pl.pallas_call(functools.partial(forward_kernel, plan), in_specs=[in_smem...  16.7 us
    ppermute x10, starting transfers between devices, gather_blocks(): other = lax.ppermute(held, axis, pairs)  14.9 us
    pallas_call x1, Pallas kernels, replicated(): pl.pallas_call(functools.partial(backward_kernel, plan), in_specs=[in_sme...  11.3 us
    ppermute x10, waiting for transfers between devices, gather_blocks(): other = lax.ppermute(held, axis, pairs)  9.57 us
    unnamed x18, local copies, waits for them, and re-layouts  2.41 us
    concatenate x6, other arithmetic, gather_blocks(): held = jnp.concatenate([held, other], axis=0)  2.38 us
    pallas_call x1, Pallas kernels, replicated(): pl.pallas_call(functools.partial(near_kernel, plan), in_specs=[in_vmem] *...  2.19 us
  transfers between devices with their start and end apart: 10, of which 5 were waited for; matrix products, arithmetic and copies ran while one was open for 6% of the time, Pallas kernels for 31%

profile of v5, /device:TPU:0, one launch (start us, length us, event | category | flops | bytes accessed | tf_op | source)
XLA Modules:
  0.0 61.8 jit_solution(1027265091030178544)
XLA Ops:
  0.6 0.8 %copy.14 = s32[16,8]{1,0:T(8,128)S(1)} copy(s32[16,8]{0,1:T(8,128)} %param.11) | data formatting | bytes 1024 | tf_op args[1]
  1.4 0.8 %copy.15 = s32[16,8]{1,0:T(8,128)S(1)} copy(s32[16,8]{0,1:T(8,128)} %param.12) | data formatting | bytes 1024 | tf_op args[2]
  2.1 0.1 add_convert_fusion
  2.2 0.8 %maximum_bitcast_fusion = bf16[1,144,128]{2,1,0:T(8,128)(2,1)S(1)} fusion(bf16[16,128]{1,0:T(8,128)(2,1)S(1)} %add_convert_fusion, bf16[128,128]{1,0:T(8,128)(2,1)} %bitcast.14), kind=kLoop, calls=%fused_computation.6 | loop fusion | flops 73728 | bytes 73728 | tf_op jit(solution)/shard_map/broadcast_in_dim | solution.py:184
  3.0 0.0 copy-start.1
  3.0 0.0 copy-start.2
  3.0 0.0 copy-start.3
  3.0 4.1 %collective-permute-start = (bf16[1,144,128]{2,1,0:T(8,128)(2,1)S(1)}, bf16[1,144,128]{2,1,0:T(8,128)(2,1)S(1)}, u32[]{:S(2)}, u32[]{:S(2)}) collective-permute-start(bf16[1,144,128]{2,1,0:T(8,128)(2,1)S(1)} %maximum_bitcast_fusion), channel_id=1, source_target_pairs={{0,4},{1,5},{2,6},{3,7},{4,0},{5,1},{6,2},{7,3},{8,12},{9,13},{10,... | collective-permute-start | bytes 110600 | tf_op jit(solution)/shard_map/ppermute | solution.py:189
  7.1 1.5 %collective-permute-start.5 = (bf16[1,128,128]{2,1,0:T(8,128)(2,1)}, bf16[1,128,128]{2,1,0:T(8,128)(2,1)S(1)}, u32[]{:S(2)}, u32[]{:S(2)}) collective-permute-start(bf16[1,128,128]{2,1,0:T(8,128)(2,1)} %bitcast.10), channel_id=1, source_target_pairs={{0,16},{8,24},{16,0},{24,8},{1,17},{9,25},{17,1},{25,9},{2,18},{10... | collective-permute-start | bytes 98312 | tf_op jit(solution)/shard_map/ppermute | solution.py:189
  8.6 0.8 %constant_dynamic-update-slice_fusion.7 = bf16[16,128,128]{2,1,0:T(8,128)(2,1)S(1)} fusion(bf16[16,8,128]{2,1,0:T(8,128)(2,1)} %param.19), kind=kLoop, calls=%fused_computation.14 | loop fusion | bytes 65536
  9.4 0.7 %broadcast_clamp_fusion.dilations = s32[2]{0:T(128)S(1)} fusion(s32[2]{0:T(128)} %param.13), kind=kLoop, calls=%fused_computation.16 | loop fusion | flops 2 | bytes 16 | tf_op jit(solution)/shard_map/jit(clip)/min | solution.py:650
  10.0 0.0 collective-permute-done
  10.1 1.6 %collective-permute-start.1 = (bf16[2,144,128]{2,1,0:T(8,128)(2,1)S(1)}, bf16[2,144,128]{2,1,0:T(8,128)(2,1)S(1)}, u32[]{:S(2)}, u32[]{:S(2)}) collective-permute-start(bf16[2,144,128]{2,1,0:T(8,128)(2,1)S(1)} %pad_maximum_fusion.4), channel_id=1, source_target_pairs={{0,2},{1,3},{2,0},{3,1},{4,6},{5,7},{6,4},{7,5},{8,10},{9,11},{10,... | collective-permute-start | bytes 221192 | tf_op jit(solution)/shard_map/ppermute | solution.py:189
  11.7 0.0 collective-permute-done.5
  11.7 0.8 %pad_maximum_fusion.5 = bf16[2,128,128]{2,1,0:T(8,128)(2,1)S(1)} fusion(bf16[1,128,128]{2,1,0:T(8,128)(2,1)S(1)} %collective-permute-done.5, bf16[1,128,128]{2,1,0:T(8,128)(2,1)} %bitcast.11), kind=kLoop, calls=%fused_computation.5 | loop fusion | flops 32768 | bytes 131072 | tf_op jit(solution)/shard_map/concatenate | solution.py:191
  12.5 2.2 %collective-permute-start.6 = (bf16[2,128,128]{2,1,0:T(8,128)(2,1)S(1)}, bf16[2,128,128]{2,1,0:T(8,128)(2,1)S(1)}, u32[]{:S(2)}, u32[]{:S(2)}) collective-permute-start(bf16[2,128,128]{2,1,0:T(8,128)(2,1)S(1)} %pad_maximum_fusion.5), channel_id=1, source_target_pairs={{0,4},{1,5},{2,6},{3,7},{4,0},{5,1},{6,2},{7,3},{8,12},{9,13},{10,... | collective-permute-start | bytes 196616 | tf_op jit(solution)/shard_map/ppermute | solution.py:189
  14.7 0.0 collective-permute-done.1
  14.7 1.6 %collective-permute-start.2 = (bf16[4,144,128]{2,1,0:T(8,128)(2,1)S(1)}, bf16[4,144,128]{2,1,0:T(8,128)(2,1)S(1)}, u32[]{:S(2)}, u32[]{:S(2)}) collective-permute-start(bf16[4,144,128]{2,1,0:T(8,128)(2,1)S(1)} %pad_maximum_fusion.2), channel_id=1, source_target_pairs={{0,1},{1,0},{2,3},{3,2},{4,5},{5,4},{6,7},{7,6},{8,9},{9,8},{10,11... | collective-permute-start | bytes 442376 | tf_op jit(solution)/shard_map/ppermute | solution.py:189
  16.3 2.1 %collective-permute-done.6 = bf16[2,128,128]{2,1,0:T(8,128)(2,1)S(1)} collective-permute-done((bf16[2,128,128]{2,1,0:T(8,128)(2,1)S(1)}, bf16[2,128,128]{2,1,0:T(8,128)(2,1)S(1)}, u32[]{:S(2)}, u32[]{:S(2)}) %collective-permute-start.6) | collective-permute-done | bytes 65568 | tf_op jit(solution)/shard_map/ppermute | solution.py:189
  18.3 0.8 %pad_maximum_fusion.3 = bf16[4,128,128]{2,1,0:T(8,128)(2,1)S(1)} fusion(bf16[2,128,128]{2,1,0:T(8,128)(2,1)S(1)} %collective-permute-done.6, bf16[1,128,128]{2,1,0:T(8,128)(2,1)S(1)} %collective-permute-done.5, bf16[1,128,128]{2,1,0:T(8,128)(2,1)} %bitcast.12), kind=kLoop, calls=%fused_computation.3 | loop fusion | flops 131072 | bytes 262144 | tf_op jit(solution)/shard_map/concatenate | solution.py:191
  19.1 0.6 collective-permute-start.7
  19.7 0.2 collective-permute-done.2
  19.9 0.0 copy-start
  19.9 0.0 copy-start.4
  20.0 1.6 %collective-permute-start.3 = (bf16[8,144,128]{2,1,0:T(8,128)(2,1)S(1)}, bf16[8,144,128]{2,1,0:T(8,128)(2,1)S(1)}, u32[]{:S(2)}, u32[]{:S(2)}) collective-permute-start(bf16[8,144,128]{2,1,0:T(8,128)(2,1)S(1)} %pad_maximum_fusion), channel_id=1, source_target_pairs={{0,16},{8,24},{16,0},{24,8},{1,17},{9,25},{17,1},{25,9},{2,18},{10... | collective-permute-start | bytes 884744 | tf_op jit(solution)/shard_map/ppermute | solution.py:189
  21.5 2.6 %collective-permute-done.7 = bf16[4,128,128]{2,1,0:T(8,128)(2,1)S(1)} collective-permute-done((bf16[4,128,128]{2,1,0:T(8,128)(2,1)S(1)}, bf16[4,128,128]{2,1,0:T(8,128)(2,1)S(1)}, u32[]{:S(2)}, u32[]{:S(2)}) %collective-permute-start.7) | collective-permute-done | bytes 131104 | tf_op jit(solution)/shard_map/ppermute | solution.py:189
  24.1 0.8 %pad_maximum_fusion.1 = bf16[8,128,128]{2,1,0:T(8,128)(2,1)S(1)} fusion(bf16[4,128,128]{2,1,0:T(8,128)(2,1)S(1)} %collective-permute-done.7, bf16[2,128,128]{2,1,0:T(8,128)(2,1)S(1)} %collective-permute-done.6, bf16[1,128,128]{2,1,0:T(8,128)(2,1)S(1)} %collective-permute-done.5, bf16[1,128,128]{2,1,0:T(8,128)(2,1)} %bitcast.13), kind=kLoop, calls=%fused_computation.1 | loop fusion | flops 393216 | bytes 524288 | tf_op jit(solution)/shard_map/concatenate | solution.py:191
  24.9 1.6 %collective-permute-start.8 = (bf16[8,128,128]{2,1,0:T(8,128)(2,1)S(1)}, bf16[8,128,128]{2,1,0:T(8,128)(2,1)S(1)}, u32[]{:S(2)}, u32[]{:S(2)}) collective-permute-start(bf16[8,128,128]{2,1,0:T(8,128)(2,1)S(1)} %pad_maximum_fusion.1), channel_id=1, source_target_pairs={{0,1},{1,0},{2,3},{3,2},{4,5},{5,4},{6,7},{7,6},{8,9},{9,8},{10,11... | collective-permute-start | bytes 786440 | tf_op jit(solution)/shard_map/ppermute | solution.py:189
  26.5 0.2 collective-permute-done.3
  26.8 0.1 collective-permute-start.4
  26.9 4.5 %collective-permute-done.8 = bf16[8,128,128]{2,1,0:T(8,128)(2,1)S(1)} collective-permute-done((bf16[8,128,128]{2,1,0:T(8,128)(2,1)S(1)}, bf16[8,128,128]{2,1,0:T(8,128)(2,1)S(1)}, u32[]{:S(2)}, u32[]{:S(2)}) %collective-permute-start.8) | collective-permute-done | bytes 262176 | tf_op jit(solution)/shard_map/ppermute | solution.py:189
  31.4 0.1 collective-permute-start.9
  31.5 0.0 copy-done.1
  31.5 0.0 copy-done.2
  31.5 0.0 copy-done.3
  31.5 2.2 %shard_map.129 = (bf16[128,16,128]{2,1,0:T(8,128)(2,1)S(1)}, bf16[128,16,128]{2,1,0:T(8,128)(2,1)S(1)}, bf16[128,16,128]{2,1,0:T(8,128)(2,1)S(1)}, bf16[2,16,64,...) custom-call(bf16[16,144,128]{2,1,0:T(8,128)(2,1)S(1)} %constant_dyna, ...), custom_call_target="tpu_custom_call" | custom-call | flops 335544320 | bytes 4194304 | tf_op jit(solution)/shard_map/pallas_call | solution.py:667
  33.7 0.0 collective-permute-done.4.far
  33.7 0.0 copy-done
  33.7 0.0 copy-done.4
  33.8 16.7 %shard_map.130 = (bf16[128,128]{1,0:T(8,128)(2,1)}, bf16[128,4096]{1,0:T(8,128)(2,1)S(1)}, bf16[128,4096]{1,0:T(8,128)(2,1)S(1)}, f32[64,64,128]{2,1,0:T(8,128)S...) custom-call(s32[2]{0:T(128)S(1)} %broadcast_clamp_fusion.dilations, ...), custom_call_target="tpu_custom_call" | custom-call | flops 2684354560 | bytes 20971520 | tf_op jit(solution)/shard_map/pallas_call | solution.py:689
  50.5 0.0 collective-permute-done.9.cot_far
  50.5 11.3 %shard_map.131 = (bf16[128,128]{1,0:T(8,128)(2,1)}, f32[9,128,128]{2,1,0:T(8,128)}, f32[9,128,128]{2,1,0:T(8,128)}) custom-call(s32[2]{0:T(128)S(1)} %broadcast_clamp_fusion.dilations, bf16[16,128,128]{2,1,0:T(8,128)(2,1)S(1)} %constant_dynamic-update-slice_fusion.3.cot_near, bf16[16,128,128]{2,1,0:T(8,128)(2,1)S(1)} %collective-permute-done.9.cot_far, ...), custom_call_target="tpu_custom_call" | custom-call | tf_op jit(solution)/shard_map/pallas_call | solution.py:721
  (10 shorter events, 0.2 us)
Async XLA Ops:
  3.0 28.5 %copy-start.1 = (bf16[9,128,128]{2,1,0:T(8,128)(2,1)S(1)}, bf16[9,128,128]{2,1,0:T(8,128)(2,1)}, u32[]{:S(2)}) copy-start(bf16[9,128,128]{2,1,0:T(8,128)(2,1)} %two.3) | copy-start | bytes 884740
  3.0 28.5 %copy-start.2 = (bf16[128,512]{1,0:T(8,128)(2,1)S(1)}, bf16[128,512]{1,0:T(8,128)(2,1)}, u32[]{:S(2)}) copy-start(bf16[128,512]{1,0:T(8,128)(2,1)} %w_proj.3) | copy-start | bytes 393220
  3.0 28.5 %copy-start.3 = (bf16[128,128]{1,0:T(8,128)(2,1)S(1)}, bf16[128,128]{1,0:T(8,128)(2,1)}, u32[]{:S(2)}) copy-start(bf16[128,128]{1,0:T(8,128)(2,1)} %w_gate.3) | copy-start | bytes 98308
  3.0 7.0 %collective-permute-start = (bf16[1,144,128]{2,1,0:T(8,128)(2,1)S(1)}, bf16[1,144,128]{2,1,0:T(8,128)(2,1)S(1)}, u32[]{:S(2)}, u32[]{:S(2)}) collective-permute-start(bf16[1,144,128]{2,1,0:T(8,128)(2,1)S(1)} %maximum_bitcast_fusion), channel_id=1, source_target_pairs={{0,4},{1,5},{2,6},{3,7},{4,0},{5,1},{6,2},{7,3},{8,12},{9,13},{10,... | collective-permute-start | bytes 110600 | tf_op jit(solution)/shard_map/ppermute | solution.py:189
  7.1 4.6 %collective-permute-start.5 = (bf16[1,128,128]{2,1,0:T(8,128)(2,1)}, bf16[1,128,128]{2,1,0:T(8,128)(2,1)S(1)}, u32[]{:S(2)}, u32[]{:S(2)}) collective-permute-start(bf16[1,128,128]{2,1,0:T(8,128)(2,1)} %bitcast.10), channel_id=1, source_target_pairs={{0,16},{8,24},{16,0},{24,8},{1,17},{9,25},{17,1},{25,9},{2,18},{10... | collective-permute-start | bytes 98312 | tf_op jit(solution)/shard_map/ppermute | solution.py:189
  10.1 4.6 %collective-permute-start.1 = (bf16[2,144,128]{2,1,0:T(8,128)(2,1)S(1)}, bf16[2,144,128]{2,1,0:T(8,128)(2,1)S(1)}, u32[]{:S(2)}, u32[]{:S(2)}) collective-permute-start(bf16[2,144,128]{2,1,0:T(8,128)(2,1)S(1)} %pad_maximum_fusion.4), channel_id=1, source_target_pairs={{0,2},{1,3},{2,0},{3,1},{4,6},{5,7},{6,4},{7,5},{8,10},{9,11},{10,... | collective-permute-start | bytes 221192 | tf_op jit(solution)/shard_map/ppermute | solution.py:189
  12.5 5.9 %collective-permute-start.6 = (bf16[2,128,128]{2,1,0:T(8,128)(2,1)S(1)}, bf16[2,128,128]{2,1,0:T(8,128)(2,1)S(1)}, u32[]{:S(2)}, u32[]{:S(2)}) collective-permute-start(bf16[2,128,128]{2,1,0:T(8,128)(2,1)S(1)} %pad_maximum_fusion.5), channel_id=1, source_target_pairs={{0,4},{1,5},{2,6},{3,7},{4,0},{5,1},{6,2},{7,3},{8,12},{9,13},{10,... | collective-permute-start | bytes 196616 | tf_op jit(solution)/shard_map/ppermute | solution.py:189
  14.7 5.2 %collective-permute-start.2 = (bf16[4,144,128]{2,1,0:T(8,128)(2,1)S(1)}, bf16[4,144,128]{2,1,0:T(8,128)(2,1)S(1)}, u32[]{:S(2)}, u32[]{:S(2)}) collective-permute-start(bf16[4,144,128]{2,1,0:T(8,128)(2,1)S(1)} %pad_maximum_fusion.2), channel_id=1, source_target_pairs={{0,1},{1,0},{2,3},{3,2},{4,5},{5,4},{6,7},{7,6},{8,9},{9,8},{10,11... | collective-permute-start | bytes 442376 | tf_op jit(solution)/shard_map/ppermute | solution.py:189
  19.1 5.0 %collective-permute-start.7 = (bf16[4,128,128]{2,1,0:T(8,128)(2,1)S(1)}, bf16[4,128,128]{2,1,0:T(8,128)(2,1)S(1)}, u32[]{:S(2)}, u32[]{:S(2)}) collective-permute-start(bf16[4,128,128]{2,1,0:T(8,128)(2,1)S(1)} %pad_maximum_fusion.3), channel_id=1, source_target_pairs={{0,2},{1,3},{2,0},{3,1},{4,6},{5,7},{6,4},{7,5},{8,10},{9,11},{10,... | collective-permute-start | bytes 393224 | tf_op jit(solution)/shard_map/ppermute | solution.py:189
  19.9 13.8 %copy-start = (bf16[9,128,128]{2,1,0:T(8,128)(2,1)S(1)}, bf16[9,128,128]{2,1,0:T(8,128)(2,1)}, u32[]{:S(2)}) copy-start(bf16[9,128,128]{2,1,0:T(8,128)(2,1)} %param.17) | copy-start | bytes 884740
  19.9 13.8 %copy-start.4 = (bf16[128,128]{1,0:T(8,128)(2,1)S(1)}, bf16[128,128]{1,0:T(8,128)(2,1)}, u32[]{:S(2)}) copy-start(bf16[128,128]{1,0:T(8,128)(2,1)} %w_out.1) | copy-start | bytes 98308
  20.0 6.8 %collective-permute-start.3 = (bf16[8,144,128]{2,1,0:T(8,128)(2,1)S(1)}, bf16[8,144,128]{2,1,0:T(8,128)(2,1)S(1)}, u32[]{:S(2)}, u32[]{:S(2)}) collective-permute-start(bf16[8,144,128]{2,1,0:T(8,128)(2,1)S(1)} %pad_maximum_fusion), channel_id=1, source_target_pairs={{0,16},{8,24},{16,0},{24,8},{1,17},{9,25},{17,1},{25,9},{2,18},{10... | collective-permute-start | bytes 884744 | tf_op jit(solution)/shard_map/ppermute | solution.py:189
  24.9 6.4 %collective-permute-start.8 = (bf16[8,128,128]{2,1,0:T(8,128)(2,1)S(1)}, bf16[8,128,128]{2,1,0:T(8,128)(2,1)S(1)}, u32[]{:S(2)}, u32[]{:S(2)}) collective-permute-start(bf16[8,128,128]{2,1,0:T(8,128)(2,1)S(1)} %pad_maximum_fusion.1), channel_id=1, source_target_pairs={{0,1},{1,0},{2,3},{3,2},{4,5},{5,4},{6,7},{7,6},{8,9},{9,8},{10,11... | collective-permute-start | bytes 786440 | tf_op jit(solution)/shard_map/ppermute | solution.py:189
  26.8 6.9 %collective-permute-start.4 = (bf16[16,144,128]{2,1,0:T(8,128)(2,1)S(1)}, bf16[16,144,128]{2,1,0:T(8,128)(2,1)S(1)}, u32[]{:S(2)}, u32[]{:S(2)}) collective-permute-start(bf16[16,144,128]{2,1,0:T(8,128)(2,1)S(1)} %constant_dynamic-update-slice_fusion.near), channel_id=1, source_target_pairs={{0,8},{8,0},{16,24},{24,16},{1,9},{9,1},{17,25},{25,17},{2,10},{10... | collective-permute-start | bytes 1769480 | tf_op jit(solution)/shard_map/ppermute | solution.py:189
  31.4 19.1 %collective-permute-start.9 = (bf16[16,128,128]{2,1,0:T(8,128)(2,1)S(1)}, bf16[16,128,128]{2,1,0:T(8,128)(2,1)S(1)}, u32[]{:S(2)}, u32[]{:S(2)}) collective-permute-start(bf16[16,128,128]{2,1,0:T(8,128)(2,1)S(1)} %constant_dynamic-update-slice_fusion.3.cot_near), channel_id=1, source_target_pairs={{0,8},{8,0},{16,24},{24,16},{1,9},{9,1},{17,25},{25,17},{2,10},{10... | collective-permute-start | bytes 1572872 | tf_op jit(solution)/shard_map/ppermute | solution.py:189

commit v6 on v5

--- a/solution.py
+++ b/solution.py
@@ -180,16 +180,9 @@
     return cols + rows, rows[:-1] + cols + rows[-1:]
 
 
-def gather_blocks(block, rounds, early=None):
-    held = block[None]
-    for step, (axis, distance) in enumerate(rounds):
-        if step == 2 and early is not None:
-            held, early = lax.optimization_barrier((held, early))
-        pairs = [(i, i ^ distance) for i in range(lax.axis_size(axis))]
-        other = lax.ppermute(held, axis, pairs)
-        if step < len(rounds) - 1:
-            held = jnp.concatenate([held, other], axis=0)
-    return held, other, early
+def exchange(held, hop):
+    axis, distance = hop
+    return lax.ppermute(held, axis, [(i, i ^ distance) for i in range(lax.axis_size(axis))])
 
 
 def place_of(position, rounds, row_place, col_place):
@@ -225,6 +218,25 @@
     )
 
 
+def pack_kernel(dilations, pair, cotangent, pair_mask, contact_mask, packed, cot, rates):
+    pixels, channels = pair.shape
+    breadth, height = pair_mask.shape
+    masks = jnp.concatenate(
+        [
+            pair_mask[...].astype(jnp.float32),
+            contact_mask[...].astype(jnp.float32),
+            jnp.zeros((breadth, channels - 2 * height), jnp.float32),
+        ],
+        axis=1,
+    )
+    tile = jnp.concatenate([masks, jnp.zeros_like(masks)], axis=0)
+    packed[0, 0:pixels] = pair[...]
+    packed[0, pixels:] = tile.astype(jnp.bfloat16)
+    cot[0] = cotangent[...]
+    for rate in range(2):
+        rates[rate] = jnp.clip(dilations[rate], 1, DMAX)
+
+
 def project_half(
     plan, core, pairs, w_proj, w_gate, left, right, swapped, gating, contact, start, turned
 ):
@@ -232,12 +244,12 @@
     channels, hidden = w_gate.shape[0], w_gate.shape[1]
     col_count, chips = tokens // breadth, tokens // height // 2
     row_place, col_place = lax.axis_index("row"), lax.axis_index("col")
-    lane = lax.broadcasted_iota(jnp.int32, (breadth, channels), 1)
-    place = lax.broadcasted_iota(jnp.int32, (breadth, channels), 0)
-    own_lane = jnp.where((lane % breadth == place) & (lane < 2 * breadth), 1.0, 0.0)
+    lane = lax.broadcasted_iota(jnp.int32, (height, breadth, channels), 2)
+    place = lax.broadcasted_iota(jnp.int32, (height, breadth, channels), 0)
+    own_lane = jnp.where((lane % height == place) & (lane < 2 * height), 1.0, 0.0)
     pick_lane = lax.broadcasted_iota(jnp.int32, (channels, 2 * channels), 0)
     pick_half = lax.broadcasted_iota(jnp.int32, (channels, 2 * channels), 1) // channels
-    pick = jnp.where(pick_lane // breadth == pick_half, 1.0, 0.0).astype(jnp.bfloat16)
+    pick = jnp.where(pick_lane // height == pick_half, 1.0, 0.0).astype(jnp.bfloat16)
     pixels = height * breadth
     rows = 8
     for first in range(0, height, rows):
@@ -253,8 +265,8 @@
                     .astype(jnp.float32)
                     .reshape(rows, breadth, channels)
                 )
-                mark = pairs[slot, pixels:, :].astype(jnp.float32)[first : first + rows]
-                marks.append(mark[:, None, :] * own_lane[None])
+                mark = pairs[slot, pixels:, :].astype(jnp.float32)[:breadth]
+                marks.append(mark[None] * own_lane[first : first + rows])
             values.append(jnp.concatenate(blocks, axis=1).reshape(rows * tokens, channels))
             masks.append(jnp.concatenate(marks, axis=1).reshape(rows * tokens, channels))
         values = jnp.concatenate(values, axis=0)
@@ -438,7 +450,7 @@
     lane = lax.broadcasted_iota(jnp.int32, (height, chips * tokens), 1)
     low = jnp.where(lane < tokens, 1.0, 0.0).astype(jnp.bfloat16)
     high = jnp.where(lane < tokens, 0.0, 1.0).astype(jnp.bfloat16)
-    batch = 8
+    batch = 32
 
     def multiply(step, carry):
         for part in range(batch):
@@ -640,16 +652,6 @@
     tokens = height * row_count
     pixels = height * breadth
     rounds, cot_rounds = exchange_plan(row_count, col_count)
-    free = channels - 2 * breadth
-    masks = jnp.pad(pair_mask, ((0, 0), (0, breadth + free))) + jnp.pad(
-        contact_mask, ((0, 0), (breadth, free))
-    )
-    packed = jnp.concatenate(
-        [pair.reshape(pixels, channels), masks.astype(jnp.bfloat16)], axis=0
-    )
-    rates = jnp.clip(dilations, 1, DMAX)
-    near, far, rates = gather_blocks(packed, rounds, rates)
-    cot_near, cot_far, _ = gather_blocks(cotangent.reshape(pixels, channels), cot_rounds)
     f32, bf16 = jnp.float32, jnp.bfloat16
     plan = (rounds, cot_rounds, height, breadth, tokens)
     chips = row_count // 2
@@ -664,6 +666,29 @@
     def shapes(*entries):
         return [jax.ShapeDtypeStruct(shape, dtype) for shape, dtype in entries]
 
+    in_smem = pl.BlockSpec(memory_space=pltpu.SMEM)
+    held, cot_held, rates = pl.pallas_call(
+        pack_kernel,
+        in_specs=[in_smem] + [in_vmem] * 4,
+        out_specs=[in_vmem, in_vmem, in_smem],
+        out_shape=shapes(
+            ((1, pixels + 2 * breadth, channels), bf16),
+            ((1, pixels, channels), bf16),
+            ((2,), jnp.int32),
+        ),
+    )(
+        dilations,
+        pair.reshape(pixels, channels),
+        cotangent.reshape(pixels, channels),
+        pair_mask.T,
+        contact_mask.T,
+    )
+    for step, (hop, cot_hop) in enumerate(zip(rounds[:-1], cot_rounds[:-1])):
+        held = jnp.concatenate([held, exchange(held, hop)], axis=0)
+        cot_other = exchange(cot_held, cot_hop)
+        if step < len(rounds) - 2:
+            cot_held = jnp.concatenate([cot_held, cot_other], axis=0)
+    near, far = held, exchange(held, rounds[-1])
     *near_parts, two_t = pl.pallas_call(
         functools.partial(near_kernel, plan),
         in_specs=[in_vmem] * 4,
@@ -677,6 +702,9 @@
             transcendentals=3 * tokens * tokens * channels // 2,
         ),
     )(near, w_proj, w_gate, conv_two)
+    cot_other, two_t = lax.optimization_barrier((cot_other, two_t))
+    cot_near = jnp.concatenate([cot_held, cot_other], axis=0)
+    cot_far = exchange(cot_near, cot_rounds[-1])
     whole = pltpu.VMEM((tokens, tokens, channels), f32)
     padded = pltpu.VMEM((tokens, line, channels), f32)
     bordered = pltpu.VMEM((line, line, channels), f32)
@@ -685,7 +713,6 @@
     alone = pltpu.VMEM(rows, bf16)
     flat = ((channels, tokens * tokens), bf16)
     sums = pltpu.VMEM((channels, 9 * channels), f32)
-    in_smem = pl.BlockSpec(memory_space=pltpu.SMEM)
     output, *held = pl.pallas_call(
         functools.partial(forward_kernel, plan),
         in_specs=[in_smem] + [in_vmem] * 12,
@@ -750,6 +777,7 @@
         powers
         and row_count * col_count >= 8
         and height * breadth == channels == w_out.shape[0]
+        and breadth == 8
         and row_count // 2 * tokens == channels
         and whole * 60 <= VMEM_LIMIT
     )

time: 62.3 us -> 61 us (0.979)
  waiting for transfers between devices: 9.57 us -> 8.73 us
  other arithmetic: 3.87 us -> 4.69 us
  starting transfers between devices: 14.9 us -> 14.1 us
  local copies, waits for them, and re-layouts: 2.48 us -> 1.73 us
    concatenate x6, other arithmetic: 2.38 us -> 4.69 us  [the longest x3 2.36 us: replicated(): held = jnp.concatenate([held, exchange(held, hop)], axis=0)]
    pallas_call x0 -> x1, Pallas kernels: none -> 1.54 us  [replicated(): pl.pallas_call(pack_kernel, in_specs=[in_smem] + [in_vmem] * 4, out_specs...]
    pallas_call x1, Pallas kernels: 16.7 us -> 15.3 us  [replicated(): pl.pallas_call(functools.partial(forward_kernel, plan), in_specs=[in_smem...]
    ppermute x10, waiting for transfers between devices: 9.57 us -> 8.73 us  [exchange(): lax.ppermute(held, axis, [(i, i ^ distance) for i in range(lax.axis_size(...]
    broadcast_in_dim x1 -> x0, other arithmetic: 0.76 us -> none  [gather_blocks(): held = block[None]]
    ppermute x10, starting transfers between devices: 14.9 us -> 14.1 us  [exchange(): lax.ppermute(held, axis, [(i, i ^ distance) for i in range(lax.axis_size(...]
    unnamed x18 -> x20, local copies, waits for them, and re-layouts: 2.41 us -> 1.65 us
    min x1 -> x0, other arithmetic: 0.66 us -> none  [replicated(): rates = jnp.clip(dilations, 1, DMAX)]
  transfers between devices with their start and end apart: 10 -> 10, of which waited for: 5 -> 4; matrix products, arithmetic and copies ran while one was open for 6% -> 11% of each run, Pallas kernels for 31% -> 29%
where the time goes in v6:
time: 61 us; the launch traced here: 60.3 us
  Pallas kernels  30.3 us (50%)
  starting transfers between devices  14.1 us (23%)
  waiting for transfers between devices  8.73 us (14%)
  other arithmetic  4.69 us (8%)
  local copies, waits for them, and re-layouts  1.73 us (3%)
  between operations  0.8 us (1%)
    pallas_call x1, Pallas kernels, replicated(): pl.pallas_call(functools.partial(forward_kernel, plan), in_specs=[in_smem...  15.3 us
    ppermute x10, starting transfers between devices, exchange(): lax.ppermute(held, axis, [(i, i ^ distance) for i in range(lax.axis_size(...  14.1 us
    pallas_call x1, Pallas kernels, replicated(): pl.pallas_call(functools.partial(backward_kernel, plan), in_specs=[in_sme...  11.3 us
    ppermute x10, waiting for transfers between devices, exchange(): lax.ppermute(held, axis, [(i, i ^ distance) for i in range(lax.axis_size(...  8.73 us
    concatenate x3, other arithmetic, replicated(): held = jnp.concatenate([held, exchange(held, hop)], axis=0)  2.36 us
    concatenate x3, other arithmetic, replicated(): cot_held = jnp.concatenate([cot_held, cot_other], axis=0)  2.33 us
    pallas_call x1, Pallas kernels, replicated(): pl.pallas_call(functools.partial(near_kernel, plan), in_specs=[in_vmem] *...  2.15 us
    unnamed x20, local copies, waits for them, and re-layouts  1.65 us
  transfers between devices with their start and end apart: 10, of which 4 were waited for; matrix products, arithmetic and copies ran while one was open for 11% of the time, Pallas kernels for 29%

profile of v6, /device:TPU:0, one launch (start us, length us, event | category | flops | bytes accessed | tf_op | source)
XLA Modules:
  0.0 60.3 jit_solution(12457637881642884092)
XLA Ops:
  0.6 0.0 copy-start.3
  0.6 0.0 copy-start.4
  0.7 0.0 copy-start.2
  0.7 1.5 %shard_map.129 = (bf16[1,144,128]{2,1,0:T(8,128)(2,1)}, bf16[1,128,128]{2,1,0:T(8,128)(2,1)}, s32[2]{0:T(128)}) custom-call(s32[2]{0:T(128)} %dilations.1, bf16[128,128]{1,0:T(8,128)(2,1)} %bitcast.9, bf16[128,128]{1,0:T(8,128)(2,1)} %bitcast.10, s32[8,16]{1,0:T(8,128)} %bitcast.11, s32[8,16]{1,0:T(8,128)} %bitcast.12), custom_call_target="tpu_custom_call" | custom-call | tf_op jit(solution)/shard_map/pallas_call | solution.py:670
  2.2 4.1 %collective-permute-start = (bf16[1,144,128]{2,1,0:T(8,128)(2,1)}, bf16[1,144,128]{2,1,0:T(8,128)(2,1)S(1)}, u32[]{:S(2)}, u32[]{:S(2)}) collective-permute-start(bf16[1,144,128]{2,1,0:T(8,128)(2,1)} %get-tuple-element.26), channel_id=1, source_target_pairs={{0,4},{1,5},{2,6},{3,7},{4,0},{5,1},{6,2},{7,3},{8,12},{9,13},{10,... | collective-permute-start | bytes 110600 | tf_op jit(solution)/shard_map/ppermute | solution.py:185
  6.3 1.5 %collective-permute-start.5 = (bf16[1,128,128]{2,1,0:T(8,128)(2,1)}, bf16[1,128,128]{2,1,0:T(8,128)(2,1)S(1)}, u32[]{:S(2)}, u32[]{:S(2)}) collective-permute-start(bf16[1,128,128]{2,1,0:T(8,128)(2,1)} %get-tuple-element.34), channel_id=1, source_target_pairs={{0,16},{8,24},{16,0},{24,8},{1,17},{9,25},{17,1},{25,9},{2,18},{10... | collective-permute-start | bytes 98312 | tf_op jit(solution)/shard_map/ppermute | solution.py:185
  7.8 0.8 %constant_dynamic-update-slice_fusion.4 = bf16[16,144,128]{2,1,0:T(8,128)(2,1)S(1)} fusion(bf16[1,144,128]{2,1,0:T(8,128)(2,1)} %get-tuple-element.26), kind=kLoop, calls=%fused_computation.10 | loop fusion | bytes 73728
  8.6 0.8 %constant_dynamic-update-slice_fusion.9 = bf16[16,128,128]{2,1,0:T(8,128)(2,1)S(1)} fusion(bf16[1,128,128]{2,1,0:T(8,128)(2,1)} %get-tuple-element.34), kind=kLoop, calls=%fused_computation.15 | loop fusion | bytes 65536
  9.3 1.1 %collective-permute-done.5 = bf16[1,128,128]{2,1,0:T(8,128)(2,1)S(1)} collective-permute-done((bf16[1,128,128]{2,1,0:T(8,128)(2,1)}, bf16[1,128,128]{2,1,0:T(8,128)(2,1)S(1)}, u32[]{:S(2)}, u32[]{:S(2)}) %collective-permute-start.5) | collective-permute-done | bytes 32800 | tf_op jit(solution)/shard_map/ppermute | solution.py:185
  10.4 0.8 %pad_maximum_fusion.5 = bf16[2,128,128]{2,1,0:T(8,128)(2,1)S(1)} fusion(bf16[1,128,128]{2,1,0:T(8,128)(2,1)S(1)} %collective-permute-done.5, bf16[1,128,128]{2,1,0:T(8,128)(2,1)} %get-tuple-element.34), kind=kLoop, calls=%fused_computation.5 | loop fusion | flops 32768 | bytes 131072 | tf_op jit(solution)/shard_map/concatenate | solution.py:690
  11.2 0.1 collective-permute-start.6
  11.3 0.0 collective-permute-done
  11.3 0.8 %pad_maximum_fusion.4 = bf16[2,144,128]{2,1,0:T(8,128)(2,1)S(1)} fusion(bf16[1,144,128]{2,1,0:T(8,128)(2,1)S(1)} %collective-permute-done, bf16[1,144,128]{2,1,0:T(8,128)(2,1)} %get-tuple-element.26), kind=kLoop, calls=%fused_computation.4 | loop fusion | flops 36864 | bytes 147456 | tf_op jit(solution)/shard_map/concatenate | solution.py:687
  12.1 1.8 %collective-permute-start.1 = (bf16[2,144,128]{2,1,0:T(8,128)(2,1)S(1)}, bf16[2,144,128]{2,1,0:T(8,128)(2,1)S(1)}, u32[]{:S(2)}, u32[]{:S(2)}) collective-permute-start(bf16[2,144,128]{2,1,0:T(8,128)(2,1)S(1)} %pad_maximum_fusion.4), channel_id=1, source_target_pairs={{0,2},{1,3},{2,0},{3,1},{4,6},{5,7},{6,4},{7,5},{8,10},{9,11},{10,... | collective-permute-start | bytes 221192 | tf_op jit(solution)/shard_map/ppermute | solution.py:185
  13.9 3.2 %collective-permute-done.1 = bf16[2,144,128]{2,1,0:T(8,128)(2,1)S(1)} collective-permute-done((bf16[2,144,128]{2,1,0:T(8,128)(2,1)S(1)}, bf16[2,144,128]{2,1,0:T(8,128)(2,1)S(1)}, u32[]{:S(2)}, u32[]{:S(2)}) %collective-permute-start.1) | collective-permute-done | bytes 73760 | tf_op jit(solution)/shard_map/ppermute | solution.py:185
  17.1 0.8 %pad_maximum_fusion.2 = bf16[4,144,128]{2,1,0:T(8,128)(2,1)S(1)} fusion(bf16[2,144,128]{2,1,0:T(8,128)(2,1)S(1)} %collective-permute-done.1, bf16[1,144,128]{2,1,0:T(8,128)(2,1)S(1)} %collective-permute-done, bf16[1,144,128]{2,1,0:T(8,128)(2,1)} %get-tuple-element.26), kind=kLoop, calls=%fused_computation.2 | loop fusion | flops 147456 | bytes 294912 | tf_op jit(solution)/shard_map/concatenate | solution.py:687
  17.9 1.6 %collective-permute-start.2 = (bf16[4,144,128]{2,1,0:T(8,128)(2,1)S(1)}, bf16[4,144,128]{2,1,0:T(8,128)(2,1)S(1)}, u32[]{:S(2)}, u32[]{:S(2)}) collective-permute-start(bf16[4,144,128]{2,1,0:T(8,128)(2,1)S(1)} %pad_maximum_fusion.2), channel_id=1, source_target_pairs={{0,1},{1,0},{2,3},{3,2},{4,5},{5,4},{6,7},{7,6},{8,9},{9,8},{10,11... | collective-permute-start | bytes 442376 | tf_op jit(solution)/shard_map/ppermute | solution.py:185
  19.5 0.0 collective-permute-done.6
  19.5 0.8 %pad_maximum_fusion.3 = bf16[4,128,128]{2,1,0:T(8,128)(2,1)S(1)} fusion(bf16[2,128,128]{2,1,0:T(8,128)(2,1)S(1)} %collective-permute-done.6, bf16[1,128,128]{2,1,0:T(8,128)(2,1)S(1)} %collective-permute-done.5, bf16[1,128,128]{2,1,0:T(8,128)(2,1)} %get-tuple-element.34), kind=kLoop, calls=%fused_computation.3 | loop fusion | flops 131072 | bytes 262144 | tf_op jit(solution)/shard_map/concatenate | solution.py:690
  20.3 1.2 %collective-permute-start.7 = (bf16[4,128,128]{2,1,0:T(8,128)(2,1)S(1)}, bf16[4,128,128]{2,1,0:T(8,128)(2,1)S(1)}, u32[]{:S(2)}, u32[]{:S(2)}) collective-permute-start(bf16[4,128,128]{2,1,0:T(8,128)(2,1)S(1)} %pad_maximum_fusion.3), channel_id=1, source_target_pairs={{0,2},{1,3},{2,0},{3,1},{4,6},{5,7},{6,4},{7,5},{8,10},{9,11},{10,... | collective-permute-start | bytes 393224 | tf_op jit(solution)/shard_map/ppermute | solution.py:185
  21.5 1.6 %collective-permute-done.2 = bf16[4,144,128]{2,1,0:T(8,128)(2,1)S(1)} collective-permute-done((bf16[4,144,128]{2,1,0:T(8,128)(2,1)S(1)}, bf16[4,144,128]{2,1,0:T(8,128)(2,1)S(1)}, u32[]{:S(2)}, u32[]{:S(2)}) %collective-permute-start.2) | collective-permute-done | bytes 147488 | tf_op jit(solution)/shard_map/ppermute | solution.py:185
  23.1 0.8 %pad_maximum_fusion = bf16[8,144,128]{2,1,0:T(8,128)(2,1)S(1)} fusion(bf16[4,144,128]{2,1,0:T(8,128)(2,1)S(1)} %collective-permute-done.2, bf16[2,144,128]{2,1,0:T(8,128)(2,1)S(1)} %collective-permute-done.1, bf16[1,144,128]{2,1,0:T(8,128)(2,1)S(1)} %collective-permute-done, bf16[1,144,128]{2,1,0:T(8,128)(2,1)} %get-tuple-element.26), kind=kLoop, calls=%fused_computation | loop fusion | flops 442368 | bytes 589824 | tf_op jit(solution)/shard_map/concatenate | solution.py:687
  23.9 0.0 copy-start
  23.9 0.0 copy-start.1
  23.9 0.0 copy-start.5
  23.9 1.6 %collective-permute-start.3 = (bf16[8,144,128]{2,1,0:T(8,128)(2,1)S(1)}, bf16[8,144,128]{2,1,0:T(8,128)(2,1)S(1)}, u32[]{:S(2)}, u32[]{:S(2)}) collective-permute-start(bf16[8,144,128]{2,1,0:T(8,128)(2,1)S(1)} %pad_maximum_fusion), channel_id=1, source_target_pairs={{0,16},{8,24},{16,0},{24,8},{1,17},{9,25},{17,1},{25,9},{2,18},{10... | collective-permute-start | bytes 884744 | tf_op jit(solution)/shard_map/ppermute | solution.py:185
  25.6 0.0 collective-permute-done.7
  25.6 0.8 %pad_maximum_fusion.1 = bf16[8,128,128]{2,1,0:T(8,128)(2,1)S(1)} fusion(bf16[4,128,128]{2,1,0:T(8,128)(2,1)S(1)} %collective-permute-done.7, bf16[2,128,128]{2,1,0:T(8,128)(2,1)S(1)} %collective-permute-done.6, bf16[1,128,128]{2,1,0:T(8,128)(2,1)S(1)} %collective-permute-done.5, bf16[1,128,128]{2,1,0:T(8,128)(2,1)} %get-tuple-element.34), kind=kLoop, calls=%fused_computation.1 | loop fusion | flops 393216 | bytes 524288 | tf_op jit(solution)/shard_map/concatenate | solution.py:690
  26.4 1.6 %collective-permute-start.8 = (bf16[8,128,128]{2,1,0:T(8,128)(2,1)S(1)}, bf16[8,128,128]{2,1,0:T(8,128)(2,1)S(1)}, u32[]{:S(2)}, u32[]{:S(2)}) collective-permute-start(bf16[8,128,128]{2,1,0:T(8,128)(2,1)S(1)} %pad_maximum_fusion.1), channel_id=1, source_target_pairs={{0,1},{1,0},{2,3},{3,2},{4,5},{5,4},{6,7},{7,6},{8,9},{9,8},{10,11... | collective-permute-start | bytes 786440 | tf_op jit(solution)/shard_map/ppermute | solution.py:185
  28.0 2.8 %collective-permute-done.3 = bf16[8,144,128]{2,1,0:T(8,128)(2,1)S(1)} collective-permute-done((bf16[8,144,128]{2,1,0:T(8,128)(2,1)S(1)}, bf16[8,144,128]{2,1,0:T(8,128)(2,1)S(1)}, u32[]{:S(2)}, u32[]{:S(2)}) %collective-permute-start.3) | collective-permute-done | bytes 294944 | tf_op jit(solution)/shard_map/ppermute | solution.py:185
  30.8 0.1 collective-permute-start.4
  30.9 0.0 copy-done.3
  30.9 0.0 copy-done.4
  30.9 0.0 copy-done.2
  30.9 2.2 %shard_map.130 = (bf16[128,16,128]{2,1,0:T(8,128)(2,1)S(1)}, bf16[128,16,128]{2,1,0:T(8,128)(2,1)S(1)}, bf16[128,16,128]{2,1,0:T(8,128)(2,1)S(1)}, bf16[2,16,64,...) custom-call(bf16[16,144,128]{2,1,0:T(8,128)(2,1)S(1)} %constant_dyna, ...), custom_call_target="tpu_custom_call" | custom-call | flops 335544320 | bytes 4194304 | tf_op jit(solution)/shard_map/pallas_call | solution.py:692
  33.1 0.0 collective-permute-done.8
  33.1 0.6 collective-permute-start.9
  33.7 0.0 collective-permute-done.4.far
  33.7 0.0 copy-done
  33.7 0.0 copy-done.1
  33.7 0.0 copy-done.5
  33.7 15.3 %shard_map.131 = (bf16[128,128]{1,0:T(8,128)(2,1)}, bf16[128,4096]{1,0:T(8,128)(2,1)S(1)}, bf16[128,4096]{1,0:T(8,128)(2,1)S(1)}, f32[64,64,128]{2,1,0:T(8,128)S...) custom-call(s32[2]{0:T(128)S(1)} %copy-done.1, bf16[16,144,128]{2,1,0:T(8,128)(2,1)S(1)} %collective-permute-done.4.far, ...), custom_call_target="tpu_custom_call" | custom-call | flops 2684354560 | bytes 20971520 | tf_op jit(solution)/shard_map/pallas_call | solution.py:716
  49.0 0.0 collective-permute-done.9.cot_far
  49.0 11.3 %shard_map.132 = (bf16[128,128]{1,0:T(8,128)(2,1)}, f32[9,128,128]{2,1,0:T(8,128)}, f32[9,128,128]{2,1,0:T(8,128)}) custom-call(s32[2]{0:T(128)S(1)} %copy-done.1, bf16[16,128,128]{2,1,0:T(8,128)(2,1)S(1)} %constant_dynamic-update-slice_fusion.5.cot_near, bf16[16,128,128]{2,1,0:T(8,128)(2,1)S(1)} %collective-permute-done.9.cot_far, ...), custom_call_target="tpu_custom_call" | custom-call | tf_op jit(solution)/shard_map/pallas_call | solution.py:748
  (8 shorter events, 0.2 us)
Async XLA Ops:
  0.6 30.3 %copy-start.3 = (bf16[128,512]{1,0:T(8,128)(2,1)S(1)}, bf16[128,512]{1,0:T(8,128)(2,1)}, u32[]{:S(2)}) copy-start(bf16[128,512]{1,0:T(8,128)(2,1)} %w_proj.3) | copy-start | bytes 393220
  0.6 30.3 %copy-start.4 = (bf16[128,128]{1,0:T(8,128)(2,1)S(1)}, bf16[128,128]{1,0:T(8,128)(2,1)}, u32[]{:S(2)}) copy-start(bf16[128,128]{1,0:T(8,128)(2,1)} %w_gate.3) | copy-start | bytes 98308
  0.7 30.3 %copy-start.2 = (bf16[9,128,128]{2,1,0:T(8,128)(2,1)S(1)}, bf16[9,128,128]{2,1,0:T(8,128)(2,1)}, u32[]{:S(2)}) copy-start(bf16[9,128,128]{2,1,0:T(8,128)(2,1)} %two.3) | copy-start | bytes 884740
  2.2 9.1 %collective-permute-start = (bf16[1,144,128]{2,1,0:T(8,128)(2,1)}, bf16[1,144,128]{2,1,0:T(8,128)(2,1)S(1)}, u32[]{:S(2)}, u32[]{:S(2)}) collective-permute-start(bf16[1,144,128]{2,1,0:T(8,128)(2,1)} %get-tuple-element.26), channel_id=1, source_target_pairs={{0,4},{1,5},{2,6},{3,7},{4,0},{5,1},{6,2},{7,3},{8,12},{9,13},{10,... | collective-permute-start | bytes 110600 | tf_op jit(solution)/shard_map/ppermute | solution.py:185
  6.3 4.1 %collective-permute-start.5 = (bf16[1,128,128]{2,1,0:T(8,128)(2,1)}, bf16[1,128,128]{2,1,0:T(8,128)(2,1)S(1)}, u32[]{:S(2)}, u32[]{:S(2)}) collective-permute-start(bf16[1,128,128]{2,1,0:T(8,128)(2,1)} %get-tuple-element.34), channel_id=1, source_target_pairs={{0,16},{8,24},{16,0},{24,8},{1,17},{9,25},{17,1},{25,9},{2,18},{10... | collective-permute-start | bytes 98312 | tf_op jit(solution)/shard_map/ppermute | solution.py:185
  11.2 8.3 %collective-permute-start.6 = (bf16[2,128,128]{2,1,0:T(8,128)(2,1)S(1)}, bf16[2,128,128]{2,1,0:T(8,128)(2,1)S(1)}, u32[]{:S(2)}, u32[]{:S(2)}) collective-permute-start(bf16[2,128,128]{2,1,0:T(8,128)(2,1)S(1)} %pad_maximum_fusion.5), channel_id=1, source_target_pairs={{0,4},{1,5},{2,6},{3,7},{4,0},{5,1},{6,2},{7,3},{8,12},{9,13},{10,... | collective-permute-start | bytes 196616 | tf_op jit(solution)/shard_map/ppermute | solution.py:185
  12.1 5.1 %collective-permute-start.1 = (bf16[2,144,128]{2,1,0:T(8,128)(2,1)S(1)}, bf16[2,144,128]{2,1,0:T(8,128)(2,1)S(1)}, u32[]{:S(2)}, u32[]{:S(2)}) collective-permute-start(bf16[2,144,128]{2,1,0:T(8,128)(2,1)S(1)} %pad_maximum_fusion.4), channel_id=1, source_target_pairs={{0,2},{1,3},{2,0},{3,1},{4,6},{5,7},{6,4},{7,5},{8,10},{9,11},{10,... | collective-permute-start | bytes 221192 | tf_op jit(solution)/shard_map/ppermute | solution.py:185
  17.9 5.2 %collective-permute-start.2 = (bf16[4,144,128]{2,1,0:T(8,128)(2,1)S(1)}, bf16[4,144,128]{2,1,0:T(8,128)(2,1)S(1)}, u32[]{:S(2)}, u32[]{:S(2)}) collective-permute-start(bf16[4,144,128]{2,1,0:T(8,128)(2,1)S(1)} %pad_maximum_fusion.2), channel_id=1, source_target_pairs={{0,1},{1,0},{2,3},{3,2},{4,5},{5,4},{6,7},{7,6},{8,9},{9,8},{10,11... | collective-permute-start | bytes 442376 | tf_op jit(solution)/shard_map/ppermute | solution.py:185
  20.3 5.2 %collective-permute-start.7 = (bf16[4,128,128]{2,1,0:T(8,128)(2,1)S(1)}, bf16[4,128,128]{2,1,0:T(8,128)(2,1)S(1)}, u32[]{:S(2)}, u32[]{:S(2)}) collective-permute-start(bf16[4,128,128]{2,1,0:T(8,128)(2,1)S(1)} %pad_maximum_fusion.3), channel_id=1, source_target_pairs={{0,2},{1,3},{2,0},{3,1},{4,6},{5,7},{6,4},{7,5},{8,10},{9,11},{10,... | collective-permute-start | bytes 393224 | tf_op jit(solution)/shard_map/ppermute | solution.py:185
  23.9 9.8 %copy-start = (bf16[9,128,128]{2,1,0:T(8,128)(2,1)S(1)}, bf16[9,128,128]{2,1,0:T(8,128)(2,1)}, u32[]{:S(2)}) copy-start(bf16[9,128,128]{2,1,0:T(8,128)(2,1)} %param.17) | copy-start | bytes 884740
  23.9 9.8 %copy-start.1 = (s32[2]{0:T(128)S(1)}, s32[2]{0:T(128)}, u32[]{:S(2)}) copy-start(s32[2]{0:T(128)} %get-tuple-element.25.dilations) | copy-start | bytes 28
  23.9 9.8 %copy-start.5 = (bf16[128,128]{1,0:T(8,128)(2,1)S(1)}, bf16[128,128]{1,0:T(8,128)(2,1)}, u32[]{:S(2)}) copy-start(bf16[128,128]{1,0:T(8,128)(2,1)} %w_out.1) | copy-start | bytes 98308
  23.9 6.8 %collective-permute-start.3 = (bf16[8,144,128]{2,1,0:T(8,128)(2,1)S(1)}, bf16[8,144,128]{2,1,0:T(8,128)(2,1)S(1)}, u32[]{:S(2)}, u32[]{:S(2)}) collective-permute-start(bf16[8,144,128]{2,1,0:T(8,128)(2,1)S(1)} %pad_maximum_fusion), channel_id=1, source_target_pairs={{0,16},{8,24},{16,0},{24,8},{1,17},{9,25},{17,1},{25,9},{2,18},{10... | collective-permute-start | bytes 884744 | tf_op jit(solution)/shard_map/ppermute | solution.py:185
  26.4 6.7 %collective-permute-start.8 = (bf16[8,128,128]{2,1,0:T(8,128)(2,1)S(1)}, bf16[8,128,128]{2,1,0:T(8,128)(2,1)S(1)}, u32[]{:S(2)}, u32[]{:S(2)}) collective-permute-start(bf16[8,128,128]{2,1,0:T(8,128)(2,1)S(1)} %pad_maximum_fusion.1), channel_id=1, source_target_pairs={{0,1},{1,0},{2,3},{3,2},{4,5},{5,4},{6,7},{7,6},{8,9},{9,8},{10,11... | collective-permute-start | bytes 786440 | tf_op jit(solution)/shard_map/ppermute | solution.py:185
  30.8 2.9 %collective-permute-start.4 = (bf16[16,144,128]{2,1,0:T(8,128)(2,1)S(1)}, bf16[16,144,128]{2,1,0:T(8,128)(2,1)S(1)}, u32[]{:S(2)}, u32[]{:S(2)}) collective-permute-start(bf16[16,144,128]{2,1,0:T(8,128)(2,1)S(1)} %constant_dynamic-update-slice_fusion.near), channel_id=1, source_target_pairs={{0,8},{8,0},{16,24},{24,16},{1,9},{9,1},{17,25},{25,17},{2,10},{10... | collective-permute-start | bytes 1769480 | tf_op jit(solution)/shard_map/ppermute | solution.py:185
  33.1 15.9 %collective-permute-start.9 = (bf16[16,128,128]{2,1,0:T(8,128)(2,1)S(1)}, bf16[16,128,128]{2,1,0:T(8,128)(2,1)S(1)}, u32[]{:S(2)}, u32[]{:S(2)}) collective-permute-start(bf16[16,128,128]{2,1,0:T(8,128)(2,1)S(1)} %constant_dynamic-update-slice_fusion.5.cot_near), channel_id=1, source_target_pairs={{0,8},{8,0},{16,24},{24,16},{1,9},{9,1},{17,25},{25,17},{2,10},{10... | collective-permute-start | bytes 1572872 | tf_op jit(solution)/shard_map/ppermute | solution.py:185

commit v7 on v6

--- a/solution.py
+++ b/solution.py
@@ -9,6 +9,7 @@
 
 DMAX = 8
 VMEM_LIMIT = 48 * 1024 * 1024
+PACK_VMEM = 4 * 1024 * 1024
 FORWARD_VMEM = 36 * 1024 * 1024
 BACKWARD_VMEM = 28 * 1024 * 1024
 
@@ -414,6 +415,7 @@
     turned_left,
     turned_right,
     products,
+    normed,
     updated,
     field,
     wide,
@@ -470,21 +472,25 @@
     chunk = 8
     size = chunk * tokens
 
-    def update(step, half, side, gating, contact, start):
-        first = step * chunk
-        turned = []
+    halves = (
+        (core, near_gating, near_contact, near_start),
+        (1 - core, far_gating, far_contact, far_start),
+    )
+    parts = height // chunk
+
+    def normalise(step):
+        half, first = step // parts, step % parts * chunk
         for row in range(chunk):
             strip = products[pl.ds(half * height + first + row, hidden, stride=2 * height), :]
-            turned.append(layer_norm(strip, axis=0).astype(jnp.bfloat16).T)
-        product_norm = jnp.concatenate(
-            [
-                strip[chip * tokens : (chip + 1) * tokens]
-                for chip in range(chips)
-                for strip in turned
-            ],
-            axis=0,
-        )
-        change = matmul(product_norm, w_out[...]).reshape(chips, chunk, tokens, channels)
+            strip = layer_norm(strip, axis=0).astype(jnp.bfloat16).T
+            for chip in range(chips):
+                normed[step, chip, row] = strip[chip * tokens : (chip + 1) * tokens]
+
+    def update(step):
+        first = step % parts * chunk
+        side, gating, contact, start = halves[step // parts]
+        change = matmul(normed[step].reshape(chips * size, hidden), w_out[...])
+        change = change.reshape(chips, chunk, tokens, channels)
         rows = pl.ds(first, chunk)
         fresh = start[:, rows].astype(jnp.float32) + gating[:, rows].astype(jnp.float32) * change
         fresh = fresh.astype(jnp.bfloat16).astype(jnp.float32)
@@ -499,25 +505,36 @@
                 first_in[chip].reshape(size, channels).astype(jnp.bfloat16).T
             )
 
-    halves = (
-        (core, near_gating, near_contact, near_start),
-        (1 - core, far_gating, far_contact, far_start),
-    )
-    for half, parts in enumerate(halves):
-        lax.fori_loop(0, height // chunk, lambda i, c: (update(i, half, *parts), c)[1], 0)
-
-    def first_conv(step, carry):
-        first = step * chunk
-        shape = (chunk, tokens, channels)
-        pre = matmul(taps(wide, first, chunk, rate_one), one[...])
+    normalise(0)
+    for step in range(1, 2 * parts):
+        normalise(step)
+        update(step - 1)
+    update(2 * parts - 1)
+
+    def first_conv(step):
+        factor[pl.ds(step * chunk, chunk)] = matmul(
+            taps(wide, step * chunk, chunk, rate_one), one[...]
+        ).reshape(chunk, tokens, channels)
+
+    def activate(step):
+        rows = pl.ds(step * chunk, chunk)
+        pre = factor[rows]
         sigma = sigmoid(pre)
         second_in = pre * sigma
-        second[pl.ds(DMAX + first, chunk), inside, :] = second_in.reshape(shape)
-        flipped_two[:, lanes(step, size)] = second_in.astype(jnp.bfloat16).T
-        factor[pl.ds(first, chunk)] = (sigma * (1.0 + pre * (1.0 - sigma))).reshape(shape)
+        second[pl.ds(DMAX + step * chunk, chunk), inside, :] = second_in
+        flipped_two[:, lanes(step, size)] = (
+            second_in.reshape(size, channels).astype(jnp.bfloat16).T
+        )
+        factor[rows] = sigma * (1.0 + pre * (1.0 - sigma))
+
+    def convolve(step, carry):
+        activate(step - 1)
+        first_conv(step)
         return carry
 
-    lax.fori_loop(0, tokens // chunk, first_conv, 0)
+    first_conv(0)
+    lax.fori_loop(1, tokens // chunk, convolve, 0)
+    activate(tokens // chunk - 1)
 
     row_start, col_start = row_place * height, col_place * breadth
     cols = pl.ds(pl.multiple_of(col_start, breadth), breadth)
@@ -599,27 +616,37 @@
 
     sum_two[...] = jnp.zeros_like(sum_two)
 
-    def back_two(step, carry):
+    sum_one[...] = jnp.zeros_like(sum_one)
+
+    def back_two(step):
         first = step * chunk
         shifted = taps(wide_cot, first, chunk, -rate_two)
         before = matmul(shifted, two_t[...]).reshape(chunk, tokens, channels)
         before = (before * factor[pl.ds(first, chunk)]).astype(jnp.bfloat16).astype(jnp.float32)
         grad_pre[pl.ds(DMAX + first, chunk), inside, :] = before
         sum_two[...] += matmul(flipped_two[:, lanes(step, size)], shifted)
-        spread(grad_pre, pl.ds(first, chunk), DMAX, -rate_one, wide_pre)
-        return carry
-
-    lax.fori_loop(0, steps, back_two, 0)
-
-    sum_one[...] = jnp.zeros_like(sum_one)
-
-    def back_one(step, carry):
+
+    def spread_pre(step):
+        spread(grad_pre, pl.ds(step * chunk, chunk), DMAX, -rate_one, wide_pre)
+
+    def back_one(step):
         sum_one[...] += matmul(
             flipped[:, lanes(step, size)], taps(wide_pre, step * chunk, chunk, -rate_one)
         )
+
+    def gradients(step, carry):
+        back_one(step - 3)
+        spread_pre(step - 1)
+        back_two(step)
         return carry
 
-    lax.fori_loop(0, steps, back_one, 0)
+    back_two(0)
+    for step in (1, 2):
+        spread_pre(step - 1)
+        back_two(step)
+    lax.fori_loop(3, steps, gradients, 0)
+    spread_pre(steps - 1)
+    lax.fori_loop(steps - 3, steps, lambda i, c: (back_one(i), c)[1], 0)
     for tap in range(9):
         columns = slice(tap * channels, (tap + 1) * channels)
         grad_one[tap] = sum_one[:, columns] * (1.0 / tokens)
@@ -676,6 +703,7 @@
             ((1, pixels, channels), bf16),
             ((2,), jnp.int32),
         ),
+        compiler_params=pltpu.CompilerParams(vmem_limit_bytes=PACK_VMEM),
     )(
         dilations,
         pair.reshape(pixels, channels),
@@ -728,6 +756,7 @@
         scratch_shapes=[pltpu.VMEM(*side), both, both, alone, alone, alone]
         + [turned] * 2
         + [pltpu.VMEM((hidden * 2 * height, chips * tokens), f32)]
+        + [pltpu.VMEM((2 * height // 8, chips, 8, tokens, hidden), bf16)]
         + [whole, padded, tripled, bordered],
         compiler_params=pltpu.CompilerParams(vmem_limit_bytes=FORWARD_VMEM),
         cost_estimate=pl.CostEstimate(

time: 61 us -> 59.7 us (0.979)
  other arithmetic: 4.69 us -> 0.11 us
  starting transfers between devices: 14.1 us -> 16.6 us
  local copies, waits for them, and re-layouts: 1.73 us -> 3.73 us
  Pallas kernels: 30.3 us -> 28.5 us
  waiting for transfers between devices: 8.73 us -> 9.69 us
    ppermute x10, starting transfers between devices: 14.1 us -> 16.6 us  [exchange(): lax.ppermute(held, axis, [(i, i ^ distance) for i in range(lax.axis_size(...]
    concatenate x3, other arithmetic: 2.36 us -> 0.06 us  [replicated(): held = jnp.concatenate([held, exchange(held, hop)], axis=0)]
    concatenate x3, other arithmetic: 2.33 us -> 0.05 us  [replicated(): cot_held = jnp.concatenate([cot_held, cot_other], axis=0)]
    unnamed x20 -> x28, local copies, waits for them, and re-layouts: 1.65 us -> 3.65 us
    ppermute x10, waiting for transfers between devices: 8.73 us -> 9.69 us  [exchange(): lax.ppermute(held, axis, [(i, i ^ distance) for i in range(lax.axis_size(...]
    pallas_call x1, Pallas kernels: 11.3 us -> 10.3 us  [replicated(): pl.pallas_call(functools.partial(backward_kernel, plan), in_specs=[in_sme...]
  transfers between devices with their start and end apart: 10 -> 10, of which waited for: 4 -> 4; matrix products, arithmetic and copies ran while one was open for 11% -> 0% of each run, Pallas kernels for 29% -> 29%
where the time goes in v7:
time: 59.7 us; the launch traced here: 59.4 us
  Pallas kernels  28.5 us (48%)
  starting transfers between devices  16.6 us (28%)
  waiting for transfers between devices  9.69 us (16%)
  local copies, waits for them, and re-layouts  3.73 us (6%)
  between operations  0.8 us (1%)
    ppermute x10, starting transfers between devices, exchange(): lax.ppermute(held, axis, [(i, i ^ distance) for i in range(lax.axis_size(...  16.6 us
    pallas_call x1, Pallas kernels, replicated(): pl.pallas_call(functools.partial(forward_kernel, plan), in_specs=[in_smem...  14.8 us
    pallas_call x1, Pallas kernels, replicated(): pl.pallas_call(functools.partial(backward_kernel, plan), in_specs=[in_sme...  10.3 us
    ppermute x10, waiting for transfers between devices, exchange(): lax.ppermute(held, axis, [(i, i ^ distance) for i in range(lax.axis_size(...  9.69 us
    unnamed x28, local copies, waits for them, and re-layouts  3.65 us
    pallas_call x1, Pallas kernels, replicated(): pl.pallas_call(functools.partial(near_kernel, plan), in_specs=[in_vmem] *...  2.17 us
  transfers between devices with their start and end apart: 10, of which 4 were waited for; matrix products, arithmetic and copies ran while one was open for 0% of the time, Pallas kernels for 29%

profile of v7, /device:TPU:0, one launch (start us, length us, event | category | flops | bytes accessed | tf_op | source)
XLA Modules:
  0.0 59.4 jit_solution(8905615971211134183)
XLA Ops:
  0.6 0.0 copy-start.1
  0.6 0.7 %copy-done.1 = bf16[16,8,128]{2,1,0:T(8,128)(2,1)S(1)} copy-done((bf16[16,8,128]{2,1,0:T(8,128)(2,1)S(1)}, bf16[16,8,128]{2,1,0:T(8,128)(2,1)}, u32[]{:S(2)}) %copy-start.1) | copy-done | bytes 32792
  1.4 0.0 copy-start.2
  1.4 0.8 %copy-done.2 = bf16[16,8,128]{2,1,0:T(8,128)(2,1)S(1)} copy-done((bf16[16,8,128]{2,1,0:T(8,128)(2,1)S(1)}, bf16[16,8,128]{2,1,0:T(8,128)(2,1)}, u32[]{:S(2)}) %copy-start.2) | copy-done | bytes 32792
  2.2 0.0 copy-start.3
  2.2 0.7 %copy-done.3 = s32[16,8]{0,1:T(8,128)S(1)} copy-done((s32[16,8]{0,1:T(8,128)S(1)}, s32[16,8]{0,1:T(8,128)}, u32[]{:S(2)}) %copy-start.3) | copy-done | bytes 536
  2.8 0.0 copy-start.4
  2.8 0.7 %copy-done.4 = s32[16,8]{0,1:T(8,128)S(1)} copy-done((s32[16,8]{0,1:T(8,128)S(1)}, s32[16,8]{0,1:T(8,128)}, u32[]{:S(2)}) %copy-start.4) | copy-done | bytes 536
  3.5 0.0 copy-start.5
  3.5 0.7 %copy-done.5 = s32[2]{0:T(128)S(1)} copy-done((s32[2]{0:T(128)S(1)}, s32[2]{0:T(128)}, u32[]{:S(2)}) %copy-start.5) | copy-done | bytes 32
  4.2 0.0 copy-start.6
  4.2 0.0 copy-start.7
  4.2 0.0 copy-start.8
  4.2 1.1 %shard_map.129 = (bf16[1,144,128]{2,1,0:T(8,128)(2,1)S(1)}, bf16[1,128,128]{2,1,0:T(8,128)(2,1)S(1)}, s32[2]{0:T(128)S(1)}) custom-call(s32[2]{0:T(128)S(1)} %copy-done.5, bf16[128,128]{1,0:T(8,128)(2,1)S(1)} %bitcast.9, bf16[128,128]{1,0:T(8,128)(2,1)S(1)} %bitcast.10, s32[8,16]{1,0:T(8,128)S(1)} %bitcast.11, s32[8,16]{1,0:T(8,128)S(1)} %bitcast.12), custom_call_target="tpu_custom_call" | custom-call | tf_op jit(solution)/shard_map/pallas_call | solution.py:697
  5.3 4.1 %collective-permute-start = (bf16[1,144,128]{2,1,0:T(8,128)(2,1)S(1)}, bf16[1,144,128]{2,1,0:T(8,128)(2,1)S(1)}, u32[]{:S(2)}, u32[]{:S(2)}) collective-permute-start(bf16[1,144,128]{2,1,0:T(8,128)(2,1)S(1)} %get-tuple-element.26), channel_id=1, source_target_pairs={{0,4},{1,5},{2,6},{3,7},{4,0},{5,1},{6,2},{7,3},{8,12},{9,13},{10,... | collective-permute-start | bytes 110600 | tf_op jit(solution)/shard_map/ppermute | solution.py:186
  9.4 1.5 %collective-permute-start.5 = (bf16[1,128,128]{2,1,0:T(8,128)(2,1)S(1)}, bf16[1,128,128]{2,1,0:T(8,128)(2,1)S(1)}, u32[]{:S(2)}, u32[]{:S(2)}) collective-permute-start(bf16[1,128,128]{2,1,0:T(8,128)(2,1)S(1)} %get-tuple-element.34), channel_id=1, source_target_pairs={{0,16},{8,24},{16,0},{24,8},{1,17},{9,25},{17,1},{25,9},{2,18},{10... | collective-permute-start | bytes 98312 | tf_op jit(solution)/shard_map/ppermute | solution.py:186
  10.9 2.4 %collective-permute-done.5 = bf16[1,128,128]{2,1,0:T(8,128)(2,1)S(1)} collective-permute-done((bf16[1,128,128]{2,1,0:T(8,128)(2,1)S(1)}, bf16[1,128,128]{2,1,0:T(8,128)(2,1)S(1)}, u32[]{:S(2)}, u32[]{:S(2)}) %collective-permute-start.5) | collective-permute-done | bytes 32800 | tf_op jit(solution)/shard_map/ppermute | solution.py:186
  13.4 0.1 collective-permute-start.6
  13.5 0.0 collective-permute-done
  13.5 1.9 %collective-permute-start.1 = (bf16[2,144,128]{2,1,0:T(8,128)(2,1)S(1)}, bf16[2,144,128]{2,1,0:T(8,128)(2,1)S(1)}, u32[]{:S(2)}, u32[]{:S(2)}) collective-permute-start(bf16[2,144,128]{2,1,0:T(8,128)(2,1)S(1)} %pad_maximum_fusion.4), channel_id=1, source_target_pairs={{0,2},{1,3},{2,0},{3,1},{4,6},{5,7},{6,4},{7,5},{8,10},{9,11},{10,... | collective-permute-start | bytes 221192 | tf_op jit(solution)/shard_map/ppermute | solution.py:186
  15.4 2.5 %collective-permute-done.1 = bf16[2,144,128]{2,1,0:T(8,128)(2,1)S(1)} collective-permute-done((bf16[2,144,128]{2,1,0:T(8,128)(2,1)S(1)}, bf16[2,144,128]{2,1,0:T(8,128)(2,1)S(1)}, u32[]{:S(2)}, u32[]{:S(2)}) %collective-permute-start.1) | collective-permute-done | bytes 73760 | tf_op jit(solution)/shard_map/ppermute | solution.py:186
  18.0 2.6 %collective-permute-start.2 = (bf16[4,144,128]{2,1,0:T(8,128)(2,1)S(1)}, bf16[4,144,128]{2,1,0:T(8,128)(2,1)S(1)}, u32[]{:S(2)}, u32[]{:S(2)}) collective-permute-start(bf16[4,144,128]{2,1,0:T(8,128)(2,1)S(1)} %pad_maximum_fusion.2), channel_id=1, source_target_pairs={{0,1},{1,0},{2,3},{3,2},{4,5},{5,4},{6,7},{7,6},{8,9},{9,8},{10,11... | collective-permute-start | bytes 442376 | tf_op jit(solution)/shard_map/ppermute | solution.py:186
  20.5 0.0 collective-permute-done.6
  20.6 0.9 %collective-permute-start.7 = (bf16[4,128,128]{2,1,0:T(8,128)(2,1)S(1)}, bf16[4,128,128]{2,1,0:T(8,128)(2,1)S(1)}, u32[]{:S(2)}, u32[]{:S(2)}) collective-permute-start(bf16[4,128,128]{2,1,0:T(8,128)(2,1)S(1)} %pad_maximum_fusion.3), channel_id=1, source_target_pairs={{0,2},{1,3},{2,0},{3,1},{4,6},{5,7},{6,4},{7,5},{8,10},{9,11},{10,... | collective-permute-start | bytes 393224 | tf_op jit(solution)/shard_map/ppermute | solution.py:186
  21.5 2.3 %collective-permute-done.2 = bf16[4,144,128]{2,1,0:T(8,128)(2,1)S(1)} collective-permute-done((bf16[4,144,128]{2,1,0:T(8,128)(2,1)S(1)}, bf16[4,144,128]{2,1,0:T(8,128)(2,1)S(1)}, u32[]{:S(2)}, u32[]{:S(2)}) %collective-permute-start.2) | collective-permute-done | bytes 147488 | tf_op jit(solution)/shard_map/ppermute | solution.py:186
  23.8 0.0 copy-start
  23.8 0.0 copy-start.9
  23.8 2.7 %collective-permute-start.3 = (bf16[8,144,128]{2,1,0:T(8,128)(2,1)S(1)}, bf16[8,144,128]{2,1,0:T(8,128)(2,1)S(1)}, u32[]{:S(2)}, u32[]{:S(2)}) collective-permute-start(bf16[8,144,128]{2,1,0:T(8,128)(2,1)S(1)} %pad_maximum_fusion), channel_id=1, source_target_pairs={{0,16},{8,24},{16,0},{24,8},{1,17},{9,25},{17,1},{25,9},{2,18},{10... | collective-permute-start | bytes 884744 | tf_op jit(solution)/shard_map/ppermute | solution.py:186
  26.5 0.0 collective-permute-done.7
  26.6 2.2 %collective-permute-start.8 = (bf16[8,128,128]{2,1,0:T(8,128)(2,1)S(1)}, bf16[8,128,128]{2,1,0:T(8,128)(2,1)S(1)}, u32[]{:S(2)}, u32[]{:S(2)}) collective-permute-start(bf16[8,128,128]{2,1,0:T(8,128)(2,1)S(1)} %pad_maximum_fusion.1), channel_id=1, source_target_pairs={{0,1},{1,0},{2,3},{3,2},{4,5},{5,4},{6,7},{7,6},{8,9},{9,8},{10,11... | collective-permute-start | bytes 786440 | tf_op jit(solution)/shard_map/ppermute | solution.py:186
  28.8 2.5 %collective-permute-done.3 = bf16[8,144,128]{2,1,0:T(8,128)(2,1)S(1)} collective-permute-done((bf16[8,144,128]{2,1,0:T(8,128)(2,1)S(1)}, bf16[8,144,128]{2,1,0:T(8,128)(2,1)S(1)}, u32[]{:S(2)}, u32[]{:S(2)}) %collective-permute-start.3) | collective-permute-done | bytes 294944 | tf_op jit(solution)/shard_map/ppermute | solution.py:186
  31.3 0.1 collective-permute-start.4
  31.4 0.0 copy-done.6
  31.4 0.0 copy-done.7
  31.4 0.0 copy-done.8
  31.4 2.2 %shard_map.130 = (bf16[128,16,128]{2,1,0:T(8,128)(2,1)S(1)}, bf16[128,16,128]{2,1,0:T(8,128)(2,1)S(1)}, bf16[128,16,128]{2,1,0:T(8,128)(2,1)S(1)}, bf16[2,16,64,...) custom-call(bf16[16,144,128]{2,1,0:T(8,128)(2,1)S(1)} %constant_dyna, ...), custom_call_target="tpu_custom_call" | custom-call | flops 335544320 | bytes 4194304 | tf_op jit(solution)/shard_map/pallas_call | solution.py:720
  33.6 0.0 collective-permute-done.8
  33.7 0.6 collective-permute-start.9
  34.2 0.0 collective-permute-done.4.far
  34.2 0.0 copy-done
  34.2 0.0 copy-done.9
  34.2 14.8 %shard_map.131 = (bf16[128,128]{1,0:T(8,128)(2,1)}, bf16[128,4096]{1,0:T(8,128)(2,1)S(1)}, bf16[128,4096]{1,0:T(8,128)(2,1)S(1)}, f32[64,64,128]{2,1,0:T(8,128)S...) custom-call(s32[2]{0:T(128)S(1)} %get-tuple-element.25.dilations, ...), custom_call_target="tpu_custom_call" | custom-call | flops 2684354560 | bytes 20971520 | tf_op jit(solution)/shard_map/pallas_call | solution.py:744
  49.1 0.0 collective-permute-done.9.cot_far
  49.1 10.3 %shard_map.132 = (bf16[128,128]{1,0:T(8,128)(2,1)}, f32[9,128,128]{2,1,0:T(8,128)}, f32[9,128,128]{2,1,0:T(8,128)}) custom-call(s32[2]{0:T(128)S(1)} %get-tuple-element.25.dilations, bf16[16,128,128]{2,1,0:T(8,128)(2,1)S(1)} %constant_dynamic-update-slice_fusion.5.cot_near, bf16[16,128,128]{2,1,0:T(8,128)(2,1)S(1)} %collective-permute-done.9.cot_far, ...), custom_call_target="tpu_custom_call" | custom-call | tf_op jit(solution)/shard_map/pallas_call | solution.py:777
  (16 shorter events, 0.3 us)
Async XLA Ops:
  0.6 0.8 %copy-start.1 = (bf16[16,8,128]{2,1,0:T(8,128)(2,1)S(1)}, bf16[16,8,128]{2,1,0:T(8,128)(2,1)}, u32[]{:S(2)}) copy-start(bf16[16,8,128]{2,1,0:T(8,128)(2,1)} %param.10) | copy-start | bytes 98308
  1.4 0.8 %copy-start.2 = (bf16[16,8,128]{2,1,0:T(8,128)(2,1)S(1)}, bf16[16,8,128]{2,1,0:T(8,128)(2,1)}, u32[]{:S(2)}) copy-start(bf16[16,8,128]{2,1,0:T(8,128)(2,1)} %param.19) | copy-start | bytes 98308
  2.2 0.7 %copy-start.3 = (s32[16,8]{0,1:T(8,128)S(1)}, s32[16,8]{0,1:T(8,128)}, u32[]{:S(2)}) copy-start(s32[16,8]{0,1:T(8,128)} %param.11) | copy-start | bytes 1540
  2.8 0.7 %copy-start.4 = (s32[16,8]{0,1:T(8,128)S(1)}, s32[16,8]{0,1:T(8,128)}, u32[]{:S(2)}) copy-start(s32[16,8]{0,1:T(8,128)} %param.12) | copy-start | bytes 1540
  3.5 0.7 %copy-start.5 = (s32[2]{0:T(128)S(1)}, s32[2]{0:T(128)}, u32[]{:S(2)}) copy-start(s32[2]{0:T(128)} %dilations.1) | copy-start | bytes 28
  4.2 27.2 %copy-start.6 = (bf16[9,128,128]{2,1,0:T(8,128)(2,1)S(1)}, bf16[9,128,128]{2,1,0:T(8,128)(2,1)}, u32[]{:S(2)}) copy-start(bf16[9,128,128]{2,1,0:T(8,128)(2,1)} %two.3) | copy-start | bytes 884740
  4.2 27.2 %copy-start.7 = (bf16[128,512]{1,0:T(8,128)(2,1)S(1)}, bf16[128,512]{1,0:T(8,128)(2,1)}, u32[]{:S(2)}) copy-start(bf16[128,512]{1,0:T(8,128)(2,1)} %w_proj.3) | copy-start | bytes 393220
  4.2 27.2 %copy-start.8 = (bf16[128,128]{1,0:T(8,128)(2,1)S(1)}, bf16[128,128]{1,0:T(8,128)(2,1)}, u32[]{:S(2)}) copy-start(bf16[128,128]{1,0:T(8,128)(2,1)} %w_gate.3) | copy-start | bytes 98308
  5.3 8.2 %collective-permute-start = (bf16[1,144,128]{2,1,0:T(8,128)(2,1)S(1)}, bf16[1,144,128]{2,1,0:T(8,128)(2,1)S(1)}, u32[]{:S(2)}, u32[]{:S(2)}) collective-permute-start(bf16[1,144,128]{2,1,0:T(8,128)(2,1)S(1)} %get-tuple-element.26), channel_id=1, source_target_pairs={{0,4},{1,5},{2,6},{3,7},{4,0},{5,1},{6,2},{7,3},{8,12},{9,13},{10,... | collective-permute-start | bytes 110600 | tf_op jit(solution)/shard_map/ppermute | solution.py:186
  9.4 3.9 %collective-permute-start.5 = (bf16[1,128,128]{2,1,0:T(8,128)(2,1)S(1)}, bf16[1,128,128]{2,1,0:T(8,128)(2,1)S(1)}, u32[]{:S(2)}, u32[]{:S(2)}) collective-permute-start(bf16[1,128,128]{2,1,0:T(8,128)(2,1)S(1)} %get-tuple-element.34), channel_id=1, source_target_pairs={{0,16},{8,24},{16,0},{24,8},{1,17},{9,25},{17,1},{25,9},{2,18},{10... | collective-permute-start | bytes 98312 | tf_op jit(solution)/shard_map/ppermute | solution.py:186
  13.4 7.2 %collective-permute-start.6 = (bf16[2,128,128]{2,1,0:T(8,128)(2,1)S(1)}, bf16[2,128,128]{2,1,0:T(8,128)(2,1)S(1)}, u32[]{:S(2)}, u32[]{:S(2)}) collective-permute-start(bf16[2,128,128]{2,1,0:T(8,128)(2,1)S(1)} %pad_maximum_fusion.5), channel_id=1, source_target_pairs={{0,4},{1,5},{2,6},{3,7},{4,0},{5,1},{6,2},{7,3},{8,12},{9,13},{10,... | collective-permute-start | bytes 196616 | tf_op jit(solution)/shard_map/ppermute | solution.py:186
  13.5 4.4 %collective-permute-start.1 = (bf16[2,144,128]{2,1,0:T(8,128)(2,1)S(1)}, bf16[2,144,128]{2,1,0:T(8,128)(2,1)S(1)}, u32[]{:S(2)}, u32[]{:S(2)}) collective-permute-start(bf16[2,144,128]{2,1,0:T(8,128)(2,1)S(1)} %pad_maximum_fusion.4), channel_id=1, source_target_pairs={{0,2},{1,3},{2,0},{3,1},{4,6},{5,7},{6,4},{7,5},{8,10},{9,11},{10,... | collective-permute-start | bytes 221192 | tf_op jit(solution)/shard_map/ppermute | solution.py:186
  18.0 5.8 %collective-permute-start.2 = (bf16[4,144,128]{2,1,0:T(8,128)(2,1)S(1)}, bf16[4,144,128]{2,1,0:T(8,128)(2,1)S(1)}, u32[]{:S(2)}, u32[]{:S(2)}) collective-permute-start(bf16[4,144,128]{2,1,0:T(8,128)(2,1)S(1)} %pad_maximum_fusion.2), channel_id=1, source_target_pairs={{0,1},{1,0},{2,3},{3,2},{4,5},{5,4},{6,7},{7,6},{8,9},{9,8},{10,11... | collective-permute-start | bytes 442376 | tf_op jit(solution)/shard_map/ppermute | solution.py:186
  20.6 6.0 %collective-permute-start.7 = (bf16[4,128,128]{2,1,0:T(8,128)(2,1)S(1)}, bf16[4,128,128]{2,1,0:T(8,128)(2,1)S(1)}, u32[]{:S(2)}, u32[]{:S(2)}) collective-permute-start(bf16[4,128,128]{2,1,0:T(8,128)(2,1)S(1)} %pad_maximum_fusion.3), channel_id=1, source_target_pairs={{0,2},{1,3},{2,0},{3,1},{4,6},{5,7},{6,4},{7,5},{8,10},{9,11},{10,... | collective-permute-start | bytes 393224 | tf_op jit(solution)/shard_map/ppermute | solution.py:186
  23.8 10.4 %copy-start = (bf16[9,128,128]{2,1,0:T(8,128)(2,1)S(1)}, bf16[9,128,128]{2,1,0:T(8,128)(2,1)}, u32[]{:S(2)}) copy-start(bf16[9,128,128]{2,1,0:T(8,128)(2,1)} %param.17) | copy-start | bytes 884740
  23.8 10.4 %copy-start.9 = (bf16[128,128]{1,0:T(8,128)(2,1)S(1)}, bf16[128,128]{1,0:T(8,128)(2,1)}, u32[]{:S(2)}) copy-start(bf16[128,128]{1,0:T(8,128)(2,1)} %w_out.1) | copy-start | bytes 98308
  23.8 7.4 %collective-permute-start.3 = (bf16[8,144,128]{2,1,0:T(8,128)(2,1)S(1)}, bf16[8,144,128]{2,1,0:T(8,128)(2,1)S(1)}, u32[]{:S(2)}, u32[]{:S(2)}) collective-permute-start(bf16[8,144,128]{2,1,0:T(8,128)(2,1)S(1)} %pad_maximum_fusion), channel_id=1, source_target_pairs={{0,16},{8,24},{16,0},{24,8},{1,17},{9,25},{17,1},{25,9},{2,18},{10... | collective-permute-start | bytes 884744 | tf_op jit(solution)/shard_map/ppermute | solution.py:186
  26.6 7.0 %collective-permute-start.8 = (bf16[8,128,128]{2,1,0:T(8,128)(2,1)S(1)}, bf16[8,128,128]{2,1,0:T(8,128)(2,1)S(1)}, u32[]{:S(2)}, u32[]{:S(2)}) collective-permute-start(bf16[8,128,128]{2,1,0:T(8,128)(2,1)S(1)} %pad_maximum_fusion.1), channel_id=1, source_target_pairs={{0,1},{1,0},{2,3},{3,2},{4,5},{5,4},{6,7},{7,6},{8,9},{9,8},{10,11... | collective-permute-start | bytes 786440 | tf_op jit(solution)/shard_map/ppermute | solution.py:186
  31.3 2.9 %collective-permute-start.4 = (bf16[16,144,128]{2,1,0:T(8,128)(2,1)S(1)}, bf16[16,144,128]{2,1,0:T(8,128)(2,1)S(1)}, u32[]{:S(2)}, u32[]{:S(2)}) collective-permute-start(bf16[16,144,128]{2,1,0:T(8,128)(2,1)S(1)} %constant_dynamic-update-slice_fusion.near), channel_id=1, source_target_pairs={{0,8},{8,0},{16,24},{24,16},{1,9},{9,1},{17,25},{25,17},{2,10},{10... | collective-permute-start | bytes 1769480 | tf_op jit(solution)/shard_map/ppermute | solution.py:186
  33.7 15.4 %collective-permute-start.9 = (bf16[16,128,128]{2,1,0:T(8,128)(2,1)S(1)}, bf16[16,128,128]{2,1,0:T(8,128)(2,1)S(1)}, u32[]{:S(2)}, u32[]{:S(2)}) collective-permute-start(bf16[16,128,128]{2,1,0:T(8,128)(2,1)S(1)} %constant_dynamic-update-slice_fusion.5.cot_near), channel_id=1, source_target_pairs={{0,8},{8,0},{16,24},{24,16},{1,9},{9,1},{17,25},{25,17},{2,10},{10... | collective-permute-start | bytes 1572872 | tf_op jit(solution)/shard_map/ppermute | solution.py:186

commit v8 on v7

--- a/solution.py
+++ b/solution.py
@@ -9,8 +9,8 @@
 
 DMAX = 8
 VMEM_LIMIT = 48 * 1024 * 1024
-PACK_VMEM = 4 * 1024 * 1024
-FORWARD_VMEM = 36 * 1024 * 1024
+PITCH = 8
+FORWARD_VMEM = 44 * 1024 * 1024
 BACKWARD_VMEM = 28 * 1024 * 1024
 
 
@@ -217,25 +217,6 @@
     return lax.dot_general(
         left, right, (((1,), (1,)), ((), ())), preferred_element_type=jnp.float32
     )
-
-
-def pack_kernel(dilations, pair, cotangent, pair_mask, contact_mask, packed, cot, rates):
-    pixels, channels = pair.shape
-    breadth, height = pair_mask.shape
-    masks = jnp.concatenate(
-        [
-            pair_mask[...].astype(jnp.float32),
-            contact_mask[...].astype(jnp.float32),
-            jnp.zeros((breadth, channels - 2 * height), jnp.float32),
-        ],
-        axis=1,
-    )
-    tile = jnp.concatenate([masks, jnp.zeros_like(masks)], axis=0)
-    packed[0, 0:pixels] = pair[...]
-    packed[0, pixels:] = tile.astype(jnp.bfloat16)
-    cot[0] = cotangent[...]
-    for rate in range(2):
-        rates[rate] = jnp.clip(dilations[rate], 1, DMAX)
 
 
 def project_half(
@@ -285,17 +266,20 @@
             side = side.reshape(chips, rows, tokens, hidden)
             for row in range(rows):
                 strip = jnp.concatenate([side[chip, row] for chip in range(chips)], axis=0)
-                target[pl.ds(first + row, hidden, stride=height), :] = strip.T
+                target[pl.ds(first + row, hidden, stride=height + PITCH), :] = strip.T
         shape = (chips, rows, tokens, channels)
         span = slice(first, first + rows)
         gating[:, span] = gates.astype(jnp.bfloat16).reshape(shape)
         contact[:, span] = masks[:, channels:].astype(jnp.bfloat16).reshape(shape)
         start[:, span] = values.astype(jnp.bfloat16).reshape(shape)
-    shape = (hidden, height, chips * tokens)
-    left[...] = turned[0][...].reshape(shape).astype(jnp.bfloat16)
-    other = turned[1][...]
-    right[...] = other.reshape(shape).astype(jnp.bfloat16)
-    swapped[...] = pltpu.roll(other, tokens, 1).reshape(shape).astype(jnp.bfloat16)
+    shape = (hidden, height + PITCH, chips * tokens)
+    mine, other = turned[0][...], turned[1][...]
+    for target, source in (
+        (left, mine),
+        (right, other),
+        (swapped, pltpu.roll(other, tokens, 1)),
+    ):
+        target[...] = source.reshape(shape)[:, :height].astype(jnp.bfloat16)
 
 
 def near_kernel(
@@ -337,9 +321,8 @@
 def spread(source, rows, pad, rate, target):
     tokens, channels = target.shape[1], source.shape[2]
     for tap in range(3):
-        moved = source[
-            pl.ds(pad + rows.start, rows.size), pl.ds(DMAX + (tap - 1) * rate, tokens), :
-        ]
+        first = DMAX + (tap - 1) * rate if tap != 1 else DMAX
+        moved = source[pl.ds(pad + rows.start, rows.size), pl.ds(first, tokens), :]
         target[pl.ds(DMAX + rows.start, rows.size), :, tap * channels : (tap + 1) * channels] = (
             moved.astype(jnp.bfloat16)
         )
@@ -364,6 +347,38 @@
         for tap in range(9)
     ]
     return jnp.concatenate(views, axis=1).astype(jnp.bfloat16)
+
+
+def row_taps(strips, first, count, rate):
+    views = [
+        strips[tap, pl.ds(DMAX + first + ((tap - 1) * rate if tap != 1 else 0), count)]
+        for tap in range(3)
+    ]
+    return views[0] + views[1] + views[2]
+
+
+def clear_ends(strips, tokens):
+    for tap in (0, 2):
+        for rows in (slice(0, DMAX), slice(DMAX + tokens, 2 * DMAX + tokens)):
+            strips[tap, rows] = jnp.zeros((DMAX,) + strips.shape[2:], jnp.float32)
+
+
+def column_taps(source, weight, first, count, strips):
+    tokens = source.shape[1]
+    flat = source[pl.ds(DMAX + first, count)].reshape(count * tokens, -1)
+    square = jnp.concatenate(
+        [
+            jnp.concatenate([weight(3 * row + col) for row in range(3)], axis=1)
+            for col in range(3)
+        ],
+        axis=0,
+    )
+    result = matmul(flat, square)
+    channels = strips.shape[3]
+    for tap in range(3):
+        strips[tap, pl.ds(DMAX + first, count)] = result[
+            :, tap * channels : (tap + 1) * channels
+        ].reshape(count, tokens, channels)
 
 
 def lanes(step, size):
@@ -420,6 +435,7 @@
     field,
     wide,
     second,
+    strips,
 ):
     _, _, height, breadth, tokens = plan
     hidden, channels = w_out.shape
@@ -429,8 +445,9 @@
     core = row_place % 2
     rate_one, rate_two = dilations[0], dilations[1]
     inside = slice(DMAX, DMAX + tokens)
-    for target in (field, wide, second):
+    for target in (field, second):
         clear_border(target, tokens)
+    clear_ends(strips, tokens)
 
     right[core] = near_right[...]
     swapped[core] = near_swapped[...]
@@ -453,6 +470,7 @@
     low = jnp.where(lane < tokens, 1.0, 0.0).astype(jnp.bfloat16)
     high = jnp.where(lane < tokens, 0.0, 1.0).astype(jnp.bfloat16)
     batch = 32
+    pitch = 2 * height + PITCH
 
     def multiply(step, carry):
         for part in range(batch):
@@ -462,8 +480,8 @@
             strips = [strip * low for strip in ahead + back]
             strips += [strip * high for strip in back + ahead]
             mine = jnp.concatenate([near_left[h], far_left[h]], axis=0)
-            products[pl.ds(pl.multiple_of(h * 2 * height, 2 * height), 2 * height), :] = (
-                matmul_nt(mine, jnp.concatenate(strips, axis=0))
+            products[pl.ds(pl.multiple_of(h * pitch, 8), 2 * height), :] = matmul_nt(
+                mine, jnp.concatenate(strips, axis=0)
             )
         return carry
 
@@ -481,7 +499,7 @@
     def normalise(step):
         half, first = step // parts, step % parts * chunk
         for row in range(chunk):
-            strip = products[pl.ds(half * height + first + row, hidden, stride=2 * height), :]
+            strip = products[pl.ds(half * height + first + row, hidden, stride=pitch), :]
             strip = layer_norm(strip, axis=0).astype(jnp.bfloat16).T
             for chip in range(chips):
                 normed[step, chip, row] = strip[chip * tokens : (chip + 1) * tokens]
@@ -505,20 +523,24 @@
                 first_in[chip].reshape(size, channels).astype(jnp.bfloat16).T
             )
 
-    normalise(0)
-    for step in range(1, 2 * parts):
-        normalise(step)
-        update(step - 1)
-    update(2 * parts - 1)
-
     def first_conv(step):
-        factor[pl.ds(step * chunk, chunk)] = matmul(
-            taps(wide, step * chunk, chunk, rate_one), one[...]
-        ).reshape(chunk, tokens, channels)
-
-    def activate(step):
+        side = halves[step // parts][0]
+        for chip in range(chips):
+            base = (chip * 2 + side) * height + step % parts * chunk
+            column_taps(wide, lambda tap: one[tap], base, chunk, strips)
+
+    count = 2 * parts
+    for step in range(count + 2):
+        if step < count:
+            normalise(step)
+        if 1 <= step <= count:
+            update(step - 1)
+        if step >= 2:
+            first_conv(step - 2)
+
+    def activate(step, carry):
         rows = pl.ds(step * chunk, chunk)
-        pre = factor[rows]
+        pre = row_taps(strips, step * chunk, chunk, rate_one)
         sigma = sigmoid(pre)
         second_in = pre * sigma
         second[pl.ds(DMAX + step * chunk, chunk), inside, :] = second_in
@@ -526,15 +548,9 @@
             second_in.reshape(size, channels).astype(jnp.bfloat16).T
         )
         factor[rows] = sigma * (1.0 + pre * (1.0 - sigma))
-
-    def convolve(step, carry):
-        activate(step - 1)
-        first_conv(step)
         return carry
 
-    first_conv(0)
-    lax.fori_loop(1, tokens // chunk, convolve, 0)
-    activate(tokens // chunk - 1)
+    lax.fori_loop(0, tokens // chunk, activate, 0)
 
     row_start, col_start = row_place * height, col_place * breadth
     cols = pl.ds(pl.multiple_of(col_start, breadth), breadth)
@@ -571,11 +587,12 @@
     wide_cot,
     wide_pre,
     grad_pre,
+    strips,
     sum_one,
     sum_two,
 ):
     _, cot_rounds, height, breadth, tokens = plan
-    channels = one.shape[1]
+    channels = one.shape[2]
     pixels = height * breadth
     row_place, col_place = lax.axis_index("row"), lax.axis_index("col")
     rate_one, rate_two = dilations[0], dilations[1]
@@ -583,6 +600,7 @@
     inside = slice(DMAX, DMAX + tokens)
     for target in (field, wide_cot, wide_pre, grad_pre):
         clear_border(target, tokens)
+    clear_ends(strips, tokens)
 
     several = 4
 
@@ -608,51 +626,58 @@
     size = chunk * tokens
     steps = tokens // chunk
 
-    def spread_cot(step, carry):
+    def spread_cot(step):
         spread(field, pl.ds(step * chunk, chunk), 0, -rate_two, wide_cot)
+
+    def hidden_conv(step):
+        column_taps(
+            wide_cot,
+            lambda tap: two_t[tap * channels : (tap + 1) * channels],
+            step * chunk,
+            chunk,
+            strips,
+        )
+
+    def prepare(step, carry):
+        hidden_conv(step - 1)
+        spread_cot(step)
         return carry
 
-    lax.fori_loop(0, steps, spread_cot, 0)
+    spread_cot(0)
+    lax.fori_loop(1, steps, prepare, 0)
+    hidden_conv(steps - 1)
 
     sum_two[...] = jnp.zeros_like(sum_two)
 
+    def back_two(step, carry):
+        first = step * chunk
+        before = row_taps(strips, first, chunk, -rate_two) * factor[pl.ds(first, chunk)]
+        grad_pre[pl.ds(DMAX + first, chunk), inside, :] = before.astype(jnp.bfloat16).astype(
+            jnp.float32
+        )
+        spread(grad_pre, pl.ds(first, chunk), DMAX, -rate_one, wide_pre)
+        sum_two[...] += matmul(
+            flipped_two[:, lanes(step, size)], taps(wide_cot, first, chunk, -rate_two)
+        )
+        return carry
+
+    lax.fori_loop(0, steps, back_two, 0)
+
     sum_one[...] = jnp.zeros_like(sum_one)
 
-    def back_two(step):
-        first = step * chunk
-        shifted = taps(wide_cot, first, chunk, -rate_two)
-        before = matmul(shifted, two_t[...]).reshape(chunk, tokens, channels)
-        before = (before * factor[pl.ds(first, chunk)]).astype(jnp.bfloat16).astype(jnp.float32)
-        grad_pre[pl.ds(DMAX + first, chunk), inside, :] = before
-        sum_two[...] += matmul(flipped_two[:, lanes(step, size)], shifted)
-
-    def spread_pre(step):
-        spread(grad_pre, pl.ds(step * chunk, chunk), DMAX, -rate_one, wide_pre)
-
-    def back_one(step):
+    def back_one(step, carry):
         sum_one[...] += matmul(
             flipped[:, lanes(step, size)], taps(wide_pre, step * chunk, chunk, -rate_one)
         )
-
-    def gradients(step, carry):
-        back_one(step - 3)
-        spread_pre(step - 1)
-        back_two(step)
         return carry
 
-    back_two(0)
-    for step in (1, 2):
-        spread_pre(step - 1)
-        back_two(step)
-    lax.fori_loop(3, steps, gradients, 0)
-    spread_pre(steps - 1)
-    lax.fori_loop(steps - 3, steps, lambda i, c: (back_one(i), c)[1], 0)
+    lax.fori_loop(0, steps, back_one, 0)
     for tap in range(9):
         columns = slice(tap * channels, (tap + 1) * channels)
         grad_one[tap] = sum_one[:, columns] * (1.0 / tokens)
         grad_two[tap] = sum_two[:, columns] * (1.0 / tokens)
 
-    one_rows = [one[tap * channels : (tap + 1) * channels] for tap in range(9)]
+    one_rows = [one[tap] for tap in range(9)]
     grad_input = own_contact[...] * matmul_nt(
         windows(
             grad_pre, -rate_one, row_place * height, col_place * breadth, height, breadth
@@ -687,30 +712,21 @@
     side = ((hidden, height, chips * tokens), bf16)
     rows = (chips, height, tokens, channels)
     halves = [side] * 3 + [(rows, bf16)] * 3
-    turned = pltpu.VMEM((hidden * height, chips * tokens), f32)
+    turned = pltpu.VMEM((hidden * (height + PITCH), chips * tokens), f32)
     stat = ((pixels, channels), f32)
 
     def shapes(*entries):
         return [jax.ShapeDtypeStruct(shape, dtype) for shape, dtype in entries]
 
     in_smem = pl.BlockSpec(memory_space=pltpu.SMEM)
-    held, cot_held, rates = pl.pallas_call(
-        pack_kernel,
-        in_specs=[in_smem] + [in_vmem] * 4,
-        out_specs=[in_vmem, in_vmem, in_smem],
-        out_shape=shapes(
-            ((1, pixels + 2 * breadth, channels), bf16),
-            ((1, pixels, channels), bf16),
-            ((2,), jnp.int32),
-        ),
-        compiler_params=pltpu.CompilerParams(vmem_limit_bytes=PACK_VMEM),
-    )(
-        dilations,
-        pair.reshape(pixels, channels),
-        cotangent.reshape(pixels, channels),
-        pair_mask.T,
-        contact_mask.T,
-    )
+    spare = channels - 2 * height
+    marks = jnp.pad(pair_mask.T, ((0, breadth), (0, height + spare))) + jnp.pad(
+        contact_mask.T, ((0, breadth), (height, spare))
+    )
+    held = jnp.concatenate([pair.reshape(pixels, channels), marks.astype(bf16)], axis=0)[None]
+    cot_held = jnp.maximum(cotangent.reshape(1, pixels, channels), jnp.finfo(bf16).min)
+    rates = jnp.clip(dilations, 1, DMAX)
+    cot_held, rates = lax.optimization_barrier((cot_held, rates))
     for step, (hop, cot_hop) in enumerate(zip(rounds[:-1], cot_rounds[:-1])):
         held = jnp.concatenate([held, exchange(held, hop)], axis=0)
         cot_other = exchange(cot_held, cot_hop)
@@ -739,6 +755,7 @@
     tripled = pltpu.VMEM((line, tokens, 3 * channels), bf16)
     both = pltpu.VMEM((2,) + side[0], bf16)
     alone = pltpu.VMEM(rows, bf16)
+    banded = pltpu.VMEM((3, line, tokens, channels), f32)
     flat = ((channels, tokens * tokens), bf16)
     sums = pltpu.VMEM((channels, 9 * channels), f32)
     output, *held = pl.pallas_call(
@@ -755,9 +772,9 @@
         ),
         scratch_shapes=[pltpu.VMEM(*side), both, both, alone, alone, alone]
         + [turned] * 2
-        + [pltpu.VMEM((hidden * 2 * height, chips * tokens), f32)]
+        + [pltpu.VMEM((hidden * (2 * height + PITCH), chips * tokens), f32)]
         + [pltpu.VMEM((2 * height // 8, chips, 8, tokens, hidden), bf16)]
-        + [whole, padded, tripled, bordered],
+        + [whole, padded, tripled, bordered, banded],
         compiler_params=pltpu.CompilerParams(vmem_limit_bytes=FORWARD_VMEM),
         cost_estimate=pl.CostEstimate(
             flops=tokens * tokens * channels * 40 * hidden,
@@ -770,7 +787,7 @@
         w_proj,
         w_gate,
         w_out,
-        conv_one.reshape(9 * channels, channels),
+        conv_one,
         conv_two,
         *near_parts,
     )
@@ -783,13 +800,13 @@
             ((9, channels, channels), f32),
             ((9, channels, channels), f32),
         ),
-        scratch_shapes=[padded, tripled, tripled, bordered, sums, sums],
+        scratch_shapes=[padded, tripled, tripled, bordered, banded, sums, sums],
         compiler_params=pltpu.CompilerParams(vmem_limit_bytes=BACKWARD_VMEM),
     )(
         rates,
         cot_near,
         cot_far,
-        conv_one.reshape(9 * channels, channels),
+        conv_one,
         two_t,
         *held,
     )

time: 59.7 us -> 56.9 us (0.953)
  other arithmetic: 0.11 us -> 3.88 us
  local copies, waits for them, and re-layouts: 3.73 us -> 0.19 us
  Pallas kernels: 28.5 us -> 26 us
    unnamed x28 -> x17, local copies, waits for them, and re-layouts: 3.65 us -> 0.12 us
    pallas_call x1, Pallas kernels: 14.8 us -> 11.4 us  [replicated(): pl.pallas_call(functools.partial(forward_kernel, plan), in_specs=[in_smem...]
    pallas_call x1, Pallas kernels: 10.3 us -> 12.7 us  [replicated(): pl.pallas_call(functools.partial(backward_kernel, plan), in_specs=[in_sme...]
    pallas_call x1 -> x0, Pallas kernels: 1.14 us -> none  [replicated(): pl.pallas_call(pack_kernel, in_specs=[in_smem] + [in_vmem] * 4, out_specs...]
    convert_element_type x0 -> x1, other arithmetic: none -> 0.83 us  [replicated(): marks.astype(bf16)]
    max x0 -> x1, other arithmetic: none -> 0.76 us  [replicated(): jnp.maximum(cotangent.reshape(1, pixels, channels), jnp.finfo(bf16).min)]
    broadcast_in_dim x0 -> x1, other arithmetic: none -> 0.76 us  [replicated(): jnp.concatenate([pair.reshape(pixels, channels), marks.astype(bf16)], axi...]
    unnamed x0 -> x1, other arithmetic: none -> 0.76 us
  transfers between devices with their start and end apart: 10 -> 10, of which waited for: 4 -> 4; matrix products, arithmetic and copies ran while one was open for 0% -> 4% of each run, Pallas kernels for 29% -> 23%
where the time goes in v8:
time: 56.9 us; the launch traced here: 56.6 us
  Pallas kernels  26 us (46%)
  starting transfers between devices  16.3 us (29%)
  waiting for transfers between devices  9.47 us (17%)
  other arithmetic  3.88 us (7%)
  between operations  0.82 us (1%)
    ppermute x10, starting transfers between devices, exchange(): lax.ppermute(held, axis, [(i, i ^ distance) for i in range(lax.axis_size(...  16.3 us
    pallas_call x1, Pallas kernels, replicated(): pl.pallas_call(functools.partial(backward_kernel, plan), in_specs=[in_sme...  12.7 us
    pallas_call x1, Pallas kernels, replicated(): pl.pallas_call(functools.partial(forward_kernel, plan), in_specs=[in_smem...  11.4 us
    ppermute x10, waiting for transfers between devices, exchange(): lax.ppermute(held, axis, [(i, i ^ distance) for i in range(lax.axis_size(...  9.47 us
    pallas_call x1, Pallas kernels, replicated(): pl.pallas_call(functools.partial(near_kernel, plan), in_specs=[in_vmem] *...  1.89 us
  transfers between devices with their start and end apart: 10, of which 4 were waited for; matrix products, arithmetic and copies ran while one was open for 4% of the time, Pallas kernels for 23%

profile of v8, /device:TPU:0, one launch (start us, length us, event | category | flops | bytes accessed | tf_op | source)
XLA Modules:
  0.0 56.6 jit_solution(9096004334285480678)
XLA Ops:
  0.6 0.0 copy-start.2
  0.6 0.0 copy-start.3
  0.7 0.0 copy-start.1
  0.7 0.8 %add_convert_fusion = bf16[16,128]{1,0:T(8,128)(2,1)S(1)} fusion(s32[8,16]{1,0:T(8,128)} %bitcast.13, s32[8,16]{1,0:T(8,128)} %bitcast.14), kind=kLoop, calls=%fused_computation.18 | loop fusion | flops 4096 | bytes 5120 | tf_op jit(solution)/shard_map/convert_element_type | solution.py:726
  1.5 0.8 %maximum_bitcast_fusion = bf16[1,144,128]{2,1,0:T(8,128)(2,1)S(1)} fusion(bf16[16,128]{1,0:T(8,128)(2,1)S(1)} %add_convert_fusion, bf16[128,128]{1,0:T(8,128)(2,1)} %bitcast.11), kind=kLoop, calls=%fused_computation.6 | loop fusion | flops 73728 | bytes 73728 | tf_op jit(solution)/shard_map/broadcast_in_dim | solution.py:726
  2.3 4.0 %collective-permute-start = (bf16[1,144,128]{2,1,0:T(8,128)(2,1)S(1)}, bf16[1,144,128]{2,1,0:T(8,128)(2,1)S(1)}, u32[]{:S(2)}, u32[]{:S(2)}) collective-permute-start(bf16[1,144,128]{2,1,0:T(8,128)(2,1)S(1)} %maximum_bitcast_fusion), channel_id=1, source_target_pairs={{0,4},{1,5},{2,6},{3,7},{4,0},{5,1},{6,2},{7,3},{8,12},{9,13},{10,... | collective-permute-start | bytes 110600 | tf_op jit(solution)/shard_map/ppermute | solution.py:186
  6.3 0.8 %maximum_bitcast_fusion.1 = bf16[1,128,128]{2,1,0:T(8,128)(2,1)S(1)} fusion(bf16[16,8,128]{2,1,0:T(8,128)(2,1)} %param.19), kind=kLoop, calls=%fused_computation.7 | loop fusion | flops 16384 | bytes 65536 | tf_op jit(solution)/shard_map/max | solution.py:727
  7.1 0.7 %broadcast_clamp_fusion.dilations = s32[2]{0:T(128)S(1)} fusion(s32[2]{0:T(128)} %param.13), kind=kLoop, calls=%fused_computation.19 | loop fusion | flops 2 | bytes 16 | tf_op jit(solution)/shard_map/jit(clip)/min | solution.py:728
  7.7 1.5 %collective-permute-start.5 = (bf16[1,128,128]{2,1,0:T(8,128)(2,1)S(1)}, bf16[1,128,128]{2,1,0:T(8,128)(2,1)S(1)}, u32[]{:S(2)}, u32[]{:S(2)}) collective-permute-start(bf16[1,128,128]{2,1,0:T(8,128)(2,1)S(1)} %maximum_bitcast_fusion.1), channel_id=1, source_target_pairs={{0,16},{8,24},{16,0},{24,8},{1,17},{9,25},{17,1},{25,9},{2,18},{10... | collective-permute-start | bytes 98312 | tf_op jit(solution)/shard_map/ppermute | solution.py:186
  9.2 0.8 %constant_dynamic-update-slice_fusion.4 = bf16[16,144,128]{2,1,0:T(8,128)(2,1)S(1)} fusion(bf16[16,128]{1,0:T(8,128)(2,1)S(1)} %add_convert_fusion, bf16[128,128]{1,0:T(8,128)(2,1)} %bitcast.12), kind=kLoop, calls=%fused_computation.12 | loop fusion | flops 73727 | bytes 73728
  10.0 1.7 %collective-permute-done.5 = bf16[1,128,128]{2,1,0:T(8,128)(2,1)S(1)} collective-permute-done((bf16[1,128,128]{2,1,0:T(8,128)(2,1)S(1)}, bf16[1,128,128]{2,1,0:T(8,128)(2,1)S(1)}, u32[]{:S(2)}, u32[]{:S(2)}) %collective-permute-start.5) | collective-permute-done | bytes 32800 | tf_op jit(solution)/shard_map/ppermute | solution.py:186
  11.6 0.1 collective-permute-start.6
  11.7 0.0 collective-permute-done
  11.7 2.0 %collective-permute-start.1 = (bf16[2,144,128]{2,1,0:T(8,128)(2,1)S(1)}, bf16[2,144,128]{2,1,0:T(8,128)(2,1)S(1)}, u32[]{:S(2)}, u32[]{:S(2)}) collective-permute-start(bf16[2,144,128]{2,1,0:T(8,128)(2,1)S(1)} %pad_maximum_fusion.4), channel_id=1, source_target_pairs={{0,2},{1,3},{2,0},{3,1},{4,6},{5,7},{6,4},{7,5},{8,10},{9,11},{10,... | collective-permute-start | bytes 221192 | tf_op jit(solution)/shard_map/ppermute | solution.py:186
  13.7 2.5 %collective-permute-done.1 = bf16[2,144,128]{2,1,0:T(8,128)(2,1)S(1)} collective-permute-done((bf16[2,144,128]{2,1,0:T(8,128)(2,1)S(1)}, bf16[2,144,128]{2,1,0:T(8,128)(2,1)S(1)}, u32[]{:S(2)}, u32[]{:S(2)}) %collective-permute-start.1) | collective-permute-done | bytes 73760 | tf_op jit(solution)/shard_map/ppermute | solution.py:186
  16.2 2.8 %collective-permute-start.2 = (bf16[4,144,128]{2,1,0:T(8,128)(2,1)S(1)}, bf16[4,144,128]{2,1,0:T(8,128)(2,1)S(1)}, u32[]{:S(2)}, u32[]{:S(2)}) collective-permute-start(bf16[4,144,128]{2,1,0:T(8,128)(2,1)S(1)} %pad_maximum_fusion.2), channel_id=1, source_target_pairs={{0,1},{1,0},{2,3},{3,2},{4,5},{5,4},{6,7},{7,6},{8,9},{9,8},{10,11... | collective-permute-start | bytes 442376 | tf_op jit(solution)/shard_map/ppermute | solution.py:186
  19.0 0.0 collective-permute-done.6
  19.0 0.7 %collective-permute-start.7 = (bf16[4,128,128]{2,1,0:T(8,128)(2,1)S(1)}, bf16[4,128,128]{2,1,0:T(8,128)(2,1)S(1)}, u32[]{:S(2)}, u32[]{:S(2)}) collective-permute-start(bf16[4,128,128]{2,1,0:T(8,128)(2,1)S(1)} %pad_maximum_fusion.3), channel_id=1, source_target_pairs={{0,2},{1,3},{2,0},{3,1},{4,6},{5,7},{6,4},{7,5},{8,10},{9,11},{10,... | collective-permute-start | bytes 393224 | tf_op jit(solution)/shard_map/ppermute | solution.py:186
  19.8 2.9 %collective-permute-done.2 = bf16[4,144,128]{2,1,0:T(8,128)(2,1)S(1)} collective-permute-done((bf16[4,144,128]{2,1,0:T(8,128)(2,1)S(1)}, bf16[4,144,128]{2,1,0:T(8,128)(2,1)S(1)}, u32[]{:S(2)}, u32[]{:S(2)}) %collective-permute-start.2) | collective-permute-done | bytes 147488 | tf_op jit(solution)/shard_map/ppermute | solution.py:186
  22.7 0.0 copy-start
  22.7 0.0 copy-start.4
  22.8 2.3 %collective-permute-start.3 = (bf16[8,144,128]{2,1,0:T(8,128)(2,1)S(1)}, bf16[8,144,128]{2,1,0:T(8,128)(2,1)S(1)}, u32[]{:S(2)}, u32[]{:S(2)}) collective-permute-start(bf16[8,144,128]{2,1,0:T(8,128)(2,1)S(1)} %pad_maximum_fusion), channel_id=1, source_target_pairs={{0,16},{8,24},{16,0},{24,8},{1,17},{9,25},{17,1},{25,9},{2,18},{10... | collective-permute-start | bytes 884744 | tf_op jit(solution)/shard_map/ppermute | solution.py:186
  25.1 0.0 collective-permute-done.7
  25.1 2.2 %collective-permute-start.8 = (bf16[8,128,128]{2,1,0:T(8,128)(2,1)S(1)}, bf16[8,128,128]{2,1,0:T(8,128)(2,1)S(1)}, u32[]{:S(2)}, u32[]{:S(2)}) collective-permute-start(bf16[8,128,128]{2,1,0:T(8,128)(2,1)S(1)} %pad_maximum_fusion.1), channel_id=1, source_target_pairs={{0,1},{1,0},{2,3},{3,2},{4,5},{5,4},{6,7},{7,6},{8,9},{9,8},{10,11... | collective-permute-start | bytes 786440 | tf_op jit(solution)/shard_map/ppermute | solution.py:186
  27.4 2.4 %collective-permute-done.3 = bf16[8,144,128]{2,1,0:T(8,128)(2,1)S(1)} collective-permute-done((bf16[8,144,128]{2,1,0:T(8,128)(2,1)S(1)}, bf16[8,144,128]{2,1,0:T(8,128)(2,1)S(1)}, u32[]{:S(2)}, u32[]{:S(2)}) %collective-permute-start.3) | collective-permute-done | bytes 294944 | tf_op jit(solution)/shard_map/ppermute | solution.py:186
  29.8 0.1 collective-permute-start.4
  30.0 0.0 copy-done.2
  30.0 0.0 copy-done.3
  30.0 0.0 copy-done.1
  30.0 1.9 %shard_map.129 = (bf16[128,16,128]{2,1,0:T(8,128)(2,1)S(1)}, bf16[128,16,128]{2,1,0:T(8,128)(2,1)S(1)}, bf16[128,16,128]{2,1,0:T(8,128)(2,1)S(1)}, bf16[2,16,64,...) custom-call(bf16[16,144,128]{2,1,0:T(8,128)(2,1)S(1)} %constant_dyna, ...), custom_call_target="tpu_custom_call" | custom-call | flops 335544320 | bytes 4194304 | tf_op jit(solution)/shard_map/pallas_call | solution.py:736
  31.9 0.0 collective-permute-done.8
  31.9 0.6 collective-permute-start.9
  32.5 0.0 collective-permute-done.4.far
  32.5 0.0 copy-done
  32.5 0.0 copy-done.4
  32.5 11.4 %shard_map.130 = (bf16[128,128]{1,0:T(8,128)(2,1)}, bf16[128,4096]{1,0:T(8,128)(2,1)S(1)}, bf16[128,4096]{1,0:T(8,128)(2,1)S(1)}, f32[64,64,128]{2,1,0:T(8,128)S...) custom-call(s32[2]{0:T(128)S(1)} %broadcast_clamp_fusion.dilations, ...), custom_call_target="tpu_custom_call" | custom-call | flops 2684354560 | bytes 20971520 | tf_op jit(solution)/shard_map/pallas_call | solution.py:761
  43.9 0.0 collective-permute-done.9.cot_far
  43.9 12.7 %shard_map.131 = (bf16[128,128]{1,0:T(8,128)(2,1)}, f32[9,128,128]{2,1,0:T(8,128)}, f32[9,128,128]{2,1,0:T(8,128)}) custom-call(s32[2]{0:T(128)S(1)} %broadcast_clamp_fusion.dilations, bf16[16,128,128]{2,1,0:T(8,128)(2,1)S(1)} %constant_dynamic-update-slice_fusion.5.cot_near, bf16[16,128,128]{2,1,0:T(8,128)(2,1)S(1)} %collective-permute-done.9.cot_far, ...), custom_call_target="tpu_custom_call" | custom-call | tf_op jit(solution)/shard_map/pallas_call | solution.py:794
  (15 shorter events, 0.3 us)
Async XLA Ops:
  0.6 29.3 %copy-start.2 = (bf16[128,512]{1,0:T(8,128)(2,1)S(1)}, bf16[128,512]{1,0:T(8,128)(2,1)}, u32[]{:S(2)}) copy-start(bf16[128,512]{1,0:T(8,128)(2,1)} %w_proj.3) | copy-start | bytes 393220
  0.6 29.3 %copy-start.3 = (bf16[128,128]{1,0:T(8,128)(2,1)S(1)}, bf16[128,128]{1,0:T(8,128)(2,1)}, u32[]{:S(2)}) copy-start(bf16[128,128]{1,0:T(8,128)(2,1)} %w_gate.3) | copy-start | bytes 98308
  0.7 29.3 %copy-start.1 = (bf16[9,128,128]{2,1,0:T(8,128)(2,1)S(1)}, bf16[9,128,128]{2,1,0:T(8,128)(2,1)}, u32[]{:S(2)}) copy-start(bf16[9,128,128]{2,1,0:T(8,128)(2,1)} %two.3) | copy-start | bytes 884740
  2.3 9.5 %collective-permute-start = (bf16[1,144,128]{2,1,0:T(8,128)(2,1)S(1)}, bf16[1,144,128]{2,1,0:T(8,128)(2,1)S(1)}, u32[]{:S(2)}, u32[]{:S(2)}) collective-permute-start(bf16[1,144,128]{2,1,0:T(8,128)(2,1)S(1)} %maximum_bitcast_fusion), channel_id=1, source_target_pairs={{0,4},{1,5},{2,6},{3,7},{4,0},{5,1},{6,2},{7,3},{8,12},{9,13},{10,... | collective-permute-start | bytes 110600 | tf_op jit(solution)/shard_map/ppermute | solution.py:186
  7.7 3.9 %collective-permute-start.5 = (bf16[1,128,128]{2,1,0:T(8,128)(2,1)S(1)}, bf16[1,128,128]{2,1,0:T(8,128)(2,1)S(1)}, u32[]{:S(2)}, u32[]{:S(2)}) collective-permute-start(bf16[1,128,128]{2,1,0:T(8,128)(2,1)S(1)} %maximum_bitcast_fusion.1), channel_id=1, source_target_pairs={{0,16},{8,24},{16,0},{24,8},{1,17},{9,25},{17,1},{25,9},{2,18},{10... | collective-permute-start | bytes 98312 | tf_op jit(solution)/shard_map/ppermute | solution.py:186
  11.6 7.3 %collective-permute-start.6 = (bf16[2,128,128]{2,1,0:T(8,128)(2,1)S(1)}, bf16[2,128,128]{2,1,0:T(8,128)(2,1)S(1)}, u32[]{:S(2)}, u32[]{:S(2)}) collective-permute-start(bf16[2,128,128]{2,1,0:T(8,128)(2,1)S(1)} %pad_maximum_fusion.5), channel_id=1, source_target_pairs={{0,4},{1,5},{2,6},{3,7},{4,0},{5,1},{6,2},{7,3},{8,12},{9,13},{10,... | collective-permute-start | bytes 196616 | tf_op jit(solution)/shard_map/ppermute | solution.py:186
  11.7 4.4 %collective-permute-start.1 = (bf16[2,144,128]{2,1,0:T(8,128)(2,1)S(1)}, bf16[2,144,128]{2,1,0:T(8,128)(2,1)S(1)}, u32[]{:S(2)}, u32[]{:S(2)}) collective-permute-start(bf16[2,144,128]{2,1,0:T(8,128)(2,1)S(1)} %pad_maximum_fusion.4), channel_id=1, source_target_pairs={{0,2},{1,3},{2,0},{3,1},{4,6},{5,7},{6,4},{7,5},{8,10},{9,11},{10,... | collective-permute-start | bytes 221192 | tf_op jit(solution)/shard_map/ppermute | solution.py:186
  16.2 6.5 %collective-permute-start.2 = (bf16[4,144,128]{2,1,0:T(8,128)(2,1)S(1)}, bf16[4,144,128]{2,1,0:T(8,128)(2,1)S(1)}, u32[]{:S(2)}, u32[]{:S(2)}) collective-permute-start(bf16[4,144,128]{2,1,0:T(8,128)(2,1)S(1)} %pad_maximum_fusion.2), channel_id=1, source_target_pairs={{0,1},{1,0},{2,3},{3,2},{4,5},{5,4},{6,7},{7,6},{8,9},{9,8},{10,11... | collective-permute-start | bytes 442376 | tf_op jit(solution)/shard_map/ppermute | solution.py:186
  19.0 6.1 %collective-permute-start.7 = (bf16[4,128,128]{2,1,0:T(8,128)(2,1)S(1)}, bf16[4,128,128]{2,1,0:T(8,128)(2,1)S(1)}, u32[]{:S(2)}, u32[]{:S(2)}) collective-permute-start(bf16[4,128,128]{2,1,0:T(8,128)(2,1)S(1)} %pad_maximum_fusion.3), channel_id=1, source_target_pairs={{0,2},{1,3},{2,0},{3,1},{4,6},{5,7},{6,4},{7,5},{8,10},{9,11},{10,... | collective-permute-start | bytes 393224 | tf_op jit(solution)/shard_map/ppermute | solution.py:186
  22.7 9.8 %copy-start = (bf16[9,128,128]{2,1,0:T(8,128)(2,1)S(1)}, bf16[9,128,128]{2,1,0:T(8,128)(2,1)}, u32[]{:S(2)}) copy-start(bf16[9,128,128]{2,1,0:T(8,128)(2,1)} %one.3) | copy-start | bytes 884740
  22.7 9.8 %copy-start.4 = (bf16[128,128]{1,0:T(8,128)(2,1)S(1)}, bf16[128,128]{1,0:T(8,128)(2,1)}, u32[]{:S(2)}) copy-start(bf16[128,128]{1,0:T(8,128)(2,1)} %w_out.1) | copy-start | bytes 98308
  22.8 7.0 %collective-permute-start.3 = (bf16[8,144,128]{2,1,0:T(8,128)(2,1)S(1)}, bf16[8,144,128]{2,1,0:T(8,128)(2,1)S(1)}, u32[]{:S(2)}, u32[]{:S(2)}) collective-permute-start(bf16[8,144,128]{2,1,0:T(8,128)(2,1)S(1)} %pad_maximum_fusion), channel_id=1, source_target_pairs={{0,16},{8,24},{16,0},{24,8},{1,17},{9,25},{17,1},{25,9},{2,18},{10... | collective-permute-start | bytes 884744 | tf_op jit(solution)/shard_map/ppermute | solution.py:186
  25.1 6.7 %collective-permute-start.8 = (bf16[8,128,128]{2,1,0:T(8,128)(2,1)S(1)}, bf16[8,128,128]{2,1,0:T(8,128)(2,1)S(1)}, u32[]{:S(2)}, u32[]{:S(2)}) collective-permute-start(bf16[8,128,128]{2,1,0:T(8,128)(2,1)S(1)} %pad_maximum_fusion.1), channel_id=1, source_target_pairs={{0,1},{1,0},{2,3},{3,2},{4,5},{5,4},{6,7},{7,6},{8,9},{9,8},{10,11... | collective-permute-start | bytes 786440 | tf_op jit(solution)/shard_map/ppermute | solution.py:186
  29.8 2.7 %collective-permute-start.4 = (bf16[16,144,128]{2,1,0:T(8,128)(2,1)S(1)}, bf16[16,144,128]{2,1,0:T(8,128)(2,1)S(1)}, u32[]{:S(2)}, u32[]{:S(2)}) collective-permute-start(bf16[16,144,128]{2,1,0:T(8,128)(2,1)S(1)} %constant_dynamic-update-slice_fusion.near), channel_id=1, source_target_pairs={{0,8},{8,0},{16,24},{24,16},{1,9},{9,1},{17,25},{25,17},{2,10},{10... | collective-permute-start | bytes 1769480 | tf_op jit(solution)/shard_map/ppermute | solution.py:186
  31.9 11.9 %collective-permute-start.9 = (bf16[16,128,128]{2,1,0:T(8,128)(2,1)S(1)}, bf16[16,128,128]{2,1,0:T(8,128)(2,1)S(1)}, u32[]{:S(2)}, u32[]{:S(2)}) collective-permute-start(bf16[16,128,128]{2,1,0:T(8,128)(2,1)S(1)} %constant_dynamic-update-slice_fusion.5.cot_near), channel_id=1, source_target_pairs={{0,8},{8,0},{16,24},{24,16},{1,9},{9,1},{17,25},{25,17},{2,10},{10... | collective-permute-start | bytes 1572872 | tf_op jit(solution)/shard_map/ppermute | solution.py:186

commit v9 on v8

--- a/solution.py
+++ b/solution.py
@@ -178,7 +178,7 @@
 
 def exchange_plan(row_count, col_count):
     rows, cols = halvings("row", row_count), halvings("col", col_count)
-    return cols + rows, rows[:-1] + cols + rows[-1:]
+    return cols + rows, cols[:-1] + rows[:-1] + cols[-1:] + rows[-1:]
 
 
 def exchange(held, hop):
@@ -587,7 +587,6 @@
     wide_cot,
     wide_pre,
     grad_pre,
-    strips,
     sum_one,
     sum_two,
 ):
@@ -600,7 +599,6 @@
     inside = slice(DMAX, DMAX + tokens)
     for target in (field, wide_cot, wide_pre, grad_pre):
         clear_border(target, tokens)
-    clear_ends(strips, tokens)
 
     several = 4
 
@@ -626,52 +624,45 @@
     size = chunk * tokens
     steps = tokens // chunk
 
-    def spread_cot(step):
+    def spread_cot(step, carry):
         spread(field, pl.ds(step * chunk, chunk), 0, -rate_two, wide_cot)
-
-    def hidden_conv(step):
-        column_taps(
-            wide_cot,
-            lambda tap: two_t[tap * channels : (tap + 1) * channels],
-            step * chunk,
-            chunk,
-            strips,
-        )
-
-    def prepare(step, carry):
-        hidden_conv(step - 1)
-        spread_cot(step)
         return carry
 
-    spread_cot(0)
-    lax.fori_loop(1, steps, prepare, 0)
-    hidden_conv(steps - 1)
+    lax.fori_loop(0, steps, spread_cot, 0)
 
     sum_two[...] = jnp.zeros_like(sum_two)
 
-    def back_two(step, carry):
+    sum_one[...] = jnp.zeros_like(sum_one)
+
+    def back_two(step):
         first = step * chunk
-        before = row_taps(strips, first, chunk, -rate_two) * factor[pl.ds(first, chunk)]
-        grad_pre[pl.ds(DMAX + first, chunk), inside, :] = before.astype(jnp.bfloat16).astype(
-            jnp.float32
-        )
-        spread(grad_pre, pl.ds(first, chunk), DMAX, -rate_one, wide_pre)
-        sum_two[...] += matmul(
-            flipped_two[:, lanes(step, size)], taps(wide_cot, first, chunk, -rate_two)
-        )
-        return carry
-
-    lax.fori_loop(0, steps, back_two, 0)
-
-    sum_one[...] = jnp.zeros_like(sum_one)
-
-    def back_one(step, carry):
+        shifted = taps(wide_cot, first, chunk, -rate_two)
+        before = matmul(shifted, two_t[...]).reshape(chunk, tokens, channels)
+        before = (before * factor[pl.ds(first, chunk)]).astype(jnp.bfloat16).astype(jnp.float32)
+        grad_pre[pl.ds(DMAX + first, chunk), inside, :] = before
+        sum_two[...] += matmul(flipped_two[:, lanes(step, size)], shifted)
+
+    def spread_pre(step):
+        spread(grad_pre, pl.ds(step * chunk, chunk), DMAX, -rate_one, wide_pre)
+
+    def back_one(step):
         sum_one[...] += matmul(
             flipped[:, lanes(step, size)], taps(wide_pre, step * chunk, chunk, -rate_one)
         )
+
+    def gradients(step, carry):
+        back_one(step - 3)
+        spread_pre(step - 1)
+        back_two(step)
         return carry
 
-    lax.fori_loop(0, steps, back_one, 0)
+    back_two(0)
+    for step in (1, 2):
+        spread_pre(step - 1)
+        back_two(step)
+    lax.fori_loop(3, steps, gradients, 0)
+    spread_pre(steps - 1)
+    lax.fori_loop(steps - 3, steps, lambda i, c: (back_one(i), c)[1], 0)
     for tap in range(9):
         columns = slice(tap * channels, (tap + 1) * channels)
         grad_one[tap] = sum_one[:, columns] * (1.0 / tokens)
@@ -720,18 +711,34 @@
 
     in_smem = pl.BlockSpec(memory_space=pltpu.SMEM)
     spare = channels - 2 * height
-    marks = jnp.pad(pair_mask.T, ((0, breadth), (0, height + spare))) + jnp.pad(
-        contact_mask.T, ((0, breadth), (height, spare))
-    )
-    held = jnp.concatenate([pair.reshape(pixels, channels), marks.astype(bf16)], axis=0)[None]
-    cot_held = jnp.maximum(cotangent.reshape(1, pixels, channels), jnp.finfo(bf16).min)
+    marks = jnp.pad(pair_mask.T, ((pixels, breadth), (0, height + spare))) + jnp.pad(
+        contact_mask.T, ((pixels, breadth), (height, spare))
+    )
+    block = pair.reshape(1, pixels, channels)
+    mine = lax.optimization_barrier(jnp.maximum(block, jnp.finfo(bf16).min))
+    above = jnp.pad(cotangent.reshape(pixels, channels), ((0, 2 * breadth), (0, 0)))
+    cot_held = (above.astype(f32) + marks.astype(f32)).astype(bf16)[None]
+    shared = len(halvings("col", col_count)) - 1
+
+    def join(*parts, axis=0):
+        return lax.optimization_barrier(jnp.concatenate(parts, axis=axis))
+
+    held = join(mine, exchange(block, rounds[0]))
+    cot_held = join(cot_held, exchange(cot_held, cot_rounds[0]))
+    for hop in rounds[1:shared]:
+        held = join(held, exchange(held, hop))
+        cot_held = join(cot_held, exchange(cot_held, hop))
+    held = join(held, cot_held[:, pixels:], axis=1)
+    cot_held = cot_held[:, :pixels]
     rates = jnp.clip(dilations, 1, DMAX)
-    cot_held, rates = lax.optimization_barrier((cot_held, rates))
-    for step, (hop, cot_hop) in enumerate(zip(rounds[:-1], cot_rounds[:-1])):
-        held = jnp.concatenate([held, exchange(held, hop)], axis=0)
-        cot_other = exchange(cot_held, cot_hop)
+    for step in range(shared, len(rounds) - 1):
+        other = exchange(held, rounds[step])
+        cot_other = exchange(cot_held, cot_rounds[step])
+        held = join(held, other)
         if step < len(rounds) - 2:
-            cot_held = jnp.concatenate([cot_held, cot_other], axis=0)
+            cot_held, rates = lax.optimization_barrier(
+                (jnp.concatenate([cot_held, cot_other], axis=0), rates)
+            )
     near, far = held, exchange(held, rounds[-1])
     *near_parts, two_t = pl.pallas_call(
         functools.partial(near_kernel, plan),
@@ -800,7 +807,7 @@
             ((9, channels, channels), f32),
             ((9, channels, channels), f32),
         ),
-        scratch_shapes=[padded, tripled, tripled, bordered, banded, sums, sums],
+        scratch_shapes=[padded, tripled, tripled, bordered, sums, sums],
         compiler_params=pltpu.CompilerParams(vmem_limit_bytes=BACKWARD_VMEM),
     )(
         rates,

time: 56.9 us -> 53.7 us (0.944)
  waiting for transfers between devices: 9.47 us -> 14 us
  starting transfers between devices: 16.3 us -> 13 us
  Pallas kernels: 26 us -> 23.7 us
  other arithmetic: 3.88 us -> 1.83 us
    ppermute x10, waiting for transfers between devices: 9.47 us -> 14 us  [exchange(): lax.ppermute(held, axis, [(i, i ^ distance) for i in range(lax.axis_size(...]
    ppermute x10, starting transfers between devices: 16.3 us -> 13 us  [exchange(): lax.ppermute(held, axis, [(i, i ^ distance) for i in range(lax.axis_size(...]
    pallas_call x1, Pallas kernels: 12.7 us -> 10.3 us  [replicated(): pl.pallas_call(functools.partial(backward_kernel, plan), in_specs=[in_sme...]
    convert_element_type x1 -> x0, other arithmetic: 0.83 us -> none  [replicated(): marks.astype(bf16)]
    unnamed x1 -> x0, other arithmetic: 0.76 us -> none
    min x1, other arithmetic: 0.66 us -> 0.01 us  [replicated(): rates = jnp.clip(dilations, 1, DMAX)]
  transfers between devices with their start and end apart: 10 -> 10, of which waited for: 4 -> 7; matrix products, arithmetic and copies ran while one was open for 4% -> 2% of each run, Pallas kernels for 23% -> 25%
where the time goes in v9:
time: 53.7 us; the launch traced here: 53.4 us
  Pallas kernels  23.7 us (44%)
  waiting for transfers between devices  14 us (26%)
  starting transfers between devices  13 us (24%)
  other arithmetic  1.83 us (3%)
  between operations  0.77 us (1%)
    ppermute x10, waiting for transfers between devices, exchange(): lax.ppermute(held, axis, [(i, i ^ distance) for i in range(lax.axis_size(...  14 us
    ppermute x10, starting transfers between devices, exchange(): lax.ppermute(held, axis, [(i, i ^ distance) for i in range(lax.axis_size(...  13 us
    pallas_call x1, Pallas kernels, replicated(): pl.pallas_call(functools.partial(forward_kernel, plan), in_specs=[in_smem...  11.5 us
    pallas_call x1, Pallas kernels, replicated(): pl.pallas_call(functools.partial(backward_kernel, plan), in_specs=[in_sme...  10.3 us
    pallas_call x1, Pallas kernels, replicated(): pl.pallas_call(functools.partial(near_kernel, plan), in_specs=[in_vmem] *...  1.89 us
  transfers between devices with their start and end apart: 10, of which 7 were waited for; matrix products, arithmetic and copies ran while one was open for 2% of the time, Pallas kernels for 25%

profile of v9, /device:TPU:0, one launch (start us, length us, event | category | flops | bytes accessed | tf_op | source)
XLA Modules:
  0.0 53.4 jit_solution(13178533549277396386)
XLA Ops:
  0.6 0.0 copy-start.5
  0.6 0.9 %fusion = bf16[1,144,128]{2,1,0:T(8,128)(2,1)S(1)} fusion(s32[8,16]{1,0:T(8,128)} %bitcast.11, s32[8,16]{1,0:T(8,128)} %bitcast.12, bf16[128,128]{1,0:T(8,128)(2,1)} %bitcast.9), kind=kLoop, calls=%fused_computation.9 | loop fusion | flops 92160 | bytes 70656 | tf_op jit(solution)/shard_map/broadcast_in_dim | solution.py:720
  1.5 4.0 %collective-permute-start = (bf16[1,144,128]{2,1,0:T(8,128)(2,1)S(1)}, bf16[1,144,128]{2,1,0:T(8,128)(2,1)S(1)}, u32[]{:S(2)}, u32[]{:S(2)}) collective-permute-start(bf16[1,144,128]{2,1,0:T(8,128)(2,1)S(1)} %fusion), channel_id=1, source_target_pairs={{0,4},{1,5},{2,6},{3,7},{4,0},{5,1},{6,2},{7,3},{8,12},{9,13},{10,... | collective-permute-start | bytes 110600 | tf_op jit(solution)/shard_map/ppermute | solution.py:186
  5.6 0.1 collective-permute-start.3
  5.6 0.8 %broadcast_maximum_fusion = bf16[1,128,128]{2,1,0:T(8,128)(2,1)S(1)} fusion(bf16[16,8,128]{2,1,0:T(8,128)(2,1)} %param.10), kind=kLoop, calls=%fused_computation.10 | loop fusion | flops 16384 | bytes 65536 | tf_op jit(solution)/shard_map/max | solution.py:718
  6.4 0.0 copy-start.1
  6.4 0.0 copy-start.2
  6.4 0.0 copy-start.3
  6.4 4.1 %collective-permute-done.3 = bf16[1,128,128]{2,1,0:T(8,128)(2,1)S(1)} collective-permute-done((bf16[1,128,128]{2,1,0:T(8,128)(2,1)}, bf16[1,128,128]{2,1,0:T(8,128)(2,1)S(1)}, u32[]{:S(2)}, u32[]{:S(2)}) %collective-permute-start.3) | collective-permute-done | bytes 32800 | tf_op jit(solution)/shard_map/ppermute | solution.py:186
  10.6 1.6 %collective-permute-start.4 = (bf16[2,128,128]{2,1,0:T(8,128)(2,1)S(1)}, bf16[2,128,128]{2,1,0:T(8,128)(2,1)S(1)}, u32[]{:S(2)}, u32[]{:S(2)}) collective-permute-start(bf16[2,128,128]{2,1,0:T(8,128)(2,1)S(1)} %pad_maximum_fusion.7), channel_id=1, source_target_pairs={{0,2},{1,3},{2,0},{3,1},{4,6},{5,7},{6,4},{7,5},{8,10},{9,11},{10,... | collective-permute-start | bytes 196616 | tf_op jit(solution)/shard_map/ppermute | solution.py:186
  12.2 0.0 collective-permute-done
  12.2 0.5 collective-permute-start.1
  12.8 2.2 %collective-permute-done.4 = bf16[2,128,128]{2,1,0:T(8,128)(2,1)S(1)} collective-permute-done((bf16[2,128,128]{2,1,0:T(8,128)(2,1)S(1)}, bf16[2,128,128]{2,1,0:T(8,128)(2,1)S(1)}, u32[]{:S(2)}, u32[]{:S(2)}) %collective-permute-start.4) | collective-permute-done | bytes 65568 | tf_op jit(solution)/shard_map/ppermute | solution.py:186
  14.9 1.7 %collective-permute-done.1 = bf16[2,144,128]{2,1,0:T(8,128)(2,1)S(1)} collective-permute-done((bf16[2,144,128]{2,1,0:T(8,128)(2,1)S(1)}, bf16[2,144,128]{2,1,0:T(8,128)(2,1)S(1)}, u32[]{:S(2)}, u32[]{:S(2)}) %collective-permute-start.1) | collective-permute-done | bytes 73760 | tf_op jit(solution)/shard_map/ppermute | solution.py:186
  16.7 1.6 %collective-permute-start.5 = (bf16[4,144,128]{2,1,0:T(8,128)(2,1)S(1)}, bf16[4,144,128]{2,1,0:T(8,128)(2,1)S(1)}, u32[]{:S(2)}, u32[]{:S(2)}) collective-permute-start(bf16[4,144,128]{2,1,0:T(8,128)(2,1)S(1)} %pad_maximum_fusion.4), channel_id=1, source_target_pairs={{0,1},{1,0},{2,3},{3,2},{4,5},{5,4},{6,7},{7,6},{8,9},{9,8},{10,11... | collective-permute-start | bytes 442376 | tf_op jit(solution)/shard_map/ppermute | solution.py:186
  18.3 1.6 %collective-permute-start.2 = (bf16[4,128,128]{2,1,0:T(8,128)(2,1)S(1)}, bf16[4,128,128]{2,1,0:T(8,128)(2,1)S(1)}, u32[]{:S(2)}, u32[]{:S(2)}) collective-permute-start(bf16[4,128,128]{2,1,0:T(8,128)(2,1)S(1)} %slice.8), channel_id=1, source_target_pairs={{0,16},{8,24},{16,0},{24,8},{1,17},{9,25},{17,1},{25,9},{2,18},{10... | collective-permute-start | bytes 393224 | tf_op jit(solution)/shard_map/ppermute | solution.py:186
  19.9 2.1 %collective-permute-done.5 = bf16[4,144,128]{2,1,0:T(8,128)(2,1)S(1)} collective-permute-done((bf16[4,144,128]{2,1,0:T(8,128)(2,1)S(1)}, bf16[4,144,128]{2,1,0:T(8,128)(2,1)S(1)}, u32[]{:S(2)}, u32[]{:S(2)}) %collective-permute-start.5) | collective-permute-done | bytes 147488 | tf_op jit(solution)/shard_map/ppermute | solution.py:186
  22.0 1.8 %collective-permute-start.6 = (bf16[8,144,128]{2,1,0:T(8,128)(2,1)S(1)}, bf16[8,144,128]{2,1,0:T(8,128)(2,1)S(1)}, u32[]{:S(2)}, u32[]{:S(2)}) collective-permute-start(bf16[8,144,128]{2,1,0:T(8,128)(2,1)S(1)} %pad_maximum_fusion.1), channel_id=1, source_target_pairs={{0,16},{8,24},{16,0},{24,8},{1,17},{9,25},{17,1},{25,9},{2,18},{10... | collective-permute-start | bytes 884744 | tf_op jit(solution)/shard_map/ppermute | solution.py:186
  23.8 0.0 copy-done.5
  23.8 0.0 copy-start
  23.8 0.0 copy-start.4
  23.8 1.0 %collective-permute-done.2 = bf16[4,128,128]{2,1,0:T(8,128)(2,1)S(1)} collective-permute-done((bf16[4,128,128]{2,1,0:T(8,128)(2,1)S(1)}, bf16[4,128,128]{2,1,0:T(8,128)(2,1)S(1)}, u32[]{:S(2)}, u32[]{:S(2)}) %collective-permute-start.2) | collective-permute-done | bytes 131104 | tf_op jit(solution)/shard_map/ppermute | solution.py:186
  24.8 1.5 %collective-permute-start.8 = (bf16[8,128,128]{2,1,0:T(8,128)(2,1)S(1)}, bf16[8,128,128]{2,1,0:T(8,128)(2,1)S(1)}, u32[]{:S(2)}, u32[]{:S(2)}) collective-permute-start(bf16[8,128,128]{2,1,0:T(8,128)(2,1)S(1)} %pad_maximum_fusion.2), channel_id=1, source_target_pairs={{0,1},{1,0},{2,3},{3,2},{4,5},{5,4},{6,7},{7,6},{8,9},{9,8},{10,11... | collective-permute-start | bytes 786440 | tf_op jit(solution)/shard_map/ppermute | solution.py:186
  26.3 2.5 %collective-permute-done.6 = bf16[8,144,128]{2,1,0:T(8,128)(2,1)S(1)} collective-permute-done((bf16[8,144,128]{2,1,0:T(8,128)(2,1)S(1)}, bf16[8,144,128]{2,1,0:T(8,128)(2,1)S(1)}, u32[]{:S(2)}, u32[]{:S(2)}) %collective-permute-start.6) | collective-permute-done | bytes 294944 | tf_op jit(solution)/shard_map/ppermute | solution.py:186
  28.8 0.1 pad_maximum_fusion.near
  28.9 0.1 collective-permute-start.7
  29.0 0.0 copy-done.1
  29.0 0.0 copy-done.2
  29.0 0.0 copy-done.3
  29.0 1.9 %shard_map.129 = (bf16[128,16,128]{2,1,0:T(8,128)(2,1)S(1)}, bf16[128,16,128]{2,1,0:T(8,128)(2,1)S(1)}, bf16[128,16,128]{2,1,0:T(8,128)(2,1)S(1)}, bf16[2,16,64,...) custom-call(bf16[16,144,128]{2,1,0:T(8,128)(2,1)S(1)} %pad_maximum_f, ...), custom_call_target="tpu_custom_call" | custom-call | flops 335544320 | bytes 4194304 | tf_op jit(solution)/shard_map/pallas_call | solution.py:743
  30.9 0.4 collective-permute-done.8
  31.3 0.2 collective-permute-start.9
  31.5 0.0 collective-permute-done.7.far
  31.5 0.0 copy-done
  31.5 0.0 copy-done.4
  31.5 11.5 %shard_map.130 = (bf16[128,128]{1,0:T(8,128)(2,1)}, bf16[128,4096]{1,0:T(8,128)(2,1)S(1)}, bf16[128,4096]{1,0:T(8,128)(2,1)S(1)}, f32[64,64,128]{2,1,0:T(8,128)S...) custom-call(s32[2]{0:T(128)S(1)} %broadcast_clamp_fusion.dilations, ...), custom_call_target="tpu_custom_call" | custom-call | flops 2684354560 | bytes 20971520 | tf_op jit(solution)/shard_map/pallas_call | solution.py:768
  43.1 0.0 collective-permute-done.9.cot_far
  43.1 10.3 %shard_map.131 = (bf16[128,128]{1,0:T(8,128)(2,1)}, f32[9,128,128]{2,1,0:T(8,128)}, f32[9,128,128]{2,1,0:T(8,128)}) custom-call(s32[2]{0:T(128)S(1)} %broadcast_clamp_fusion.dilations, bf16[16,128,128]{2,1,0:T(8,128)(2,1)S(1)} %constant_dynamic-update-slice_fusion.cot_near, bf16[16,128,128]{2,1,0:T(8,128)(2,1)S(1)} %collective-permute-done.9.cot_far, ...), custom_call_target="tpu_custom_call" | custom-call | tf_op jit(solution)/shard_map/pallas_call | solution.py:801
  (12 shorter events, 0.2 us)
Async XLA Ops:
  0.6 23.2 %copy-start.5 = (s32[2]{0:T(128)S(1)}, s32[2]{0:T(128)}, u32[]{:S(2)}) copy-start(s32[2]{0:T(128)} %param.13) | copy-start | bytes 28
  1.5 10.7 %collective-permute-start = (bf16[1,144,128]{2,1,0:T(8,128)(2,1)S(1)}, bf16[1,144,128]{2,1,0:T(8,128)(2,1)S(1)}, u32[]{:S(2)}, u32[]{:S(2)}) collective-permute-start(bf16[1,144,128]{2,1,0:T(8,128)(2,1)S(1)} %fusion), channel_id=1, source_target_pairs={{0,4},{1,5},{2,6},{3,7},{4,0},{5,1},{6,2},{7,3},{8,12},{9,13},{10,... | collective-permute-start | bytes 110600 | tf_op jit(solution)/shard_map/ppermute | solution.py:186
  5.6 5.0 %collective-permute-start.3 = (bf16[1,128,128]{2,1,0:T(8,128)(2,1)}, bf16[1,128,128]{2,1,0:T(8,128)(2,1)S(1)}, u32[]{:S(2)}, u32[]{:S(2)}) collective-permute-start(bf16[1,128,128]{2,1,0:T(8,128)(2,1)} %bitcast.10), channel_id=1, source_target_pairs={{0,4},{1,5},{2,6},{3,7},{4,0},{5,1},{6,2},{7,3},{8,12},{9,13},{10,... | collective-permute-start | bytes 98312 | tf_op jit(solution)/shard_map/ppermute | solution.py:186
  6.4 22.6 %copy-start.1 = (bf16[9,128,128]{2,1,0:T(8,128)(2,1)S(1)}, bf16[9,128,128]{2,1,0:T(8,128)(2,1)}, u32[]{:S(2)}) copy-start(bf16[9,128,128]{2,1,0:T(8,128)(2,1)} %two.3) | copy-start | bytes 884740
  6.4 22.6 %copy-start.2 = (bf16[128,512]{1,0:T(8,128)(2,1)S(1)}, bf16[128,512]{1,0:T(8,128)(2,1)}, u32[]{:S(2)}) copy-start(bf16[128,512]{1,0:T(8,128)(2,1)} %w_proj.3) | copy-start | bytes 393220
  6.4 22.6 %copy-start.3 = (bf16[128,128]{1,0:T(8,128)(2,1)S(1)}, bf16[128,128]{1,0:T(8,128)(2,1)}, u32[]{:S(2)}) copy-start(bf16[128,128]{1,0:T(8,128)(2,1)} %w_gate.3) | copy-start | bytes 98308
  10.6 4.3 %collective-permute-start.4 = (bf16[2,128,128]{2,1,0:T(8,128)(2,1)S(1)}, bf16[2,128,128]{2,1,0:T(8,128)(2,1)S(1)}, u32[]{:S(2)}, u32[]{:S(2)}) collective-permute-start(bf16[2,128,128]{2,1,0:T(8,128)(2,1)S(1)} %pad_maximum_fusion.7), channel_id=1, source_target_pairs={{0,2},{1,3},{2,0},{3,1},{4,6},{5,7},{6,4},{7,5},{8,10},{9,11},{10,... | collective-permute-start | bytes 196616 | tf_op jit(solution)/shard_map/ppermute | solution.py:186
  12.2 4.4 %collective-permute-start.1 = (bf16[2,144,128]{2,1,0:T(8,128)(2,1)S(1)}, bf16[2,144,128]{2,1,0:T(8,128)(2,1)S(1)}, u32[]{:S(2)}, u32[]{:S(2)}) collective-permute-start(bf16[2,144,128]{2,1,0:T(8,128)(2,1)S(1)} %pad_maximum_fusion.6), channel_id=1, source_target_pairs={{0,2},{1,3},{2,0},{3,1},{4,6},{5,7},{6,4},{7,5},{8,10},{9,11},{10,... | collective-permute-start | bytes 221192 | tf_op jit(solution)/shard_map/ppermute | solution.py:186
  16.7 5.3 %collective-permute-start.5 = (bf16[4,144,128]{2,1,0:T(8,128)(2,1)S(1)}, bf16[4,144,128]{2,1,0:T(8,128)(2,1)S(1)}, u32[]{:S(2)}, u32[]{:S(2)}) collective-permute-start(bf16[4,144,128]{2,1,0:T(8,128)(2,1)S(1)} %pad_maximum_fusion.4), channel_id=1, source_target_pairs={{0,1},{1,0},{2,3},{3,2},{4,5},{5,4},{6,7},{7,6},{8,9},{9,8},{10,11... | collective-permute-start | bytes 442376 | tf_op jit(solution)/shard_map/ppermute | solution.py:186
  18.3 6.5 %collective-permute-start.2 = (bf16[4,128,128]{2,1,0:T(8,128)(2,1)S(1)}, bf16[4,128,128]{2,1,0:T(8,128)(2,1)S(1)}, u32[]{:S(2)}, u32[]{:S(2)}) collective-permute-start(bf16[4,128,128]{2,1,0:T(8,128)(2,1)S(1)} %slice.8), channel_id=1, source_target_pairs={{0,16},{8,24},{16,0},{24,8},{1,17},{9,25},{17,1},{25,9},{2,18},{10... | collective-permute-start | bytes 393224 | tf_op jit(solution)/shard_map/ppermute | solution.py:186
  22.0 6.8 %collective-permute-start.6 = (bf16[8,144,128]{2,1,0:T(8,128)(2,1)S(1)}, bf16[8,144,128]{2,1,0:T(8,128)(2,1)S(1)}, u32[]{:S(2)}, u32[]{:S(2)}) collective-permute-start(bf16[8,144,128]{2,1,0:T(8,128)(2,1)S(1)} %pad_maximum_fusion.1), channel_id=1, source_target_pairs={{0,16},{8,24},{16,0},{24,8},{1,17},{9,25},{17,1},{25,9},{2,18},{10... | collective-permute-start | bytes 884744 | tf_op jit(solution)/shard_map/ppermute | solution.py:186
  23.8 7.7 %copy-start = (bf16[9,128,128]{2,1,0:T(8,128)(2,1)S(1)}, bf16[9,128,128]{2,1,0:T(8,128)(2,1)}, u32[]{:S(2)}) copy-start(bf16[9,128,128]{2,1,0:T(8,128)(2,1)} %one.3) | copy-start | bytes 884740
  23.8 7.7 %copy-start.4 = (bf16[128,128]{1,0:T(8,128)(2,1)S(1)}, bf16[128,128]{1,0:T(8,128)(2,1)}, u32[]{:S(2)}) copy-start(bf16[128,128]{1,0:T(8,128)(2,1)} %w_out.1) | copy-start | bytes 98308
  24.8 6.4 %collective-permute-start.8 = (bf16[8,128,128]{2,1,0:T(8,128)(2,1)S(1)}, bf16[8,128,128]{2,1,0:T(8,128)(2,1)S(1)}, u32[]{:S(2)}, u32[]{:S(2)}) collective-permute-start(bf16[8,128,128]{2,1,0:T(8,128)(2,1)S(1)} %pad_maximum_fusion.2), channel_id=1, source_target_pairs={{0,1},{1,0},{2,3},{3,2},{4,5},{5,4},{6,7},{7,6},{8,9},{9,8},{10,11... | collective-permute-start | bytes 786440 | tf_op jit(solution)/shard_map/ppermute | solution.py:186
  28.9 2.6 %collective-permute-start.7 = (bf16[16,144,128]{2,1,0:T(8,128)(2,1)S(1)}, bf16[16,144,128]{2,1,0:T(8,128)(2,1)S(1)}, u32[]{:S(2)}, u32[]{:S(2)}) collective-permute-start(bf16[16,144,128]{2,1,0:T(8,128)(2,1)S(1)} %pad_maximum_fusion.near), channel_id=1, source_target_pairs={{0,8},{8,0},{16,24},{24,16},{1,9},{9,1},{17,25},{25,17},{2,10},{10... | collective-permute-start | bytes 1769480 | tf_op jit(solution)/shard_map/ppermute | solution.py:186
  31.3 11.7 %collective-permute-start.9 = (bf16[16,128,128]{2,1,0:T(8,128)(2,1)S(1)}, bf16[16,128,128]{2,1,0:T(8,128)(2,1)S(1)}, u32[]{:S(2)}, u32[]{:S(2)}) collective-permute-start(bf16[16,128,128]{2,1,0:T(8,128)(2,1)S(1)} %constant_dynamic-update-slice_fusion.cot_near), channel_id=1, source_target_pairs={{0,8},{8,0},{16,24},{24,16},{1,9},{9,1},{17,25},{25,17},{2,10},{10... | collective-permute-start | bytes 1572872 | tf_op jit(solution)/shard_map/ppermute | solution.py:186

commit v10 on v9

--- a/solution.py
+++ b/solution.py
@@ -11,7 +11,7 @@
 VMEM_LIMIT = 48 * 1024 * 1024
 PITCH = 8
 FORWARD_VMEM = 44 * 1024 * 1024
-BACKWARD_VMEM = 28 * 1024 * 1024
+BACKWARD_VMEM = 36 * 1024 * 1024
 
 
 EPSILON = 1e-05
@@ -178,7 +178,7 @@
 
 def exchange_plan(row_count, col_count):
     rows, cols = halvings("row", row_count), halvings("col", col_count)
-    return cols + rows, cols[:-1] + rows[:-1] + cols[-1:] + rows[-1:]
+    return cols + rows, rows[:-1] + cols + rows[-1:]
 
 
 def exchange(held, hop):
@@ -469,7 +469,7 @@
     lane = lax.broadcasted_iota(jnp.int32, (height, chips * tokens), 1)
     low = jnp.where(lane < tokens, 1.0, 0.0).astype(jnp.bfloat16)
     high = jnp.where(lane < tokens, 0.0, 1.0).astype(jnp.bfloat16)
-    batch = 32
+    batch = 64
     pitch = 2 * height + PITCH
 
     def multiply(step, carry):
@@ -538,19 +538,21 @@
         if step >= 2:
             first_conv(step - 2)
 
+    deep = 2 * chunk
+
     def activate(step, carry):
-        rows = pl.ds(step * chunk, chunk)
-        pre = row_taps(strips, step * chunk, chunk, rate_one)
+        rows = pl.ds(step * deep, deep)
+        pre = row_taps(strips, step * deep, deep, rate_one)
         sigma = sigmoid(pre)
         second_in = pre * sigma
-        second[pl.ds(DMAX + step * chunk, chunk), inside, :] = second_in
-        flipped_two[:, lanes(step, size)] = (
-            second_in.reshape(size, channels).astype(jnp.bfloat16).T
+        second[pl.ds(DMAX + step * deep, deep), inside, :] = second_in
+        flipped_two[:, lanes(step, deep * tokens)] = (
+            second_in.reshape(deep * tokens, channels).astype(jnp.bfloat16).T
         )
         factor[rows] = sigma * (1.0 + pre * (1.0 - sigma))
         return carry
 
-    lax.fori_loop(0, tokens // chunk, activate, 0)
+    lax.fori_loop(0, tokens // deep, activate, 0)
 
     row_start, col_start = row_place * height, col_place * breadth
     cols = pl.ds(pl.multiple_of(col_start, breadth), breadth)
@@ -589,6 +591,9 @@
     grad_pre,
     sum_one,
     sum_two,
+    scaled_one,
+    scaled_two,
+    sent,
 ):
     _, cot_rounds, height, breadth, tokens = plan
     channels = one.shape[2]
@@ -600,7 +605,7 @@
     for target in (field, wide_cot, wide_pre, grad_pre):
         clear_border(target, tokens)
 
-    several = 4
+    several = 8
 
     def place_cot(source, base):
         def body(step, carry):
@@ -609,9 +614,7 @@
                 row, col = place_of(base + slot, cot_rounds, row_place, col_place)
                 cols = pl.ds(pl.multiple_of(DMAX + col * breadth, breadth), breadth)
                 field[pl.ds(row * height, height), cols, :] = (
-                    source[slot]
-                    .astype(jnp.float32)
-                    .reshape(height, breadth, channels)
+                    source[slot].astype(jnp.float32).reshape(height, breadth, channels)
                 )
             return carry
 
@@ -619,8 +622,7 @@
 
     place_cot(cot_near, 0)
     place_cot(cot_far, half)
-
-    chunk = 8
+    chunk = 16
     size = chunk * tokens
     steps = tokens // chunk
 
@@ -629,10 +631,6 @@
         return carry
 
     lax.fori_loop(0, steps, spread_cot, 0)
-
-    sum_two[...] = jnp.zeros_like(sum_two)
-
-    sum_one[...] = jnp.zeros_like(sum_one)
 
     def back_two(step):
         first = step * chunk
@@ -640,33 +638,36 @@
         before = matmul(shifted, two_t[...]).reshape(chunk, tokens, channels)
         before = (before * factor[pl.ds(first, chunk)]).astype(jnp.bfloat16).astype(jnp.float32)
         grad_pre[pl.ds(DMAX + first, chunk), inside, :] = before
-        sum_two[...] += matmul(flipped_two[:, lanes(step, size)], shifted)
+        part = matmul(flipped_two[:, step * size : (step + 1) * size], shifted)
+        sum_two[...] = part if step == 0 else sum_two[...] + part
 
     def spread_pre(step):
         spread(grad_pre, pl.ds(step * chunk, chunk), DMAX, -rate_one, wide_pre)
 
     def back_one(step):
-        sum_one[...] += matmul(
-            flipped[:, lanes(step, size)], taps(wide_pre, step * chunk, chunk, -rate_one)
-        )
-
-    def gradients(step, carry):
-        back_one(step - 3)
-        spread_pre(step - 1)
+        shifted = taps(wide_pre, step * chunk, chunk, -rate_one)
+        part = matmul(flipped[:, step * size : (step + 1) * size], shifted)
+        sum_one[...] = part if step == 0 else sum_one[...] + part
+
+    def finish(total, scaled, target, place):
+        for tap in range(9):
+            columns = slice(tap * channels, (tap + 1) * channels)
+            scaled[tap] = total[:, columns] * (1.0 / tokens)
+        copy = pltpu.make_async_copy(scaled, target, sent.at[place])
+        copy.start()
+        return copy
+
+    for step in range(steps):
+        if step >= 3:
+            back_one(step - 3)
+        if step >= 1:
+            spread_pre(step - 1)
         back_two(step)
-        return carry
-
-    back_two(0)
-    for step in (1, 2):
-        spread_pre(step - 1)
-        back_two(step)
-    lax.fori_loop(3, steps, gradients, 0)
+    copies = [finish(sum_two, scaled_two, grad_two, 1)]
     spread_pre(steps - 1)
-    lax.fori_loop(steps - 3, steps, lambda i, c: (back_one(i), c)[1], 0)
-    for tap in range(9):
-        columns = slice(tap * channels, (tap + 1) * channels)
-        grad_one[tap] = sum_one[:, columns] * (1.0 / tokens)
-        grad_two[tap] = sum_two[:, columns] * (1.0 / tokens)
+    for step in range(max(steps - 3, 0), steps):
+        back_one(step)
+    copies.append(finish(sum_one, scaled_one, grad_one, 0))
 
     one_rows = [one[tap] for tap in range(9)]
     grad_input = own_contact[...] * matmul_nt(
@@ -684,6 +685,8 @@
         - scaled * jnp.mean(grad_input * scaled, axis=-1, keepdims=True)
     )
     grad_pair[...] = (cot_near[0].astype(jnp.float32) + grad_norm).astype(jnp.bfloat16)
+    for copy in copies:
+        copy.wait()
 
 
 def replicated(
@@ -714,31 +717,21 @@
     marks = jnp.pad(pair_mask.T, ((pixels, breadth), (0, height + spare))) + jnp.pad(
         contact_mask.T, ((pixels, breadth), (height, spare))
     )
-    block = pair.reshape(1, pixels, channels)
-    mine = lax.optimization_barrier(jnp.maximum(block, jnp.finfo(bf16).min))
-    above = jnp.pad(cotangent.reshape(pixels, channels), ((0, 2 * breadth), (0, 0)))
-    cot_held = (above.astype(f32) + marks.astype(f32)).astype(bf16)[None]
-    shared = len(halvings("col", col_count)) - 1
-
-    def join(*parts, axis=0):
-        return lax.optimization_barrier(jnp.concatenate(parts, axis=axis))
-
-    held = join(mine, exchange(block, rounds[0]))
-    cot_held = join(cot_held, exchange(cot_held, cot_rounds[0]))
-    for hop in rounds[1:shared]:
-        held = join(held, exchange(held, hop))
-        cot_held = join(cot_held, exchange(cot_held, hop))
-    held = join(held, cot_held[:, pixels:], axis=1)
-    cot_held = cot_held[:, :pixels]
+    above = jnp.pad(pair.reshape(pixels, channels), ((0, 2 * breadth), (0, 0)))
+    held = (above.astype(f32) + marks.astype(f32)).astype(bf16)[None]
+    block = cotangent.reshape(1, pixels, channels)
+    cot_held = lax.optimization_barrier(jnp.maximum(block, jnp.finfo(bf16).min))
     rates = jnp.clip(dilations, 1, DMAX)
-    for step in range(shared, len(rounds) - 1):
+    for step in range(len(rounds) - 1):
         other = exchange(held, rounds[step])
-        cot_other = exchange(cot_held, cot_rounds[step])
-        held = join(held, other)
+        cot_other = exchange(cot_held if step else block, cot_rounds[step])
+        held = lax.optimization_barrier(jnp.concatenate([held, other], axis=0))
         if step < len(rounds) - 2:
-            cot_held, rates = lax.optimization_barrier(
-                (jnp.concatenate([cot_held, cot_other], axis=0), rates)
-            )
+            cot_held = jnp.concatenate([cot_held, cot_other], axis=0)
+            if step == len(rounds) - 3:
+                cot_held, rates = lax.optimization_barrier((cot_held, rates))
+            else:
+                cot_held = lax.optimization_barrier(cot_held)
     near, far = held, exchange(held, rounds[-1])
     *near_parts, two_t = pl.pallas_call(
         functools.partial(near_kernel, plan),
@@ -801,13 +794,15 @@
     grad_pair, grad_one, grad_two = pl.pallas_call(
         functools.partial(backward_kernel, plan),
         in_specs=[in_smem] + [in_vmem] * 9,
-        out_specs=[in_vmem] * 3,
+        out_specs=[in_vmem] + [pl.BlockSpec(memory_space=pltpu.HBM)] * 2,
         out_shape=shapes(
             ((pixels, channels), bf16),
             ((9, channels, channels), f32),
             ((9, channels, channels), f32),
         ),
-        scratch_shapes=[padded, tripled, tripled, bordered, sums, sums],
+        scratch_shapes=[padded, tripled, tripled, bordered, sums, sums]
+        + [pltpu.VMEM((9, channels, channels), f32)] * 2
+        + [pltpu.SemaphoreType.DMA((2,))],
         compiler_params=pltpu.CompilerParams(vmem_limit_bytes=BACKWARD_VMEM),
     )(
         rates,

time: 53.7 us -> 49.4 us (0.920)
  waiting for transfers between devices: 14 us -> 5.33 us
  starting transfers between devices: 13 us -> 17.3 us
  other arithmetic: 1.83 us -> 2.52 us
  Pallas kernels: 23.7 us -> 23.1 us
    ppermute x10, waiting for transfers between devices: 14 us -> 5.33 us  [exchange(): lax.ppermute(held, axis, [(i, i ^ distance) for i in range(lax.axis_size(...]
    ppermute x10, starting transfers between devices: 13 us -> 17.3 us  [exchange(): lax.ppermute(held, axis, [(i, i ^ distance) for i in range(lax.axis_size(...]
    min x1, other arithmetic: 0.01 us -> 0.66 us  [replicated(): rates = jnp.clip(dilations, 1, DMAX)]
  transfers between devices with their start and end apart: 10 -> 10, of which waited for: 7 -> 5; matrix products, arithmetic and copies ran while one was open for 2% -> 3% of each run, Pallas kernels for 25% -> 26%
where the time goes in v10:
time: 49.4 us; the launch traced here: 49.2 us
  Pallas kernels  23.1 us (47%)
  starting transfers between devices  17.3 us (35%)
  waiting for transfers between devices  5.33 us (11%)
  other arithmetic  2.52 us (5%)
  between operations  0.92 us (2%)
    ppermute x10, starting transfers between devices, exchange(): lax.ppermute(held, axis, [(i, i ^ distance) for i in range(lax.axis_size(...  17.3 us
    pallas_call x1, Pallas kernels, replicated(): pl.pallas_call(functools.partial(forward_kernel, plan), in_specs=[in_smem...  11.1 us
    pallas_call x1, Pallas kernels, replicated(): pl.pallas_call(functools.partial(backward_kernel, plan), in_specs=[in_sme...  10.1 us
    ppermute x10, waiting for transfers between devices, exchange(): lax.ppermute(held, axis, [(i, i ^ distance) for i in range(lax.axis_size(...  5.33 us
    pallas_call x1, Pallas kernels, replicated(): pl.pallas_call(functools.partial(near_kernel, plan), in_specs=[in_vmem] *...  1.89 us
  transfers between devices with their start and end apart: 10, of which 5 were waited for; matrix products, arithmetic and copies ran while one was open for 3% of the time, Pallas kernels for 26%

profile of v10, /device:TPU:0, one launch (start us, length us, event | category | flops | bytes accessed | tf_op | source)
XLA Modules:
  0.0 49.2 jit_solution(1529173195539011078)
XLA Ops:
  0.6 0.0 copy-start.2
  0.6 0.0 copy-start.3
  0.7 0.0 copy-start.1
  0.7 0.9 %fusion = bf16[1,144,128]{2,1,0:T(8,128)(2,1)S(1)} fusion(s32[8,16]{1,0:T(8,128)} %bitcast.11, s32[8,16]{1,0:T(8,128)} %bitcast.12, bf16[128,128]{1,0:T(8,128)(2,1)} %bitcast.9), kind=kLoop, calls=%fused_computation.8 | loop fusion | flops 92160 | bytes 70656 | tf_op jit(solution)/shard_map/broadcast_in_dim | solution.py:721
  1.6 4.0 %collective-permute-start.3 = (bf16[1,144,128]{2,1,0:T(8,128)(2,1)S(1)}, bf16[1,144,128]{2,1,0:T(8,128)(2,1)S(1)}, u32[]{:S(2)}, u32[]{:S(2)}) collective-permute-start(bf16[1,144,128]{2,1,0:T(8,128)(2,1)S(1)} %fusion), channel_id=1, source_target_pairs={{0,4},{1,5},{2,6},{3,7},{4,0},{5,1},{6,2},{7,3},{8,12},{9,13},{10,... | collective-permute-start | bytes 110600 | tf_op jit(solution)/shard_map/ppermute | solution.py:186
  5.6 1.5 %collective-permute-start = (bf16[1,128,128]{2,1,0:T(8,128)(2,1)}, bf16[1,128,128]{2,1,0:T(8,128)(2,1)S(1)}, u32[]{:S(2)}, u32[]{:S(2)}) collective-permute-start(bf16[1,128,128]{2,1,0:T(8,128)(2,1)} %bitcast.10), channel_id=1, source_target_pairs={{0,16},{8,24},{16,0},{24,8},{1,17},{9,25},{17,1},{25,9},{2,18},{10... | collective-permute-start | bytes 98312 | tf_op jit(solution)/shard_map/ppermute | solution.py:186
  7.1 0.8 %broadcast_maximum_fusion = bf16[1,128,128]{2,1,0:T(8,128)(2,1)S(1)} fusion(bf16[16,8,128]{2,1,0:T(8,128)(2,1)} %param.19), kind=kLoop, calls=%fused_computation.9 | loop fusion | flops 16384 | bytes 65536 | tf_op jit(solution)/shard_map/max | solution.py:723
  7.9 0.0 collective-permute-done.3
  8.0 1.6 %collective-permute-start.4 = (bf16[2,144,128]{2,1,0:T(8,128)(2,1)S(1)}, bf16[2,144,128]{2,1,0:T(8,128)(2,1)S(1)}, u32[]{:S(2)}, u32[]{:S(2)}) collective-permute-start(bf16[2,144,128]{2,1,0:T(8,128)(2,1)S(1)} %pad_maximum_fusion.5), channel_id=1, source_target_pairs={{0,2},{1,3},{2,0},{3,1},{4,6},{5,7},{6,4},{7,5},{8,10},{9,11},{10,... | collective-permute-start | bytes 221192 | tf_op jit(solution)/shard_map/ppermute | solution.py:186
  9.6 0.2 collective-permute-done
  9.8 2.7 %collective-permute-start.1 = (bf16[2,128,128]{2,1,0:T(8,128)(2,1)S(1)}, bf16[2,128,128]{2,1,0:T(8,128)(2,1)S(1)}, u32[]{:S(2)}, u32[]{:S(2)}) collective-permute-start(bf16[2,128,128]{2,1,0:T(8,128)(2,1)S(1)} %pad_maximum_fusion.6), channel_id=1, source_target_pairs={{0,4},{1,5},{2,6},{3,7},{4,0},{5,1},{6,2},{7,3},{8,12},{9,13},{10,... | collective-permute-start | bytes 196616 | tf_op jit(solution)/shard_map/ppermute | solution.py:186
  12.5 0.6 %collective-permute-done.4 = bf16[2,144,128]{2,1,0:T(8,128)(2,1)S(1)} collective-permute-done((bf16[2,144,128]{2,1,0:T(8,128)(2,1)S(1)}, bf16[2,144,128]{2,1,0:T(8,128)(2,1)S(1)}, u32[]{:S(2)}, u32[]{:S(2)}) %collective-permute-start.4) | collective-permute-done | bytes 73760 | tf_op jit(solution)/shard_map/ppermute | solution.py:186
  13.1 1.8 %collective-permute-start.5 = (bf16[4,144,128]{2,1,0:T(8,128)(2,1)S(1)}, bf16[4,144,128]{2,1,0:T(8,128)(2,1)S(1)}, u32[]{:S(2)}, u32[]{:S(2)}) collective-permute-start(bf16[4,144,128]{2,1,0:T(8,128)(2,1)S(1)} %pad_maximum_fusion.3), channel_id=1, source_target_pairs={{0,1},{1,0},{2,3},{3,2},{4,5},{5,4},{6,7},{7,6},{8,9},{9,8},{10,11... | collective-permute-start | bytes 442376 | tf_op jit(solution)/shard_map/ppermute | solution.py:186
  14.9 0.1 collective-permute-done.1
  15.0 1.6 %collective-permute-start.2 = (bf16[4,128,128]{2,1,0:T(8,128)(2,1)S(1)}, bf16[4,128,128]{2,1,0:T(8,128)(2,1)S(1)}, u32[]{:S(2)}, u32[]{:S(2)}) collective-permute-start(bf16[4,128,128]{2,1,0:T(8,128)(2,1)S(1)} %pad_maximum_fusion.4), channel_id=1, source_target_pairs={{0,2},{1,3},{2,0},{3,1},{4,6},{5,7},{6,4},{7,5},{8,10},{9,11},{10,... | collective-permute-start | bytes 393224 | tf_op jit(solution)/shard_map/ppermute | solution.py:186
  16.6 1.7 %collective-permute-done.5 = bf16[4,144,128]{2,1,0:T(8,128)(2,1)S(1)} collective-permute-done((bf16[4,144,128]{2,1,0:T(8,128)(2,1)S(1)}, bf16[4,144,128]{2,1,0:T(8,128)(2,1)S(1)}, u32[]{:S(2)}, u32[]{:S(2)}) %collective-permute-start.5) | collective-permute-done | bytes 147488 | tf_op jit(solution)/shard_map/ppermute | solution.py:186
  18.3 1.8 %collective-permute-start.6 = (bf16[8,144,128]{2,1,0:T(8,128)(2,1)S(1)}, bf16[8,144,128]{2,1,0:T(8,128)(2,1)S(1)}, u32[]{:S(2)}, u32[]{:S(2)}) collective-permute-start(bf16[8,144,128]{2,1,0:T(8,128)(2,1)S(1)} %pad_maximum_fusion.1), channel_id=1, source_target_pairs={{0,16},{8,24},{16,0},{24,8},{1,17},{9,25},{17,1},{25,9},{2,18},{10... | collective-permute-start | bytes 884744 | tf_op jit(solution)/shard_map/ppermute | solution.py:186
  20.1 0.7 %broadcast_clamp_fusion.dilations = s32[2]{0:T(128)S(1)} fusion(s32[2]{0:T(128)} %param.13), kind=kLoop, calls=%fused_computation.12 | loop fusion | flops 2 | bytes 16 | tf_op jit(solution)/shard_map/jit(clip)/min | solution.py:724
  20.8 0.0 copy-start
  20.8 0.0 copy-start.4
  20.8 0.0 collective-permute-done.2
  20.8 1.6 %collective-permute-start.8 = (bf16[8,128,128]{2,1,0:T(8,128)(2,1)S(1)}, bf16[8,128,128]{2,1,0:T(8,128)(2,1)S(1)}, u32[]{:S(2)}, u32[]{:S(2)}) collective-permute-start(bf16[8,128,128]{2,1,0:T(8,128)(2,1)S(1)} %pad_maximum_fusion.2), channel_id=1, source_target_pairs={{0,1},{1,0},{2,3},{3,2},{4,5},{5,4},{6,7},{7,6},{8,9},{9,8},{10,11... | collective-permute-start | bytes 786440 | tf_op jit(solution)/shard_map/ppermute | solution.py:186
  22.4 2.7 %collective-permute-done.6 = bf16[8,144,128]{2,1,0:T(8,128)(2,1)S(1)} collective-permute-done((bf16[8,144,128]{2,1,0:T(8,128)(2,1)S(1)}, bf16[8,144,128]{2,1,0:T(8,128)(2,1)S(1)}, u32[]{:S(2)}, u32[]{:S(2)}) %collective-permute-start.6) | collective-permute-done | bytes 294944 | tf_op jit(solution)/shard_map/ppermute | solution.py:186
  25.1 0.1 pad_maximum_fusion.near
  25.2 0.1 collective-permute-start.7
  25.3 0.0 copy-done.2
  25.3 0.0 copy-done.3
  25.3 0.0 copy-done.1
  25.3 1.9 %shard_map.129 = (bf16[128,16,128]{2,1,0:T(8,128)(2,1)S(1)}, bf16[128,16,128]{2,1,0:T(8,128)(2,1)S(1)}, bf16[128,16,128]{2,1,0:T(8,128)(2,1)S(1)}, bf16[2,16,64,...) custom-call(bf16[16,144,128]{2,1,0:T(8,128)(2,1)S(1)} %pad_maximum_f, ...), custom_call_target="tpu_custom_call" | custom-call | flops 335544320 | bytes 4194304 | tf_op jit(solution)/shard_map/pallas_call | solution.py:736
  27.2 0.0 collective-permute-done.8
  27.3 0.5 %collective-permute-start.9 = (bf16[16,128,128]{2,1,0:T(8,128)(2,1)S(1)}, bf16[16,128,128]{2,1,0:T(8,128)(2,1)S(1)}, u32[]{:S(2)}, u32[]{:S(2)}) collective-permute-start(bf16[16,128,128]{2,1,0:T(8,128)(2,1)S(1)} %constant_dynamic-update-slice_fusion.cot_near), channel_id=1, source_target_pairs={{0,8},{8,0},{16,24},{24,16},{1,9},{9,1},{17,25},{25,17},{2,10},{10... | collective-permute-start | bytes 1572872 | tf_op jit(solution)/shard_map/ppermute | solution.py:186
  27.8 0.0 collective-permute-done.7.far
  27.8 0.0 copy-done
  27.8 0.0 copy-done.4
  27.8 11.1 %shard_map.130 = (bf16[128,128]{1,0:T(8,128)(2,1)}, bf16[128,4096]{1,0:T(8,128)(2,1)S(1)}, bf16[128,4096]{1,0:T(8,128)(2,1)S(1)}, f32[64,64,128]{2,1,0:T(8,128)S...) custom-call(s32[2]{0:T(128)S(1)} %broadcast_clamp_fusion.dilations, ...), custom_call_target="tpu_custom_call" | custom-call | flops 2684354560 | bytes 20971520 | tf_op jit(solution)/shard_map/pallas_call | solution.py:761
  38.9 0.0 collective-permute-done.9.cot_far
  38.9 10.1 %shard_map.131 = (bf16[128,128]{1,0:T(8,128)(2,1)}, f32[9,128,128]{2,1,0:T(8,128)}, f32[9,128,128]{2,1,0:T(8,128)}) custom-call(s32[2]{0:T(128)S(1)} %broadcast_clamp_fusion.dilations, bf16[16,128,128]{2,1,0:T(8,128)(2,1)S(1)} %constant_dynamic-update-slice_fusion.cot_near, bf16[16,128,128]{2,1,0:T(8,128)(2,1)S(1)} %collective-permute-done.9.cot_far, ...), custom_call_target="tpu_custom_call" | custom-call | tf_op jit(solution)/shard_map/pallas_call | solution.py:794
  (8 shorter events, 0.2 us)
Async XLA Ops:
  0.6 24.7 %copy-start.2 = (bf16[128,512]{1,0:T(8,128)(2,1)S(1)}, bf16[128,512]{1,0:T(8,128)(2,1)}, u32[]{:S(2)}) copy-start(bf16[128,512]{1,0:T(8,128)(2,1)} %w_proj.3) | copy-start | bytes 393220
  0.6 24.7 %copy-start.3 = (bf16[128,128]{1,0:T(8,128)(2,1)S(1)}, bf16[128,128]{1,0:T(8,128)(2,1)}, u32[]{:S(2)}) copy-start(bf16[128,128]{1,0:T(8,128)(2,1)} %w_gate.3) | copy-start | bytes 98308
  0.7 24.7 %copy-start.1 = (bf16[9,128,128]{2,1,0:T(8,128)(2,1)S(1)}, bf16[9,128,128]{2,1,0:T(8,128)(2,1)}, u32[]{:S(2)}) copy-start(bf16[9,128,128]{2,1,0:T(8,128)(2,1)} %two.3) | copy-start | bytes 884740
  1.6 6.4 %collective-permute-start.3 = (bf16[1,144,128]{2,1,0:T(8,128)(2,1)S(1)}, bf16[1,144,128]{2,1,0:T(8,128)(2,1)S(1)}, u32[]{:S(2)}, u32[]{:S(2)}) collective-permute-start(bf16[1,144,128]{2,1,0:T(8,128)(2,1)S(1)} %fusion), channel_id=1, source_target_pairs={{0,4},{1,5},{2,6},{3,7},{4,0},{5,1},{6,2},{7,3},{8,12},{9,13},{10,... | collective-permute-start | bytes 110600 | tf_op jit(solution)/shard_map/ppermute | solution.py:186
  5.6 4.1 %collective-permute-start = (bf16[1,128,128]{2,1,0:T(8,128)(2,1)}, bf16[1,128,128]{2,1,0:T(8,128)(2,1)S(1)}, u32[]{:S(2)}, u32[]{:S(2)}) collective-permute-start(bf16[1,128,128]{2,1,0:T(8,128)(2,1)} %bitcast.10), channel_id=1, source_target_pairs={{0,16},{8,24},{16,0},{24,8},{1,17},{9,25},{17,1},{25,9},{2,18},{10... | collective-permute-start | bytes 98312 | tf_op jit(solution)/shard_map/ppermute | solution.py:186
  8.0 5.1 %collective-permute-start.4 = (bf16[2,144,128]{2,1,0:T(8,128)(2,1)S(1)}, bf16[2,144,128]{2,1,0:T(8,128)(2,1)S(1)}, u32[]{:S(2)}, u32[]{:S(2)}) collective-permute-start(bf16[2,144,128]{2,1,0:T(8,128)(2,1)S(1)} %pad_maximum_fusion.5), channel_id=1, source_target_pairs={{0,2},{1,3},{2,0},{3,1},{4,6},{5,7},{6,4},{7,5},{8,10},{9,11},{10,... | collective-permute-start | bytes 221192 | tf_op jit(solution)/shard_map/ppermute | solution.py:186
  9.8 5.2 %collective-permute-start.1 = (bf16[2,128,128]{2,1,0:T(8,128)(2,1)S(1)}, bf16[2,128,128]{2,1,0:T(8,128)(2,1)S(1)}, u32[]{:S(2)}, u32[]{:S(2)}) collective-permute-start(bf16[2,128,128]{2,1,0:T(8,128)(2,1)S(1)} %pad_maximum_fusion.6), channel_id=1, source_target_pairs={{0,4},{1,5},{2,6},{3,7},{4,0},{5,1},{6,2},{7,3},{8,12},{9,13},{10,... | collective-permute-start | bytes 196616 | tf_op jit(solution)/shard_map/ppermute | solution.py:186
  13.1 5.2 %collective-permute-start.5 = (bf16[4,144,128]{2,1,0:T(8,128)(2,1)S(1)}, bf16[4,144,128]{2,1,0:T(8,128)(2,1)S(1)}, u32[]{:S(2)}, u32[]{:S(2)}) collective-permute-start(bf16[4,144,128]{2,1,0:T(8,128)(2,1)S(1)} %pad_maximum_fusion.3), channel_id=1, source_target_pairs={{0,1},{1,0},{2,3},{3,2},{4,5},{5,4},{6,7},{7,6},{8,9},{9,8},{10,11... | collective-permute-start | bytes 442376 | tf_op jit(solution)/shard_map/ppermute | solution.py:186
  15.0 5.8 %collective-permute-start.2 = (bf16[4,128,128]{2,1,0:T(8,128)(2,1)S(1)}, bf16[4,128,128]{2,1,0:T(8,128)(2,1)S(1)}, u32[]{:S(2)}, u32[]{:S(2)}) collective-permute-start(bf16[4,128,128]{2,1,0:T(8,128)(2,1)S(1)} %pad_maximum_fusion.4), channel_id=1, source_target_pairs={{0,2},{1,3},{2,0},{3,1},{4,6},{5,7},{6,4},{7,5},{8,10},{9,11},{10,... | collective-permute-start | bytes 393224 | tf_op jit(solution)/shard_map/ppermute | solution.py:186
  18.3 6.8 %collective-permute-start.6 = (bf16[8,144,128]{2,1,0:T(8,128)(2,1)S(1)}, bf16[8,144,128]{2,1,0:T(8,128)(2,1)S(1)}, u32[]{:S(2)}, u32[]{:S(2)}) collective-permute-start(bf16[8,144,128]{2,1,0:T(8,128)(2,1)S(1)} %pad_maximum_fusion.1), channel_id=1, source_target_pairs={{0,16},{8,24},{16,0},{24,8},{1,17},{9,25},{17,1},{25,9},{2,18},{10... | collective-permute-start | bytes 884744 | tf_op jit(solution)/shard_map/ppermute | solution.py:186
  20.8 7.1 %copy-start = (bf16[9,128,128]{2,1,0:T(8,128)(2,1)S(1)}, bf16[9,128,128]{2,1,0:T(8,128)(2,1)}, u32[]{:S(2)}) copy-start(bf16[9,128,128]{2,1,0:T(8,128)(2,1)} %one.3) | copy-start | bytes 884740
  20.8 7.1 %copy-start.4 = (bf16[128,128]{1,0:T(8,128)(2,1)S(1)}, bf16[128,128]{1,0:T(8,128)(2,1)}, u32[]{:S(2)}) copy-start(bf16[128,128]{1,0:T(8,128)(2,1)} %w_out.1) | copy-start | bytes 98308
  20.8 6.4 %collective-permute-start.8 = (bf16[8,128,128]{2,1,0:T(8,128)(2,1)S(1)}, bf16[8,128,128]{2,1,0:T(8,128)(2,1)S(1)}, u32[]{:S(2)}, u32[]{:S(2)}) collective-permute-start(bf16[8,128,128]{2,1,0:T(8,128)(2,1)S(1)} %pad_maximum_fusion.2), channel_id=1, source_target_pairs={{0,1},{1,0},{2,3},{3,2},{4,5},{5,4},{6,7},{7,6},{8,9},{9,8},{10,11... | collective-permute-start | bytes 786440 | tf_op jit(solution)/shard_map/ppermute | solution.py:186
  25.2 2.6 %collective-permute-start.7 = (bf16[16,144,128]{2,1,0:T(8,128)(2,1)S(1)}, bf16[16,144,128]{2,1,0:T(8,128)(2,1)S(1)}, u32[]{:S(2)}, u32[]{:S(2)}) collective-permute-start(bf16[16,144,128]{2,1,0:T(8,128)(2,1)S(1)} %pad_maximum_fusion.near), channel_id=1, source_target_pairs={{0,8},{8,0},{16,24},{24,16},{1,9},{9,1},{17,25},{25,17},{2,10},{10... | collective-permute-start | bytes 1769480 | tf_op jit(solution)/shard_map/ppermute | solution.py:186
  27.3 11.7 %collective-permute-start.9 = (bf16[16,128,128]{2,1,0:T(8,128)(2,1)S(1)}, bf16[16,128,128]{2,1,0:T(8,128)(2,1)S(1)}, u32[]{:S(2)}, u32[]{:S(2)}) collective-permute-start(bf16[16,128,128]{2,1,0:T(8,128)(2,1)S(1)} %constant_dynamic-update-slice_fusion.cot_near), channel_id=1, source_target_pairs={{0,8},{8,0},{16,24},{24,16},{1,9},{9,1},{17,25},{25,17},{2,10},{10... | collective-permute-start | bytes 1572872 | tf_op jit(solution)/shard_map/ppermute | solution.py:186

commit v11 on v10

--- a/solution.py
+++ b/solution.py
@@ -197,11 +197,10 @@
     return row, col
 
 
-def slot_of(row_change, col_change, rounds):
-    slot = 0
-    for step, (axis, distance) in enumerate(rounds[:-1]):
-        change = row_change if axis == "row" else col_change
-        slot = slot | (((change // distance) & 1) << step)
+def slot_of(row_change, col, col_count, row_rounds):
+    slot = col
+    for step, (_, distance) in enumerate(row_rounds[:-1]):
+        slot = slot + ((row_change // distance) & 1) * (col_count << step)
     return slot
 
 
@@ -225,7 +224,7 @@
     rounds, _, height, breadth, tokens = plan
     channels, hidden = w_gate.shape[0], w_gate.shape[1]
     col_count, chips = tokens // breadth, tokens // height // 2
-    row_place, col_place = lax.axis_index("row"), lax.axis_index("col")
+    row_place = lax.axis_index("row")
     lane = lax.broadcasted_iota(jnp.int32, (height, breadth, channels), 2)
     place = lax.broadcasted_iota(jnp.int32, (height, breadth, channels), 0)
     own_lane = jnp.where((lane % height == place) & (lane < 2 * height), 1.0, 0.0)
@@ -240,8 +239,7 @@
             row_change = (chip * 2 + core) ^ row_place
             blocks, marks = [], []
             for col in range(col_count):
-                col_change = col_place ^ col
-                slot = slot_of(row_change, col_change, rounds)
+                slot = slot_of(row_change, col, col_count, rounds)
                 blocks.append(
                     pairs[slot, first * breadth : (first + rows) * breadth, :]
                     .astype(jnp.float32)
@@ -699,7 +697,7 @@
     pixels = height * breadth
     rounds, cot_rounds = exchange_plan(row_count, col_count)
     f32, bf16 = jnp.float32, jnp.bfloat16
-    plan = (rounds, cot_rounds, height, breadth, tokens)
+    plan = (halvings("row", row_count), cot_rounds, height, breadth, tokens)
     chips = row_count // 2
     line = tokens + 2 * DMAX
     in_vmem = pl.BlockSpec(memory_space=pltpu.VMEM)
@@ -722,16 +720,19 @@
     block = cotangent.reshape(1, pixels, channels)
     cot_held = lax.optimization_barrier(jnp.maximum(block, jnp.finfo(bf16).min))
     rates = jnp.clip(dilations, 1, DMAX)
-    for step in range(len(rounds) - 1):
-        other = exchange(held, rounds[step])
+    for step in range(len(cot_rounds) - 1):
         cot_other = exchange(cot_held if step else block, cot_rounds[step])
-        held = lax.optimization_barrier(jnp.concatenate([held, other], axis=0))
         if step < len(rounds) - 2:
             cot_held = jnp.concatenate([cot_held, cot_other], axis=0)
             if step == len(rounds) - 3:
                 cot_held, rates = lax.optimization_barrier((cot_held, rates))
             else:
                 cot_held = lax.optimization_barrier(cot_held)
+    held = lax.all_to_all(
+        jnp.broadcast_to(held, (col_count,) + held.shape[1:]), "col", 0, 0, tiled=True
+    )
+    for hop in halvings("row", row_count)[:-1]:
+        held = lax.optimization_barrier(jnp.concatenate([held, exchange(held, hop)], axis=0))
     near, far = held, exchange(held, rounds[-1])
     *near_parts, two_t = pl.pallas_call(
         functools.partial(near_kernel, plan),

time: 49.4 us -> 55.4 us (1.12)
  waiting for transfers between devices: 5.33 us -> 12.8 us
  starting transfers between devices: 17.3 us -> 15 us
  local copies, waits for them, and re-layouts: 0.07 us -> 0.83 us
    ppermute x10 -> x7, starting transfers between devices: 17.3 us -> 7.73 us  [exchange(): lax.ppermute(held, axis, [(i, i ^ distance) for i in range(lax.axis_size(...]
    ppermute x10 -> x7, waiting for transfers between devices: 5.33 us -> 12.8 us  [exchange(): lax.ppermute(held, axis, [(i, i ^ distance) for i in range(lax.axis_size(...]
    all_to_all x0 -> x1, starting transfers between devices: none -> 7.28 us  [replicated(): lax.all_to_all(jnp.broadcast_to(held, (col_count,) + held.shape[1:]), 'co...]
    broadcast_in_dim x1 -> x0, other arithmetic: 0.92 us -> none  [replicated(): held = (above.astype(f32) + marks.astype(f32)).astype(bf16)[None]]
    convert_element_type x0 -> x1, other arithmetic: none -> 0.92 us  [replicated(): held = (above.astype(f32) + marks.astype(f32)).astype(bf16)[None]]
    broadcast_in_dim x0 -> x1, local copies, waits for them, and re-layouts: none -> 0.75 us  [replicated(): jnp.broadcast_to(held, (col_count,) + held.shape[1:])]
  transfers between devices with their start and end apart: 10 -> 8, of which waited for: 5 -> 5; matrix products, arithmetic and copies ran while one was open for 3% -> 3% of each run, Pallas kernels for 26% -> 23%
where the time goes in v11:
time: 55.4 us; the launch traced here: 55.1 us
  Pallas kernels  23 us (42%)
  starting transfers between devices  15 us (27%)
  waiting for transfers between devices  12.8 us (23%)
  other arithmetic  2.47 us (4%)
  between operations  0.94 us (2%)
  local copies, waits for them, and re-layouts  0.83 us (1%)
    ppermute x7, waiting for transfers between devices, exchange(): lax.ppermute(held, axis, [(i, i ^ distance) for i in range(lax.axis_size(...  12.8 us
    pallas_call x1, Pallas kernels, replicated(): pl.pallas_call(functools.partial(forward_kernel, plan), in_specs=[in_smem...  10.9 us
    pallas_call x1, Pallas kernels, replicated(): pl.pallas_call(functools.partial(backward_kernel, plan), in_specs=[in_sme...  10.3 us
    ppermute x7, starting transfers between devices, exchange(): lax.ppermute(held, axis, [(i, i ^ distance) for i in range(lax.axis_size(...  7.73 us
    all_to_all x1, starting transfers between devices, replicated(): lax.all_to_all(jnp.broadcast_to(held, (col_count,) + held.shape[1:]), 'co...  7.28 us
    pallas_call x1, Pallas kernels, replicated(): pl.pallas_call(functools.partial(near_kernel, plan), in_specs=[in_vmem] *...  1.81 us
  transfers between devices with their start and end apart: 8, of which 5 were waited for; matrix products, arithmetic and copies ran while one was open for 3% of the time, Pallas kernels for 23%

profile of v11, /device:TPU:0, one launch (start us, length us, event | category | flops | bytes accessed | tf_op | source)
XLA Modules:
  0.0 55.1 jit_solution(1613674140505595142)
XLA Ops:
  0.6 0.0 copy-start.2
  0.6 0.0 copy-start.3
  0.7 0.0 copy-start.1
  0.7 0.9 %add_convert_fusion = bf16[144,128]{1,0:T(8,128)(2,1)S(1)} fusion(s32[8,16]{1,0:T(8,128)} %bitcast.9, s32[8,16]{1,0:T(8,128)} %bitcast.10, bf16[128,128]{1,0:T(8,128)(2,1)} %bitcast.7), kind=kLoop, calls=%fused_computation.3 | loop fusion | flops 92160 | bytes 70656 | tf_op jit(solution)/shard_map/convert_element_type | solution.py:719
  1.6 0.8 %broadcast_in_dim.2 = bf16[8,144,128]{2,1,0:T(8,128)(2,1)} broadcast(bf16[144,128]{1,0:T(8,128)(2,1)S(1)} %add_convert_fusion), dimensions={1,2} | broadcast | bytes 331776 | tf_op jit(solution)/shard_map/broadcast_in_dim | solution.py:732
  2.3 7.3 %all-to-all-start = ((bf16[8,144,128]{2,1,0:T(8,128)(2,1)}), bf16[8,144,128]{2,1,0:T(8,128)(2,1)S(1)}, u32[]{:S(2)}, u32[]{:S(2)}) async-start(bf16[8,144,128]{2,1,0:T(8,128)(2,1)} %broadcast_in_dim.2), calls=%async_computation | async-start | bytes 589824 | tf_op jit(solution)/shard_map/all_to_all | solution.py:731
  9.6 1.5 %collective-permute-start = (bf16[1,128,128]{2,1,0:T(8,128)(2,1)}, bf16[1,128,128]{2,1,0:T(8,128)(2,1)S(1)}, u32[]{:S(2)}, u32[]{:S(2)}) collective-permute-start(bf16[1,128,128]{2,1,0:T(8,128)(2,1)} %bitcast.8), channel_id=1, source_target_pairs={{0,16},{8,24},{16,0},{24,8},{1,17},{9,25},{17,1},{25,9},{2,18},{10... | collective-permute-start | bytes 98312 | tf_op jit(solution)/shard_map/ppermute | solution.py:186
  11.1 0.8 %broadcast_maximum_fusion = bf16[1,128,128]{2,1,0:T(8,128)(2,1)S(1)} fusion(bf16[16,8,128]{2,1,0:T(8,128)(2,1)} %param.19), kind=kLoop, calls=%fused_computation.5 | loop fusion | flops 16384 | bytes 65536 | tf_op jit(solution)/shard_map/max | solution.py:721
  11.9 1.8 %collective-permute-done = bf16[1,128,128]{2,1,0:T(8,128)(2,1)S(1)} collective-permute-done((bf16[1,128,128]{2,1,0:T(8,128)(2,1)}, bf16[1,128,128]{2,1,0:T(8,128)(2,1)S(1)}, u32[]{:S(2)}, u32[]{:S(2)}) %collective-permute-start) | collective-permute-done | bytes 32800 | tf_op jit(solution)/shard_map/ppermute | solution.py:186
  13.7 3.0 %collective-permute-start.1 = (bf16[2,128,128]{2,1,0:T(8,128)(2,1)S(1)}, bf16[2,128,128]{2,1,0:T(8,128)(2,1)S(1)}, u32[]{:S(2)}, u32[]{:S(2)}) collective-permute-start(bf16[2,128,128]{2,1,0:T(8,128)(2,1)S(1)} %pad_maximum_fusion.3), channel_id=1, source_target_pairs={{0,4},{1,5},{2,6},{3,7},{4,0},{5,1},{6,2},{7,3},{8,12},{9,13},{10,... | collective-permute-start | bytes 196616 | tf_op jit(solution)/shard_map/ppermute | solution.py:186
  16.7 5.3 %collective-permute-done.1 = bf16[2,128,128]{2,1,0:T(8,128)(2,1)S(1)} collective-permute-done((bf16[2,128,128]{2,1,0:T(8,128)(2,1)S(1)}, bf16[2,128,128]{2,1,0:T(8,128)(2,1)S(1)}, u32[]{:S(2)}, u32[]{:S(2)}) %collective-permute-start.1) | collective-permute-done | bytes 65568 | tf_op jit(solution)/shard_map/ppermute | solution.py:186
  22.1 0.1 collective-permute-start.2
  22.1 0.0 all-to-all-done
  22.1 1.6 %collective-permute-start.3 = (bf16[8,144,128]{2,1,0:T(8,128)(2,1)S(1)}, bf16[8,144,128]{2,1,0:T(8,128)(2,1)S(1)}, u32[]{:S(2)}, u32[]{:S(2)}) collective-permute-start(bf16[8,144,128]{2,1,0:T(8,128)(2,1)S(1)} %all-to-all-done), channel_id=1, source_target_pairs={{0,16},{8,24},{16,0},{24,8},{1,17},{9,25},{17,1},{25,9},{2,18},{10... | collective-permute-start | bytes 884744 | tf_op jit(solution)/shard_map/ppermute | solution.py:186
  23.7 0.7 %broadcast_clamp_fusion.dilations = s32[2]{0:T(128)S(1)} fusion(s32[2]{0:T(128)} %param.13), kind=kLoop, calls=%fused_computation.8 | loop fusion | flops 2 | bytes 16 | tf_op jit(solution)/shard_map/jit(clip)/min | solution.py:722
  24.4 0.0 copy-start
  24.4 0.0 copy-start.4
  24.4 2.7 %collective-permute-done.2 = bf16[4,128,128]{2,1,0:T(8,128)(2,1)S(1)} collective-permute-done((bf16[4,128,128]{2,1,0:T(8,128)(2,1)S(1)}, bf16[4,128,128]{2,1,0:T(8,128)(2,1)S(1)}, u32[]{:S(2)}, u32[]{:S(2)}) %collective-permute-start.2) | collective-permute-done | bytes 131104 | tf_op jit(solution)/shard_map/ppermute | solution.py:186
  27.1 1.5 %collective-permute-start.5 = (bf16[8,128,128]{2,1,0:T(8,128)(2,1)S(1)}, bf16[8,128,128]{2,1,0:T(8,128)(2,1)S(1)}, u32[]{:S(2)}, u32[]{:S(2)}) collective-permute-start(bf16[8,128,128]{2,1,0:T(8,128)(2,1)S(1)} %pad_maximum_fusion.1), channel_id=1, source_target_pairs={{0,1},{1,0},{2,3},{3,2},{4,5},{5,4},{6,7},{7,6},{8,9},{9,8},{10,11... | collective-permute-start | bytes 786440 | tf_op jit(solution)/shard_map/ppermute | solution.py:186
  28.6 1.1 %collective-permute-done.3 = bf16[8,144,128]{2,1,0:T(8,128)(2,1)S(1)} collective-permute-done((bf16[8,144,128]{2,1,0:T(8,128)(2,1)S(1)}, bf16[8,144,128]{2,1,0:T(8,128)(2,1)S(1)}, u32[]{:S(2)}, u32[]{:S(2)}) %collective-permute-start.3) | collective-permute-done | bytes 294944 | tf_op jit(solution)/shard_map/ppermute | solution.py:186
  29.7 0.1 pad_maximum_fusion.near
  29.7 0.1 collective-permute-start.4
  29.8 0.0 copy-done.2
  29.8 0.0 copy-done.3
  29.9 0.0 copy-done.1
  29.9 1.8 %shard_map.129 = (bf16[128,16,128]{2,1,0:T(8,128)(2,1)S(1)}, bf16[128,16,128]{2,1,0:T(8,128)(2,1)S(1)}, bf16[128,16,128]{2,1,0:T(8,128)(2,1)S(1)}, bf16[2,16,64,...) custom-call(bf16[16,144,128]{2,1,0:T(8,128)(2,1)S(1)} %pad_maximum_f, ...), custom_call_target="tpu_custom_call" | custom-call | flops 335544320 | bytes 4194304 | tf_op jit(solution)/shard_map/pallas_call | solution.py:737
  31.7 1.9 %collective-permute-done.5 = bf16[8,128,128]{2,1,0:T(8,128)(2,1)S(1)} collective-permute-done((bf16[8,128,128]{2,1,0:T(8,128)(2,1)S(1)}, bf16[8,128,128]{2,1,0:T(8,128)(2,1)S(1)}, u32[]{:S(2)}, u32[]{:S(2)}) %collective-permute-start.5) | collective-permute-done | bytes 262176 | tf_op jit(solution)/shard_map/ppermute | solution.py:186
  33.6 0.1 collective-permute-start.6
  33.7 0.0 collective-permute-done.4.far
  33.7 0.0 copy-done
  33.7 0.0 copy-done.4
  33.7 10.9 %shard_map.130 = (bf16[128,128]{1,0:T(8,128)(2,1)}, bf16[128,4096]{1,0:T(8,128)(2,1)S(1)}, bf16[128,4096]{1,0:T(8,128)(2,1)S(1)}, f32[64,64,128]{2,1,0:T(8,128)S...) custom-call(s32[2]{0:T(128)S(1)} %broadcast_clamp_fusion.dilations, ...), custom_call_target="tpu_custom_call" | custom-call | flops 2684354560 | bytes 20971520 | tf_op jit(solution)/shard_map/pallas_call | solution.py:762
  44.6 0.0 collective-permute-done.6.cot_far
  44.6 10.3 %shard_map.131 = (bf16[128,128]{1,0:T(8,128)(2,1)}, f32[9,128,128]{2,1,0:T(8,128)}, f32[9,128,128]{2,1,0:T(8,128)}) custom-call(s32[2]{0:T(128)S(1)} %broadcast_clamp_fusion.dilations, bf16[16,128,128]{2,1,0:T(8,128)(2,1)S(1)} %constant_dynamic-update-slice_fusion.cot_near, bf16[16,128,128]{2,1,0:T(8,128)(2,1)S(1)} %collective-permute-done.6.cot_far, ...), custom_call_target="tpu_custom_call" | custom-call | tf_op jit(solution)/shard_map/pallas_call | solution.py:795
  (5 shorter events, 0.1 us)
Async XLA Ops:
  0.6 29.2 %copy-start.2 = (bf16[128,512]{1,0:T(8,128)(2,1)S(1)}, bf16[128,512]{1,0:T(8,128)(2,1)}, u32[]{:S(2)}) copy-start(bf16[128,512]{1,0:T(8,128)(2,1)} %w_proj.3) | copy-start | bytes 393220
  0.6 29.2 %copy-start.3 = (bf16[128,128]{1,0:T(8,128)(2,1)S(1)}, bf16[128,128]{1,0:T(8,128)(2,1)}, u32[]{:S(2)}) copy-start(bf16[128,128]{1,0:T(8,128)(2,1)} %w_gate.3) | copy-start | bytes 98308
  0.7 29.2 %copy-start.1 = (bf16[9,128,128]{2,1,0:T(8,128)(2,1)S(1)}, bf16[9,128,128]{2,1,0:T(8,128)(2,1)}, u32[]{:S(2)}) copy-start(bf16[9,128,128]{2,1,0:T(8,128)(2,1)} %two.3) | copy-start | bytes 884740
  2.3 19.8 %all-to-all-start = ((bf16[8,144,128]{2,1,0:T(8,128)(2,1)}), bf16[8,144,128]{2,1,0:T(8,128)(2,1)S(1)}, u32[]{:S(2)}, u32[]{:S(2)}) async-start(bf16[8,144,128]{2,1,0:T(8,128)(2,1)} %broadcast_in_dim.2), calls=%async_computation | async-start | bytes 589824 | tf_op jit(solution)/shard_map/all_to_all | solution.py:731
  9.6 4.1 %collective-permute-start = (bf16[1,128,128]{2,1,0:T(8,128)(2,1)}, bf16[1,128,128]{2,1,0:T(8,128)(2,1)S(1)}, u32[]{:S(2)}, u32[]{:S(2)}) collective-permute-start(bf16[1,128,128]{2,1,0:T(8,128)(2,1)} %bitcast.8), channel_id=1, source_target_pairs={{0,16},{8,24},{16,0},{24,8},{1,17},{9,25},{17,1},{25,9},{2,18},{10... | collective-permute-start | bytes 98312 | tf_op jit(solution)/shard_map/ppermute | solution.py:186
  13.7 8.3 %collective-permute-start.1 = (bf16[2,128,128]{2,1,0:T(8,128)(2,1)S(1)}, bf16[2,128,128]{2,1,0:T(8,128)(2,1)S(1)}, u32[]{:S(2)}, u32[]{:S(2)}) collective-permute-start(bf16[2,128,128]{2,1,0:T(8,128)(2,1)S(1)} %pad_maximum_fusion.3), channel_id=1, source_target_pairs={{0,4},{1,5},{2,6},{3,7},{4,0},{5,1},{6,2},{7,3},{8,12},{9,13},{10,... | collective-permute-start | bytes 196616 | tf_op jit(solution)/shard_map/ppermute | solution.py:186
  22.1 5.0 %collective-permute-start.2 = (bf16[4,128,128]{2,1,0:T(8,128)(2,1)S(1)}, bf16[4,128,128]{2,1,0:T(8,128)(2,1)S(1)}, u32[]{:S(2)}, u32[]{:S(2)}) collective-permute-start(bf16[4,128,128]{2,1,0:T(8,128)(2,1)S(1)} %pad_maximum_fusion.2), channel_id=1, source_target_pairs={{0,2},{1,3},{2,0},{3,1},{4,6},{5,7},{6,4},{7,5},{8,10},{9,11},{10,... | collective-permute-start | bytes 393224 | tf_op jit(solution)/shard_map/ppermute | solution.py:186
  22.1 7.5 %collective-permute-start.3 = (bf16[8,144,128]{2,1,0:T(8,128)(2,1)S(1)}, bf16[8,144,128]{2,1,0:T(8,128)(2,1)S(1)}, u32[]{:S(2)}, u32[]{:S(2)}) collective-permute-start(bf16[8,144,128]{2,1,0:T(8,128)(2,1)S(1)} %all-to-all-done), channel_id=1, source_target_pairs={{0,16},{8,24},{16,0},{24,8},{1,17},{9,25},{17,1},{25,9},{2,18},{10... | collective-permute-start | bytes 884744 | tf_op jit(solution)/shard_map/ppermute | solution.py:186
  24.4 9.3 %copy-start = (bf16[9,128,128]{2,1,0:T(8,128)(2,1)S(1)}, bf16[9,128,128]{2,1,0:T(8,128)(2,1)}, u32[]{:S(2)}) copy-start(bf16[9,128,128]{2,1,0:T(8,128)(2,1)} %one.3) | copy-start | bytes 884740
  24.4 9.3 %copy-start.4 = (bf16[128,128]{1,0:T(8,128)(2,1)S(1)}, bf16[128,128]{1,0:T(8,128)(2,1)}, u32[]{:S(2)}) copy-start(bf16[128,128]{1,0:T(8,128)(2,1)} %w_out.1) | copy-start | bytes 98308
  27.1 6.4 %collective-permute-start.5 = (bf16[8,128,128]{2,1,0:T(8,128)(2,1)S(1)}, bf16[8,128,128]{2,1,0:T(8,128)(2,1)S(1)}, u32[]{:S(2)}, u32[]{:S(2)}) collective-permute-start(bf16[8,128,128]{2,1,0:T(8,128)(2,1)S(1)} %pad_maximum_fusion.1), channel_id=1, source_target_pairs={{0,1},{1,0},{2,3},{3,2},{4,5},{5,4},{6,7},{7,6},{8,9},{9,8},{10,11... | collective-permute-start | bytes 786440 | tf_op jit(solution)/shard_map/ppermute | solution.py:186
  29.7 4.0 %collective-permute-start.4 = (bf16[16,144,128]{2,1,0:T(8,128)(2,1)S(1)}, bf16[16,144,128]{2,1,0:T(8,128)(2,1)S(1)}, u32[]{:S(2)}, u32[]{:S(2)}) collective-permute-start(bf16[16,144,128]{2,1,0:T(8,128)(2,1)S(1)} %pad_maximum_fusion.near), channel_id=1, source_target_pairs={{0,8},{8,0},{16,24},{24,16},{1,9},{9,1},{17,25},{25,17},{2,10},{10... | collective-permute-start | bytes 1769480 | tf_op jit(solution)/shard_map/ppermute | solution.py:186
  33.6 11.0 %collective-permute-start.6 = (bf16[16,128,128]{2,1,0:T(8,128)(2,1)S(1)}, bf16[16,128,128]{2,1,0:T(8,128)(2,1)S(1)}, u32[]{:S(2)}, u32[]{:S(2)}) collective-permute-start(bf16[16,128,128]{2,1,0:T(8,128)(2,1)S(1)} %constant_dynamic-update-slice_fusion.cot_near), channel_id=1, source_target_pairs={{0,8},{8,0},{16,24},{24,16},{1,9},{9,1},{17,25},{25,17},{2,10},{10... | collective-permute-start | bytes 1572872 | tf_op jit(solution)/shard_map/ppermute | solution.py:186

commit v12 on v10

--- a/solution.py
+++ b/solution.py
@@ -211,6 +211,13 @@
 
 def matmul(left, right):
     return jnp.dot(left, right, preferred_element_type=jnp.float32)
+
+
+def matmul_by_rows(left, right):
+    rows = 256
+    return jnp.concatenate(
+        [matmul(left[i : i + rows], right) for i in range(0, left.shape[0], rows)], axis=0
+    )
 
 
 def matmul_nt(left, right):
@@ -373,7 +380,7 @@
         ],
         axis=0,
     )
-    result = matmul(flat, square)
+    result = matmul_by_rows(flat, square)
     channels = strips.shape[3]
     for tap in range(3):
         strips[tap, pl.ds(DMAX + first, count)] = result[
@@ -635,7 +642,7 @@
     def back_two(step):
         first = step * chunk
         shifted = taps(wide_cot, first, chunk, -rate_two)
-        before = matmul(shifted, two_t[...]).reshape(chunk, tokens, channels)
+        before = matmul_by_rows(shifted, two_t[...]).reshape(chunk, tokens, channels)
         before = (before * factor[pl.ds(first, chunk)]).astype(jnp.bfloat16).astype(jnp.float32)
         grad_pre[pl.ds(DMAX + first, chunk), inside, :] = before
         part = matmul(flipped_two[:, step * size : (step + 1) * size], shifted)
@@ -649,25 +656,29 @@
         part = matmul(flipped[:, step * size : (step + 1) * size], shifted)
         sum_one[...] = part if step == 0 else sum_one[...] + part
 
-    def finish(total, scaled, target, place):
-        for tap in range(9):
+    def finish(total, scaled, target, row):
+        for tap in range(3 * row, 3 * row + 3):
             columns = slice(tap * channels, (tap + 1) * channels)
             scaled[tap] = total[:, columns] * (1.0 / tokens)
-        copy = pltpu.make_async_copy(scaled, target, sent.at[place])
+        taps_done = pl.ds(3 * row, 3)
+        copy = pltpu.make_async_copy(
+            scaled.at[taps_done], target.at[taps_done], sent.at[len(copies)]
+        )
         copy.start()
-        return copy
-
+        copies.append(copy)
+
+    copies = []
     for step in range(steps):
         if step >= 3:
             back_one(step - 3)
         if step >= 1:
             spread_pre(step - 1)
         back_two(step)
-    copies = [finish(sum_two, scaled_two, grad_two, 1)]
     spread_pre(steps - 1)
-    for step in range(max(steps - 3, 0), steps):
+    for row in range(3):
+        finish(sum_two, scaled_two, grad_two, row)
+    for step in range(max(steps - 3, 0), steps - 1):
         back_one(step)
-    copies.append(finish(sum_one, scaled_one, grad_one, 0))
 
     one_rows = [one[tap] for tap in range(9)]
     grad_input = own_contact[...] * matmul_nt(
@@ -685,6 +696,15 @@
         - scaled * jnp.mean(grad_input * scaled, axis=-1, keepdims=True)
     )
     grad_pair[...] = (cot_near[0].astype(jnp.float32) + grad_norm).astype(jnp.bfloat16)
+
+    last = steps - 1
+    for row in range(3):
+        columns = slice(3 * row * channels, 3 * (row + 1) * channels)
+        moved = pl.ds(DMAX + last * chunk - (row - 1) * rate_one, chunk)
+        sum_one[:, columns] += matmul(
+            flipped[:, last * size : (last + 1) * size], wide_pre[moved].reshape(size, -1)
+        )
+        finish(sum_one, scaled_one, grad_one, row)
     for copy in copies:
         copy.wait()
 
@@ -802,7 +822,7 @@
         ),
         scratch_shapes=[padded, tripled, tripled, bordered, sums, sums]
         + [pltpu.VMEM((9, channels, channels), f32)] * 2
-        + [pltpu.SemaphoreType.DMA((2,))],
+        + [pltpu.SemaphoreType.DMA((6,))],
         compiler_params=pltpu.CompilerParams(vmem_limit_bytes=BACKWARD_VMEM),
     )(
         rates,

time: 49.4 us -> 48.4 us (0.980)
  Pallas kernels: 23.1 us -> 22 us
    pallas_call x1, Pallas kernels: 10.1 us -> 9.01 us  [replicated(): pl.pallas_call(functools.partial(backward_kernel, plan), in_specs=[in_sme...]
  transfers between devices with their start and end apart: 10 -> 10, of which waited for: 5 -> 5; matrix products, arithmetic and copies ran while one was open for 3% -> 3% of each run, Pallas kernels for 26% -> 27%
where the time goes in v12:
time: 48.4 us; the launch traced here: 48.1 us
  Pallas kernels  22 us (45%)
  starting transfers between devices  17.3 us (36%)
  waiting for transfers between devices  5.33 us (11%)
  other arithmetic  2.52 us (5%)
  between operations  0.92 us (2%)
    ppermute x10, starting transfers between devices, exchange(): lax.ppermute(held, axis, [(i, i ^ distance) for i in range(lax.axis_size(...  17.3 us
    pallas_call x1, Pallas kernels, replicated(): pl.pallas_call(functools.partial(forward_kernel, plan), in_specs=[in_smem...  11.1 us
    pallas_call x1, Pallas kernels, replicated(): pl.pallas_call(functools.partial(backward_kernel, plan), in_specs=[in_sme...  9.01 us
    ppermute x10, waiting for transfers between devices, exchange(): lax.ppermute(held, axis, [(i, i ^ distance) for i in range(lax.axis_size(...  5.33 us
    pallas_call x1, Pallas kernels, replicated(): pl.pallas_call(functools.partial(near_kernel, plan), in_specs=[in_vmem] *...  1.89 us
  transfers between devices with their start and end apart: 10, of which 5 were waited for; matrix products, arithmetic and copies ran while one was open for 3% of the time, Pallas kernels for 27%

profile of v12, /device:TPU:0, one launch (start us, length us, event | category | flops | bytes accessed | tf_op | source)
XLA Modules:
  0.0 48.1 jit_solution(10141896056691232842)
XLA Ops:
  0.6 0.0 copy-start.2
  0.6 0.0 copy-start.3
  0.7 0.0 copy-start.1
  0.7 0.9 %fusion = bf16[1,144,128]{2,1,0:T(8,128)(2,1)S(1)} fusion(s32[8,16]{1,0:T(8,128)} %bitcast.11, s32[8,16]{1,0:T(8,128)} %bitcast.12, bf16[128,128]{1,0:T(8,128)(2,1)} %bitcast.9), kind=kLoop, calls=%fused_computation.8 | loop fusion | flops 92160 | bytes 70656 | tf_op jit(solution)/shard_map/broadcast_in_dim | solution.py:741
  1.6 4.0 %collective-permute-start.3 = (bf16[1,144,128]{2,1,0:T(8,128)(2,1)S(1)}, bf16[1,144,128]{2,1,0:T(8,128)(2,1)S(1)}, u32[]{:S(2)}, u32[]{:S(2)}) collective-permute-start(bf16[1,144,128]{2,1,0:T(8,128)(2,1)S(1)} %fusion), channel_id=1, source_target_pairs={{0,4},{1,5},{2,6},{3,7},{4,0},{5,1},{6,2},{7,3},{8,12},{9,13},{10,... | collective-permute-start | bytes 110600 | tf_op jit(solution)/shard_map/ppermute | solution.py:186
  5.6 1.5 %collective-permute-start = (bf16[1,128,128]{2,1,0:T(8,128)(2,1)}, bf16[1,128,128]{2,1,0:T(8,128)(2,1)S(1)}, u32[]{:S(2)}, u32[]{:S(2)}) collective-permute-start(bf16[1,128,128]{2,1,0:T(8,128)(2,1)} %bitcast.10), channel_id=1, source_target_pairs={{0,16},{8,24},{16,0},{24,8},{1,17},{9,25},{17,1},{25,9},{2,18},{10... | collective-permute-start | bytes 98312 | tf_op jit(solution)/shard_map/ppermute | solution.py:186
  7.1 0.8 %broadcast_maximum_fusion = bf16[1,128,128]{2,1,0:T(8,128)(2,1)S(1)} fusion(bf16[16,8,128]{2,1,0:T(8,128)(2,1)} %param.19), kind=kLoop, calls=%fused_computation.9 | loop fusion | flops 16384 | bytes 65536 | tf_op jit(solution)/shard_map/max | solution.py:743
  7.9 0.0 collective-permute-done.3
  8.0 1.6 %collective-permute-start.4 = (bf16[2,144,128]{2,1,0:T(8,128)(2,1)S(1)}, bf16[2,144,128]{2,1,0:T(8,128)(2,1)S(1)}, u32[]{:S(2)}, u32[]{:S(2)}) collective-permute-start(bf16[2,144,128]{2,1,0:T(8,128)(2,1)S(1)} %pad_maximum_fusion.5), channel_id=1, source_target_pairs={{0,2},{1,3},{2,0},{3,1},{4,6},{5,7},{6,4},{7,5},{8,10},{9,11},{10,... | collective-permute-start | bytes 221192 | tf_op jit(solution)/shard_map/ppermute | solution.py:186
  9.6 0.2 collective-permute-done
  9.8 2.7 %collective-permute-start.1 = (bf16[2,128,128]{2,1,0:T(8,128)(2,1)S(1)}, bf16[2,128,128]{2,1,0:T(8,128)(2,1)S(1)}, u32[]{:S(2)}, u32[]{:S(2)}) collective-permute-start(bf16[2,128,128]{2,1,0:T(8,128)(2,1)S(1)} %pad_maximum_fusion.6), channel_id=1, source_target_pairs={{0,4},{1,5},{2,6},{3,7},{4,0},{5,1},{6,2},{7,3},{8,12},{9,13},{10,... | collective-permute-start | bytes 196616 | tf_op jit(solution)/shard_map/ppermute | solution.py:186
  12.5 0.6 %collective-permute-done.4 = bf16[2,144,128]{2,1,0:T(8,128)(2,1)S(1)} collective-permute-done((bf16[2,144,128]{2,1,0:T(8,128)(2,1)S(1)}, bf16[2,144,128]{2,1,0:T(8,128)(2,1)S(1)}, u32[]{:S(2)}, u32[]{:S(2)}) %collective-permute-start.4) | collective-permute-done | bytes 73760 | tf_op jit(solution)/shard_map/ppermute | solution.py:186
  13.1 1.8 %collective-permute-start.5 = (bf16[4,144,128]{2,1,0:T(8,128)(2,1)S(1)}, bf16[4,144,128]{2,1,0:T(8,128)(2,1)S(1)}, u32[]{:S(2)}, u32[]{:S(2)}) collective-permute-start(bf16[4,144,128]{2,1,0:T(8,128)(2,1)S(1)} %pad_maximum_fusion.3), channel_id=1, source_target_pairs={{0,1},{1,0},{2,3},{3,2},{4,5},{5,4},{6,7},{7,6},{8,9},{9,8},{10,11... | collective-permute-start | bytes 442376 | tf_op jit(solution)/shard_map/ppermute | solution.py:186
  14.9 0.1 collective-permute-done.1
  15.0 1.6 %collective-permute-start.2 = (bf16[4,128,128]{2,1,0:T(8,128)(2,1)S(1)}, bf16[4,128,128]{2,1,0:T(8,128)(2,1)S(1)}, u32[]{:S(2)}, u32[]{:S(2)}) collective-permute-start(bf16[4,128,128]{2,1,0:T(8,128)(2,1)S(1)} %pad_maximum_fusion.4), channel_id=1, source_target_pairs={{0,2},{1,3},{2,0},{3,1},{4,6},{5,7},{6,4},{7,5},{8,10},{9,11},{10,... | collective-permute-start | bytes 393224 | tf_op jit(solution)/shard_map/ppermute | solution.py:186
  16.6 1.7 %collective-permute-done.5 = bf16[4,144,128]{2,1,0:T(8,128)(2,1)S(1)} collective-permute-done((bf16[4,144,128]{2,1,0:T(8,128)(2,1)S(1)}, bf16[4,144,128]{2,1,0:T(8,128)(2,1)S(1)}, u32[]{:S(2)}, u32[]{:S(2)}) %collective-permute-start.5) | collective-permute-done | bytes 147488 | tf_op jit(solution)/shard_map/ppermute | solution.py:186
  18.3 1.8 %collective-permute-start.6 = (bf16[8,144,128]{2,1,0:T(8,128)(2,1)S(1)}, bf16[8,144,128]{2,1,0:T(8,128)(2,1)S(1)}, u32[]{:S(2)}, u32[]{:S(2)}) collective-permute-start(bf16[8,144,128]{2,1,0:T(8,128)(2,1)S(1)} %pad_maximum_fusion.1), channel_id=1, source_target_pairs={{0,16},{8,24},{16,0},{24,8},{1,17},{9,25},{17,1},{25,9},{2,18},{10... | collective-permute-start | bytes 884744 | tf_op jit(solution)/shard_map/ppermute | solution.py:186
  20.1 0.7 %broadcast_clamp_fusion.dilations = s32[2]{0:T(128)S(1)} fusion(s32[2]{0:T(128)} %param.13), kind=kLoop, calls=%fused_computation.12 | loop fusion | flops 2 | bytes 16 | tf_op jit(solution)/shard_map/jit(clip)/min | solution.py:744
  20.8 0.0 copy-start
  20.8 0.0 copy-start.4
  20.8 0.0 collective-permute-done.2
  20.8 1.6 %collective-permute-start.8 = (bf16[8,128,128]{2,1,0:T(8,128)(2,1)S(1)}, bf16[8,128,128]{2,1,0:T(8,128)(2,1)S(1)}, u32[]{:S(2)}, u32[]{:S(2)}) collective-permute-start(bf16[8,128,128]{2,1,0:T(8,128)(2,1)S(1)} %pad_maximum_fusion.2), channel_id=1, source_target_pairs={{0,1},{1,0},{2,3},{3,2},{4,5},{5,4},{6,7},{7,6},{8,9},{9,8},{10,11... | collective-permute-start | bytes 786440 | tf_op jit(solution)/shard_map/ppermute | solution.py:186
  22.4 2.7 %collective-permute-done.6 = bf16[8,144,128]{2,1,0:T(8,128)(2,1)S(1)} collective-permute-done((bf16[8,144,128]{2,1,0:T(8,128)(2,1)S(1)}, bf16[8,144,128]{2,1,0:T(8,128)(2,1)S(1)}, u32[]{:S(2)}, u32[]{:S(2)}) %collective-permute-start.6) | collective-permute-done | bytes 294944 | tf_op jit(solution)/shard_map/ppermute | solution.py:186
  25.1 0.1 pad_maximum_fusion.near
  25.2 0.1 collective-permute-start.7
  25.3 0.0 copy-done.2
  25.3 0.0 copy-done.3
  25.3 0.0 copy-done.1
  25.3 1.9 %shard_map.129 = (bf16[128,16,128]{2,1,0:T(8,128)(2,1)S(1)}, bf16[128,16,128]{2,1,0:T(8,128)(2,1)S(1)}, bf16[128,16,128]{2,1,0:T(8,128)(2,1)S(1)}, bf16[2,16,64,...) custom-call(bf16[16,144,128]{2,1,0:T(8,128)(2,1)S(1)} %pad_maximum_f, ...), custom_call_target="tpu_custom_call" | custom-call | flops 335544320 | bytes 4194304 | tf_op jit(solution)/shard_map/pallas_call | solution.py:756
  27.2 0.0 collective-permute-done.8
  27.3 0.5 %collective-permute-start.9 = (bf16[16,128,128]{2,1,0:T(8,128)(2,1)S(1)}, bf16[16,128,128]{2,1,0:T(8,128)(2,1)S(1)}, u32[]{:S(2)}, u32[]{:S(2)}) collective-permute-start(bf16[16,128,128]{2,1,0:T(8,128)(2,1)S(1)} %constant_dynamic-update-slice_fusion.cot_near), channel_id=1, source_target_pairs={{0,8},{8,0},{16,24},{24,16},{1,9},{9,1},{17,25},{25,17},{2,10},{10... | collective-permute-start | bytes 1572872 | tf_op jit(solution)/shard_map/ppermute | solution.py:186
  27.8 0.0 collective-permute-done.7.far
  27.8 0.0 copy-done
  27.8 0.0 copy-done.4
  27.8 11.1 %shard_map.130 = (bf16[128,128]{1,0:T(8,128)(2,1)}, bf16[128,4096]{1,0:T(8,128)(2,1)S(1)}, bf16[128,4096]{1,0:T(8,128)(2,1)S(1)}, f32[64,64,128]{2,1,0:T(8,128)S...) custom-call(s32[2]{0:T(128)S(1)} %broadcast_clamp_fusion.dilations, ...), custom_call_target="tpu_custom_call" | custom-call | flops 2684354560 | bytes 20971520 | tf_op jit(solution)/shard_map/pallas_call | solution.py:781
  39.0 0.0 collective-permute-done.9.cot_far
  39.0 9.0 %shard_map.131 = (bf16[128,128]{1,0:T(8,128)(2,1)}, f32[9,128,128]{2,1,0:T(8,128)}, f32[9,128,128]{2,1,0:T(8,128)}) custom-call(s32[2]{0:T(128)S(1)} %broadcast_clamp_fusion.dilations, bf16[16,128,128]{2,1,0:T(8,128)(2,1)S(1)} %constant_dynamic-update-slice_fusion.cot_near, bf16[16,128,128]{2,1,0:T(8,128)(2,1)S(1)} %collective-permute-done.9.cot_far, ...), custom_call_target="tpu_custom_call" | custom-call | tf_op jit(solution)/shard_map/pallas_call | solution.py:814
  (8 shorter events, 0.2 us)
Async XLA Ops:
  0.6 24.7 %copy-start.2 = (bf16[128,512]{1,0:T(8,128)(2,1)S(1)}, bf16[128,512]{1,0:T(8,128)(2,1)}, u32[]{:S(2)}) copy-start(bf16[128,512]{1,0:T(8,128)(2,1)} %w_proj.3) | copy-start | bytes 393220
  0.6 24.7 %copy-start.3 = (bf16[128,128]{1,0:T(8,128)(2,1)S(1)}, bf16[128,128]{1,0:T(8,128)(2,1)}, u32[]{:S(2)}) copy-start(bf16[128,128]{1,0:T(8,128)(2,1)} %w_gate.3) | copy-start | bytes 98308
  0.7 24.7 %copy-start.1 = (bf16[9,128,128]{2,1,0:T(8,128)(2,1)S(1)}, bf16[9,128,128]{2,1,0:T(8,128)(2,1)}, u32[]{:S(2)}) copy-start(bf16[9,128,128]{2,1,0:T(8,128)(2,1)} %two.3) | copy-start | bytes 884740
  1.6 6.4 %collective-permute-start.3 = (bf16[1,144,128]{2,1,0:T(8,128)(2,1)S(1)}, bf16[1,144,128]{2,1,0:T(8,128)(2,1)S(1)}, u32[]{:S(2)}, u32[]{:S(2)}) collective-permute-start(bf16[1,144,128]{2,1,0:T(8,128)(2,1)S(1)} %fusion), channel_id=1, source_target_pairs={{0,4},{1,5},{2,6},{3,7},{4,0},{5,1},{6,2},{7,3},{8,12},{9,13},{10,... | collective-permute-start | bytes 110600 | tf_op jit(solution)/shard_map/ppermute | solution.py:186
  5.6 4.1 %collective-permute-start = (bf16[1,128,128]{2,1,0:T(8,128)(2,1)}, bf16[1,128,128]{2,1,0:T(8,128)(2,1)S(1)}, u32[]{:S(2)}, u32[]{:S(2)}) collective-permute-start(bf16[1,128,128]{2,1,0:T(8,128)(2,1)} %bitcast.10), channel_id=1, source_target_pairs={{0,16},{8,24},{16,0},{24,8},{1,17},{9,25},{17,1},{25,9},{2,18},{10... | collective-permute-start | bytes 98312 | tf_op jit(solution)/shard_map/ppermute | solution.py:186
  8.0 5.1 %collective-permute-start.4 = (bf16[2,144,128]{2,1,0:T(8,128)(2,1)S(1)}, bf16[2,144,128]{2,1,0:T(8,128)(2,1)S(1)}, u32[]{:S(2)}, u32[]{:S(2)}) collective-permute-start(bf16[2,144,128]{2,1,0:T(8,128)(2,1)S(1)} %pad_maximum_fusion.5), channel_id=1, source_target_pairs={{0,2},{1,3},{2,0},{3,1},{4,6},{5,7},{6,4},{7,5},{8,10},{9,11},{10,... | collective-permute-start | bytes 221192 | tf_op jit(solution)/shard_map/ppermute | solution.py:186
  9.8 5.2 %collective-permute-start.1 = (bf16[2,128,128]{2,1,0:T(8,128)(2,1)S(1)}, bf16[2,128,128]{2,1,0:T(8,128)(2,1)S(1)}, u32[]{:S(2)}, u32[]{:S(2)}) collective-permute-start(bf16[2,128,128]{2,1,0:T(8,128)(2,1)S(1)} %pad_maximum_fusion.6), channel_id=1, source_target_pairs={{0,4},{1,5},{2,6},{3,7},{4,0},{5,1},{6,2},{7,3},{8,12},{9,13},{10,... | collective-permute-start | bytes 196616 | tf_op jit(solution)/shard_map/ppermute | solution.py:186
  13.1 5.2 %collective-permute-start.5 = (bf16[4,144,128]{2,1,0:T(8,128)(2,1)S(1)}, bf16[4,144,128]{2,1,0:T(8,128)(2,1)S(1)}, u32[]{:S(2)}, u32[]{:S(2)}) collective-permute-start(bf16[4,144,128]{2,1,0:T(8,128)(2,1)S(1)} %pad_maximum_fusion.3), channel_id=1, source_target_pairs={{0,1},{1,0},{2,3},{3,2},{4,5},{5,4},{6,7},{7,6},{8,9},{9,8},{10,11... | collective-permute-start | bytes 442376 | tf_op jit(solution)/shard_map/ppermute | solution.py:186
  15.0 5.8 %collective-permute-start.2 = (bf16[4,128,128]{2,1,0:T(8,128)(2,1)S(1)}, bf16[4,128,128]{2,1,0:T(8,128)(2,1)S(1)}, u32[]{:S(2)}, u32[]{:S(2)}) collective-permute-start(bf16[4,128,128]{2,1,0:T(8,128)(2,1)S(1)} %pad_maximum_fusion.4), channel_id=1, source_target_pairs={{0,2},{1,3},{2,0},{3,1},{4,6},{5,7},{6,4},{7,5},{8,10},{9,11},{10,... | collective-permute-start | bytes 393224 | tf_op jit(solution)/shard_map/ppermute | solution.py:186
  18.3 6.8 %collective-permute-start.6 = (bf16[8,144,128]{2,1,0:T(8,128)(2,1)S(1)}, bf16[8,144,128]{2,1,0:T(8,128)(2,1)S(1)}, u32[]{:S(2)}, u32[]{:S(2)}) collective-permute-start(bf16[8,144,128]{2,1,0:T(8,128)(2,1)S(1)} %pad_maximum_fusion.1), channel_id=1, source_target_pairs={{0,16},{8,24},{16,0},{24,8},{1,17},{9,25},{17,1},{25,9},{2,18},{10... | collective-permute-start | bytes 884744 | tf_op jit(solution)/shard_map/ppermute | solution.py:186
  20.8 7.1 %copy-start = (bf16[9,128,128]{2,1,0:T(8,128)(2,1)S(1)}, bf16[9,128,128]{2,1,0:T(8,128)(2,1)}, u32[]{:S(2)}) copy-start(bf16[9,128,128]{2,1,0:T(8,128)(2,1)} %one.3) | copy-start | bytes 884740
  20.8 7.1 %copy-start.4 = (bf16[128,128]{1,0:T(8,128)(2,1)S(1)}, bf16[128,128]{1,0:T(8,128)(2,1)}, u32[]{:S(2)}) copy-start(bf16[128,128]{1,0:T(8,128)(2,1)} %w_out.1) | copy-start | bytes 98308
  20.8 6.4 %collective-permute-start.8 = (bf16[8,128,128]{2,1,0:T(8,128)(2,1)S(1)}, bf16[8,128,128]{2,1,0:T(8,128)(2,1)S(1)}, u32[]{:S(2)}, u32[]{:S(2)}) collective-permute-start(bf16[8,128,128]{2,1,0:T(8,128)(2,1)S(1)} %pad_maximum_fusion.2), channel_id=1, source_target_pairs={{0,1},{1,0},{2,3},{3,2},{4,5},{5,4},{6,7},{7,6},{8,9},{9,8},{10,11... | collective-permute-start | bytes 786440 | tf_op jit(solution)/shard_map/ppermute | solution.py:186
  25.2 2.6 %collective-permute-start.7 = (bf16[16,144,128]{2,1,0:T(8,128)(2,1)S(1)}, bf16[16,144,128]{2,1,0:T(8,128)(2,1)S(1)}, u32[]{:S(2)}, u32[]{:S(2)}) collective-permute-start(bf16[16,144,128]{2,1,0:T(8,128)(2,1)S(1)} %pad_maximum_fusion.near), channel_id=1, source_target_pairs={{0,8},{8,0},{16,24},{24,16},{1,9},{9,1},{17,25},{25,17},{2,10},{10... | collective-permute-start | bytes 1769480 | tf_op jit(solution)/shard_map/ppermute | solution.py:186
  27.3 11.7 %collective-permute-start.9 = (bf16[16,128,128]{2,1,0:T(8,128)(2,1)S(1)}, bf16[16,128,128]{2,1,0:T(8,128)(2,1)S(1)}, u32[]{:S(2)}, u32[]{:S(2)}) collective-permute-start(bf16[16,128,128]{2,1,0:T(8,128)(2,1)S(1)} %constant_dynamic-update-slice_fusion.cot_near), channel_id=1, source_target_pairs={{0,8},{8,0},{16,24},{24,16},{1,9},{9,1},{17,25},{25,17},{2,10},{10... | collective-permute-start | bytes 1572872 | tf_op jit(solution)/shard_map/ppermute | solution.py:186

commit v13 on v12

--- a/solution.py
+++ b/solution.py
@@ -10,7 +10,7 @@
 DMAX = 8
 VMEM_LIMIT = 48 * 1024 * 1024
 PITCH = 8
-FORWARD_VMEM = 44 * 1024 * 1024
+FORWARD_VMEM = 32 * 1024 * 1024
 BACKWARD_VMEM = 36 * 1024 * 1024
 
 
@@ -370,9 +370,16 @@
             strips[tap, rows] = jnp.zeros((DMAX,) + strips.shape[2:], jnp.float32)
 
 
-def column_taps(source, weight, first, count, strips):
-    tokens = source.shape[1]
-    flat = source[pl.ds(DMAX + first, count)].reshape(count * tokens, -1)
+def column_taps(source, weight, rate, first, count, strips):
+    tokens = strips.shape[2]
+    columns = [DMAX - rate, DMAX, DMAX + rate]
+    flat = jnp.concatenate(
+        [
+            source[pl.ds(first, count), pl.ds(column, tokens), :].reshape(count * tokens, -1)
+            for column in columns
+        ],
+        axis=1,
+    ).astype(jnp.bfloat16)
     square = jnp.concatenate(
         [
             jnp.concatenate([weight(3 * row + col) for row in range(3)], axis=1)
@@ -415,17 +422,14 @@
     w_gate,
     w_out,
     one,
-    two,
     near_left,
     near_right,
     near_swapped,
     near_gating,
     near_contact,
     near_start,
-    output,
+    strips,
     flipped,
-    flipped_two,
-    factor,
     mine,
     own_contact,
     far_left,
@@ -440,9 +444,6 @@
     normed,
     updated,
     field,
-    wide,
-    second,
-    strips,
 ):
     _, _, height, breadth, tokens = plan
     hidden, channels = w_out.shape
@@ -450,10 +451,9 @@
     chips = tokens // height // 2
     row_place, col_place = lax.axis_index("row"), lax.axis_index("col")
     core = row_place % 2
-    rate_one, rate_two = dilations[0], dilations[1]
+    rate_one = dilations[0]
     inside = slice(DMAX, DMAX + tokens)
-    for target in (field, second):
-        clear_border(target, tokens)
+    clear_border(field, tokens)
     clear_ends(strips, tokens)
 
     right[core] = near_right[...]
@@ -520,12 +520,11 @@
         fresh = start[:, rows].astype(jnp.float32) + gating[:, rows].astype(jnp.float32) * change
         fresh = fresh.astype(jnp.bfloat16).astype(jnp.float32)
         first_in = layer_norm(fresh) * contact[:, rows].astype(jnp.float32)
+        if step < parts:
+            updated[:, rows] = fresh
         for chip in range(chips):
             base = (chip * 2 + side) * height + first
-            rows = pl.ds(base, chunk)
-            updated[rows] = fresh[chip]
-            field[rows, inside, :] = first_in[chip]
-            spread(field, rows, 0, rate_one, wide)
+            field[pl.ds(base, chunk), inside, :] = first_in[chip]
             flipped[:, pl.ds(pl.multiple_of(base * tokens, size), size)] = (
                 first_in[chip].reshape(size, channels).astype(jnp.bfloat16).T
             )
@@ -534,7 +533,7 @@
         side = halves[step // parts][0]
         for chip in range(chips):
             base = (chip * 2 + side) * height + step % parts * chunk
-            column_taps(wide, lambda tap: one[tap], base, chunk, strips)
+            column_taps(field, lambda tap: one[tap], rate_one, base, chunk, strips)
 
     count = 2 * parts
     for step in range(count + 2):
@@ -545,31 +544,8 @@
         if step >= 2:
             first_conv(step - 2)
 
-    deep = 2 * chunk
-
-    def activate(step, carry):
-        rows = pl.ds(step * deep, deep)
-        pre = row_taps(strips, step * deep, deep, rate_one)
-        sigma = sigmoid(pre)
-        second_in = pre * sigma
-        second[pl.ds(DMAX + step * deep, deep), inside, :] = second_in
-        flipped_two[:, lanes(step, deep * tokens)] = (
-            second_in.reshape(deep * tokens, channels).astype(jnp.bfloat16).T
-        )
-        factor[rows] = sigma * (1.0 + pre * (1.0 - sigma))
-        return carry
-
-    lax.fori_loop(0, tokens // deep, activate, 0)
-
-    row_start, col_start = row_place * height, col_place * breadth
-    cols = pl.ds(pl.multiple_of(col_start, breadth), breadth)
-    fresh = updated[pl.ds(row_start, height), cols, :].reshape(pixels, channels)
-    mine[...] = fresh
-    second_pre = matmul(
-        windows(second, rate_two, row_start, col_start, height, breadth),
-        two[...].reshape(9 * channels, channels),
-    )
-    output[...] = (fresh + second_pre).astype(jnp.bfloat16)
+    cols = pl.ds(pl.multiple_of(col_place * breadth, breadth), breadth)
+    mine[...] = updated[row_place // 2, :, cols, :].reshape(pixels, channels)
     marks = near_contact[row_place // 2].astype(jnp.float32)
     place_col = lax.broadcasted_iota(jnp.int32, (tokens, channels), 0) // breadth
     marks = jnp.where((place_col == col_place)[None], marks, 0.0)
@@ -583,12 +559,13 @@
     cot_near,
     cot_far,
     one,
+    two,
     two_t,
+    strips,
     flipped,
-    flipped_two,
-    factor,
     mine,
     own_contact,
+    output,
     grad_pair,
     grad_one,
     grad_two,
@@ -596,6 +573,7 @@
     wide_cot,
     wide_pre,
     grad_pre,
+    second,
     sum_one,
     sum_two,
     scaled_one,
@@ -609,7 +587,7 @@
     rate_one, rate_two = dilations[0], dilations[1]
     half = cot_far.shape[0]
     inside = slice(DMAX, DMAX + tokens)
-    for target in (field, wide_cot, wide_pre, grad_pre):
+    for target in (field, wide_cot, wide_pre, grad_pre, second):
         clear_border(target, tokens)
 
     several = 8
@@ -641,11 +619,17 @@
 
     def back_two(step):
         first = step * chunk
+        rows = pl.ds(DMAX + first, chunk)
+        pre = row_taps(strips, first, chunk, rate_one)
+        sigma = sigmoid(pre)
+        second_in = pre * sigma
+        second[rows, inside, :] = second_in
+        factor = sigma * (1.0 + pre * (1.0 - sigma))
+        turned = second_in.reshape(size, channels).astype(jnp.bfloat16).T
         shifted = taps(wide_cot, first, chunk, -rate_two)
         before = matmul_by_rows(shifted, two_t[...]).reshape(chunk, tokens, channels)
-        before = (before * factor[pl.ds(first, chunk)]).astype(jnp.bfloat16).astype(jnp.float32)
-        grad_pre[pl.ds(DMAX + first, chunk), inside, :] = before
-        part = matmul(flipped_two[:, step * size : (step + 1) * size], shifted)
+        grad_pre[rows, inside, :] = (before * factor).astype(jnp.bfloat16).astype(jnp.float32)
+        part = matmul(turned, shifted)
         sum_two[...] = part if step == 0 else sum_two[...] + part
 
     def spread_pre(step):
@@ -680,11 +664,14 @@
     for step in range(max(steps - 3, 0), steps - 1):
         back_one(step)
 
+    spot = (row_place * height, col_place * breadth, height, breadth)
+    second_pre = matmul(
+        windows(second, rate_two, *spot), two[...].reshape(9 * channels, channels)
+    )
+    output[...] = (mine[...] + second_pre).astype(jnp.bfloat16)
     one_rows = [one[tap] for tap in range(9)]
     grad_input = own_contact[...] * matmul_nt(
-        windows(
-            grad_pre, -rate_one, row_place * height, col_place * breadth, height, breadth
-        ),
+        windows(grad_pre, -rate_one, *spot),
         jnp.concatenate(one_rows, axis=1),
     )
     centre = mine[...] - jnp.mean(mine[...], axis=-1, keepdims=True)
@@ -769,37 +756,28 @@
     cot_other, two_t = lax.optimization_barrier((cot_other, two_t))
     cot_near = jnp.concatenate([cot_held, cot_other], axis=0)
     cot_far = exchange(cot_near, cot_rounds[-1])
-    whole = pltpu.VMEM((tokens, tokens, channels), f32)
     padded = pltpu.VMEM((tokens, line, channels), f32)
     bordered = pltpu.VMEM((line, line, channels), f32)
     tripled = pltpu.VMEM((line, tokens, 3 * channels), bf16)
     both = pltpu.VMEM((2,) + side[0], bf16)
     alone = pltpu.VMEM(rows, bf16)
-    banded = pltpu.VMEM((3, line, tokens, channels), f32)
     flat = ((channels, tokens * tokens), bf16)
     sums = pltpu.VMEM((channels, 9 * channels), f32)
-    output, *held = pl.pallas_call(
+    held = pl.pallas_call(
         functools.partial(forward_kernel, plan),
-        in_specs=[in_smem] + [in_vmem] * 12,
-        out_specs=[in_vmem] * 6,
-        out_shape=shapes(
-            ((pixels, channels), bf16),
-            flat,
-            flat,
-            ((tokens, tokens, channels), f32),
-            stat,
-            stat,
-        ),
+        in_specs=[in_smem] + [in_vmem] * 11,
+        out_specs=[in_vmem] * 4,
+        out_shape=shapes(((3, line, tokens, channels), f32), flat, stat, stat),
         scratch_shapes=[pltpu.VMEM(*side), both, both, alone, alone, alone]
         + [turned] * 2
         + [pltpu.VMEM((hidden * (2 * height + PITCH), chips * tokens), f32)]
         + [pltpu.VMEM((2 * height // 8, chips, 8, tokens, hidden), bf16)]
-        + [whole, padded, tripled, bordered, banded],
+        + [pltpu.VMEM(rows, f32), padded],
         compiler_params=pltpu.CompilerParams(vmem_limit_bytes=FORWARD_VMEM),
         cost_estimate=pl.CostEstimate(
-            flops=tokens * tokens * channels * 40 * hidden,
+            flops=tokens * tokens * channels * 30 * hidden,
             bytes_accessed=40 * tokens * tokens * channels,
-            transcendentals=4 * tokens * tokens * channels,
+            transcendentals=2 * tokens * tokens * channels,
         ),
     )(
         rates,
@@ -808,19 +786,19 @@
         w_gate,
         w_out,
         conv_one,
-        conv_two,
         *near_parts,
     )
-    grad_pair, grad_one, grad_two = pl.pallas_call(
+    output, grad_pair, grad_one, grad_two = pl.pallas_call(
         functools.partial(backward_kernel, plan),
         in_specs=[in_smem] + [in_vmem] * 9,
-        out_specs=[in_vmem] + [pl.BlockSpec(memory_space=pltpu.HBM)] * 2,
+        out_specs=[in_vmem] * 2 + [pl.BlockSpec(memory_space=pltpu.HBM)] * 2,
         out_shape=shapes(
+            ((pixels, channels), bf16),
             ((pixels, channels), bf16),
             ((9, channels, channels), f32),
             ((9, channels, channels), f32),
         ),
-        scratch_shapes=[padded, tripled, tripled, bordered, sums, sums]
+        scratch_shapes=[padded, tripled, tripled, bordered, bordered, sums, sums]
         + [pltpu.VMEM((9, channels, channels), f32)] * 2
         + [pltpu.SemaphoreType.DMA((6,))],
         compiler_params=pltpu.CompilerParams(vmem_limit_bytes=BACKWARD_VMEM),
@@ -829,6 +807,7 @@
         cot_near,
         cot_far,
         conv_one,
+        conv_two,
         two_t,
         *held,
     )

time: 48.4 us -> 53.4 us (1.10)
  local copies, waits for them, and re-layouts: 0.07 us -> 6.06 us
  Pallas kernels: 22 us -> 20.8 us
    unnamed x11 -> x17, local copies, waits for them, and re-layouts: 0.04 us -> 6.02 us
    pallas_call x1, Pallas kernels: 11.1 us -> 9.69 us  [replicated(): pl.pallas_call(functools.partial(forward_kernel, plan), in_specs=[in_smem...]
  transfers between devices with their start and end apart: 10 -> 10, of which waited for: 5 -> 5; matrix products, arithmetic and copies ran while one was open for 3% -> 3% of each run, Pallas kernels for 27% -> 22%
where the time goes in v13:
time: 53.4 us; the launch traced here: 52.9 us
  Pallas kernels  20.8 us (39%)
  starting transfers between devices  17.3 us (32%)
  local copies, waits for them, and re-layouts  6.06 us (11%)
  waiting for transfers between devices  5.32 us (10%)
  other arithmetic  2.51 us (5%)
  between operations  0.91 us (2%)
    ppermute x10, starting transfers between devices, exchange(): lax.ppermute(held, axis, [(i, i ^ distance) for i in range(lax.axis_size(...  17.3 us
    pallas_call x1, Pallas kernels, replicated(): pl.pallas_call(functools.partial(forward_kernel, plan), in_specs=[in_smem...  9.69 us
    pallas_call x1, Pallas kernels, replicated(): pl.pallas_call(functools.partial(backward_kernel, plan), in_specs=[in_sme...  9.2 us
    unnamed x17, local copies, waits for them, and re-layouts  6.02 us
    ppermute x10, waiting for transfers between devices, exchange(): lax.ppermute(held, axis, [(i, i ^ distance) for i in range(lax.axis_size(...  5.32 us
    pallas_call x1, Pallas kernels, replicated(): pl.pallas_call(functools.partial(near_kernel, plan), in_specs=[in_vmem] *...  1.87 us
  transfers between devices with their start and end apart: 10, of which 5 were waited for; matrix products, arithmetic and copies ran while one was open for 3% of the time, Pallas kernels for 22%

profile of v13, /device:TPU:0, one launch (start us, length us, event | category | flops | bytes accessed | tf_op | source)
XLA Modules:
  0.0 52.9 jit_solution(13373964212159200659)
XLA Ops:
  0.6 0.0 copy-start.2
  0.6 0.9 %fusion = bf16[1,144,128]{2,1,0:T(8,128)(2,1)S(1)} fusion(s32[8,16]{1,0:T(8,128)} %bitcast.11, s32[8,16]{1,0:T(8,128)} %bitcast.12, bf16[128,128]{1,0:T(8,128)(2,1)} %bitcast.9), kind=kLoop, calls=%fused_computation.8 | loop fusion | flops 92160 | bytes 70656 | tf_op jit(solution)/shard_map/broadcast_in_dim | solution.py:728
  1.6 4.0 %collective-permute-start.4 = (bf16[1,144,128]{2,1,0:T(8,128)(2,1)S(1)}, bf16[1,144,128]{2,1,0:T(8,128)(2,1)S(1)}, u32[]{:S(2)}, u32[]{:S(2)}) collective-permute-start(bf16[1,144,128]{2,1,0:T(8,128)(2,1)S(1)} %fusion), channel_id=1, source_target_pairs={{0,4},{1,5},{2,6},{3,7},{4,0},{5,1},{6,2},{7,3},{8,12},{9,13},{10,... | collective-permute-start | bytes 110600 | tf_op jit(solution)/shard_map/ppermute | solution.py:186
  5.6 1.5 %collective-permute-start = (bf16[1,128,128]{2,1,0:T(8,128)(2,1)}, bf16[1,128,128]{2,1,0:T(8,128)(2,1)S(1)}, u32[]{:S(2)}, u32[]{:S(2)}) collective-permute-start(bf16[1,128,128]{2,1,0:T(8,128)(2,1)} %bitcast.10), channel_id=1, source_target_pairs={{0,16},{8,24},{16,0},{24,8},{1,17},{9,25},{17,1},{25,9},{2,18},{10... | collective-permute-start | bytes 98312 | tf_op jit(solution)/shard_map/ppermute | solution.py:186
  7.1 0.8 %broadcast_maximum_fusion = bf16[1,128,128]{2,1,0:T(8,128)(2,1)S(1)} fusion(bf16[16,8,128]{2,1,0:T(8,128)(2,1)} %param.19), kind=kLoop, calls=%fused_computation.9 | loop fusion | flops 16384 | bytes 65536 | tf_op jit(solution)/shard_map/max | solution.py:730
  7.9 0.0 collective-permute-done.4
  7.9 1.6 %collective-permute-start.5 = (bf16[2,144,128]{2,1,0:T(8,128)(2,1)S(1)}, bf16[2,144,128]{2,1,0:T(8,128)(2,1)S(1)}, u32[]{:S(2)}, u32[]{:S(2)}) collective-permute-start(bf16[2,144,128]{2,1,0:T(8,128)(2,1)S(1)} %pad_maximum_fusion.5), channel_id=1, source_target_pairs={{0,2},{1,3},{2,0},{3,1},{4,6},{5,7},{6,4},{7,5},{8,10},{9,11},{10,... | collective-permute-start | bytes 221192 | tf_op jit(solution)/shard_map/ppermute | solution.py:186
  9.5 0.2 collective-permute-done
  9.7 2.7 %collective-permute-start.1 = (bf16[2,128,128]{2,1,0:T(8,128)(2,1)S(1)}, bf16[2,128,128]{2,1,0:T(8,128)(2,1)S(1)}, u32[]{:S(2)}, u32[]{:S(2)}) collective-permute-start(bf16[2,128,128]{2,1,0:T(8,128)(2,1)S(1)} %pad_maximum_fusion.6), channel_id=1, source_target_pairs={{0,4},{1,5},{2,6},{3,7},{4,0},{5,1},{6,2},{7,3},{8,12},{9,13},{10,... | collective-permute-start | bytes 196616 | tf_op jit(solution)/shard_map/ppermute | solution.py:186
  12.5 0.6 %collective-permute-done.5 = bf16[2,144,128]{2,1,0:T(8,128)(2,1)S(1)} collective-permute-done((bf16[2,144,128]{2,1,0:T(8,128)(2,1)S(1)}, bf16[2,144,128]{2,1,0:T(8,128)(2,1)S(1)}, u32[]{:S(2)}, u32[]{:S(2)}) %collective-permute-start.5) | collective-permute-done | bytes 73760 | tf_op jit(solution)/shard_map/ppermute | solution.py:186
  13.1 1.8 %collective-permute-start.6 = (bf16[4,144,128]{2,1,0:T(8,128)(2,1)S(1)}, bf16[4,144,128]{2,1,0:T(8,128)(2,1)S(1)}, u32[]{:S(2)}, u32[]{:S(2)}) collective-permute-start(bf16[4,144,128]{2,1,0:T(8,128)(2,1)S(1)} %pad_maximum_fusion.3), channel_id=1, source_target_pairs={{0,1},{1,0},{2,3},{3,2},{4,5},{5,4},{6,7},{7,6},{8,9},{9,8},{10,11... | collective-permute-start | bytes 442376 | tf_op jit(solution)/shard_map/ppermute | solution.py:186
  14.9 0.1 collective-permute-done.1
  15.0 1.6 %collective-permute-start.2 = (bf16[4,128,128]{2,1,0:T(8,128)(2,1)S(1)}, bf16[4,128,128]{2,1,0:T(8,128)(2,1)S(1)}, u32[]{:S(2)}, u32[]{:S(2)}) collective-permute-start(bf16[4,128,128]{2,1,0:T(8,128)(2,1)S(1)} %pad_maximum_fusion.4), channel_id=1, source_target_pairs={{0,2},{1,3},{2,0},{3,1},{4,6},{5,7},{6,4},{7,5},{8,10},{9,11},{10,... | collective-permute-start | bytes 393224 | tf_op jit(solution)/shard_map/ppermute | solution.py:186
  16.6 1.7 %collective-permute-done.6 = bf16[4,144,128]{2,1,0:T(8,128)(2,1)S(1)} collective-permute-done((bf16[4,144,128]{2,1,0:T(8,128)(2,1)S(1)}, bf16[4,144,128]{2,1,0:T(8,128)(2,1)S(1)}, u32[]{:S(2)}, u32[]{:S(2)}) %collective-permute-start.6) | collective-permute-done | bytes 147488 | tf_op jit(solution)/shard_map/ppermute | solution.py:186
  18.3 1.8 %collective-permute-start.7 = (bf16[8,144,128]{2,1,0:T(8,128)(2,1)S(1)}, bf16[8,144,128]{2,1,0:T(8,128)(2,1)S(1)}, u32[]{:S(2)}, u32[]{:S(2)}) collective-permute-start(bf16[8,144,128]{2,1,0:T(8,128)(2,1)S(1)} %pad_maximum_fusion.1), channel_id=1, source_target_pairs={{0,16},{8,24},{16,0},{24,8},{1,17},{9,25},{17,1},{25,9},{2,18},{10... | collective-permute-start | bytes 884744 | tf_op jit(solution)/shard_map/ppermute | solution.py:186
  20.1 0.7 %broadcast_clamp_fusion.dilations = s32[2]{0:T(128)S(1)} fusion(s32[2]{0:T(128)} %param.13), kind=kLoop, calls=%fused_computation.12 | loop fusion | flops 2 | bytes 16 | tf_op jit(solution)/shard_map/jit(clip)/min | solution.py:731
  20.7 0.0 collective-permute-done.2
  20.8 1.6 %collective-permute-start.3 = (bf16[8,128,128]{2,1,0:T(8,128)(2,1)S(1)}, bf16[8,128,128]{2,1,0:T(8,128)(2,1)S(1)}, u32[]{:S(2)}, u32[]{:S(2)}) collective-permute-start(bf16[8,128,128]{2,1,0:T(8,128)(2,1)S(1)} %pad_maximum_fusion.2), channel_id=1, source_target_pairs={{0,1},{1,0},{2,3},{3,2},{4,5},{5,4},{6,7},{7,6},{8,9},{9,8},{10,11... | collective-permute-start | bytes 786440 | tf_op jit(solution)/shard_map/ppermute | solution.py:186
  22.4 2.7 %collective-permute-done.7 = bf16[8,144,128]{2,1,0:T(8,128)(2,1)S(1)} collective-permute-done((bf16[8,144,128]{2,1,0:T(8,128)(2,1)S(1)}, bf16[8,144,128]{2,1,0:T(8,128)(2,1)S(1)}, u32[]{:S(2)}, u32[]{:S(2)}) %collective-permute-start.7) | collective-permute-done | bytes 294944 | tf_op jit(solution)/shard_map/ppermute | solution.py:186
  25.1 0.1 pad_maximum_fusion.near
  25.2 0.1 collective-permute-start.9
  25.3 0.0 copy-start.1
  25.3 1.0 %copy-done.1 = bf16[9,128,128]{2,1,0:T(8,128)(2,1)S(1)} copy-done((bf16[9,128,128]{2,1,0:T(8,128)(2,1)S(1)}, bf16[9,128,128]{2,1,0:T(8,128)(2,1)}, u32[]{:S(2)}) %copy-start.1) | copy-done | bytes 294936
  26.2 0.0 copy-start.3
  26.2 0.9 %copy-done.3 = bf16[128,512]{1,0:T(8,128)(2,1)S(1)} copy-done((bf16[128,512]{1,0:T(8,128)(2,1)S(1)}, bf16[128,512]{1,0:T(8,128)(2,1)}, u32[]{:S(2)}) %copy-start.3) | copy-done | bytes 131096
  27.1 0.0 copy-start.5
  27.1 0.8 %copy-done.5 = bf16[128,128]{1,0:T(8,128)(2,1)S(1)} copy-done((bf16[128,128]{1,0:T(8,128)(2,1)S(1)}, bf16[128,128]{1,0:T(8,128)(2,1)}, u32[]{:S(2)}) %copy-start.5) | copy-done | bytes 32792
  27.9 1.9 %shard_map.129 = (bf16[128,16,128]{2,1,0:T(8,128)(2,1)S(1)}, bf16[128,16,128]{2,1,0:T(8,128)(2,1)S(1)}, bf16[128,16,128]{2,1,0:T(8,128)(2,1)S(1)}, bf16[2,16,64,...) custom-call(bf16[16,144,128]{2,1,0:T(8,128)(2,1)S(1)} %pad_maximum_f, ...), custom_call_target="tpu_custom_call" | custom-call | flops 335544320 | bytes 4194304 | tf_op jit(solution)/shard_map/pallas_call | solution.py:743
  29.8 0.0 collective-permute-done.3
  29.8 0.6 %collective-permute-start.8 = (bf16[16,128,128]{2,1,0:T(8,128)(2,1)S(1)}, bf16[16,128,128]{2,1,0:T(8,128)(2,1)S(1)}, u32[]{:S(2)}, u32[]{:S(2)}) collective-permute-start(bf16[16,128,128]{2,1,0:T(8,128)(2,1)S(1)} %constant_dynamic-update-slice_fusion.cot_near), channel_id=1, source_target_pairs={{0,8},{8,0},{16,24},{24,16},{1,9},{9,1},{17,25},{25,17},{2,10},{10... | collective-permute-start | bytes 1572872 | tf_op jit(solution)/shard_map/ppermute | solution.py:186
  30.4 0.0 collective-permute-done.9.far
  30.4 0.0 copy-start
  30.4 1.0 %copy-done = bf16[9,128,128]{2,1,0:T(8,128)(2,1)S(1)} copy-done((bf16[9,128,128]{2,1,0:T(8,128)(2,1)S(1)}, bf16[9,128,128]{2,1,0:T(8,128)(2,1)}, u32[]{:S(2)}) %copy-start) | copy-done | bytes 294936
  31.4 0.0 copy-start.4
  31.4 0.9 %copy-done.4 = bf16[128,512]{1,0:T(8,128)(2,1)S(1)} copy-done((bf16[128,512]{1,0:T(8,128)(2,1)S(1)}, bf16[128,512]{1,0:T(8,128)(2,1)}, u32[]{:S(2)}) %copy-start.4) | copy-done | bytes 131096
  32.3 0.0 copy-start.6
  32.3 0.8 %copy-done.6 = bf16[128,128]{1,0:T(8,128)(2,1)S(1)} copy-done((bf16[128,128]{1,0:T(8,128)(2,1)S(1)}, bf16[128,128]{1,0:T(8,128)(2,1)}, u32[]{:S(2)}) %copy-start.6) | copy-done | bytes 32792
  33.0 0.0 copy-start.7
  33.0 0.8 %copy-done.7 = bf16[128,128]{1,0:T(8,128)(2,1)S(1)} copy-done((bf16[128,128]{1,0:T(8,128)(2,1)S(1)}, bf16[128,128]{1,0:T(8,128)(2,1)}, u32[]{:S(2)}) %copy-start.7) | copy-done | bytes 32792
  33.8 9.7 %shard_map.130 = (f32[3,80,64,128]{3,2,1,0:T(8,128)S(1)}, bf16[128,4096]{1,0:T(8,128)(2,1)S(1)}, f32[128,128]{1,0:T(8,128)S(1)}, f32[128,128]{1,0:T(8,128)S(1)}) custom-call(s32[2]{0:T(128)S(1)} %broadcast_clamp_fusion.dilations, bf16[16,144,128]{2,1,0:T(8,128)(2,1)S(1)} %collective-permute-done.9.far, bf16[128,512]{1,0:T(8,128)(2,1)S(1)} %copy-done.4, ...), custom_call_target="tpu_custom_call" | custom-call | flops 2013265920 | bytes 20971520 | tf_op jit(solution)/shard_map/pallas_call | solution.py:766
  43.5 0.0 collective-permute-done.8.cot_far
  43.5 0.0 copy-done.2
  43.5 9.2 %shard_map.131 = (bf16[128,128]{1,0:T(8,128)(2,1)}, bf16[128,128]{1,0:T(8,128)(2,1)}, f32[9,128,128]{2,1,0:T(8,128)}, f32[9,128,128]{2,1,0:T(8,128)}) custom-call(s32[2]{0:T(128)S(1)} %broadcast_clamp_fusion.dilations, bf16[16,128,128]{2,1,0:T(8,128)(2,1)S(1)} %constant_dynamic-update-slice_fusion.cot_near, ...), custom_call_target="tpu_custom_call" | custom-call | tf_op jit(solution)/shard_map/pallas_call | solution.py:791
  (8 shorter events, 0.2 us)
Async XLA Ops:
  0.6 42.9 %copy-start.2 = (bf16[9,128,128]{2,1,0:T(8,128)(2,1)S(1)}, bf16[9,128,128]{2,1,0:T(8,128)(2,1)}, u32[]{:S(2)}) copy-start(bf16[9,128,128]{2,1,0:T(8,128)(2,1)} %two.3) | copy-start | bytes 884740
  1.6 6.4 %collective-permute-start.4 = (bf16[1,144,128]{2,1,0:T(8,128)(2,1)S(1)}, bf16[1,144,128]{2,1,0:T(8,128)(2,1)S(1)}, u32[]{:S(2)}, u32[]{:S(2)}) collective-permute-start(bf16[1,144,128]{2,1,0:T(8,128)(2,1)S(1)} %fusion), channel_id=1, source_target_pairs={{0,4},{1,5},{2,6},{3,7},{4,0},{5,1},{6,2},{7,3},{8,12},{9,13},{10,... | collective-permute-start | bytes 110600 | tf_op jit(solution)/shard_map/ppermute | solution.py:186
  5.6 4.1 %collective-permute-start = (bf16[1,128,128]{2,1,0:T(8,128)(2,1)}, bf16[1,128,128]{2,1,0:T(8,128)(2,1)S(1)}, u32[]{:S(2)}, u32[]{:S(2)}) collective-permute-start(bf16[1,128,128]{2,1,0:T(8,128)(2,1)} %bitcast.10), channel_id=1, source_target_pairs={{0,16},{8,24},{16,0},{24,8},{1,17},{9,25},{17,1},{25,9},{2,18},{10... | collective-permute-start | bytes 98312 | tf_op jit(solution)/shard_map/ppermute | solution.py:186
  7.9 5.1 %collective-permute-start.5 = (bf16[2,144,128]{2,1,0:T(8,128)(2,1)S(1)}, bf16[2,144,128]{2,1,0:T(8,128)(2,1)S(1)}, u32[]{:S(2)}, u32[]{:S(2)}) collective-permute-start(bf16[2,144,128]{2,1,0:T(8,128)(2,1)S(1)} %pad_maximum_fusion.5), channel_id=1, source_target_pairs={{0,2},{1,3},{2,0},{3,1},{4,6},{5,7},{6,4},{7,5},{8,10},{9,11},{10,... | collective-permute-start | bytes 221192 | tf_op jit(solution)/shard_map/ppermute | solution.py:186
  9.7 5.2 %collective-permute-start.1 = (bf16[2,128,128]{2,1,0:T(8,128)(2,1)S(1)}, bf16[2,128,128]{2,1,0:T(8,128)(2,1)S(1)}, u32[]{:S(2)}, u32[]{:S(2)}) collective-permute-start(bf16[2,128,128]{2,1,0:T(8,128)(2,1)S(1)} %pad_maximum_fusion.6), channel_id=1, source_target_pairs={{0,4},{1,5},{2,6},{3,7},{4,0},{5,1},{6,2},{7,3},{8,12},{9,13},{10,... | collective-permute-start | bytes 196616 | tf_op jit(solution)/shard_map/ppermute | solution.py:186
  13.1 5.2 %collective-permute-start.6 = (bf16[4,144,128]{2,1,0:T(8,128)(2,1)S(1)}, bf16[4,144,128]{2,1,0:T(8,128)(2,1)S(1)}, u32[]{:S(2)}, u32[]{:S(2)}) collective-permute-start(bf16[4,144,128]{2,1,0:T(8,128)(2,1)S(1)} %pad_maximum_fusion.3), channel_id=1, source_target_pairs={{0,1},{1,0},{2,3},{3,2},{4,5},{5,4},{6,7},{7,6},{8,9},{9,8},{10,11... | collective-permute-start | bytes 442376 | tf_op jit(solution)/shard_map/ppermute | solution.py:186
  15.0 5.8 %collective-permute-start.2 = (bf16[4,128,128]{2,1,0:T(8,128)(2,1)S(1)}, bf16[4,128,128]{2,1,0:T(8,128)(2,1)S(1)}, u32[]{:S(2)}, u32[]{:S(2)}) collective-permute-start(bf16[4,128,128]{2,1,0:T(8,128)(2,1)S(1)} %pad_maximum_fusion.4), channel_id=1, source_target_pairs={{0,2},{1,3},{2,0},{3,1},{4,6},{5,7},{6,4},{7,5},{8,10},{9,11},{10,... | collective-permute-start | bytes 393224 | tf_op jit(solution)/shard_map/ppermute | solution.py:186
  18.3 6.8 %collective-permute-start.7 = (bf16[8,144,128]{2,1,0:T(8,128)(2,1)S(1)}, bf16[8,144,128]{2,1,0:T(8,128)(2,1)S(1)}, u32[]{:S(2)}, u32[]{:S(2)}) collective-permute-start(bf16[8,144,128]{2,1,0:T(8,128)(2,1)S(1)} %pad_maximum_fusion.1), channel_id=1, source_target_pairs={{0,16},{8,24},{16,0},{24,8},{1,17},{9,25},{17,1},{25,9},{2,18},{10... | collective-permute-start | bytes 884744 | tf_op jit(solution)/shard_map/ppermute | solution.py:186
  20.8 9.0 %collective-permute-start.3 = (bf16[8,128,128]{2,1,0:T(8,128)(2,1)S(1)}, bf16[8,128,128]{2,1,0:T(8,128)(2,1)S(1)}, u32[]{:S(2)}, u32[]{:S(2)}) collective-permute-start(bf16[8,128,128]{2,1,0:T(8,128)(2,1)S(1)} %pad_maximum_fusion.2), channel_id=1, source_target_pairs={{0,1},{1,0},{2,3},{3,2},{4,5},{5,4},{6,7},{7,6},{8,9},{9,8},{10,11... | collective-permute-start | bytes 786440 | tf_op jit(solution)/shard_map/ppermute | solution.py:186
  25.2 5.2 %collective-permute-start.9 = (bf16[16,144,128]{2,1,0:T(8,128)(2,1)S(1)}, bf16[16,144,128]{2,1,0:T(8,128)(2,1)S(1)}, u32[]{:S(2)}, u32[]{:S(2)}) collective-permute-start(bf16[16,144,128]{2,1,0:T(8,128)(2,1)S(1)} %pad_maximum_fusion.near), channel_id=1, source_target_pairs={{0,8},{8,0},{16,24},{24,16},{1,9},{9,1},{17,25},{25,17},{2,10},{10... | collective-permute-start | bytes 1769480 | tf_op jit(solution)/shard_map/ppermute | solution.py:186
  25.3 1.0 %copy-start.1 = (bf16[9,128,128]{2,1,0:T(8,128)(2,1)S(1)}, bf16[9,128,128]{2,1,0:T(8,128)(2,1)}, u32[]{:S(2)}) copy-start(bf16[9,128,128]{2,1,0:T(8,128)(2,1)} %two.3) | copy-start | bytes 884740
  26.2 0.9 %copy-start.3 = (bf16[128,512]{1,0:T(8,128)(2,1)S(1)}, bf16[128,512]{1,0:T(8,128)(2,1)}, u32[]{:S(2)}) copy-start(bf16[128,512]{1,0:T(8,128)(2,1)} %w_proj.3) | copy-start | bytes 393220
  27.1 0.8 %copy-start.5 = (bf16[128,128]{1,0:T(8,128)(2,1)S(1)}, bf16[128,128]{1,0:T(8,128)(2,1)}, u32[]{:S(2)}) copy-start(bf16[128,128]{1,0:T(8,128)(2,1)} %w_gate.3) | copy-start | bytes 98308
  29.8 13.7 %collective-permute-start.8 = (bf16[16,128,128]{2,1,0:T(8,128)(2,1)S(1)}, bf16[16,128,128]{2,1,0:T(8,128)(2,1)S(1)}, u32[]{:S(2)}, u32[]{:S(2)}) collective-permute-start(bf16[16,128,128]{2,1,0:T(8,128)(2,1)S(1)} %constant_dynamic-update-slice_fusion.cot_near), channel_id=1, source_target_pairs={{0,8},{8,0},{16,24},{24,16},{1,9},{9,1},{17,25},{25,17},{2,10},{10... | collective-permute-start | bytes 1572872 | tf_op jit(solution)/shard_map/ppermute | solution.py:186
  30.4 1.0 %copy-start = (bf16[9,128,128]{2,1,0:T(8,128)(2,1)S(1)}, bf16[9,128,128]{2,1,0:T(8,128)(2,1)}, u32[]{:S(2)}) copy-start(bf16[9,128,128]{2,1,0:T(8,128)(2,1)} %one.3) | copy-start | bytes 884740
  31.4 0.9 %copy-start.4 = (bf16[128,512]{1,0:T(8,128)(2,1)S(1)}, bf16[128,512]{1,0:T(8,128)(2,1)}, u32[]{:S(2)}) copy-start(bf16[128,512]{1,0:T(8,128)(2,1)} %w_proj.3) | copy-start | bytes 393220
  32.3 0.8 %copy-start.6 = (bf16[128,128]{1,0:T(8,128)(2,1)S(1)}, bf16[128,128]{1,0:T(8,128)(2,1)}, u32[]{:S(2)}) copy-start(bf16[128,128]{1,0:T(8,128)(2,1)} %w_gate.3) | copy-start | bytes 98308
  33.0 0.8 %copy-start.7 = (bf16[128,128]{1,0:T(8,128)(2,1)S(1)}, bf16[128,128]{1,0:T(8,128)(2,1)}, u32[]{:S(2)}) copy-start(bf16[128,128]{1,0:T(8,128)(2,1)} %w_out.1) | copy-start | bytes 98308

commit v14 on v13

--- a/solution.py
+++ b/solution.py
@@ -302,10 +302,12 @@
     contact,
     start,
     two_t,
+    two_copy,
     turned_left,
     turned_right,
 ):
     core = lax.axis_index("row") % 2
+    two_copy[...] = two[...]
     channels = two.shape[1]
     for tap in range(9):
         two_t[tap * channels : (tap + 1) * channels] = two[tap].T
@@ -728,23 +730,36 @@
     held = (above.astype(f32) + marks.astype(f32)).astype(bf16)[None]
     block = cotangent.reshape(1, pixels, channels)
     cot_held = lax.optimization_barrier(jnp.maximum(block, jnp.finfo(bf16).min))
-    rates = jnp.clip(dilations, 1, DMAX)
+    def read(*weights):
+        return [jnp.maximum(weight, jnp.finfo(bf16).min) for weight in weights]
+
+    dense, kernels = (dilations, w_proj, w_gate, w_out), (conv_one, conv_two)
     for step in range(len(rounds) - 1):
         other = exchange(held, rounds[step])
         cot_other = exchange(cot_held if step else block, cot_rounds[step])
-        held = lax.optimization_barrier(jnp.concatenate([held, other], axis=0))
+        held = jnp.concatenate([held, other], axis=0)
+        if step == len(rounds) - 4:
+            cot_other, dense = lax.optimization_barrier((cot_other, dense))
+            rates = jnp.clip(dense[0], 1, DMAX)
+            dense = read(*dense[1:])
+        if step == len(rounds) - 3:
+            cot_other, kernels = lax.optimization_barrier((cot_other, kernels))
+            kernels = read(*kernels)
         if step < len(rounds) - 2:
-            cot_held = jnp.concatenate([cot_held, cot_other], axis=0)
-            if step == len(rounds) - 3:
-                cot_held, rates = lax.optimization_barrier((cot_held, rates))
-            else:
-                cot_held = lax.optimization_barrier(cot_held)
+            held = lax.optimization_barrier(held)
+            cot_held = lax.optimization_barrier(jnp.concatenate([cot_held, cot_other], axis=0))
+        else:
+            held, rates, dense, kernels = lax.optimization_barrier((held, rates, dense, kernels))
+    w_proj, w_gate, w_out = dense
+    conv_one, conv_two = kernels
     near, far = held, exchange(held, rounds[-1])
-    *near_parts, two_t = pl.pallas_call(
+    *near_parts, two_t, two = pl.pallas_call(
         functools.partial(near_kernel, plan),
         in_specs=[in_vmem] * 4,
-        out_specs=[in_vmem] * 7,
-        out_shape=shapes(*halves, ((9 * channels, channels), bf16)),
+        out_specs=[in_vmem] * 8,
+        out_shape=shapes(
+            *halves, ((9 * channels, channels), bf16), ((9, channels, channels), bf16)
+        ),
         scratch_shapes=[turned] * 2,
         compiler_params=pltpu.CompilerParams(vmem_limit_bytes=VMEM_LIMIT // 3),
         cost_estimate=pl.CostEstimate(
@@ -775,9 +790,9 @@
         + [pltpu.VMEM(rows, f32), padded],
         compiler_params=pltpu.CompilerParams(vmem_limit_bytes=FORWARD_VMEM),
         cost_estimate=pl.CostEstimate(
-            flops=tokens * tokens * channels * 30 * hidden,
+            flops=tokens * tokens * channels * 40 * hidden,
             bytes_accessed=40 * tokens * tokens * channels,
-            transcendentals=2 * tokens * tokens * channels,
+            transcendentals=4 * tokens * tokens * channels,
         ),
     )(
         rates,
@@ -807,7 +822,7 @@
         cot_near,
         cot_far,
         conv_one,
-        conv_two,
+        two,
         two_t,
         *held,
     )
@@ -822,7 +837,7 @@
     whole = (tokens + 2 * DMAX) ** 2 * channels
     return (
         powers
-        and row_count * col_count >= 8
+        and row_count * col_count >= 16
         and height * breadth == channels == w_out.shape[0]
         and breadth == 8
         and row_count // 2 * tokens == channels

time: 53.4 us -> 54.1 us (1.013)
  local copies, waits for them, and re-layouts: 6.06 us -> 0 us
  waiting for transfers between devices: 5.32 us -> 10.6 us
  other arithmetic: 2.51 us -> 5.33 us
  starting transfers between devices: 17.3 us -> 16.2 us
    unnamed x17 -> x0, local copies, waits for them, and re-layouts: 6.02 us -> none
    ppermute x10, waiting for transfers between devices: 5.32 us -> 10.6 us  [exchange(): lax.ppermute(held, axis, [(i, i ^ distance) for i in range(lax.axis_size(...]
    max x0 -> x3, other arithmetic: none -> 2.8 us  [read(): return [jnp.maximum(weight, jnp.finfo(bf16).min) for weight in weights]]
    ppermute x10, starting transfers between devices: 17.3 us -> 16.2 us  [exchange(): lax.ppermute(held, axis, [(i, i ^ distance) for i in range(lax.axis_size(...]
  transfers between devices with their start and end apart: 10 -> 10, of which waited for: 5 -> 4; matrix products, arithmetic and copies ran while one was open for 3% -> 8% of each run, Pallas kernels for 22% -> 22%
where the time goes in v14:
time: 54.1 us; the launch traced here: 53.8 us
  Pallas kernels  20.8 us (38%)
  starting transfers between devices  16.2 us (30%)
  waiting for transfers between devices  10.6 us (20%)
  other arithmetic  5.33 us (10%)
  between operations  0.89 us (2%)
    ppermute x10, starting transfers between devices, exchange(): lax.ppermute(held, axis, [(i, i ^ distance) for i in range(lax.axis_size(...  16.2 us
    ppermute x10, waiting for transfers between devices, exchange(): lax.ppermute(held, axis, [(i, i ^ distance) for i in range(lax.axis_size(...  10.6 us
    pallas_call x1, Pallas kernels, replicated(): pl.pallas_call(functools.partial(forward_kernel, plan), in_specs=[in_smem...  9.7 us
    pallas_call x1, Pallas kernels, replicated(): pl.pallas_call(functools.partial(backward_kernel, plan), in_specs=[in_sme...  9.21 us
    max x3, other arithmetic, read(): return [jnp.maximum(weight, jnp.finfo(bf16).min) for weight in weights]  2.8 us
    pallas_call x1, Pallas kernels, replicated(): pl.pallas_call(functools.partial(near_kernel, plan), in_specs=[in_vmem] *...  1.92 us
  transfers between devices with their start and end apart: 10, of which 4 were waited for; matrix products, arithmetic and copies ran while one was open for 8% of the time, Pallas kernels for 22%

profile of v14, /device:TPU:0, one launch (start us, length us, event | category | flops | bytes accessed | tf_op | source)
XLA Modules:
  0.0 53.8 jit_solution(18103595505252903633)
XLA Ops:
  0.6 0.9 %fusion = bf16[1,144,128]{2,1,0:T(8,128)(2,1)S(1)} fusion(s32[8,16]{1,0:T(8,128)} %bitcast.11, s32[8,16]{1,0:T(8,128)} %bitcast.12, bf16[128,128]{1,0:T(8,128)(2,1)} %bitcast.9), kind=kLoop, calls=%fused_computation.12 | loop fusion | flops 92160 | bytes 70656 | tf_op jit(solution)/shard_map/broadcast_in_dim | solution.py:730
  1.5 4.0 %collective-permute-start = (bf16[1,144,128]{2,1,0:T(8,128)(2,1)S(1)}, bf16[1,144,128]{2,1,0:T(8,128)(2,1)S(1)}, u32[]{:S(2)}, u32[]{:S(2)}) collective-permute-start(bf16[1,144,128]{2,1,0:T(8,128)(2,1)S(1)} %fusion), channel_id=1, source_target_pairs={{0,4},{1,5},{2,6},{3,7},{4,0},{5,1},{6,2},{7,3},{8,12},{9,13},{10,... | collective-permute-start | bytes 110600 | tf_op jit(solution)/shard_map/ppermute | solution.py:186
  5.5 1.5 %collective-permute-start.4 = (bf16[1,128,128]{2,1,0:T(8,128)(2,1)}, bf16[1,128,128]{2,1,0:T(8,128)(2,1)S(1)}, u32[]{:S(2)}, u32[]{:S(2)}) collective-permute-start(bf16[1,128,128]{2,1,0:T(8,128)(2,1)} %bitcast.10), channel_id=1, source_target_pairs={{0,16},{8,24},{16,0},{24,8},{1,17},{9,25},{17,1},{25,9},{2,18},{10... | collective-permute-start | bytes 98312 | tf_op jit(solution)/shard_map/ppermute | solution.py:186
  7.0 0.8 %broadcast_maximum_fusion.5 = bf16[1,128,128]{2,1,0:T(8,128)(2,1)S(1)} fusion(bf16[16,8,128]{2,1,0:T(8,128)(2,1)} %param.19), kind=kLoop, calls=%fused_computation.15 | loop fusion | flops 16384 | bytes 65536 | tf_op jit(solution)/shard_map/max | solution.py:732
  7.8 1.8 %collective-permute-done.4 = bf16[1,128,128]{2,1,0:T(8,128)(2,1)S(1)} collective-permute-done((bf16[1,128,128]{2,1,0:T(8,128)(2,1)}, bf16[1,128,128]{2,1,0:T(8,128)(2,1)S(1)}, u32[]{:S(2)}, u32[]{:S(2)}) %collective-permute-start.4) | collective-permute-done | bytes 32800 | tf_op jit(solution)/shard_map/ppermute | solution.py:186
  9.7 0.1 collective-permute-start.5
  9.8 0.0 collective-permute-done
  9.8 1.9 %collective-permute-start.1 = (bf16[2,144,128]{2,1,0:T(8,128)(2,1)S(1)}, bf16[2,144,128]{2,1,0:T(8,128)(2,1)S(1)}, u32[]{:S(2)}, u32[]{:S(2)}) collective-permute-start(bf16[2,144,128]{2,1,0:T(8,128)(2,1)S(1)} %pad_maximum_fusion.6), channel_id=1, source_target_pairs={{0,2},{1,3},{2,0},{3,1},{4,6},{5,7},{6,4},{7,5},{8,10},{9,11},{10,... | collective-permute-start | bytes 221192 | tf_op jit(solution)/shard_map/ppermute | solution.py:186
  11.7 3.2 %collective-permute-done.5 = bf16[2,128,128]{2,1,0:T(8,128)(2,1)S(1)} collective-permute-done((bf16[2,128,128]{2,1,0:T(8,128)(2,1)S(1)}, bf16[2,128,128]{2,1,0:T(8,128)(2,1)S(1)}, u32[]{:S(2)}, u32[]{:S(2)}) %collective-permute-start.5) | collective-permute-done | bytes 65568 | tf_op jit(solution)/shard_map/ppermute | solution.py:186
  15.0 2.3 %collective-permute-start.6 = (bf16[4,128,128]{2,1,0:T(8,128)(2,1)S(1)}, bf16[4,128,128]{2,1,0:T(8,128)(2,1)S(1)}, u32[]{:S(2)}, u32[]{:S(2)}) collective-permute-start(bf16[4,128,128]{2,1,0:T(8,128)(2,1)S(1)} %pad_maximum_fusion.5), channel_id=1, source_target_pairs={{0,2},{1,3},{2,0},{3,1},{4,6},{5,7},{6,4},{7,5},{8,10},{9,11},{10,... | collective-permute-start | bytes 393224 | tf_op jit(solution)/shard_map/ppermute | solution.py:186
  17.3 0.9 %broadcast_maximum_fusion.2.w_proj = bf16[128,512]{1,0:T(8,128)(2,1)S(1)} fusion(bf16[128,512]{1,0:T(8,128)(2,1)} %param.14), kind=kLoop, calls=%fused_computation.11 | loop fusion | flops 65536 | bytes 262144 | tf_op jit(solution)/shard_map/max | solution.py:734
  18.2 0.8 %broadcast_maximum_fusion.3 = (bf16[128,128]{1,0:T(8,128)(2,1)S(1)}, bf16[128,128]{1,0:T(8,128)(2,1)S(1)}) fusion(bf16[128,128]{1,0:T(8,128)(2,1)} %param.16, bf16[128,128]{1,0:T(8,128)(2,1)} %param.15), kind=kLoop, calls=%fused_computation.13 | loop fusion | flops 32768 | bytes 131072 | tf_op jit(solution)/shard_map/max | solution.py:734
  19.0 0.0 collective-permute-done.1
  19.0 1.6 %collective-permute-start.2 = (bf16[4,144,128]{2,1,0:T(8,128)(2,1)S(1)}, bf16[4,144,128]{2,1,0:T(8,128)(2,1)S(1)}, u32[]{:S(2)}, u32[]{:S(2)}) collective-permute-start(bf16[4,144,128]{2,1,0:T(8,128)(2,1)S(1)} %pad_maximum_fusion.4), channel_id=1, source_target_pairs={{0,1},{1,0},{2,3},{3,2},{4,5},{5,4},{6,7},{7,6},{8,9},{9,8},{10,11... | collective-permute-start | bytes 442376 | tf_op jit(solution)/shard_map/ppermute | solution.py:186
  20.6 0.7 %broadcast_clamp_fusion.dilations = s32[2]{0:T(128)S(1)} fusion(s32[2]{0:T(128)} %param.13), kind=kLoop, calls=%fused_computation.16 | loop fusion | flops 2 | bytes 16 | tf_op jit(solution)/shard_map/jit(clip)/min | solution.py:743
  21.2 0.0 collective-permute-done.6
  21.2 3.5 %collective-permute-done.2 = bf16[4,144,128]{2,1,0:T(8,128)(2,1)S(1)} collective-permute-done((bf16[4,144,128]{2,1,0:T(8,128)(2,1)S(1)}, bf16[4,144,128]{2,1,0:T(8,128)(2,1)S(1)}, u32[]{:S(2)}, u32[]{:S(2)}) %collective-permute-start.2) | collective-permute-done | bytes 147488 | tf_op jit(solution)/shard_map/ppermute | solution.py:186
  24.8 2.5 %collective-permute-start.3 = (bf16[8,144,128]{2,1,0:T(8,128)(2,1)S(1)}, bf16[8,144,128]{2,1,0:T(8,128)(2,1)S(1)}, u32[]{:S(2)}, u32[]{:S(2)}) collective-permute-start(bf16[8,144,128]{2,1,0:T(8,128)(2,1)S(1)} %pad_maximum_fusion.2), channel_id=1, source_target_pairs={{0,16},{8,24},{16,0},{24,8},{1,17},{9,25},{17,1},{25,9},{2,18},{10... | collective-permute-start | bytes 884744 | tf_op jit(solution)/shard_map/ppermute | solution.py:186
  27.4 1.6 %collective-permute-start.7 = (bf16[8,128,128]{2,1,0:T(8,128)(2,1)S(1)}, bf16[8,128,128]{2,1,0:T(8,128)(2,1)S(1)}, u32[]{:S(2)}, u32[]{:S(2)}) collective-permute-start(bf16[8,128,128]{2,1,0:T(8,128)(2,1)S(1)} %pad_maximum_fusion.3), channel_id=1, source_target_pairs={{0,1},{1,0},{2,3},{3,2},{4,5},{5,4},{6,7},{7,6},{8,9},{9,8},{10,11... | collective-permute-start | bytes 786440 | tf_op jit(solution)/shard_map/ppermute | solution.py:186
  28.9 1.1 %broadcast_maximum_fusion = (bf16[9,128,128]{2,1,0:T(8,128)(2,1)S(1)}, bf16[9,128,128]{2,1,0:T(8,128)(2,1)S(1)}) fusion(bf16[9,128,128]{2,1,0:T(8,128)(2,1)} %param.18, bf16[9,128,128]{2,1,0:T(8,128)(2,1)} %param.17), kind=kLoop, calls=%fused_computation.5 | loop fusion | flops 294912 | bytes 1179648 | tf_op jit(solution)/shard_map/max | solution.py:734
  30.0 2.0 %collective-permute-done.3 = bf16[8,144,128]{2,1,0:T(8,128)(2,1)S(1)} collective-permute-done((bf16[8,144,128]{2,1,0:T(8,128)(2,1)S(1)}, bf16[8,144,128]{2,1,0:T(8,128)(2,1)S(1)}, u32[]{:S(2)}, u32[]{:S(2)}) %collective-permute-start.3) | collective-permute-done | bytes 294944 | tf_op jit(solution)/shard_map/ppermute | solution.py:186
  32.0 0.1 pad_maximum_fusion.near
  32.1 0.1 collective-permute-start.9
  32.2 1.9 %shard_map.129 = (bf16[128,16,128]{2,1,0:T(8,128)(2,1)S(1)}, bf16[128,16,128]{2,1,0:T(8,128)(2,1)S(1)}, bf16[128,16,128]{2,1,0:T(8,128)(2,1)S(1)}, bf16[2,16,64,...) custom-call(bf16[16,144,128]{2,1,0:T(8,128)(2,1)S(1)} %pad_maximum_f, ...), custom_call_target="tpu_custom_call" | custom-call | flops 335544320 | bytes 4194304 | tf_op jit(solution)/shard_map/pallas_call | solution.py:756
  34.1 0.0 collective-permute-done.7
  34.2 0.6 %collective-permute-start.8 = (bf16[16,128,128]{2,1,0:T(8,128)(2,1)S(1)}, bf16[16,128,128]{2,1,0:T(8,128)(2,1)S(1)}, u32[]{:S(2)}, u32[]{:S(2)}) collective-permute-start(bf16[16,128,128]{2,1,0:T(8,128)(2,1)S(1)} %pad_maximum_fusion.1.cot_near), channel_id=1, source_target_pairs={{0,8},{8,0},{16,24},{24,16},{1,9},{9,1},{17,25},{25,17},{2,10},{10... | collective-permute-start | bytes 1572872 | tf_op jit(solution)/shard_map/ppermute | solution.py:186
  34.7 0.0 collective-permute-done.9.far
  34.7 9.7 %shard_map.130 = (f32[3,80,64,128]{3,2,1,0:T(8,128)S(1)}, bf16[128,4096]{1,0:T(8,128)(2,1)S(1)}, f32[128,128]{1,0:T(8,128)S(1)}, f32[128,128]{1,0:T(8,128)S(1)}) custom-call(s32[2]{0:T(128)S(1)} %broadcast_clamp_fusion.dilations, bf16[16,144,128]{2,1,0:T(8,128)(2,1)S(1)} %collective-permute-done.9.far, bf16[128,512]{1,0:T(8,128)(2,1)S(1)} %broadcast_maximum_fusion.2.w_proj, ...), custom_call_target="tpu_custom_call" | custom-call | flops 2684354560 | bytes 20971520 | tf_op jit(solution)/shard_map/pallas_call | solution.py:781
  44.4 0.0 collective-permute-done.8.cot_far
  44.4 9.2 %shard_map.131 = (bf16[128,128]{1,0:T(8,128)(2,1)}, bf16[128,128]{1,0:T(8,128)(2,1)}, f32[9,128,128]{2,1,0:T(8,128)}, f32[9,128,128]{2,1,0:T(8,128)}) custom-call(s32[2]{0:T(128)S(1)} %broadcast_clamp_fusion.dilations, bf16[16,128,128]{2,1,0:T(8,128)(2,1)S(1)} %pad_maximum_fusion.1.cot_near, bf16[16,128,128]{2,1,0:T(8,128)(2,1)S(1)} %collective-permute-done.8.cot_far, ...), custom_call_target="tpu_custom_call" | custom-call | tf_op jit(solution)/shard_map/pallas_call | solution.py:806
  (7 shorter events, 0.1 us)
Async XLA Ops:
  1.5 8.3 %collective-permute-start = (bf16[1,144,128]{2,1,0:T(8,128)(2,1)S(1)}, bf16[1,144,128]{2,1,0:T(8,128)(2,1)S(1)}, u32[]{:S(2)}, u32[]{:S(2)}) collective-permute-start(bf16[1,144,128]{2,1,0:T(8,128)(2,1)S(1)} %fusion), channel_id=1, source_target_pairs={{0,4},{1,5},{2,6},{3,7},{4,0},{5,1},{6,2},{7,3},{8,12},{9,13},{10,... | collective-permute-start | bytes 110600 | tf_op jit(solution)/shard_map/ppermute | solution.py:186
  5.5 4.1 %collective-permute-start.4 = (bf16[1,128,128]{2,1,0:T(8,128)(2,1)}, bf16[1,128,128]{2,1,0:T(8,128)(2,1)S(1)}, u32[]{:S(2)}, u32[]{:S(2)}) collective-permute-start(bf16[1,128,128]{2,1,0:T(8,128)(2,1)} %bitcast.10), channel_id=1, source_target_pairs={{0,16},{8,24},{16,0},{24,8},{1,17},{9,25},{17,1},{25,9},{2,18},{10... | collective-permute-start | bytes 98312 | tf_op jit(solution)/shard_map/ppermute | solution.py:186
  9.7 5.3 %collective-permute-start.5 = (bf16[2,128,128]{2,1,0:T(8,128)(2,1)S(1)}, bf16[2,128,128]{2,1,0:T(8,128)(2,1)S(1)}, u32[]{:S(2)}, u32[]{:S(2)}) collective-permute-start(bf16[2,128,128]{2,1,0:T(8,128)(2,1)S(1)} %pad_maximum_fusion.7), channel_id=1, source_target_pairs={{0,4},{1,5},{2,6},{3,7},{4,0},{5,1},{6,2},{7,3},{8,12},{9,13},{10,... | collective-permute-start | bytes 196616 | tf_op jit(solution)/shard_map/ppermute | solution.py:186
  9.8 9.1 %collective-permute-start.1 = (bf16[2,144,128]{2,1,0:T(8,128)(2,1)S(1)}, bf16[2,144,128]{2,1,0:T(8,128)(2,1)S(1)}, u32[]{:S(2)}, u32[]{:S(2)}) collective-permute-start(bf16[2,144,128]{2,1,0:T(8,128)(2,1)S(1)} %pad_maximum_fusion.6), channel_id=1, source_target_pairs={{0,2},{1,3},{2,0},{3,1},{4,6},{5,7},{6,4},{7,5},{8,10},{9,11},{10,... | collective-permute-start | bytes 221192 | tf_op jit(solution)/shard_map/ppermute | solution.py:186
  15.0 6.3 %collective-permute-start.6 = (bf16[4,128,128]{2,1,0:T(8,128)(2,1)S(1)}, bf16[4,128,128]{2,1,0:T(8,128)(2,1)S(1)}, u32[]{:S(2)}, u32[]{:S(2)}) collective-permute-start(bf16[4,128,128]{2,1,0:T(8,128)(2,1)S(1)} %pad_maximum_fusion.5), channel_id=1, source_target_pairs={{0,2},{1,3},{2,0},{3,1},{4,6},{5,7},{6,4},{7,5},{8,10},{9,11},{10,... | collective-permute-start | bytes 393224 | tf_op jit(solution)/shard_map/ppermute | solution.py:186
  19.0 5.8 %collective-permute-start.2 = (bf16[4,144,128]{2,1,0:T(8,128)(2,1)S(1)}, bf16[4,144,128]{2,1,0:T(8,128)(2,1)S(1)}, u32[]{:S(2)}, u32[]{:S(2)}) collective-permute-start(bf16[4,144,128]{2,1,0:T(8,128)(2,1)S(1)} %pad_maximum_fusion.4), channel_id=1, source_target_pairs={{0,1},{1,0},{2,3},{3,2},{4,5},{5,4},{6,7},{7,6},{8,9},{9,8},{10,11... | collective-permute-start | bytes 442376 | tf_op jit(solution)/shard_map/ppermute | solution.py:186
  24.8 7.2 %collective-permute-start.3 = (bf16[8,144,128]{2,1,0:T(8,128)(2,1)S(1)}, bf16[8,144,128]{2,1,0:T(8,128)(2,1)S(1)}, u32[]{:S(2)}, u32[]{:S(2)}) collective-permute-start(bf16[8,144,128]{2,1,0:T(8,128)(2,1)S(1)} %pad_maximum_fusion.2), channel_id=1, source_target_pairs={{0,16},{8,24},{16,0},{24,8},{1,17},{9,25},{17,1},{25,9},{2,18},{10... | collective-permute-start | bytes 884744 | tf_op jit(solution)/shard_map/ppermute | solution.py:186
  27.4 6.7 %collective-permute-start.7 = (bf16[8,128,128]{2,1,0:T(8,128)(2,1)S(1)}, bf16[8,128,128]{2,1,0:T(8,128)(2,1)S(1)}, u32[]{:S(2)}, u32[]{:S(2)}) collective-permute-start(bf16[8,128,128]{2,1,0:T(8,128)(2,1)S(1)} %pad_maximum_fusion.3), channel_id=1, source_target_pairs={{0,1},{1,0},{2,3},{3,2},{4,5},{5,4},{6,7},{7,6},{8,9},{9,8},{10,11... | collective-permute-start | bytes 786440 | tf_op jit(solution)/shard_map/ppermute | solution.py:186
  32.1 2.6 %collective-permute-start.9 = (bf16[16,144,128]{2,1,0:T(8,128)(2,1)S(1)}, bf16[16,144,128]{2,1,0:T(8,128)(2,1)S(1)}, u32[]{:S(2)}, u32[]{:S(2)}) collective-permute-start(bf16[16,144,128]{2,1,0:T(8,128)(2,1)S(1)} %pad_maximum_fusion.near), channel_id=1, source_target_pairs={{0,8},{8,0},{16,24},{24,16},{1,9},{9,1},{17,25},{25,17},{2,10},{10... | collective-permute-start | bytes 1769480 | tf_op jit(solution)/shard_map/ppermute | solution.py:186
  34.2 10.3 %collective-permute-start.8 = (bf16[16,128,128]{2,1,0:T(8,128)(2,1)S(1)}, bf16[16,128,128]{2,1,0:T(8,128)(2,1)S(1)}, u32[]{:S(2)}, u32[]{:S(2)}) collective-permute-start(bf16[16,128,128]{2,1,0:T(8,128)(2,1)S(1)} %pad_maximum_fusion.1.cot_near), channel_id=1, source_target_pairs={{0,8},{8,0},{16,24},{24,16},{1,9},{9,1},{17,25},{25,17},{2,10},{10... | collective-permute-start | bytes 1572872 | tf_op jit(solution)/shard_map/ppermute | solution.py:186

commit v15 on v13

--- a/solution.py
+++ b/solution.py
@@ -302,10 +302,12 @@
     contact,
     start,
     two_t,
+    two_copy,
     turned_left,
     turned_right,
 ):
     core = lax.axis_index("row") % 2
+    two_copy[...] = two[...]
     channels = two.shape[1]
     for tap in range(9):
         two_t[tap * channels : (tap + 1) * channels] = two[tap].T
@@ -428,7 +430,7 @@
     near_gating,
     near_contact,
     near_start,
-    strips,
+    pre,
     flipped,
     mine,
     own_contact,
@@ -444,6 +446,7 @@
     normed,
     updated,
     field,
+    strips,
 ):
     _, _, height, breadth, tokens = plan
     hidden, channels = w_out.shape
@@ -544,6 +547,12 @@
         if step >= 2:
             first_conv(step - 2)
 
+    def add_taps(step, carry):
+        pre[pl.ds(step * chunk, chunk)] = row_taps(strips, step * chunk, chunk, rate_one)
+        return carry
+
+    lax.fori_loop(0, tokens // chunk, add_taps, 0)
+
     cols = pl.ds(pl.multiple_of(col_place * breadth, breadth), breadth)
     mine[...] = updated[row_place // 2, :, cols, :].reshape(pixels, channels)
     marks = near_contact[row_place // 2].astype(jnp.float32)
@@ -561,7 +570,7 @@
     one,
     two,
     two_t,
-    strips,
+    pre,
     flipped,
     mine,
     own_contact,
@@ -620,11 +629,11 @@
     def back_two(step):
         first = step * chunk
         rows = pl.ds(DMAX + first, chunk)
-        pre = row_taps(strips, first, chunk, rate_one)
-        sigma = sigmoid(pre)
-        second_in = pre * sigma
+        before_act = pre[pl.ds(first, chunk)]
+        sigma = sigmoid(before_act)
+        second_in = before_act * sigma
         second[rows, inside, :] = second_in
-        factor = sigma * (1.0 + pre * (1.0 - sigma))
+        factor = sigma * (1.0 + before_act * (1.0 - sigma))
         turned = second_in.reshape(size, channels).astype(jnp.bfloat16).T
         shifted = taps(wide_cot, first, chunk, -rate_two)
         before = matmul_by_rows(shifted, two_t[...]).reshape(chunk, tokens, channels)
@@ -740,11 +749,13 @@
             else:
                 cot_held = lax.optimization_barrier(cot_held)
     near, far = held, exchange(held, rounds[-1])
-    *near_parts, two_t = pl.pallas_call(
+    *near_parts, two_t, two = pl.pallas_call(
         functools.partial(near_kernel, plan),
         in_specs=[in_vmem] * 4,
-        out_specs=[in_vmem] * 7,
-        out_shape=shapes(*halves, ((9 * channels, channels), bf16)),
+        out_specs=[in_vmem] * 8,
+        out_shape=shapes(
+            *halves, ((9 * channels, channels), bf16), ((9, channels, channels), bf16)
+        ),
         scratch_shapes=[turned] * 2,
         compiler_params=pltpu.CompilerParams(vmem_limit_bytes=VMEM_LIMIT // 3),
         cost_estimate=pl.CostEstimate(
@@ -767,17 +778,18 @@
         functools.partial(forward_kernel, plan),
         in_specs=[in_smem] + [in_vmem] * 11,
         out_specs=[in_vmem] * 4,
-        out_shape=shapes(((3, line, tokens, channels), f32), flat, stat, stat),
+        out_shape=shapes(((tokens, tokens, channels), f32), flat, stat, stat),
         scratch_shapes=[pltpu.VMEM(*side), both, both, alone, alone, alone]
         + [turned] * 2
         + [pltpu.VMEM((hidden * (2 * height + PITCH), chips * tokens), f32)]
         + [pltpu.VMEM((2 * height // 8, chips, 8, tokens, hidden), bf16)]
-        + [pltpu.VMEM(rows, f32), padded],
+        + [pltpu.VMEM(rows, f32), padded]
+        + [pltpu.VMEM((3, line, tokens, channels), f32)],
         compiler_params=pltpu.CompilerParams(vmem_limit_bytes=FORWARD_VMEM),
         cost_estimate=pl.CostEstimate(
-            flops=tokens * tokens * channels * 30 * hidden,
+            flops=tokens * tokens * channels * 40 * hidden,
             bytes_accessed=40 * tokens * tokens * channels,
-            transcendentals=2 * tokens * tokens * channels,
+            transcendentals=4 * tokens * tokens * channels,
         ),
     )(
         rates,
@@ -807,7 +819,7 @@
         cot_near,
         cot_far,
         conv_one,
-        conv_two,
+        two,
         two_t,
         *held,
     )

time: 53.4 us -> 47.5 us (0.89)
  local copies, waits for them, and re-layouts: 6.06 us -> 0.08 us
    unnamed x17 -> x11, local copies, waits for them, and re-layouts: 6.02 us -> 0.04 us
  transfers between devices with their start and end apart: 10 -> 10, of which waited for: 5 -> 5; matrix products, arithmetic and copies ran while one was open for 3% -> 4% of each run, Pallas kernels for 22% -> 25%
where the time goes in v15:
time: 47.5 us; the launch traced here: 47.2 us
  Pallas kernels  21.1 us (44%)
  starting transfers between devices  17.3 us (36%)
  waiting for transfers between devices  5.31 us (11%)
  other arithmetic  2.52 us (5%)
  between operations  0.94 us (2%)
    ppermute x10, starting transfers between devices, exchange(): lax.ppermute(held, axis, [(i, i ^ distance) for i in range(lax.axis_size(...  17.3 us
    pallas_call x1, Pallas kernels, replicated(): pl.pallas_call(functools.partial(forward_kernel, plan), in_specs=[in_smem...  10 us
    pallas_call x1, Pallas kernels, replicated(): pl.pallas_call(functools.partial(backward_kernel, plan), in_specs=[in_sme...  9.16 us
    ppermute x10, waiting for transfers between devices, exchange(): lax.ppermute(held, axis, [(i, i ^ distance) for i in range(lax.axis_size(...  5.31 us
    pallas_call x1, Pallas kernels, replicated(): pl.pallas_call(functools.partial(near_kernel, plan), in_specs=[in_vmem] *...  1.91 us
  transfers between devices with their start and end apart: 10, of which 5 were waited for; matrix products, arithmetic and copies ran while one was open for 4% of the time, Pallas kernels for 25%

profile of v15, /device:TPU:0, one launch (start us, length us, event | category | flops | bytes accessed | tf_op | source)
XLA Modules:
  0.0 47.2 jit_solution(3697554404871449377)
XLA Ops:
  0.6 0.0 copy-start.2
  0.6 0.0 copy-start.3
  0.7 0.0 copy-start.1
  0.7 0.9 %fusion = bf16[1,144,128]{2,1,0:T(8,128)(2,1)S(1)} fusion(s32[8,16]{1,0:T(8,128)} %bitcast.11, s32[8,16]{1,0:T(8,128)} %bitcast.12, bf16[128,128]{1,0:T(8,128)(2,1)} %bitcast.9), kind=kLoop, calls=%fused_computation.8 | loop fusion | flops 92160 | bytes 70656 | tf_op jit(solution)/shard_map/broadcast_in_dim | solution.py:737
  1.6 4.0 %collective-permute-start.4 = (bf16[1,144,128]{2,1,0:T(8,128)(2,1)S(1)}, bf16[1,144,128]{2,1,0:T(8,128)(2,1)S(1)}, u32[]{:S(2)}, u32[]{:S(2)}) collective-permute-start(bf16[1,144,128]{2,1,0:T(8,128)(2,1)S(1)} %fusion), channel_id=1, source_target_pairs={{0,4},{1,5},{2,6},{3,7},{4,0},{5,1},{6,2},{7,3},{8,12},{9,13},{10,... | collective-permute-start | bytes 110600 | tf_op jit(solution)/shard_map/ppermute | solution.py:186
  5.6 1.5 %collective-permute-start = (bf16[1,128,128]{2,1,0:T(8,128)(2,1)}, bf16[1,128,128]{2,1,0:T(8,128)(2,1)S(1)}, u32[]{:S(2)}, u32[]{:S(2)}) collective-permute-start(bf16[1,128,128]{2,1,0:T(8,128)(2,1)} %bitcast.10), channel_id=1, source_target_pairs={{0,16},{8,24},{16,0},{24,8},{1,17},{9,25},{17,1},{25,9},{2,18},{10... | collective-permute-start | bytes 98312 | tf_op jit(solution)/shard_map/ppermute | solution.py:186
  7.1 0.8 %broadcast_maximum_fusion = bf16[1,128,128]{2,1,0:T(8,128)(2,1)S(1)} fusion(bf16[16,8,128]{2,1,0:T(8,128)(2,1)} %param.19), kind=kLoop, calls=%fused_computation.9 | loop fusion | flops 16384 | bytes 65536 | tf_op jit(solution)/shard_map/max | solution.py:739
  7.9 0.0 collective-permute-done.4
  8.0 1.6 %collective-permute-start.5 = (bf16[2,144,128]{2,1,0:T(8,128)(2,1)S(1)}, bf16[2,144,128]{2,1,0:T(8,128)(2,1)S(1)}, u32[]{:S(2)}, u32[]{:S(2)}) collective-permute-start(bf16[2,144,128]{2,1,0:T(8,128)(2,1)S(1)} %pad_maximum_fusion.5), channel_id=1, source_target_pairs={{0,2},{1,3},{2,0},{3,1},{4,6},{5,7},{6,4},{7,5},{8,10},{9,11},{10,... | collective-permute-start | bytes 221192 | tf_op jit(solution)/shard_map/ppermute | solution.py:186
  9.6 0.2 collective-permute-done
  9.8 2.7 %collective-permute-start.1 = (bf16[2,128,128]{2,1,0:T(8,128)(2,1)S(1)}, bf16[2,128,128]{2,1,0:T(8,128)(2,1)S(1)}, u32[]{:S(2)}, u32[]{:S(2)}) collective-permute-start(bf16[2,128,128]{2,1,0:T(8,128)(2,1)S(1)} %pad_maximum_fusion.6), channel_id=1, source_target_pairs={{0,4},{1,5},{2,6},{3,7},{4,0},{5,1},{6,2},{7,3},{8,12},{9,13},{10,... | collective-permute-start | bytes 196616 | tf_op jit(solution)/shard_map/ppermute | solution.py:186
  12.5 0.6 %collective-permute-done.5 = bf16[2,144,128]{2,1,0:T(8,128)(2,1)S(1)} collective-permute-done((bf16[2,144,128]{2,1,0:T(8,128)(2,1)S(1)}, bf16[2,144,128]{2,1,0:T(8,128)(2,1)S(1)}, u32[]{:S(2)}, u32[]{:S(2)}) %collective-permute-start.5) | collective-permute-done | bytes 73760 | tf_op jit(solution)/shard_map/ppermute | solution.py:186
  13.1 1.8 %collective-permute-start.6 = (bf16[4,144,128]{2,1,0:T(8,128)(2,1)S(1)}, bf16[4,144,128]{2,1,0:T(8,128)(2,1)S(1)}, u32[]{:S(2)}, u32[]{:S(2)}) collective-permute-start(bf16[4,144,128]{2,1,0:T(8,128)(2,1)S(1)} %pad_maximum_fusion.3), channel_id=1, source_target_pairs={{0,1},{1,0},{2,3},{3,2},{4,5},{5,4},{6,7},{7,6},{8,9},{9,8},{10,11... | collective-permute-start | bytes 442376 | tf_op jit(solution)/shard_map/ppermute | solution.py:186
  14.9 0.1 collective-permute-done.1
  15.0 1.6 %collective-permute-start.2 = (bf16[4,128,128]{2,1,0:T(8,128)(2,1)S(1)}, bf16[4,128,128]{2,1,0:T(8,128)(2,1)S(1)}, u32[]{:S(2)}, u32[]{:S(2)}) collective-permute-start(bf16[4,128,128]{2,1,0:T(8,128)(2,1)S(1)} %pad_maximum_fusion.4), channel_id=1, source_target_pairs={{0,2},{1,3},{2,0},{3,1},{4,6},{5,7},{6,4},{7,5},{8,10},{9,11},{10,... | collective-permute-start | bytes 393224 | tf_op jit(solution)/shard_map/ppermute | solution.py:186
  16.6 1.7 %collective-permute-done.6 = bf16[4,144,128]{2,1,0:T(8,128)(2,1)S(1)} collective-permute-done((bf16[4,144,128]{2,1,0:T(8,128)(2,1)S(1)}, bf16[4,144,128]{2,1,0:T(8,128)(2,1)S(1)}, u32[]{:S(2)}, u32[]{:S(2)}) %collective-permute-start.6) | collective-permute-done | bytes 147488 | tf_op jit(solution)/shard_map/ppermute | solution.py:186
  18.3 1.8 %collective-permute-start.7 = (bf16[8,144,128]{2,1,0:T(8,128)(2,1)S(1)}, bf16[8,144,128]{2,1,0:T(8,128)(2,1)S(1)}, u32[]{:S(2)}, u32[]{:S(2)}) collective-permute-start(bf16[8,144,128]{2,1,0:T(8,128)(2,1)S(1)} %pad_maximum_fusion.1), channel_id=1, source_target_pairs={{0,16},{8,24},{16,0},{24,8},{1,17},{9,25},{17,1},{25,9},{2,18},{10... | collective-permute-start | bytes 884744 | tf_op jit(solution)/shard_map/ppermute | solution.py:186
  20.1 0.7 %broadcast_clamp_fusion.dilations = s32[2]{0:T(128)S(1)} fusion(s32[2]{0:T(128)} %param.13), kind=kLoop, calls=%fused_computation.12 | loop fusion | flops 2 | bytes 16 | tf_op jit(solution)/shard_map/jit(clip)/min | solution.py:740
  20.8 0.0 copy-start
  20.8 0.0 copy-start.4
  20.8 0.0 collective-permute-done.2
  20.8 1.6 %collective-permute-start.3 = (bf16[8,128,128]{2,1,0:T(8,128)(2,1)S(1)}, bf16[8,128,128]{2,1,0:T(8,128)(2,1)S(1)}, u32[]{:S(2)}, u32[]{:S(2)}) collective-permute-start(bf16[8,128,128]{2,1,0:T(8,128)(2,1)S(1)} %pad_maximum_fusion.2), channel_id=1, source_target_pairs={{0,1},{1,0},{2,3},{3,2},{4,5},{5,4},{6,7},{7,6},{8,9},{9,8},{10,11... | collective-permute-start | bytes 786440 | tf_op jit(solution)/shard_map/ppermute | solution.py:186
  22.4 2.7 %collective-permute-done.7 = bf16[8,144,128]{2,1,0:T(8,128)(2,1)S(1)} collective-permute-done((bf16[8,144,128]{2,1,0:T(8,128)(2,1)S(1)}, bf16[8,144,128]{2,1,0:T(8,128)(2,1)S(1)}, u32[]{:S(2)}, u32[]{:S(2)}) %collective-permute-start.7) | collective-permute-done | bytes 294944 | tf_op jit(solution)/shard_map/ppermute | solution.py:186
  25.1 0.1 pad_maximum_fusion.near
  25.2 0.1 collective-permute-start.9
  25.3 0.0 copy-done.2
  25.3 0.0 copy-done.3
  25.3 0.0 copy-done.1
  25.3 1.9 %shard_map.129 = (bf16[128,16,128]{2,1,0:T(8,128)(2,1)S(1)}, bf16[128,16,128]{2,1,0:T(8,128)(2,1)S(1)}, bf16[128,16,128]{2,1,0:T(8,128)(2,1)S(1)}, bf16[2,16,64,...) custom-call(bf16[16,144,128]{2,1,0:T(8,128)(2,1)S(1)} %pad_maximum_f, ...), custom_call_target="tpu_custom_call" | custom-call | flops 335544320 | bytes 4194304 | tf_op jit(solution)/shard_map/pallas_call | solution.py:752
  27.2 0.0 collective-permute-done.3
  27.3 0.6 %collective-permute-start.8 = (bf16[16,128,128]{2,1,0:T(8,128)(2,1)S(1)}, bf16[16,128,128]{2,1,0:T(8,128)(2,1)S(1)}, u32[]{:S(2)}, u32[]{:S(2)}) collective-permute-start(bf16[16,128,128]{2,1,0:T(8,128)(2,1)S(1)} %constant_dynamic-update-slice_fusion.cot_near), channel_id=1, source_target_pairs={{0,8},{8,0},{16,24},{24,16},{1,9},{9,1},{17,25},{25,17},{2,10},{10... | collective-permute-start | bytes 1572872 | tf_op jit(solution)/shard_map/ppermute | solution.py:186
  27.9 0.0 collective-permute-done.9.far
  27.9 0.0 copy-done
  27.9 0.0 copy-done.4
  27.9 10.0 %shard_map.130 = (f32[64,64,128]{2,1,0:T(8,128)S(1)}, bf16[128,4096]{1,0:T(8,128)(2,1)S(1)}, f32[128,128]{1,0:T(8,128)S(1)}, f32[128,128]{1,0:T(8,128)S(1)}) custom-call(s32[2]{0:T(128)S(1)} %broadcast_clamp_fusion.dilations, bf16[16,144,128]{2,1,0:T(8,128)(2,1)S(1)} %collective-permute-done.9.far, bf16[128,512]{1,0:T(8,128)(2,1)S(1)} %copy-done.2, ...), custom_call_target="tpu_custom_call" | custom-call | flops 2684354560 | bytes 20971520 | tf_op jit(solution)/shard_map/pallas_call | solution.py:777
  37.9 0.0 collective-permute-done.8.cot_far
  37.9 9.2 %shard_map.131 = (bf16[128,128]{1,0:T(8,128)(2,1)}, bf16[128,128]{1,0:T(8,128)(2,1)}, f32[9,128,128]{2,1,0:T(8,128)}, f32[9,128,128]{2,1,0:T(8,128)}) custom-call(s32[2]{0:T(128)S(1)} %broadcast_clamp_fusion.dilations, bf16[16,128,128]{2,1,0:T(8,128)(2,1)S(1)} %constant_dynamic-update-slice_fusion.cot_near, ...), custom_call_target="tpu_custom_call" | custom-call | tf_op jit(solution)/shard_map/pallas_call | solution.py:803
  (8 shorter events, 0.2 us)
Async XLA Ops:
  0.6 24.7 %copy-start.2 = (bf16[128,512]{1,0:T(8,128)(2,1)S(1)}, bf16[128,512]{1,0:T(8,128)(2,1)}, u32[]{:S(2)}) copy-start(bf16[128,512]{1,0:T(8,128)(2,1)} %w_proj.3) | copy-start | bytes 393220
  0.6 24.7 %copy-start.3 = (bf16[128,128]{1,0:T(8,128)(2,1)S(1)}, bf16[128,128]{1,0:T(8,128)(2,1)}, u32[]{:S(2)}) copy-start(bf16[128,128]{1,0:T(8,128)(2,1)} %w_gate.3) | copy-start | bytes 98308
  0.7 24.7 %copy-start.1 = (bf16[9,128,128]{2,1,0:T(8,128)(2,1)S(1)}, bf16[9,128,128]{2,1,0:T(8,128)(2,1)}, u32[]{:S(2)}) copy-start(bf16[9,128,128]{2,1,0:T(8,128)(2,1)} %two.1) | copy-start | bytes 884740
  1.6 6.4 %collective-permute-start.4 = (bf16[1,144,128]{2,1,0:T(8,128)(2,1)S(1)}, bf16[1,144,128]{2,1,0:T(8,128)(2,1)S(1)}, u32[]{:S(2)}, u32[]{:S(2)}) collective-permute-start(bf16[1,144,128]{2,1,0:T(8,128)(2,1)S(1)} %fusion), channel_id=1, source_target_pairs={{0,4},{1,5},{2,6},{3,7},{4,0},{5,1},{6,2},{7,3},{8,12},{9,13},{10,... | collective-permute-start | bytes 110600 | tf_op jit(solution)/shard_map/ppermute | solution.py:186
  5.6 4.1 %collective-permute-start = (bf16[1,128,128]{2,1,0:T(8,128)(2,1)}, bf16[1,128,128]{2,1,0:T(8,128)(2,1)S(1)}, u32[]{:S(2)}, u32[]{:S(2)}) collective-permute-start(bf16[1,128,128]{2,1,0:T(8,128)(2,1)} %bitcast.10), channel_id=1, source_target_pairs={{0,16},{8,24},{16,0},{24,8},{1,17},{9,25},{17,1},{25,9},{2,18},{10... | collective-permute-start | bytes 98312 | tf_op jit(solution)/shard_map/ppermute | solution.py:186
  8.0 5.1 %collective-permute-start.5 = (bf16[2,144,128]{2,1,0:T(8,128)(2,1)S(1)}, bf16[2,144,128]{2,1,0:T(8,128)(2,1)S(1)}, u32[]{:S(2)}, u32[]{:S(2)}) collective-permute-start(bf16[2,144,128]{2,1,0:T(8,128)(2,1)S(1)} %pad_maximum_fusion.5), channel_id=1, source_target_pairs={{0,2},{1,3},{2,0},{3,1},{4,6},{5,7},{6,4},{7,5},{8,10},{9,11},{10,... | collective-permute-start | bytes 221192 | tf_op jit(solution)/shard_map/ppermute | solution.py:186
  9.8 5.2 %collective-permute-start.1 = (bf16[2,128,128]{2,1,0:T(8,128)(2,1)S(1)}, bf16[2,128,128]{2,1,0:T(8,128)(2,1)S(1)}, u32[]{:S(2)}, u32[]{:S(2)}) collective-permute-start(bf16[2,128,128]{2,1,0:T(8,128)(2,1)S(1)} %pad_maximum_fusion.6), channel_id=1, source_target_pairs={{0,4},{1,5},{2,6},{3,7},{4,0},{5,1},{6,2},{7,3},{8,12},{9,13},{10,... | collective-permute-start | bytes 196616 | tf_op jit(solution)/shard_map/ppermute | solution.py:186
  13.1 5.2 %collective-permute-start.6 = (bf16[4,144,128]{2,1,0:T(8,128)(2,1)S(1)}, bf16[4,144,128]{2,1,0:T(8,128)(2,1)S(1)}, u32[]{:S(2)}, u32[]{:S(2)}) collective-permute-start(bf16[4,144,128]{2,1,0:T(8,128)(2,1)S(1)} %pad_maximum_fusion.3), channel_id=1, source_target_pairs={{0,1},{1,0},{2,3},{3,2},{4,5},{5,4},{6,7},{7,6},{8,9},{9,8},{10,11... | collective-permute-start | bytes 442376 | tf_op jit(solution)/shard_map/ppermute | solution.py:186
  15.0 5.8 %collective-permute-start.2 = (bf16[4,128,128]{2,1,0:T(8,128)(2,1)S(1)}, bf16[4,128,128]{2,1,0:T(8,128)(2,1)S(1)}, u32[]{:S(2)}, u32[]{:S(2)}) collective-permute-start(bf16[4,128,128]{2,1,0:T(8,128)(2,1)S(1)} %pad_maximum_fusion.4), channel_id=1, source_target_pairs={{0,2},{1,3},{2,0},{3,1},{4,6},{5,7},{6,4},{7,5},{8,10},{9,11},{10,... | collective-permute-start | bytes 393224 | tf_op jit(solution)/shard_map/ppermute | solution.py:186
  18.3 6.8 %collective-permute-start.7 = (bf16[8,144,128]{2,1,0:T(8,128)(2,1)S(1)}, bf16[8,144,128]{2,1,0:T(8,128)(2,1)S(1)}, u32[]{:S(2)}, u32[]{:S(2)}) collective-permute-start(bf16[8,144,128]{2,1,0:T(8,128)(2,1)S(1)} %pad_maximum_fusion.1), channel_id=1, source_target_pairs={{0,16},{8,24},{16,0},{24,8},{1,17},{9,25},{17,1},{25,9},{2,18},{10... | collective-permute-start | bytes 884744 | tf_op jit(solution)/shard_map/ppermute | solution.py:186
  20.8 7.1 %copy-start = (bf16[9,128,128]{2,1,0:T(8,128)(2,1)S(1)}, bf16[9,128,128]{2,1,0:T(8,128)(2,1)}, u32[]{:S(2)}) copy-start(bf16[9,128,128]{2,1,0:T(8,128)(2,1)} %one.3) | copy-start | bytes 884740
  20.8 7.1 %copy-start.4 = (bf16[128,128]{1,0:T(8,128)(2,1)S(1)}, bf16[128,128]{1,0:T(8,128)(2,1)}, u32[]{:S(2)}) copy-start(bf16[128,128]{1,0:T(8,128)(2,1)} %w_out.1) | copy-start | bytes 98308
  20.8 6.4 %collective-permute-start.3 = (bf16[8,128,128]{2,1,0:T(8,128)(2,1)S(1)}, bf16[8,128,128]{2,1,0:T(8,128)(2,1)S(1)}, u32[]{:S(2)}, u32[]{:S(2)}) collective-permute-start(bf16[8,128,128]{2,1,0:T(8,128)(2,1)S(1)} %pad_maximum_fusion.2), channel_id=1, source_target_pairs={{0,1},{1,0},{2,3},{3,2},{4,5},{5,4},{6,7},{7,6},{8,9},{9,8},{10,11... | collective-permute-start | bytes 786440 | tf_op jit(solution)/shard_map/ppermute | solution.py:186
  25.2 2.7 %collective-permute-start.9 = (bf16[16,144,128]{2,1,0:T(8,128)(2,1)S(1)}, bf16[16,144,128]{2,1,0:T(8,128)(2,1)S(1)}, u32[]{:S(2)}, u32[]{:S(2)}) collective-permute-start(bf16[16,144,128]{2,1,0:T(8,128)(2,1)S(1)} %pad_maximum_fusion.near), channel_id=1, source_target_pairs={{0,8},{8,0},{16,24},{24,16},{1,9},{9,1},{17,25},{25,17},{2,10},{10... | collective-permute-start | bytes 1769480 | tf_op jit(solution)/shard_map/ppermute | solution.py:186
  27.3 10.6 %collective-permute-start.8 = (bf16[16,128,128]{2,1,0:T(8,128)(2,1)S(1)}, bf16[16,128,128]{2,1,0:T(8,128)(2,1)S(1)}, u32[]{:S(2)}, u32[]{:S(2)}) collective-permute-start(bf16[16,128,128]{2,1,0:T(8,128)(2,1)S(1)} %constant_dynamic-update-slice_fusion.cot_near), channel_id=1, source_target_pairs={{0,8},{8,0},{16,24},{24,16},{1,9},{9,1},{17,25},{25,17},{2,10},{10... | collective-permute-start | bytes 1572872 | tf_op jit(solution)/shard_map/ppermute | solution.py:186

commit v16 on v15

--- a/solution.py
+++ b/solution.py
@@ -479,7 +479,7 @@
     lane = lax.broadcasted_iota(jnp.int32, (height, chips * tokens), 1)
     low = jnp.where(lane < tokens, 1.0, 0.0).astype(jnp.bfloat16)
     high = jnp.where(lane < tokens, 0.0, 1.0).astype(jnp.bfloat16)
-    batch = 64
+    batch = 128
     pitch = 2 * height + PITCH
 
     def multiply(step, carry):
@@ -540,18 +540,15 @@
 
     count = 2 * parts
     for step in range(count + 2):
+        if step >= 2:
+            first_conv(step - 2)
         if step < count:
             normalise(step)
         if 1 <= step <= count:
             update(step - 1)
-        if step >= 2:
-            first_conv(step - 2)
-
-    def add_taps(step, carry):
-        pre[pl.ds(step * chunk, chunk)] = row_taps(strips, step * chunk, chunk, rate_one)
-        return carry
-
-    lax.fori_loop(0, tokens // chunk, add_taps, 0)
+
+    for first in range(0, tokens, chunk):
+        pre[pl.ds(first, chunk)] = row_taps(strips, first, chunk, rate_one)
 
     cols = pl.ds(pl.multiple_of(col_place * breadth, breadth), breadth)
     mine[...] = updated[row_place // 2, :, cols, :].reshape(pixels, channels)
@@ -667,11 +664,12 @@
         if step >= 1:
             spread_pre(step - 1)
         back_two(step)
-    spread_pre(steps - 1)
     for row in range(3):
         finish(sum_two, scaled_two, grad_two, row)
-    for step in range(max(steps - 3, 0), steps - 1):
+    for step in range(max(steps - 3, 0), steps - 2):
         back_one(step)
+    spread_pre(steps - 1)
+    back_one(steps - 2)
 
     spot = (row_place * height, col_place * breadth, height, breadth)
     second_pre = matmul(

time: 47.5 us -> 47.1 us (level)
    pallas_call x1, Pallas kernels: 10 us -> 9.47 us  [replicated(): pl.pallas_call(functools.partial(forward_kernel, plan), in_specs=[in_smem...]
  transfers between devices with their start and end apart: 10 -> 10, of which waited for: 5 -> 5; matrix products, arithmetic and copies ran while one was open for 4% -> 4% of each run, Pallas kernels for 25% -> 24%
where the time goes in v16:
time: 47.1 us; the launch traced here: 46.9 us
  Pallas kernels  20.8 us (44%)
  starting transfers between devices  17.3 us (37%)
  waiting for transfers between devices  5.31 us (11%)
  other arithmetic  2.52 us (5%)
  between operations  0.93 us (2%)
    ppermute x10, starting transfers between devices, exchange(): lax.ppermute(held, axis, [(i, i ^ distance) for i in range(lax.axis_size(...  17.3 us
    pallas_call x1, Pallas kernels, replicated(): pl.pallas_call(functools.partial(forward_kernel, plan), in_specs=[in_smem...  9.47 us
    pallas_call x1, Pallas kernels, replicated(): pl.pallas_call(functools.partial(backward_kernel, plan), in_specs=[in_sme...  9.4 us
    ppermute x10, waiting for transfers between devices, exchange(): lax.ppermute(held, axis, [(i, i ^ distance) for i in range(lax.axis_size(...  5.31 us
    pallas_call x1, Pallas kernels, replicated(): pl.pallas_call(functools.partial(near_kernel, plan), in_specs=[in_vmem] *...  1.91 us
  transfers between devices with their start and end apart: 10, of which 5 were waited for; matrix products, arithmetic and copies ran while one was open for 4% of the time, Pallas kernels for 24%

profile of v16, /device:TPU:0, one launch (start us, length us, event | category | flops | bytes accessed | tf_op | source)
XLA Modules:
  0.0 46.9 jit_solution(10228546501766476822)
XLA Ops:
  0.6 0.0 copy-start.2
  0.6 0.0 copy-start.3
  0.7 0.0 copy-start.1
  0.7 0.9 %fusion = bf16[1,144,128]{2,1,0:T(8,128)(2,1)S(1)} fusion(s32[8,16]{1,0:T(8,128)} %bitcast.11, s32[8,16]{1,0:T(8,128)} %bitcast.12, bf16[128,128]{1,0:T(8,128)(2,1)} %bitcast.9), kind=kLoop, calls=%fused_computation.8 | loop fusion | flops 92160 | bytes 70656 | tf_op jit(solution)/shard_map/broadcast_in_dim | solution.py:735
  1.6 4.0 %collective-permute-start.4 = (bf16[1,144,128]{2,1,0:T(8,128)(2,1)S(1)}, bf16[1,144,128]{2,1,0:T(8,128)(2,1)S(1)}, u32[]{:S(2)}, u32[]{:S(2)}) collective-permute-start(bf16[1,144,128]{2,1,0:T(8,128)(2,1)S(1)} %fusion), channel_id=1, source_target_pairs={{0,4},{1,5},{2,6},{3,7},{4,0},{5,1},{6,2},{7,3},{8,12},{9,13},{10,... | collective-permute-start | bytes 110600 | tf_op jit(solution)/shard_map/ppermute | solution.py:186
  5.6 1.5 %collective-permute-start = (bf16[1,128,128]{2,1,0:T(8,128)(2,1)}, bf16[1,128,128]{2,1,0:T(8,128)(2,1)S(1)}, u32[]{:S(2)}, u32[]{:S(2)}) collective-permute-start(bf16[1,128,128]{2,1,0:T(8,128)(2,1)} %bitcast.10), channel_id=1, source_target_pairs={{0,16},{8,24},{16,0},{24,8},{1,17},{9,25},{17,1},{25,9},{2,18},{10... | collective-permute-start | bytes 98312 | tf_op jit(solution)/shard_map/ppermute | solution.py:186
  7.1 0.8 %broadcast_maximum_fusion = bf16[1,128,128]{2,1,0:T(8,128)(2,1)S(1)} fusion(bf16[16,8,128]{2,1,0:T(8,128)(2,1)} %param.19), kind=kLoop, calls=%fused_computation.9 | loop fusion | flops 16384 | bytes 65536 | tf_op jit(solution)/shard_map/max | solution.py:737
  7.9 0.0 collective-permute-done.4
  8.0 1.6 %collective-permute-start.5 = (bf16[2,144,128]{2,1,0:T(8,128)(2,1)S(1)}, bf16[2,144,128]{2,1,0:T(8,128)(2,1)S(1)}, u32[]{:S(2)}, u32[]{:S(2)}) collective-permute-start(bf16[2,144,128]{2,1,0:T(8,128)(2,1)S(1)} %pad_maximum_fusion.5), channel_id=1, source_target_pairs={{0,2},{1,3},{2,0},{3,1},{4,6},{5,7},{6,4},{7,5},{8,10},{9,11},{10,... | collective-permute-start | bytes 221192 | tf_op jit(solution)/shard_map/ppermute | solution.py:186
  9.6 0.2 collective-permute-done
  9.8 2.7 %collective-permute-start.1 = (bf16[2,128,128]{2,1,0:T(8,128)(2,1)S(1)}, bf16[2,128,128]{2,1,0:T(8,128)(2,1)S(1)}, u32[]{:S(2)}, u32[]{:S(2)}) collective-permute-start(bf16[2,128,128]{2,1,0:T(8,128)(2,1)S(1)} %pad_maximum_fusion.6), channel_id=1, source_target_pairs={{0,4},{1,5},{2,6},{3,7},{4,0},{5,1},{6,2},{7,3},{8,12},{9,13},{10,... | collective-permute-start | bytes 196616 | tf_op jit(solution)/shard_map/ppermute | solution.py:186
  12.5 0.6 %collective-permute-done.5 = bf16[2,144,128]{2,1,0:T(8,128)(2,1)S(1)} collective-permute-done((bf16[2,144,128]{2,1,0:T(8,128)(2,1)S(1)}, bf16[2,144,128]{2,1,0:T(8,128)(2,1)S(1)}, u32[]{:S(2)}, u32[]{:S(2)}) %collective-permute-start.5) | collective-permute-done | bytes 73760 | tf_op jit(solution)/shard_map/ppermute | solution.py:186
  13.1 1.8 %collective-permute-start.6 = (bf16[4,144,128]{2,1,0:T(8,128)(2,1)S(1)}, bf16[4,144,128]{2,1,0:T(8,128)(2,1)S(1)}, u32[]{:S(2)}, u32[]{:S(2)}) collective-permute-start(bf16[4,144,128]{2,1,0:T(8,128)(2,1)S(1)} %pad_maximum_fusion.3), channel_id=1, source_target_pairs={{0,1},{1,0},{2,3},{3,2},{4,5},{5,4},{6,7},{7,6},{8,9},{9,8},{10,11... | collective-permute-start | bytes 442376 | tf_op jit(solution)/shard_map/ppermute | solution.py:186
  14.9 0.1 collective-permute-done.1
  15.0 1.6 %collective-permute-start.2 = (bf16[4,128,128]{2,1,0:T(8,128)(2,1)S(1)}, bf16[4,128,128]{2,1,0:T(8,128)(2,1)S(1)}, u32[]{:S(2)}, u32[]{:S(2)}) collective-permute-start(bf16[4,128,128]{2,1,0:T(8,128)(2,1)S(1)} %pad_maximum_fusion.4), channel_id=1, source_target_pairs={{0,2},{1,3},{2,0},{3,1},{4,6},{5,7},{6,4},{7,5},{8,10},{9,11},{10,... | collective-permute-start | bytes 393224 | tf_op jit(solution)/shard_map/ppermute | solution.py:186
  16.6 1.7 %collective-permute-done.6 = bf16[4,144,128]{2,1,0:T(8,128)(2,1)S(1)} collective-permute-done((bf16[4,144,128]{2,1,0:T(8,128)(2,1)S(1)}, bf16[4,144,128]{2,1,0:T(8,128)(2,1)S(1)}, u32[]{:S(2)}, u32[]{:S(2)}) %collective-permute-start.6) | collective-permute-done | bytes 147488 | tf_op jit(solution)/shard_map/ppermute | solution.py:186
  18.3 1.8 %collective-permute-start.7 = (bf16[8,144,128]{2,1,0:T(8,128)(2,1)S(1)}, bf16[8,144,128]{2,1,0:T(8,128)(2,1)S(1)}, u32[]{:S(2)}, u32[]{:S(2)}) collective-permute-start(bf16[8,144,128]{2,1,0:T(8,128)(2,1)S(1)} %pad_maximum_fusion.1), channel_id=1, source_target_pairs={{0,16},{8,24},{16,0},{24,8},{1,17},{9,25},{17,1},{25,9},{2,18},{10... | collective-permute-start | bytes 884744 | tf_op jit(solution)/shard_map/ppermute | solution.py:186
  20.1 0.7 %broadcast_clamp_fusion.dilations = s32[2]{0:T(128)S(1)} fusion(s32[2]{0:T(128)} %param.13), kind=kLoop, calls=%fused_computation.12 | loop fusion | flops 2 | bytes 16 | tf_op jit(solution)/shard_map/jit(clip)/min | solution.py:738
  20.8 0.0 copy-start
  20.8 0.0 copy-start.4
  20.8 0.0 collective-permute-done.2
  20.8 1.6 %collective-permute-start.3 = (bf16[8,128,128]{2,1,0:T(8,128)(2,1)S(1)}, bf16[8,128,128]{2,1,0:T(8,128)(2,1)S(1)}, u32[]{:S(2)}, u32[]{:S(2)}) collective-permute-start(bf16[8,128,128]{2,1,0:T(8,128)(2,1)S(1)} %pad_maximum_fusion.2), channel_id=1, source_target_pairs={{0,1},{1,0},{2,3},{3,2},{4,5},{5,4},{6,7},{7,6},{8,9},{9,8},{10,11... | collective-permute-start | bytes 786440 | tf_op jit(solution)/shard_map/ppermute | solution.py:186
  22.4 2.7 %collective-permute-done.7 = bf16[8,144,128]{2,1,0:T(8,128)(2,1)S(1)} collective-permute-done((bf16[8,144,128]{2,1,0:T(8,128)(2,1)S(1)}, bf16[8,144,128]{2,1,0:T(8,128)(2,1)S(1)}, u32[]{:S(2)}, u32[]{:S(2)}) %collective-permute-start.7) | collective-permute-done | bytes 294944 | tf_op jit(solution)/shard_map/ppermute | solution.py:186
  25.1 0.1 pad_maximum_fusion.near
  25.2 0.1 collective-permute-start.9
  25.3 0.0 copy-done.2
  25.3 0.0 copy-done.3
  25.3 0.0 copy-done.1
  25.3 1.9 %shard_map.129 = (bf16[128,16,128]{2,1,0:T(8,128)(2,1)S(1)}, bf16[128,16,128]{2,1,0:T(8,128)(2,1)S(1)}, bf16[128,16,128]{2,1,0:T(8,128)(2,1)S(1)}, bf16[2,16,64,...) custom-call(bf16[16,144,128]{2,1,0:T(8,128)(2,1)S(1)} %pad_maximum_f, ...), custom_call_target="tpu_custom_call" | custom-call | flops 335544320 | bytes 4194304 | tf_op jit(solution)/shard_map/pallas_call | solution.py:750
  27.2 0.0 collective-permute-done.3
  27.3 0.6 %collective-permute-start.8 = (bf16[16,128,128]{2,1,0:T(8,128)(2,1)S(1)}, bf16[16,128,128]{2,1,0:T(8,128)(2,1)S(1)}, u32[]{:S(2)}, u32[]{:S(2)}) collective-permute-start(bf16[16,128,128]{2,1,0:T(8,128)(2,1)S(1)} %constant_dynamic-update-slice_fusion.cot_near), channel_id=1, source_target_pairs={{0,8},{8,0},{16,24},{24,16},{1,9},{9,1},{17,25},{25,17},{2,10},{10... | collective-permute-start | bytes 1572872 | tf_op jit(solution)/shard_map/ppermute | solution.py:186
  27.9 0.0 collective-permute-done.9.far
  27.9 0.0 copy-done
  27.9 0.0 copy-done.4
  27.9 9.5 %shard_map.130 = (f32[64,64,128]{2,1,0:T(8,128)S(1)}, bf16[128,4096]{1,0:T(8,128)(2,1)S(1)}, f32[128,128]{1,0:T(8,128)S(1)}, f32[128,128]{1,0:T(8,128)S(1)}) custom-call(s32[2]{0:T(128)S(1)} %broadcast_clamp_fusion.dilations, bf16[16,144,128]{2,1,0:T(8,128)(2,1)S(1)} %collective-permute-done.9.far, bf16[128,512]{1,0:T(8,128)(2,1)S(1)} %copy-done.2, ...), custom_call_target="tpu_custom_call" | custom-call | flops 2684354560 | bytes 20971520 | tf_op jit(solution)/shard_map/pallas_call | solution.py:775
  37.3 0.0 collective-permute-done.8.cot_far
  37.4 9.4 %shard_map.131 = (bf16[128,128]{1,0:T(8,128)(2,1)}, bf16[128,128]{1,0:T(8,128)(2,1)}, f32[9,128,128]{2,1,0:T(8,128)}, f32[9,128,128]{2,1,0:T(8,128)}) custom-call(s32[2]{0:T(128)S(1)} %broadcast_clamp_fusion.dilations, bf16[16,128,128]{2,1,0:T(8,128)(2,1)S(1)} %constant_dynamic-update-slice_fusion.cot_near, ...), custom_call_target="tpu_custom_call" | custom-call | tf_op jit(solution)/shard_map/pallas_call | solution.py:801
  (8 shorter events, 0.2 us)
Async XLA Ops:
  0.6 24.7 %copy-start.2 = (bf16[128,512]{1,0:T(8,128)(2,1)S(1)}, bf16[128,512]{1,0:T(8,128)(2,1)}, u32[]{:S(2)}) copy-start(bf16[128,512]{1,0:T(8,128)(2,1)} %w_proj.3) | copy-start | bytes 393220
  0.6 24.7 %copy-start.3 = (bf16[128,128]{1,0:T(8,128)(2,1)S(1)}, bf16[128,128]{1,0:T(8,128)(2,1)}, u32[]{:S(2)}) copy-start(bf16[128,128]{1,0:T(8,128)(2,1)} %w_gate.3) | copy-start | bytes 98308
  0.7 24.7 %copy-start.1 = (bf16[9,128,128]{2,1,0:T(8,128)(2,1)S(1)}, bf16[9,128,128]{2,1,0:T(8,128)(2,1)}, u32[]{:S(2)}) copy-start(bf16[9,128,128]{2,1,0:T(8,128)(2,1)} %two.1) | copy-start | bytes 884740
  1.6 6.4 %collective-permute-start.4 = (bf16[1,144,128]{2,1,0:T(8,128)(2,1)S(1)}, bf16[1,144,128]{2,1,0:T(8,128)(2,1)S(1)}, u32[]{:S(2)}, u32[]{:S(2)}) collective-permute-start(bf16[1,144,128]{2,1,0:T(8,128)(2,1)S(1)} %fusion), channel_id=1, source_target_pairs={{0,4},{1,5},{2,6},{3,7},{4,0},{5,1},{6,2},{7,3},{8,12},{9,13},{10,... | collective-permute-start | bytes 110600 | tf_op jit(solution)/shard_map/ppermute | solution.py:186
  5.6 4.1 %collective-permute-start = (bf16[1,128,128]{2,1,0:T(8,128)(2,1)}, bf16[1,128,128]{2,1,0:T(8,128)(2,1)S(1)}, u32[]{:S(2)}, u32[]{:S(2)}) collective-permute-start(bf16[1,128,128]{2,1,0:T(8,128)(2,1)} %bitcast.10), channel_id=1, source_target_pairs={{0,16},{8,24},{16,0},{24,8},{1,17},{9,25},{17,1},{25,9},{2,18},{10... | collective-permute-start | bytes 98312 | tf_op jit(solution)/shard_map/ppermute | solution.py:186
  8.0 5.1 %collective-permute-start.5 = (bf16[2,144,128]{2,1,0:T(8,128)(2,1)S(1)}, bf16[2,144,128]{2,1,0:T(8,128)(2,1)S(1)}, u32[]{:S(2)}, u32[]{:S(2)}) collective-permute-start(bf16[2,144,128]{2,1,0:T(8,128)(2,1)S(1)} %pad_maximum_fusion.5), channel_id=1, source_target_pairs={{0,2},{1,3},{2,0},{3,1},{4,6},{5,7},{6,4},{7,5},{8,10},{9,11},{10,... | collective-permute-start | bytes 221192 | tf_op jit(solution)/shard_map/ppermute | solution.py:186
  9.8 5.2 %collective-permute-start.1 = (bf16[2,128,128]{2,1,0:T(8,128)(2,1)S(1)}, bf16[2,128,128]{2,1,0:T(8,128)(2,1)S(1)}, u32[]{:S(2)}, u32[]{:S(2)}) collective-permute-start(bf16[2,128,128]{2,1,0:T(8,128)(2,1)S(1)} %pad_maximum_fusion.6), channel_id=1, source_target_pairs={{0,4},{1,5},{2,6},{3,7},{4,0},{5,1},{6,2},{7,3},{8,12},{9,13},{10,... | collective-permute-start | bytes 196616 | tf_op jit(solution)/shard_map/ppermute | solution.py:186
  13.1 5.2 %collective-permute-start.6 = (bf16[4,144,128]{2,1,0:T(8,128)(2,1)S(1)}, bf16[4,144,128]{2,1,0:T(8,128)(2,1)S(1)}, u32[]{:S(2)}, u32[]{:S(2)}) collective-permute-start(bf16[4,144,128]{2,1,0:T(8,128)(2,1)S(1)} %pad_maximum_fusion.3), channel_id=1, source_target_pairs={{0,1},{1,0},{2,3},{3,2},{4,5},{5,4},{6,7},{7,6},{8,9},{9,8},{10,11... | collective-permute-start | bytes 442376 | tf_op jit(solution)/shard_map/ppermute | solution.py:186
  15.0 5.8 %collective-permute-start.2 = (bf16[4,128,128]{2,1,0:T(8,128)(2,1)S(1)}, bf16[4,128,128]{2,1,0:T(8,128)(2,1)S(1)}, u32[]{:S(2)}, u32[]{:S(2)}) collective-permute-start(bf16[4,128,128]{2,1,0:T(8,128)(2,1)S(1)} %pad_maximum_fusion.4), channel_id=1, source_target_pairs={{0,2},{1,3},{2,0},{3,1},{4,6},{5,7},{6,4},{7,5},{8,10},{9,11},{10,... | collective-permute-start | bytes 393224 | tf_op jit(solution)/shard_map/ppermute | solution.py:186
  18.3 6.8 %collective-permute-start.7 = (bf16[8,144,128]{2,1,0:T(8,128)(2,1)S(1)}, bf16[8,144,128]{2,1,0:T(8,128)(2,1)S(1)}, u32[]{:S(2)}, u32[]{:S(2)}) collective-permute-start(bf16[8,144,128]{2,1,0:T(8,128)(2,1)S(1)} %pad_maximum_fusion.1), channel_id=1, source_target_pairs={{0,16},{8,24},{16,0},{24,8},{1,17},{9,25},{17,1},{25,9},{2,18},{10... | collective-permute-start | bytes 884744 | tf_op jit(solution)/shard_map/ppermute | solution.py:186
  20.8 7.1 %copy-start = (bf16[9,128,128]{2,1,0:T(8,128)(2,1)S(1)}, bf16[9,128,128]{2,1,0:T(8,128)(2,1)}, u32[]{:S(2)}) copy-start(bf16[9,128,128]{2,1,0:T(8,128)(2,1)} %one.3) | copy-start | bytes 884740
  20.8 7.1 %copy-start.4 = (bf16[128,128]{1,0:T(8,128)(2,1)S(1)}, bf16[128,128]{1,0:T(8,128)(2,1)}, u32[]{:S(2)}) copy-start(bf16[128,128]{1,0:T(8,128)(2,1)} %w_out.1) | copy-start | bytes 98308
  20.8 6.4 %collective-permute-start.3 = (bf16[8,128,128]{2,1,0:T(8,128)(2,1)S(1)}, bf16[8,128,128]{2,1,0:T(8,128)(2,1)S(1)}, u32[]{:S(2)}, u32[]{:S(2)}) collective-permute-start(bf16[8,128,128]{2,1,0:T(8,128)(2,1)S(1)} %pad_maximum_fusion.2), channel_id=1, source_target_pairs={{0,1},{1,0},{2,3},{3,2},{4,5},{5,4},{6,7},{7,6},{8,9},{9,8},{10,11... | collective-permute-start | bytes 786440 | tf_op jit(solution)/shard_map/ppermute | solution.py:186
  25.2 2.7 %collective-permute-start.9 = (bf16[16,144,128]{2,1,0:T(8,128)(2,1)S(1)}, bf16[16,144,128]{2,1,0:T(8,128)(2,1)S(1)}, u32[]{:S(2)}, u32[]{:S(2)}) collective-permute-start(bf16[16,144,128]{2,1,0:T(8,128)(2,1)S(1)} %pad_maximum_fusion.near), channel_id=1, source_target_pairs={{0,8},{8,0},{16,24},{24,16},{1,9},{9,1},{17,25},{25,17},{2,10},{10... | collective-permute-start | bytes 1769480 | tf_op jit(solution)/shard_map/ppermute | solution.py:186
  27.3 10.1 %collective-permute-start.8 = (bf16[16,128,128]{2,1,0:T(8,128)(2,1)S(1)}, bf16[16,128,128]{2,1,0:T(8,128)(2,1)S(1)}, u32[]{:S(2)}, u32[]{:S(2)}) collective-permute-start(bf16[16,128,128]{2,1,0:T(8,128)(2,1)S(1)} %constant_dynamic-update-slice_fusion.cot_near), channel_id=1, source_target_pairs={{0,8},{8,0},{16,24},{24,16},{1,9},{9,1},{17,25},{25,17},{2,10},{10... | collective-permute-start | bytes 1572872 | tf_op jit(solution)/shard_map/ppermute | solution.py:186

commit v17 on v16

--- a/solution.py
+++ b/solution.py
@@ -346,13 +346,19 @@
     return jnp.concatenate(views, axis=1)
 
 
-def windows(source, rate, row_start, col_start, height, breadth):
+def silu(values):
+    return values * sigmoid(values)
+
+
+def windows(source, rate, row_start, col_start, height, breadth, change=lambda values: values):
     views = [
-        source[
-            pl.ds(row_start + DMAX + (tap // 3 - 1) * rate, height),
-            pl.ds(col_start + DMAX + (tap % 3 - 1) * rate, breadth),
-            :,
-        ].reshape(height * breadth, -1)
+        change(
+            source[
+                pl.ds(row_start + DMAX + (tap // 3 - 1) * rate, height),
+                pl.ds(col_start + DMAX + (tap % 3 - 1) * rate, breadth),
+                :,
+            ]
+        ).reshape(height * breadth, -1)
         for tap in range(9)
     ]
     return jnp.concatenate(views, axis=1).astype(jnp.bfloat16)
@@ -360,7 +366,9 @@
 
 def row_taps(strips, first, count, rate):
     views = [
-        strips[tap, pl.ds(DMAX + first + ((tap - 1) * rate if tap != 1 else 0), count)]
+        strips[tap, pl.ds(DMAX + first + ((tap - 1) * rate if tap != 1 else 0), count)].astype(
+            jnp.float32
+        )
         for tap in range(3)
     ]
     return views[0] + views[1] + views[2]
@@ -369,7 +377,7 @@
 def clear_ends(strips, tokens):
     for tap in (0, 2):
         for rows in (slice(0, DMAX), slice(DMAX + tokens, 2 * DMAX + tokens)):
-            strips[tap, rows] = jnp.zeros((DMAX,) + strips.shape[2:], jnp.float32)
+            strips[tap, rows] = jnp.zeros((DMAX,) + strips.shape[2:], strips.dtype)
 
 
 def column_taps(source, weight, rate, first, count, strips):
@@ -394,7 +402,13 @@
     for tap in range(3):
         strips[tap, pl.ds(DMAX + first, count)] = result[
             :, tap * channels : (tap + 1) * channels
-        ].reshape(count, tokens, channels)
+        ].reshape(count, tokens, channels).astype(strips.dtype)
+
+
+def clear_around(target, row_start, col_start, height, breadth):
+    shape = (height + 2 * DMAX, breadth + 2 * DMAX, target.shape[2])
+    cols = pl.ds(pl.multiple_of(col_start, 8), shape[1])
+    target[pl.ds(row_start, shape[0]), cols, :] = jnp.zeros(shape, target.dtype)
 
 
 def lanes(step, size):
@@ -547,8 +561,9 @@
         if 1 <= step <= count:
             update(step - 1)
 
+    clear_around(pre, row_place * height, col_place * breadth, height, breadth)
     for first in range(0, tokens, chunk):
-        pre[pl.ds(first, chunk)] = row_taps(strips, first, chunk, rate_one)
+        pre[pl.ds(DMAX + first, chunk), inside, :] = row_taps(strips, first, chunk, rate_one)
 
     cols = pl.ds(pl.multiple_of(col_place * breadth, breadth), breadth)
     mine[...] = updated[row_place // 2, :, cols, :].reshape(pixels, channels)
@@ -579,7 +594,6 @@
     wide_cot,
     wide_pre,
     grad_pre,
-    second,
     sum_one,
     sum_two,
     scaled_one,
@@ -593,7 +607,7 @@
     rate_one, rate_two = dilations[0], dilations[1]
     half = cot_far.shape[0]
     inside = slice(DMAX, DMAX + tokens)
-    for target in (field, wide_cot, wide_pre, grad_pre, second):
+    for target in (field, wide_cot, wide_pre, grad_pre):
         clear_border(target, tokens)
 
     several = 8
@@ -626,10 +640,9 @@
     def back_two(step):
         first = step * chunk
         rows = pl.ds(DMAX + first, chunk)
-        before_act = pre[pl.ds(first, chunk)]
+        before_act = pre[rows, inside, :]
         sigma = sigmoid(before_act)
         second_in = before_act * sigma
-        second[rows, inside, :] = second_in
         factor = sigma * (1.0 + before_act * (1.0 - sigma))
         turned = second_in.reshape(size, channels).astype(jnp.bfloat16).T
         shifted = taps(wide_cot, first, chunk, -rate_two)
@@ -664,16 +677,15 @@
         if step >= 1:
             spread_pre(step - 1)
         back_two(step)
+    spread_pre(steps - 1)
     for row in range(3):
         finish(sum_two, scaled_two, grad_two, row)
-    for step in range(max(steps - 3, 0), steps - 2):
+    for step in range(max(steps - 3, 0), steps - 1):
         back_one(step)
-    spread_pre(steps - 1)
-    back_one(steps - 2)
 
     spot = (row_place * height, col_place * breadth, height, breadth)
     second_pre = matmul(
-        windows(second, rate_two, *spot), two[...].reshape(9 * channels, channels)
+        windows(pre, rate_two, *spot, silu), two[...].reshape(9 * channels, channels)
     )
     output[...] = (mine[...] + second_pre).astype(jnp.bfloat16)
     one_rows = [one[tap] for tap in range(9)]
@@ -776,13 +788,13 @@
         functools.partial(forward_kernel, plan),
         in_specs=[in_smem] + [in_vmem] * 11,
         out_specs=[in_vmem] * 4,
-        out_shape=shapes(((tokens, tokens, channels), f32), flat, stat, stat),
+        out_shape=shapes(((line, line, channels), f32), flat, stat, stat),
         scratch_shapes=[pltpu.VMEM(*side), both, both, alone, alone, alone]
         + [turned] * 2
         + [pltpu.VMEM((hidden * (2 * height + PITCH), chips * tokens), f32)]
         + [pltpu.VMEM((2 * height // 8, chips, 8, tokens, hidden), bf16)]
         + [pltpu.VMEM(rows, f32), padded]
-        + [pltpu.VMEM((3, line, tokens, channels), f32)],
+        + [pltpu.VMEM((3, line, tokens, channels), bf16)],
         compiler_params=pltpu.CompilerParams(vmem_limit_bytes=FORWARD_VMEM),
         cost_estimate=pl.CostEstimate(
             flops=tokens * tokens * channels * 40 * hidden,
@@ -808,7 +820,7 @@
             ((9, channels, channels), f32),
             ((9, channels, channels), f32),
         ),
-        scratch_shapes=[padded, tripled, tripled, bordered, bordered, sums, sums]
+        scratch_shapes=[padded, tripled, tripled, bordered, sums, sums]
         + [pltpu.VMEM((9, channels, channels), f32)] * 2
         + [pltpu.SemaphoreType.DMA((6,))],
         compiler_params=pltpu.CompilerParams(vmem_limit_bytes=BACKWARD_VMEM),

time: 47.1 us -> 47.3 us (level)
  transfers between devices with their start and end apart: 10 -> 10, of which waited for: 5 -> 5; matrix products, arithmetic and copies ran while one was open for 4% -> 4% of each run, Pallas kernels for 24% -> 25%
where the time goes in v17:
time: 47.3 us; the launch traced here: 47.1 us
  Pallas kernels  21 us (44%)
  starting transfers between devices  17.3 us (37%)
  waiting for transfers between devices  5.32 us (11%)
  other arithmetic  2.53 us (5%)
  between operations  0.95 us (2%)
    ppermute x10, starting transfers between devices, exchange(): lax.ppermute(held, axis, [(i, i ^ distance) for i in range(lax.axis_size(...  17.3 us
    pallas_call x1, Pallas kernels, replicated(): pl.pallas_call(functools.partial(forward_kernel, plan), in_specs=[in_smem...  9.75 us
    pallas_call x1, Pallas kernels, replicated(): pl.pallas_call(functools.partial(backward_kernel, plan), in_specs=[in_sme...  9.29 us
    ppermute x10, waiting for transfers between devices, exchange(): lax.ppermute(held, axis, [(i, i ^ distance) for i in range(lax.axis_size(...  5.32 us
    pallas_call x1, Pallas kernels, replicated(): pl.pallas_call(functools.partial(near_kernel, plan), in_specs=[in_vmem] *...  1.91 us
  transfers between devices with their start and end apart: 10, of which 5 were waited for; matrix products, arithmetic and copies ran while one was open for 4% of the time, Pallas kernels for 25%

profile of v17, /device:TPU:0, one launch (start us, length us, event | category | flops | bytes accessed | tf_op | source)
XLA Modules:
  0.0 47.1 jit_solution(6859386359464024714)
XLA Ops:
  0.6 0.0 copy-start.2
  0.6 0.0 copy-start.3
  0.7 0.0 copy-start.1
  0.7 0.0 copy-start.4
  0.7 0.0 copy-start
  0.7 0.9 %fusion = bf16[1,144,128]{2,1,0:T(8,128)(2,1)S(1)} fusion(s32[8,16]{1,0:T(8,128)} %bitcast.11, s32[8,16]{1,0:T(8,128)} %bitcast.12, bf16[128,128]{1,0:T(8,128)(2,1)} %bitcast.9), kind=kLoop, calls=%fused_computation.8 | loop fusion | flops 92160 | bytes 70656 | tf_op jit(solution)/shard_map/broadcast_in_dim | solution.py:747
  1.6 4.0 %collective-permute-start.4 = (bf16[1,144,128]{2,1,0:T(8,128)(2,1)S(1)}, bf16[1,144,128]{2,1,0:T(8,128)(2,1)S(1)}, u32[]{:S(2)}, u32[]{:S(2)}) collective-permute-start(bf16[1,144,128]{2,1,0:T(8,128)(2,1)S(1)} %fusion), channel_id=1, source_target_pairs={{0,4},{1,5},{2,6},{3,7},{4,0},{5,1},{6,2},{7,3},{8,12},{9,13},{10,... | collective-permute-start | bytes 110600 | tf_op jit(solution)/shard_map/ppermute | solution.py:186
  5.7 1.5 %collective-permute-start = (bf16[1,128,128]{2,1,0:T(8,128)(2,1)}, bf16[1,128,128]{2,1,0:T(8,128)(2,1)S(1)}, u32[]{:S(2)}, u32[]{:S(2)}) collective-permute-start(bf16[1,128,128]{2,1,0:T(8,128)(2,1)} %bitcast.10), channel_id=1, source_target_pairs={{0,16},{8,24},{16,0},{24,8},{1,17},{9,25},{17,1},{25,9},{2,18},{10... | collective-permute-start | bytes 98312 | tf_op jit(solution)/shard_map/ppermute | solution.py:186
  7.1 0.8 %broadcast_maximum_fusion = bf16[1,128,128]{2,1,0:T(8,128)(2,1)S(1)} fusion(bf16[16,8,128]{2,1,0:T(8,128)(2,1)} %param.19), kind=kLoop, calls=%fused_computation.9 | loop fusion | flops 16384 | bytes 65536 | tf_op jit(solution)/shard_map/max | solution.py:749
  7.9 0.0 collective-permute-done.4
  8.0 1.6 %collective-permute-start.5 = (bf16[2,144,128]{2,1,0:T(8,128)(2,1)S(1)}, bf16[2,144,128]{2,1,0:T(8,128)(2,1)S(1)}, u32[]{:S(2)}, u32[]{:S(2)}) collective-permute-start(bf16[2,144,128]{2,1,0:T(8,128)(2,1)S(1)} %pad_maximum_fusion.5), channel_id=1, source_target_pairs={{0,2},{1,3},{2,0},{3,1},{4,6},{5,7},{6,4},{7,5},{8,10},{9,11},{10,... | collective-permute-start | bytes 221192 | tf_op jit(solution)/shard_map/ppermute | solution.py:186
  9.6 0.2 collective-permute-done
  9.8 2.7 %collective-permute-start.1 = (bf16[2,128,128]{2,1,0:T(8,128)(2,1)S(1)}, bf16[2,128,128]{2,1,0:T(8,128)(2,1)S(1)}, u32[]{:S(2)}, u32[]{:S(2)}) collective-permute-start(bf16[2,128,128]{2,1,0:T(8,128)(2,1)S(1)} %pad_maximum_fusion.6), channel_id=1, source_target_pairs={{0,4},{1,5},{2,6},{3,7},{4,0},{5,1},{6,2},{7,3},{8,12},{9,13},{10,... | collective-permute-start | bytes 196616 | tf_op jit(solution)/shard_map/ppermute | solution.py:186
  12.5 0.6 %collective-permute-done.5 = bf16[2,144,128]{2,1,0:T(8,128)(2,1)S(1)} collective-permute-done((bf16[2,144,128]{2,1,0:T(8,128)(2,1)S(1)}, bf16[2,144,128]{2,1,0:T(8,128)(2,1)S(1)}, u32[]{:S(2)}, u32[]{:S(2)}) %collective-permute-start.5) | collective-permute-done | bytes 73760 | tf_op jit(solution)/shard_map/ppermute | solution.py:186
  13.1 1.8 %collective-permute-start.6 = (bf16[4,144,128]{2,1,0:T(8,128)(2,1)S(1)}, bf16[4,144,128]{2,1,0:T(8,128)(2,1)S(1)}, u32[]{:S(2)}, u32[]{:S(2)}) collective-permute-start(bf16[4,144,128]{2,1,0:T(8,128)(2,1)S(1)} %pad_maximum_fusion.3), channel_id=1, source_target_pairs={{0,1},{1,0},{2,3},{3,2},{4,5},{5,4},{6,7},{7,6},{8,9},{9,8},{10,11... | collective-permute-start | bytes 442376 | tf_op jit(solution)/shard_map/ppermute | solution.py:186
  14.9 0.1 collective-permute-done.1
  15.0 1.6 %collective-permute-start.2 = (bf16[4,128,128]{2,1,0:T(8,128)(2,1)S(1)}, bf16[4,128,128]{2,1,0:T(8,128)(2,1)S(1)}, u32[]{:S(2)}, u32[]{:S(2)}) collective-permute-start(bf16[4,128,128]{2,1,0:T(8,128)(2,1)S(1)} %pad_maximum_fusion.4), channel_id=1, source_target_pairs={{0,2},{1,3},{2,0},{3,1},{4,6},{5,7},{6,4},{7,5},{8,10},{9,11},{10,... | collective-permute-start | bytes 393224 | tf_op jit(solution)/shard_map/ppermute | solution.py:186
  16.7 1.7 %collective-permute-done.6 = bf16[4,144,128]{2,1,0:T(8,128)(2,1)S(1)} collective-permute-done((bf16[4,144,128]{2,1,0:T(8,128)(2,1)S(1)}, bf16[4,144,128]{2,1,0:T(8,128)(2,1)S(1)}, u32[]{:S(2)}, u32[]{:S(2)}) %collective-permute-start.6) | collective-permute-done | bytes 147488 | tf_op jit(solution)/shard_map/ppermute | solution.py:186
  18.4 1.8 %collective-permute-start.7 = (bf16[8,144,128]{2,1,0:T(8,128)(2,1)S(1)}, bf16[8,144,128]{2,1,0:T(8,128)(2,1)S(1)}, u32[]{:S(2)}, u32[]{:S(2)}) collective-permute-start(bf16[8,144,128]{2,1,0:T(8,128)(2,1)S(1)} %pad_maximum_fusion.1), channel_id=1, source_target_pairs={{0,16},{8,24},{16,0},{24,8},{1,17},{9,25},{17,1},{25,9},{2,18},{10... | collective-permute-start | bytes 884744 | tf_op jit(solution)/shard_map/ppermute | solution.py:186
  20.1 0.7 %broadcast_clamp_fusion.dilations = s32[2]{0:T(128)S(1)} fusion(s32[2]{0:T(128)} %param.13), kind=kLoop, calls=%fused_computation.12 | loop fusion | flops 2 | bytes 16 | tf_op jit(solution)/shard_map/jit(clip)/min | solution.py:750
  20.8 0.0 collective-permute-done.2
  20.8 1.6 %collective-permute-start.3 = (bf16[8,128,128]{2,1,0:T(8,128)(2,1)S(1)}, bf16[8,128,128]{2,1,0:T(8,128)(2,1)S(1)}, u32[]{:S(2)}, u32[]{:S(2)}) collective-permute-start(bf16[8,128,128]{2,1,0:T(8,128)(2,1)S(1)} %pad_maximum_fusion.2), channel_id=1, source_target_pairs={{0,1},{1,0},{2,3},{3,2},{4,5},{5,4},{6,7},{7,6},{8,9},{9,8},{10,11... | collective-permute-start | bytes 786440 | tf_op jit(solution)/shard_map/ppermute | solution.py:186
  22.4 2.7 %collective-permute-done.7 = bf16[8,144,128]{2,1,0:T(8,128)(2,1)S(1)} collective-permute-done((bf16[8,144,128]{2,1,0:T(8,128)(2,1)S(1)}, bf16[8,144,128]{2,1,0:T(8,128)(2,1)S(1)}, u32[]{:S(2)}, u32[]{:S(2)}) %collective-permute-start.7) | collective-permute-done | bytes 294944 | tf_op jit(solution)/shard_map/ppermute | solution.py:186
  25.2 0.1 pad_maximum_fusion.near
  25.2 0.1 collective-permute-start.9
  25.3 0.0 copy-done.2
  25.3 0.0 copy-done.3
  25.3 0.0 copy-done.1
  25.4 1.9 %shard_map.129 = (bf16[128,16,128]{2,1,0:T(8,128)(2,1)S(1)}, bf16[128,16,128]{2,1,0:T(8,128)(2,1)S(1)}, bf16[128,16,128]{2,1,0:T(8,128)(2,1)S(1)}, bf16[2,16,64,...) custom-call(bf16[16,144,128]{2,1,0:T(8,128)(2,1)S(1)} %pad_maximum_f, ...), custom_call_target="tpu_custom_call" | custom-call | flops 335544320 | bytes 4194304 | tf_op jit(solution)/shard_map/pallas_call | solution.py:762
  27.3 0.0 collective-permute-done.3
  27.3 0.6 %collective-permute-start.8 = (bf16[16,128,128]{2,1,0:T(8,128)(2,1)S(1)}, bf16[16,128,128]{2,1,0:T(8,128)(2,1)S(1)}, u32[]{:S(2)}, u32[]{:S(2)}) collective-permute-start(bf16[16,128,128]{2,1,0:T(8,128)(2,1)S(1)} %constant_dynamic-update-slice_fusion.cot_near), channel_id=1, source_target_pairs={{0,8},{8,0},{16,24},{24,16},{1,9},{9,1},{17,25},{25,17},{2,10},{10... | collective-permute-start | bytes 1572872 | tf_op jit(solution)/shard_map/ppermute | solution.py:186
  27.9 0.0 collective-permute-done.9.far
  27.9 0.0 copy-done.4
  27.9 0.0 copy-done
  27.9 9.8 %shard_map.130 = (f32[80,80,128]{2,1,0:T(8,128)S(1)}, bf16[128,4096]{1,0:T(8,128)(2,1)S(1)}, f32[128,128]{1,0:T(8,128)S(1)}, f32[128,128]{1,0:T(8,128)S(1)}) custom-call(s32[2]{0:T(128)S(1)} %broadcast_clamp_fusion.dilations, bf16[16,144,128]{2,1,0:T(8,128)(2,1)S(1)} %collective-permute-done.9.far, bf16[128,512]{1,0:T(8,128)(2,1)S(1)} %copy-done.2, ...), custom_call_target="tpu_custom_call" | custom-call | flops 2684354560 | bytes 20971520 | tf_op jit(solution)/shard_map/pallas_call | solution.py:787
  37.7 0.0 collective-permute-done.8.cot_far
  37.7 9.3 %shard_map.131 = (bf16[128,128]{1,0:T(8,128)(2,1)}, bf16[128,128]{1,0:T(8,128)(2,1)}, f32[9,128,128]{2,1,0:T(8,128)}, f32[9,128,128]{2,1,0:T(8,128)}) custom-call(s32[2]{0:T(128)S(1)} %broadcast_clamp_fusion.dilations, bf16[16,128,128]{2,1,0:T(8,128)(2,1)S(1)} %constant_dynamic-update-slice_fusion.cot_near, ...), custom_call_target="tpu_custom_call" | custom-call | tf_op jit(solution)/shard_map/pallas_call | solution.py:813
  (8 shorter events, 0.2 us)
Async XLA Ops:
  0.6 24.7 %copy-start.2 = (bf16[128,512]{1,0:T(8,128)(2,1)S(1)}, bf16[128,512]{1,0:T(8,128)(2,1)}, u32[]{:S(2)}) copy-start(bf16[128,512]{1,0:T(8,128)(2,1)} %w_proj.3) | copy-start | bytes 393220
  0.6 24.7 %copy-start.3 = (bf16[128,128]{1,0:T(8,128)(2,1)S(1)}, bf16[128,128]{1,0:T(8,128)(2,1)}, u32[]{:S(2)}) copy-start(bf16[128,128]{1,0:T(8,128)(2,1)} %w_gate.3) | copy-start | bytes 98308
  0.7 24.7 %copy-start.1 = (bf16[9,128,128]{2,1,0:T(8,128)(2,1)S(1)}, bf16[9,128,128]{2,1,0:T(8,128)(2,1)}, u32[]{:S(2)}) copy-start(bf16[9,128,128]{2,1,0:T(8,128)(2,1)} %two.1) | copy-start | bytes 884740
  0.7 27.2 %copy-start.4 = (bf16[128,128]{1,0:T(8,128)(2,1)S(1)}, bf16[128,128]{1,0:T(8,128)(2,1)}, u32[]{:S(2)}) copy-start(bf16[128,128]{1,0:T(8,128)(2,1)} %w_out.1) | copy-start | bytes 98308
  0.7 27.2 %copy-start = (bf16[9,128,128]{2,1,0:T(8,128)(2,1)S(1)}, bf16[9,128,128]{2,1,0:T(8,128)(2,1)}, u32[]{:S(2)}) copy-start(bf16[9,128,128]{2,1,0:T(8,128)(2,1)} %one.3) | copy-start | bytes 884740
  1.6 6.4 %collective-permute-start.4 = (bf16[1,144,128]{2,1,0:T(8,128)(2,1)S(1)}, bf16[1,144,128]{2,1,0:T(8,128)(2,1)S(1)}, u32[]{:S(2)}, u32[]{:S(2)}) collective-permute-start(bf16[1,144,128]{2,1,0:T(8,128)(2,1)S(1)} %fusion), channel_id=1, source_target_pairs={{0,4},{1,5},{2,6},{3,7},{4,0},{5,1},{6,2},{7,3},{8,12},{9,13},{10,... | collective-permute-start | bytes 110600 | tf_op jit(solution)/shard_map/ppermute | solution.py:186
  5.7 4.1 %collective-permute-start = (bf16[1,128,128]{2,1,0:T(8,128)(2,1)}, bf16[1,128,128]{2,1,0:T(8,128)(2,1)S(1)}, u32[]{:S(2)}, u32[]{:S(2)}) collective-permute-start(bf16[1,128,128]{2,1,0:T(8,128)(2,1)} %bitcast.10), channel_id=1, source_target_pairs={{0,16},{8,24},{16,0},{24,8},{1,17},{9,25},{17,1},{25,9},{2,18},{10... | collective-permute-start | bytes 98312 | tf_op jit(solution)/shard_map/ppermute | solution.py:186
  8.0 5.1 %collective-permute-start.5 = (bf16[2,144,128]{2,1,0:T(8,128)(2,1)S(1)}, bf16[2,144,128]{2,1,0:T(8,128)(2,1)S(1)}, u32[]{:S(2)}, u32[]{:S(2)}) collective-permute-start(bf16[2,144,128]{2,1,0:T(8,128)(2,1)S(1)} %pad_maximum_fusion.5), channel_id=1, source_target_pairs={{0,2},{1,3},{2,0},{3,1},{4,6},{5,7},{6,4},{7,5},{8,10},{9,11},{10,... | collective-permute-start | bytes 221192 | tf_op jit(solution)/shard_map/ppermute | solution.py:186
  9.8 5.2 %collective-permute-start.1 = (bf16[2,128,128]{2,1,0:T(8,128)(2,1)S(1)}, bf16[2,128,128]{2,1,0:T(8,128)(2,1)S(1)}, u32[]{:S(2)}, u32[]{:S(2)}) collective-permute-start(bf16[2,128,128]{2,1,0:T(8,128)(2,1)S(1)} %pad_maximum_fusion.6), channel_id=1, source_target_pairs={{0,4},{1,5},{2,6},{3,7},{4,0},{5,1},{6,2},{7,3},{8,12},{9,13},{10,... | collective-permute-start | bytes 196616 | tf_op jit(solution)/shard_map/ppermute | solution.py:186
  13.1 5.2 %collective-permute-start.6 = (bf16[4,144,128]{2,1,0:T(8,128)(2,1)S(1)}, bf16[4,144,128]{2,1,0:T(8,128)(2,1)S(1)}, u32[]{:S(2)}, u32[]{:S(2)}) collective-permute-start(bf16[4,144,128]{2,1,0:T(8,128)(2,1)S(1)} %pad_maximum_fusion.3), channel_id=1, source_target_pairs={{0,1},{1,0},{2,3},{3,2},{4,5},{5,4},{6,7},{7,6},{8,9},{9,8},{10,11... | collective-permute-start | bytes 442376 | tf_op jit(solution)/shard_map/ppermute | solution.py:186
  15.0 5.8 %collective-permute-start.2 = (bf16[4,128,128]{2,1,0:T(8,128)(2,1)S(1)}, bf16[4,128,128]{2,1,0:T(8,128)(2,1)S(1)}, u32[]{:S(2)}, u32[]{:S(2)}) collective-permute-start(bf16[4,128,128]{2,1,0:T(8,128)(2,1)S(1)} %pad_maximum_fusion.4), channel_id=1, source_target_pairs={{0,2},{1,3},{2,0},{3,1},{4,6},{5,7},{6,4},{7,5},{8,10},{9,11},{10,... | collective-permute-start | bytes 393224 | tf_op jit(solution)/shard_map/ppermute | solution.py:186
  18.4 6.8 %collective-permute-start.7 = (bf16[8,144,128]{2,1,0:T(8,128)(2,1)S(1)}, bf16[8,144,128]{2,1,0:T(8,128)(2,1)S(1)}, u32[]{:S(2)}, u32[]{:S(2)}) collective-permute-start(bf16[8,144,128]{2,1,0:T(8,128)(2,1)S(1)} %pad_maximum_fusion.1), channel_id=1, source_target_pairs={{0,16},{8,24},{16,0},{24,8},{1,17},{9,25},{17,1},{25,9},{2,18},{10... | collective-permute-start | bytes 884744 | tf_op jit(solution)/shard_map/ppermute | solution.py:186
  20.8 6.4 %collective-permute-start.3 = (bf16[8,128,128]{2,1,0:T(8,128)(2,1)S(1)}, bf16[8,128,128]{2,1,0:T(8,128)(2,1)S(1)}, u32[]{:S(2)}, u32[]{:S(2)}) collective-permute-start(bf16[8,128,128]{2,1,0:T(8,128)(2,1)S(1)} %pad_maximum_fusion.2), channel_id=1, source_target_pairs={{0,1},{1,0},{2,3},{3,2},{4,5},{5,4},{6,7},{7,6},{8,9},{9,8},{10,11... | collective-permute-start | bytes 786440 | tf_op jit(solution)/shard_map/ppermute | solution.py:186
  25.2 2.7 %collective-permute-start.9 = (bf16[16,144,128]{2,1,0:T(8,128)(2,1)S(1)}, bf16[16,144,128]{2,1,0:T(8,128)(2,1)S(1)}, u32[]{:S(2)}, u32[]{:S(2)}) collective-permute-start(bf16[16,144,128]{2,1,0:T(8,128)(2,1)S(1)} %pad_maximum_fusion.near), channel_id=1, source_target_pairs={{0,8},{8,0},{16,24},{24,16},{1,9},{9,1},{17,25},{25,17},{2,10},{10... | collective-permute-start | bytes 1769480 | tf_op jit(solution)/shard_map/ppermute | solution.py:186
  27.3 10.3 %collective-permute-start.8 = (bf16[16,128,128]{2,1,0:T(8,128)(2,1)S(1)}, bf16[16,128,128]{2,1,0:T(8,128)(2,1)S(1)}, u32[]{:S(2)}, u32[]{:S(2)}) collective-permute-start(bf16[16,128,128]{2,1,0:T(8,128)(2,1)S(1)} %constant_dynamic-update-slice_fusion.cot_near), channel_id=1, source_target_pairs={{0,8},{8,0},{16,24},{24,16},{1,9},{9,1},{17,25},{25,17},{2,10},{10... | collective-permute-start | bytes 1572872 | tf_op jit(solution)/shard_map/ppermute | solution.py:186

commit v18 on v16

--- a/solution.py
+++ b/solution.py
@@ -617,11 +617,8 @@
     size = chunk * tokens
     steps = tokens // chunk
 
-    def spread_cot(step, carry):
+    def spread_cot(step):
         spread(field, pl.ds(step * chunk, chunk), 0, -rate_two, wide_cot)
-        return carry
-
-    lax.fori_loop(0, steps, spread_cot, 0)
 
     def back_two(step):
         first = step * chunk
@@ -658,18 +655,21 @@
         copies.append(copy)
 
     copies = []
+    for step in range(min(2, steps)):
+        spread_cot(step)
     for step in range(steps):
         if step >= 3:
             back_one(step - 3)
         if step >= 1:
             spread_pre(step - 1)
         back_two(step)
+        if step + 2 < steps:
+            spread_cot(step + 2)
+    spread_pre(steps - 1)
     for row in range(3):
         finish(sum_two, scaled_two, grad_two, row)
-    for step in range(max(steps - 3, 0), steps - 2):
+    for step in range(max(steps - 3, 0), steps - 1):
         back_one(step)
-    spread_pre(steps - 1)
-    back_one(steps - 2)
 
     spot = (row_place * height, col_place * breadth, height, breadth)
     second_pre = matmul(

time: 47.1 us -> 47 us (level)
  no operation moved by 1% of the time
where the time goes in v18:
time: 47 us; the launch traced here: 46.8 us
  Pallas kernels  20.7 us (44%)
  starting transfers between devices  17.3 us (37%)
  waiting for transfers between devices  5.31 us (11%)
  other arithmetic  2.52 us (5%)
  between operations  0.93 us (2%)
    ppermute x10, starting transfers between devices, exchange(): lax.ppermute(held, axis, [(i, i ^ distance) for i in range(lax.axis_size(...  17.3 us
    pallas_call x1, Pallas kernels, replicated(): pl.pallas_call(functools.partial(forward_kernel, plan), in_specs=[in_smem...  9.47 us
    pallas_call x1, Pallas kernels, replicated(): pl.pallas_call(functools.partial(backward_kernel, plan), in_specs=[in_sme...  9.3 us
    ppermute x10, waiting for transfers between devices, exchange(): lax.ppermute(held, axis, [(i, i ^ distance) for i in range(lax.axis_size(...  5.31 us
    pallas_call x1, Pallas kernels, replicated(): pl.pallas_call(functools.partial(near_kernel, plan), in_specs=[in_vmem] *...  1.91 us
  transfers between devices with their start and end apart: 10, of which 5 were waited for; matrix products, arithmetic and copies ran while one was open for 4% of the time, Pallas kernels for 24%

profile of v18, /device:TPU:0, one launch (start us, length us, event | category | flops | bytes accessed | tf_op | source)
XLA Modules:
  0.0 46.8 jit_solution(4832081975675603735)
XLA Ops:
  0.6 0.0 copy-start.2
  0.6 0.0 copy-start.3
  0.7 0.0 copy-start.1
  0.7 0.9 %fusion = bf16[1,144,128]{2,1,0:T(8,128)(2,1)S(1)} fusion(s32[8,16]{1,0:T(8,128)} %bitcast.11, s32[8,16]{1,0:T(8,128)} %bitcast.12, bf16[128,128]{1,0:T(8,128)(2,1)} %bitcast.9), kind=kLoop, calls=%fused_computation.8 | loop fusion | flops 92160 | bytes 70656 | tf_op jit(solution)/shard_map/broadcast_in_dim | solution.py:735
  1.6 4.0 %collective-permute-start.4 = (bf16[1,144,128]{2,1,0:T(8,128)(2,1)S(1)}, bf16[1,144,128]{2,1,0:T(8,128)(2,1)S(1)}, u32[]{:S(2)}, u32[]{:S(2)}) collective-permute-start(bf16[1,144,128]{2,1,0:T(8,128)(2,1)S(1)} %fusion), channel_id=1, source_target_pairs={{0,4},{1,5},{2,6},{3,7},{4,0},{5,1},{6,2},{7,3},{8,12},{9,13},{10,... | collective-permute-start | bytes 110600 | tf_op jit(solution)/shard_map/ppermute | solution.py:186
  5.6 1.5 %collective-permute-start = (bf16[1,128,128]{2,1,0:T(8,128)(2,1)}, bf16[1,128,128]{2,1,0:T(8,128)(2,1)S(1)}, u32[]{:S(2)}, u32[]{:S(2)}) collective-permute-start(bf16[1,128,128]{2,1,0:T(8,128)(2,1)} %bitcast.10), channel_id=1, source_target_pairs={{0,16},{8,24},{16,0},{24,8},{1,17},{9,25},{17,1},{25,9},{2,18},{10... | collective-permute-start | bytes 98312 | tf_op jit(solution)/shard_map/ppermute | solution.py:186
  7.1 0.8 %broadcast_maximum_fusion = bf16[1,128,128]{2,1,0:T(8,128)(2,1)S(1)} fusion(bf16[16,8,128]{2,1,0:T(8,128)(2,1)} %param.19), kind=kLoop, calls=%fused_computation.9 | loop fusion | flops 16384 | bytes 65536 | tf_op jit(solution)/shard_map/max | solution.py:737
  7.9 0.0 collective-permute-done.4
  8.0 1.6 %collective-permute-start.5 = (bf16[2,144,128]{2,1,0:T(8,128)(2,1)S(1)}, bf16[2,144,128]{2,1,0:T(8,128)(2,1)S(1)}, u32[]{:S(2)}, u32[]{:S(2)}) collective-permute-start(bf16[2,144,128]{2,1,0:T(8,128)(2,1)S(1)} %pad_maximum_fusion.5), channel_id=1, source_target_pairs={{0,2},{1,3},{2,0},{3,1},{4,6},{5,7},{6,4},{7,5},{8,10},{9,11},{10,... | collective-permute-start | bytes 221192 | tf_op jit(solution)/shard_map/ppermute | solution.py:186
  9.6 0.2 collective-permute-done
  9.8 2.7 %collective-permute-start.1 = (bf16[2,128,128]{2,1,0:T(8,128)(2,1)S(1)}, bf16[2,128,128]{2,1,0:T(8,128)(2,1)S(1)}, u32[]{:S(2)}, u32[]{:S(2)}) collective-permute-start(bf16[2,128,128]{2,1,0:T(8,128)(2,1)S(1)} %pad_maximum_fusion.6), channel_id=1, source_target_pairs={{0,4},{1,5},{2,6},{3,7},{4,0},{5,1},{6,2},{7,3},{8,12},{9,13},{10,... | collective-permute-start | bytes 196616 | tf_op jit(solution)/shard_map/ppermute | solution.py:186
  12.5 0.6 %collective-permute-done.5 = bf16[2,144,128]{2,1,0:T(8,128)(2,1)S(1)} collective-permute-done((bf16[2,144,128]{2,1,0:T(8,128)(2,1)S(1)}, bf16[2,144,128]{2,1,0:T(8,128)(2,1)S(1)}, u32[]{:S(2)}, u32[]{:S(2)}) %collective-permute-start.5) | collective-permute-done | bytes 73760 | tf_op jit(solution)/shard_map/ppermute | solution.py:186
  13.1 1.8 %collective-permute-start.6 = (bf16[4,144,128]{2,1,0:T(8,128)(2,1)S(1)}, bf16[4,144,128]{2,1,0:T(8,128)(2,1)S(1)}, u32[]{:S(2)}, u32[]{:S(2)}) collective-permute-start(bf16[4,144,128]{2,1,0:T(8,128)(2,1)S(1)} %pad_maximum_fusion.3), channel_id=1, source_target_pairs={{0,1},{1,0},{2,3},{3,2},{4,5},{5,4},{6,7},{7,6},{8,9},{9,8},{10,11... | collective-permute-start | bytes 442376 | tf_op jit(solution)/shard_map/ppermute | solution.py:186
  14.9 0.1 collective-permute-done.1
  15.0 1.6 %collective-permute-start.2 = (bf16[4,128,128]{2,1,0:T(8,128)(2,1)S(1)}, bf16[4,128,128]{2,1,0:T(8,128)(2,1)S(1)}, u32[]{:S(2)}, u32[]{:S(2)}) collective-permute-start(bf16[4,128,128]{2,1,0:T(8,128)(2,1)S(1)} %pad_maximum_fusion.4), channel_id=1, source_target_pairs={{0,2},{1,3},{2,0},{3,1},{4,6},{5,7},{6,4},{7,5},{8,10},{9,11},{10,... | collective-permute-start | bytes 393224 | tf_op jit(solution)/shard_map/ppermute | solution.py:186
  16.6 1.7 %collective-permute-done.6 = bf16[4,144,128]{2,1,0:T(8,128)(2,1)S(1)} collective-permute-done((bf16[4,144,128]{2,1,0:T(8,128)(2,1)S(1)}, bf16[4,144,128]{2,1,0:T(8,128)(2,1)S(1)}, u32[]{:S(2)}, u32[]{:S(2)}) %collective-permute-start.6) | collective-permute-done | bytes 147488 | tf_op jit(solution)/shard_map/ppermute | solution.py:186
  18.3 1.8 %collective-permute-start.7 = (bf16[8,144,128]{2,1,0:T(8,128)(2,1)S(1)}, bf16[8,144,128]{2,1,0:T(8,128)(2,1)S(1)}, u32[]{:S(2)}, u32[]{:S(2)}) collective-permute-start(bf16[8,144,128]{2,1,0:T(8,128)(2,1)S(1)} %pad_maximum_fusion.1), channel_id=1, source_target_pairs={{0,16},{8,24},{16,0},{24,8},{1,17},{9,25},{17,1},{25,9},{2,18},{10... | collective-permute-start | bytes 884744 | tf_op jit(solution)/shard_map/ppermute | solution.py:186
  20.1 0.7 %broadcast_clamp_fusion.dilations = s32[2]{0:T(128)S(1)} fusion(s32[2]{0:T(128)} %param.13), kind=kLoop, calls=%fused_computation.12 | loop fusion | flops 2 | bytes 16 | tf_op jit(solution)/shard_map/jit(clip)/min | solution.py:738
  20.8 0.0 copy-start
  20.8 0.0 copy-start.4
  20.8 0.0 collective-permute-done.2
  20.8 1.6 %collective-permute-start.3 = (bf16[8,128,128]{2,1,0:T(8,128)(2,1)S(1)}, bf16[8,128,128]{2,1,0:T(8,128)(2,1)S(1)}, u32[]{:S(2)}, u32[]{:S(2)}) collective-permute-start(bf16[8,128,128]{2,1,0:T(8,128)(2,1)S(1)} %pad_maximum_fusion.2), channel_id=1, source_target_pairs={{0,1},{1,0},{2,3},{3,2},{4,5},{5,4},{6,7},{7,6},{8,9},{9,8},{10,11... | collective-permute-start | bytes 786440 | tf_op jit(solution)/shard_map/ppermute | solution.py:186
  22.4 2.7 %collective-permute-done.7 = bf16[8,144,128]{2,1,0:T(8,128)(2,1)S(1)} collective-permute-done((bf16[8,144,128]{2,1,0:T(8,128)(2,1)S(1)}, bf16[8,144,128]{2,1,0:T(8,128)(2,1)S(1)}, u32[]{:S(2)}, u32[]{:S(2)}) %collective-permute-start.7) | collective-permute-done | bytes 294944 | tf_op jit(solution)/shard_map/ppermute | solution.py:186
  25.1 0.1 pad_maximum_fusion.near
  25.2 0.1 collective-permute-start.9
  25.3 0.0 copy-done.2
  25.3 0.0 copy-done.3
  25.3 0.0 copy-done.1
  25.3 1.9 %shard_map.129 = (bf16[128,16,128]{2,1,0:T(8,128)(2,1)S(1)}, bf16[128,16,128]{2,1,0:T(8,128)(2,1)S(1)}, bf16[128,16,128]{2,1,0:T(8,128)(2,1)S(1)}, bf16[2,16,64,...) custom-call(bf16[16,144,128]{2,1,0:T(8,128)(2,1)S(1)} %pad_maximum_f, ...), custom_call_target="tpu_custom_call" | custom-call | flops 335544320 | bytes 4194304 | tf_op jit(solution)/shard_map/pallas_call | solution.py:750
  27.2 0.0 collective-permute-done.3
  27.3 0.6 %collective-permute-start.8 = (bf16[16,128,128]{2,1,0:T(8,128)(2,1)S(1)}, bf16[16,128,128]{2,1,0:T(8,128)(2,1)S(1)}, u32[]{:S(2)}, u32[]{:S(2)}) collective-permute-start(bf16[16,128,128]{2,1,0:T(8,128)(2,1)S(1)} %constant_dynamic-update-slice_fusion.cot_near), channel_id=1, source_target_pairs={{0,8},{8,0},{16,24},{24,16},{1,9},{9,1},{17,25},{25,17},{2,10},{10... | collective-permute-start | bytes 1572872 | tf_op jit(solution)/shard_map/ppermute | solution.py:186
  27.9 0.0 collective-permute-done.9.far
  27.9 0.0 copy-done
  27.9 0.0 copy-done.4
  27.9 9.5 %shard_map.130 = (f32[64,64,128]{2,1,0:T(8,128)S(1)}, bf16[128,4096]{1,0:T(8,128)(2,1)S(1)}, f32[128,128]{1,0:T(8,128)S(1)}, f32[128,128]{1,0:T(8,128)S(1)}) custom-call(s32[2]{0:T(128)S(1)} %broadcast_clamp_fusion.dilations, bf16[16,144,128]{2,1,0:T(8,128)(2,1)S(1)} %collective-permute-done.9.far, bf16[128,512]{1,0:T(8,128)(2,1)S(1)} %copy-done.2, ...), custom_call_target="tpu_custom_call" | custom-call | flops 2684354560 | bytes 20971520 | tf_op jit(solution)/shard_map/pallas_call | solution.py:775
  37.3 0.0 collective-permute-done.8.cot_far
  37.4 9.3 %shard_map.131 = (bf16[128,128]{1,0:T(8,128)(2,1)}, bf16[128,128]{1,0:T(8,128)(2,1)}, f32[9,128,128]{2,1,0:T(8,128)}, f32[9,128,128]{2,1,0:T(8,128)}) custom-call(s32[2]{0:T(128)S(1)} %broadcast_clamp_fusion.dilations, bf16[16,128,128]{2,1,0:T(8,128)(2,1)S(1)} %constant_dynamic-update-slice_fusion.cot_near, ...), custom_call_target="tpu_custom_call" | custom-call | tf_op jit(solution)/shard_map/pallas_call | solution.py:801
  (8 shorter events, 0.2 us)
Async XLA Ops:
  0.6 24.7 %copy-start.2 = (bf16[128,512]{1,0:T(8,128)(2,1)S(1)}, bf16[128,512]{1,0:T(8,128)(2,1)}, u32[]{:S(2)}) copy-start(bf16[128,512]{1,0:T(8,128)(2,1)} %w_proj.3) | copy-start | bytes 393220
  0.6 24.7 %copy-start.3 = (bf16[128,128]{1,0:T(8,128)(2,1)S(1)}, bf16[128,128]{1,0:T(8,128)(2,1)}, u32[]{:S(2)}) copy-start(bf16[128,128]{1,0:T(8,128)(2,1)} %w_gate.3) | copy-start | bytes 98308
  0.7 24.7 %copy-start.1 = (bf16[9,128,128]{2,1,0:T(8,128)(2,1)S(1)}, bf16[9,128,128]{2,1,0:T(8,128)(2,1)}, u32[]{:S(2)}) copy-start(bf16[9,128,128]{2,1,0:T(8,128)(2,1)} %two.1) | copy-start | bytes 884740
  1.6 6.4 %collective-permute-start.4 = (bf16[1,144,128]{2,1,0:T(8,128)(2,1)S(1)}, bf16[1,144,128]{2,1,0:T(8,128)(2,1)S(1)}, u32[]{:S(2)}, u32[]{:S(2)}) collective-permute-start(bf16[1,144,128]{2,1,0:T(8,128)(2,1)S(1)} %fusion), channel_id=1, source_target_pairs={{0,4},{1,5},{2,6},{3,7},{4,0},{5,1},{6,2},{7,3},{8,12},{9,13},{10,... | collective-permute-start | bytes 110600 | tf_op jit(solution)/shard_map/ppermute | solution.py:186
  5.6 4.1 %collective-permute-start = (bf16[1,128,128]{2,1,0:T(8,128)(2,1)}, bf16[1,128,128]{2,1,0:T(8,128)(2,1)S(1)}, u32[]{:S(2)}, u32[]{:S(2)}) collective-permute-start(bf16[1,128,128]{2,1,0:T(8,128)(2,1)} %bitcast.10), channel_id=1, source_target_pairs={{0,16},{8,24},{16,0},{24,8},{1,17},{9,25},{17,1},{25,9},{2,18},{10... | collective-permute-start | bytes 98312 | tf_op jit(solution)/shard_map/ppermute | solution.py:186
  8.0 5.1 %collective-permute-start.5 = (bf16[2,144,128]{2,1,0:T(8,128)(2,1)S(1)}, bf16[2,144,128]{2,1,0:T(8,128)(2,1)S(1)}, u32[]{:S(2)}, u32[]{:S(2)}) collective-permute-start(bf16[2,144,128]{2,1,0:T(8,128)(2,1)S(1)} %pad_maximum_fusion.5), channel_id=1, source_target_pairs={{0,2},{1,3},{2,0},{3,1},{4,6},{5,7},{6,4},{7,5},{8,10},{9,11},{10,... | collective-permute-start | bytes 221192 | tf_op jit(solution)/shard_map/ppermute | solution.py:186
  9.8 5.2 %collective-permute-start.1 = (bf16[2,128,128]{2,1,0:T(8,128)(2,1)S(1)}, bf16[2,128,128]{2,1,0:T(8,128)(2,1)S(1)}, u32[]{:S(2)}, u32[]{:S(2)}) collective-permute-start(bf16[2,128,128]{2,1,0:T(8,128)(2,1)S(1)} %pad_maximum_fusion.6), channel_id=1, source_target_pairs={{0,4},{1,5},{2,6},{3,7},{4,0},{5,1},{6,2},{7,3},{8,12},{9,13},{10,... | collective-permute-start | bytes 196616 | tf_op jit(solution)/shard_map/ppermute | solution.py:186
  13.1 5.2 %collective-permute-start.6 = (bf16[4,144,128]{2,1,0:T(8,128)(2,1)S(1)}, bf16[4,144,128]{2,1,0:T(8,128)(2,1)S(1)}, u32[]{:S(2)}, u32[]{:S(2)}) collective-permute-start(bf16[4,144,128]{2,1,0:T(8,128)(2,1)S(1)} %pad_maximum_fusion.3), channel_id=1, source_target_pairs={{0,1},{1,0},{2,3},{3,2},{4,5},{5,4},{6,7},{7,6},{8,9},{9,8},{10,11... | collective-permute-start | bytes 442376 | tf_op jit(solution)/shard_map/ppermute | solution.py:186
  15.0 5.8 %collective-permute-start.2 = (bf16[4,128,128]{2,1,0:T(8,128)(2,1)S(1)}, bf16[4,128,128]{2,1,0:T(8,128)(2,1)S(1)}, u32[]{:S(2)}, u32[]{:S(2)}) collective-permute-start(bf16[4,128,128]{2,1,0:T(8,128)(2,1)S(1)} %pad_maximum_fusion.4), channel_id=1, source_target_pairs={{0,2},{1,3},{2,0},{3,1},{4,6},{5,7},{6,4},{7,5},{8,10},{9,11},{10,... | collective-permute-start | bytes 393224 | tf_op jit(solution)/shard_map/ppermute | solution.py:186
  18.3 6.8 %collective-permute-start.7 = (bf16[8,144,128]{2,1,0:T(8,128)(2,1)S(1)}, bf16[8,144,128]{2,1,0:T(8,128)(2,1)S(1)}, u32[]{:S(2)}, u32[]{:S(2)}) collective-permute-start(bf16[8,144,128]{2,1,0:T(8,128)(2,1)S(1)} %pad_maximum_fusion.1), channel_id=1, source_target_pairs={{0,16},{8,24},{16,0},{24,8},{1,17},{9,25},{17,1},{25,9},{2,18},{10... | collective-permute-start | bytes 884744 | tf_op jit(solution)/shard_map/ppermute | solution.py:186
  20.8 7.1 %copy-start = (bf16[9,128,128]{2,1,0:T(8,128)(2,1)S(1)}, bf16[9,128,128]{2,1,0:T(8,128)(2,1)}, u32[]{:S(2)}) copy-start(bf16[9,128,128]{2,1,0:T(8,128)(2,1)} %one.3) | copy-start | bytes 884740
  20.8 7.1 %copy-start.4 = (bf16[128,128]{1,0:T(8,128)(2,1)S(1)}, bf16[128,128]{1,0:T(8,128)(2,1)}, u32[]{:S(2)}) copy-start(bf16[128,128]{1,0:T(8,128)(2,1)} %w_out.1) | copy-start | bytes 98308
  20.8 6.4 %collective-permute-start.3 = (bf16[8,128,128]{2,1,0:T(8,128)(2,1)S(1)}, bf16[8,128,128]{2,1,0:T(8,128)(2,1)S(1)}, u32[]{:S(2)}, u32[]{:S(2)}) collective-permute-start(bf16[8,128,128]{2,1,0:T(8,128)(2,1)S(1)} %pad_maximum_fusion.2), channel_id=1, source_target_pairs={{0,1},{1,0},{2,3},{3,2},{4,5},{5,4},{6,7},{7,6},{8,9},{9,8},{10,11... | collective-permute-start | bytes 786440 | tf_op jit(solution)/shard_map/ppermute | solution.py:186
  25.2 2.7 %collective-permute-start.9 = (bf16[16,144,128]{2,1,0:T(8,128)(2,1)S(1)}, bf16[16,144,128]{2,1,0:T(8,128)(2,1)S(1)}, u32[]{:S(2)}, u32[]{:S(2)}) collective-permute-start(bf16[16,144,128]{2,1,0:T(8,128)(2,1)S(1)} %pad_maximum_fusion.near), channel_id=1, source_target_pairs={{0,8},{8,0},{16,24},{24,16},{1,9},{9,1},{17,25},{25,17},{2,10},{10... | collective-permute-start | bytes 1769480 | tf_op jit(solution)/shard_map/ppermute | solution.py:186
  27.3 10.1 %collective-permute-start.8 = (bf16[16,128,128]{2,1,0:T(8,128)(2,1)S(1)}, bf16[16,128,128]{2,1,0:T(8,128)(2,1)S(1)}, u32[]{:S(2)}, u32[]{:S(2)}) collective-permute-start(bf16[16,128,128]{2,1,0:T(8,128)(2,1)S(1)} %constant_dynamic-update-slice_fusion.cot_near), channel_id=1, source_target_pairs={{0,8},{8,0},{16,24},{24,16},{1,9},{9,1},{17,25},{25,17},{2,10},{10... | collective-permute-start | bytes 1572872 | tf_op jit(solution)/shard_map/ppermute | solution.py:186
